TPU v7x, 128 devices: a whole 4x4x4 slice. The times are simulated.
128 devices in a mesh: dp: 2 (over core), node: 16 (over z, x), local: 4 (over y).
Axes of the slice: x: 4, y: 4, z: 4, core: 2. Of those that a mesh axis runs over, the one named last changes fastest.
Arguments:
- tokens: bfloat16 [16384, 3584], P(('dp', 'node', 'local')), parts along dimension 0, may hold values from -6 to 6
- gate_scores: float32 [16384, 4], P(('dp', 'node', 'local')), parts along dimension 0, may hold values from 0.1 to 1
- expert_ids: int32 [16384, 4], P(('dp', 'node', 'local')), parts along dimension 0, may hold values from 0 to 63, as said below
- w_gate: bfloat16 [64, 3584, 1024], P(('node', 'local')), may hold values from -0.09375 to 0.09375
- w_up: bfloat16 [64, 3584, 1024], P(('node', 'local')), may hold values from -0.09375 to 0.09375
- w_down: bfloat16 [64, 1024, 3584], P(('node', 'local')), may hold values from -0.1875 to 0.1875
Outputs:
- mixed: bfloat16 [16384, 3584], P(('dp', 'node', 'local')), parts along dimension 0
There are 2 independent parts, one for each index of `dp`. A program takes and returns all parts, laid end to end along the dimension named above; an argument that names none is the same for every part. Nothing has to cross between parts.
Inputs may be any that keep to these rules, and one draw needn't show every extreme that they name: `expert_ids`: expert e belongs to node group e // 4 and lives on the device of index e along node and local together. Each token names 4 different experts in exactly 2 different node groups, at least one in each. The 128 tokens of one device name every node group exactly 16 times, and in every node group one expert is named by all 16 of them, so no expert is named more than 16 times by the tokens of one device.
All inputs are finite; a program needn't handle non-finite values.
Results may differ from a plain program's by a relative error of at most 0.0075.
Values may be sent and summed in bfloat16 or wider, within the bound.
No kernel may reach another device: no remote copies, remote signals or barrier semaphores. Data moves between devices by JAX's collectives and lax.ppermute only.
A program may use at most 192 MiB of HBM per device.

v0:
```python
import jax
import jax.numpy as jnp
from jax import lax
from jax.sharding import PartitionSpec as P

MAXNODES = 2


def quantize(tokens):
    count_rows, width = tokens.shape
    tiles = tokens.astype(jnp.float32).reshape(count_rows, width // 128, 128)
    largest = jnp.max(jnp.abs(tiles), axis=-1)
    tile_scale = ((largest + 1e-06) / 448.0).astype(jnp.bfloat16)
    scale_wide = lax.optimization_barrier(tile_scale).astype(jnp.float32)
    quantized = (tiles / scale_wide[..., None]).astype(jnp.bfloat16)
    return (quantized.reshape(count_rows, width), tile_scale)


def restore(quantized, tile_scale):
    dims_all = quantized.shape
    tiles = quantized.reshape(dims_all[:-1] + (dims_all[-1] // 128, 128)).astype(jnp.float32)
    return (
        (tiles * tile_scale.astype(jnp.float32)[..., None]).reshape(dims_all).astype(jnp.bfloat16)
    )


def expert_rows(row_block, gate_matrix, up_matrix, down_matrix):
    gate_act = jnp.dot(row_block, gate_matrix, preferred_element_type=jnp.float32)
    up_act = jnp.dot(row_block, up_matrix, preferred_element_type=jnp.float32)
    hidden = (jax.nn.silu(gate_act) * up_act).astype(jnp.bfloat16)
    return jnp.dot(hidden, down_matrix, preferred_element_type=jnp.float32).astype(jnp.bfloat16)


def make_slots(chosen, weight, capacity):
    tok_count = chosen.shape[0]
    slot_rank = jnp.cumsum(chosen, axis=0) - chosen
    slot_pick = chosen[:, :, None] * (
        slot_rank[:, :, None] == jnp.arange(capacity, dtype=jnp.int32)
    ).astype(jnp.int32)
    slot_token = jnp.sum(slot_pick * jnp.arange(tok_count, dtype=jnp.int32)[:, None, None], axis=0)
    slot_gate = jnp.sum(slot_pick.astype(jnp.float32) * weight[:, :, None], axis=0)
    return (slot_token, slot_gate)


def per_device(tokens, gate_scores, expert_ids, w_gate, w_up, w_down):
    tok_count, width = tokens.shape
    quantized, tile_scale = quantize(tokens)
    gates = (2.5 * gate_scores / jnp.sum(gate_scores, axis=-1, keepdims=True)).astype(jnp.bfloat16)
    gate_wide = lax.optimization_barrier(gates).astype(jnp.float32)
    node_count = lax.axis_size("node")
    local_count = lax.axis_size("local")
    experts_all = node_count * local_count
    capacity = MAXNODES * tok_count // node_count
    gate_matrix = w_gate[0]
    up_matrix = w_up[0]
    down_matrix = w_down[0]
    expert_hits = (expert_ids[:, :, None] == jnp.arange(experts_all, dtype=jnp.int32)).astype(
        jnp.int32
    )
    expert_gate = jnp.sum(gate_wide[:, :, None] * expert_hits.astype(jnp.float32), axis=1)
    chosen = jnp.sum(expert_hits, axis=1)
    slot_token, slot_gate = make_slots(chosen, expert_gate, capacity)
    send_tiles = quantized[slot_token]
    send_scale = tile_scale[slot_token]
    arrived_tiles = lax.all_to_all(
        send_tiles, ("node", "local"), split_axis=0, concat_axis=0, tiled=True
    )
    arrived_scale = lax.all_to_all(
        send_scale, ("node", "local"), split_axis=0, concat_axis=0, tiled=True
    )
    row_block = restore(arrived_tiles, arrived_scale)
    result = expert_rows(row_block.reshape(-1, width), gate_matrix, up_matrix, down_matrix)
    returned = lax.all_to_all(
        result.reshape(row_block.shape), ("node", "local"), split_axis=0, concat_axis=0, tiled=True
    )
    values = returned.astype(jnp.float32) * slot_gate[..., None]
    mixed = jax.ops.segment_sum(
        values.reshape(-1, width), slot_token.reshape(-1), num_segments=tok_count
    )
    return mixed.astype(jnp.bfloat16)


def solution(mesh):
    in_specs = (
        P(("dp", "node", "local"), None),
        P(("dp", "node", "local"), None),
        P(("dp", "node", "local"), None),
        P(("node", "local"), None, None),
        P(("node", "local"), None, None),
        P(("node", "local"), None, None),
    )
    out_specs = P(("dp", "node", "local"), None)
    return jax.shard_map(
        per_device, mesh=mesh, in_specs=in_specs, out_specs=out_specs, check_vma=False
    )
```

profile of v0, /device:TPU:0, one launch (start us, length us, event | category | flops | bytes accessed | tf_op | source)
XLA Modules:
  0.0 321.6 jit_solution(5930006788894141087)
XLA Ops:
  0.0 0.7 convert_reduce_fusion
  0.7 0.1 copy.27
  0.8 0.2 reduce_window_sum.11
  1.0 0.1 copy.29
  1.1 1.2 fusion.10
  2.2 2.6 convert_abs_fusion
  4.9 0.0 copy-start
  4.9 1.9 copy.30
  6.8 0.1 reduce_max.9
  6.9 0.1 copy.32
  7.1 0.1 reshape.51
  7.1 3.2 gather_fusion.1
  10.4 0.9 reshape.78
  11.3 11.5 %all-to-all-start.1 = ((bf16[64,2,224]{2,1,0:T(2,128)(2,1)}), bf16[64,2,224]{2,1,0:T(2,128)(2,1)S(1)}, u32[]{:S(2)}, u32[]{:S(2)}) async-start(bf16[64,2,224]{2,1,0:T(2,128)(2,1)} %reshape.78), calls=%async_computation.1 | async-start | bytes 131072 | tf_op jit(solution)/shard_map/all_to_all | solution.py:68
  22.8 0.1 div.31
  22.9 1.7 copy.31
  24.6 0.0 copy-done
  24.6 1.7 fusion.7
  26.4 7.3 %gather_fusion = bf16[1024,3584]{1,0:T(8,128)(2,1)} fusion(bf16[128,3584]{1,0:T(8,128)(2,1)S(1)} %fusion.7, s32[1024]{0:T(1024)S(1)} %broadcast_clamp_fusion), kind=kCustom, calls=%fused_computation | custom fusion | bytes 14684160 | tf_op jit(solution)/shard_map/gather | solution.py:63
  33.7 0.0 all-to-all-done.1
  33.7 10.7 %all-to-all-start = ((bf16[64,16,3584]{2,1,0:T(8,128)(2,1)}), bf16[64,16,3584]{2,1,0:T(8,128)(2,1)}, u32[]{:S(2)}, u32[]{:S(2)}) async-start(bf16[64,16,3584]{2,1,0:T(8,128)(2,1)} %bitcast.25), calls=%async_computation | async-start | bytes 14680064 | tf_op jit(solution)/shard_map/all_to_all | solution.py:65
  44.5 0.2 reshape.79
  44.7 8.5 %mul.68 = f32[64,16,28,128]{3,2,1,0:T(8,128)} broadcast(bf16[64,16,28]{2,1,0:T(8,128)(2,1)S(1)} %reshape.79), dimensions={0,1,2} | broadcast | bytes 14737408 | tf_op jit(solution)/shard_map/mul | solution.py:23
  53.2 16.9 %mul.69 = f32[64,16,3584]{2,1,0:T(8,128)} reshape(f32[64,16,28,128]{3,2,1,0:T(8,128)} %mul.68) | data formatting | bytes 29360128 | tf_op jit(solution)/shard_map/mul | solution.py:23
  70.0 65.4 %all-to-all-done = bf16[64,16,3584]{2,1,0:T(8,128)(2,1)} async-done(((bf16[64,16,3584]{2,1,0:T(8,128)(2,1)}), bf16[64,16,3584]{2,1,0:T(8,128)(2,1)}, u32[]{:S(2)}, u32[]{:S(2)}) %all-to-all-start) | async-done | bytes 7340064 | tf_op jit(solution)/shard_map/all_to_all | solution.py:65
  135.5 0.0 slice-start
  135.5 8.2 %multiply_convert_fusion = bf16[64,16,3584]{2,1,0:T(8,128)(2,1)S(1)} fusion(f32[64,16,3584]{2,1,0:T(8,128)} %mul.69, bf16[64,16,3584]{2,1,0:T(8,128)(2,1)} %all-to-all-done), kind=kLoop, calls=%fused_computation.4 | loop fusion | flops 11010048 | bytes 29360128 | tf_op jit(solution)/shard_map/convert_element_type | solution.py:23
  143.7 0.0 slice-start.1
  143.7 0.0 slice-start.2
  143.7 10.1 %fusion.1 = f32[1024,1024]{1,0:T(8,128)S(1)} fusion(bf16[1024,3584]{1,0:T(8,128)(2,1)S(1)} %bitcast.27, bf16[1,3584,1024]{2,1,0:T(8,128)(2,1)} %param.10), kind=kOutput, calls=%fused_computation.7 | convolution fusion | flops 7516192768 | bytes 18874368 | tf_op jit(solution)/shard_map/dot_general | solution.py:29
  153.8 0.0 slice-done
  153.8 0.0 slice-done.1
  153.8 0.0 slice-start.3
  153.8 8.6 %multiply_convert_fusion.1 = bf16[1024,1024]{1,0:T(8,128)(2,1)S(1)} fusion(f32[1024,1024]{1,0:T(8,128)S(1)} %fusion.1, bf16[1024,3584]{1,0:T(8,128)(2,1)S(1)} %bitcast.28, bf16[1,3584,1024]{2,1,0:T(8,128)(2,1)S(1)} %bitcast.34), kind=kOutput, calls=%fused_computation.11 | convolution fusion | flops 7522484224 | bytes 20971520 | tf_op jit(solution)/shard_map/dot_general | solution.py:28
  162.4 0.0 slice-done.2
  162.4 0.0 slice-done.3
  162.5 9.8 %convolution_convert_fusion = bf16[1024,3584]{1,0:T(8,128)(2,1)} fusion(bf16[1024,1024]{1,0:T(8,128)(2,1)S(1)} %multiply_convert_fusion.1, bf16[1,1024,3584]{2,1,0:T(8,128)(2,1)S(1)} %bitcast.36), kind=kOutput, calls=%fused_computation.5 | convolution fusion | flops 7519862784 | bytes 16777216 | tf_op jit(solution)/shard_map/dot_general | solution.py:31
  172.3 0.0 copy-start.2
  172.3 0.0 copy-start.1
  172.3 15.8 %all-to-all-start.2 = ((bf16[64,16,3584]{2,1,0:T(8,128)(2,1)}), bf16[64,16,3584]{2,1,0:T(8,128)(2,1)}, u32[]{:S(2)}, u32[]{:S(2)}) async-start(bf16[64,16,3584]{2,1,0:T(8,128)(2,1)} %bitcast.29), calls=%async_computation.2 | async-start | bytes 14680064 | tf_op jit(solution)/shard_map/all_to_all | solution.py:73
  188.0 0.1 reshape.67
  188.1 0.0 copy-done.2
  188.2 0.0 copy-done.1
  188.2 0.2 fusion.12
  188.4 97.1 %all-to-all-done.2 = bf16[64,16,3584]{2,1,0:T(8,128)(2,1)} async-done(((bf16[64,16,3584]{2,1,0:T(8,128)(2,1)}), bf16[64,16,3584]{2,1,0:T(8,128)(2,1)}, u32[]{:S(2)}, u32[]{:S(2)}) %all-to-all-start.2) | async-done | bytes 7340064 | tf_op jit(solution)/shard_map/all_to_all | solution.py:73
  285.5 10.8 %convert_multiply_fusion = f32[64,16,3584]{2,1,0:T(8,128)} fusion(bf16[64,16,3584]{2,1,0:T(8,128)(2,1)} %all-to-all-done.2, f32[64,16]{1,0:T(8,128)S(1)} %fusion.12), kind=kLoop, calls=%fused_computation.3 | loop fusion | flops 7340032 | bytes 22024192 | tf_op jit(solution)/shard_map/mul | solution.py:76
  296.3 24.3 %scatter_custom_fusion = f32[128,3584]{1,0:T(8,128)S(1)} fusion(s32[1024]{0:T(1024)S(1)} %reshape.67, f32[1024,3584]{1,0:T(8,128)} %bitcast.26, f32[]{:T(128)} %constant.8.clone.1), kind=kCustom, calls=%fused_computation.15 | custom fusion | flops 3670016 | bytes 1835520 | tf_op jit(solution)/shard_map/scatter-add | solution.py:77
  320.6 1.0 convert_element_type.66
  (10 shorter events, 0.1 us)
Async XLA Ops:
  4.9 19.7 %copy-start = (bf16[128,3584]{1,0:T(8,128)(2,1)S(1)}, bf16[128,3584]{1,0:T(8,128)(2,1)}, u32[]{:S(2)}) copy-start(bf16[128,3584]{1,0:T(8,128)(2,1)} %param.6) | copy-start | bytes 2752516
  11.3 22.4 %all-to-all-start.1 = ((bf16[64,2,224]{2,1,0:T(2,128)(2,1)}), bf16[64,2,224]{2,1,0:T(2,128)(2,1)S(1)}, u32[]{:S(2)}, u32[]{:S(2)}) async-start(bf16[64,2,224]{2,1,0:T(2,128)(2,1)} %reshape.78), calls=%async_computation.1 | async-start | bytes 131072 | tf_op jit(solution)/shard_map/all_to_all | solution.py:68
  33.7 101.8 %all-to-all-start = ((bf16[64,16,3584]{2,1,0:T(8,128)(2,1)}), bf16[64,16,3584]{2,1,0:T(8,128)(2,1)}, u32[]{:S(2)}, u32[]{:S(2)}) async-start(bf16[64,16,3584]{2,1,0:T(8,128)(2,1)} %bitcast.25), calls=%async_computation | async-start | bytes 14680064 | tf_op jit(solution)/shard_map/all_to_all | solution.py:65
  135.5 18.3 %slice-start = ((s8[7340032]{0:T(1024)(128)(4,1)}), s8[4194304]{0:T(1024)(128)(4,1)S(1)}, s32[]{:S(2)}) async-start(s8[7340032]{0:T(1024)(128)(4,1)} %bitcast.33), calls=%async_computation.3 | async-start | bytes 8388608
  143.7 10.1 %slice-start.1 = ((s8[7340032]{0:T(1024)(128)(4,1)}), s8[3145728]{0:T(1024)(128)(4,1)S(1)}, s32[]{:S(2)}) async-start(s8[7340032]{0:T(1024)(128)(4,1)} %bitcast.33), calls=%async_computation.4 | async-start | bytes 6291456
  143.7 18.8 %slice-start.2 = ((s8[7340032]{0:T(1024)(128)(4,1)}), s8[4194304]{0:T(1024)(128)(4,1)S(1)}, s32[]{:S(2)}) async-start(s8[7340032]{0:T(1024)(128)(4,1)} %bitcast.35), calls=%async_computation.5 | async-start | bytes 8388608
  153.8 8.6 %slice-start.3 = ((s8[7340032]{0:T(1024)(128)(4,1)}), s8[3145728]{0:T(1024)(128)(4,1)S(1)}, s32[]{:S(2)}) async-start(s8[7340032]{0:T(1024)(128)(4,1)} %bitcast.35), calls=%async_computation.6 | async-start | bytes 6291456
  172.3 15.8 %copy-start.2 = (f32[128,4]{0,1:T(4,128)S(1)}, f32[128,4]{0,1:T(4,128)}, u32[]{:S(2)}) copy-start(f32[128,4]{0,1:T(4,128)} %param.7) | copy-start | bytes 6148
  172.3 15.9 %copy-start.1 = (s32[128,4]{0,1:T(4,128)S(1)}, s32[128,4]{0,1:T(4,128)}, u32[]{:S(2)}) copy-start(s32[128,4]{0,1:T(4,128)} %param.8) | copy-start | bytes 6148
  172.3 113.2 %all-to-all-start.2 = ((bf16[64,16,3584]{2,1,0:T(8,128)(2,1)}), bf16[64,16,3584]{2,1,0:T(8,128)(2,1)}, u32[]{:S(2)}, u32[]{:S(2)}) async-start(bf16[64,16,3584]{2,1,0:T(8,128)(2,1)} %bitcast.29), calls=%async_computation.2 | async-start | bytes 14680064 | tf_op jit(solution)/shard_map/all_to_all | solution.py:73
where the time goes:
time: 325 us; the launch traced here: 322 us
  waiting for transfers between devices  162 us (50%)
  other arithmetic  51.2 us (16%)
  local copies, waits for them, and re-layouts  41.2 us (13%)
  starting transfers between devices  38 us (12%)
  matrix products  28.5 us (9%)
    all_to_all x1, waiting for transfers between devices, per_device(): lax.all_to_all(result.reshape(row_block.shape), ('node', 'local'), split_...  97.1 us
    all_to_all x1, waiting for transfers between devices, per_device(): lax.all_to_all(send_tiles, ('node', 'local'), split_axis=0, concat_axis=0...  65.4 us
    mul x2, local copies, waits for them, and re-layouts, restore(): tiles * tile_scale.astype(jnp.float32)[..., None]  25.3 us
    scatter-add x1, other arithmetic, per_device(): jax.ops.segment_sum(values.reshape(-1, width), slot_token.reshape(-1), nu...  24.3 us
    all_to_all x1, starting transfers between devices, per_device(): lax.all_to_all(result.reshape(row_block.shape), ('node', 'local'), split_...  15.8 us
    all_to_all x1, starting transfers between devices, per_device(): lax.all_to_all(send_scale, ('node', 'local'), split_axis=0, concat_axis=0...  11.5 us
    mul x1, other arithmetic, per_device(): values = returned.astype(jnp.float32) * slot_gate[..., None]  10.8 us
    all_to_all x1, starting transfers between devices, per_device(): lax.all_to_all(send_tiles, ('node', 'local'), split_axis=0, concat_axis=0...  10.7 us
  transfers between devices with their start and end apart: 3, of which 2 were waited for; matrix products, arithmetic and copies ran while one was open for 11% of the time, Pallas kernels for 0%

commit v1 on v0

v1 whole, which is shorter than its diff:
```python
import functools

import jax
import jax.numpy as jnp
from jax import lax
from jax.experimental import pallas as pl
from jax.experimental.pallas import tpu as pltpu
from jax.sharding import PartitionSpec as P

LANES = 128
PIECE = 128
VMEM = 60 * 1024 * 1024


def slot_maps(ids_t, groups, per_group):
    slots, tokens = groups * per_group, ids_t.shape[1]
    slot = lax.broadcasted_iota(jnp.int32, (slots, tokens), 0)
    half_rows = per_group // 2
    half = slots // 2
    group = (slot % half) // half_rows
    rank = (slot // half) * half_rows + slot % half_rows
    named = jnp.zeros((slots, tokens), jnp.bool_)
    for k in range(ids_t.shape[0]):
        named = named | (ids_t[k : k + 1, :] // 4 == group)
    before = lax.broadcasted_iota(jnp.int32, (tokens, tokens), 0) < lax.broadcasted_iota(
        jnp.int32, (tokens, tokens), 1
    )
    earlier = jnp.dot(
        named.astype(jnp.bfloat16), before.astype(jnp.bfloat16), preferred_element_type=jnp.float32
    )
    mine = named & (earlier == rank.astype(jnp.float32))
    return mine, group


def prepare_kernel(locals_, groups, per_group, tok, scores_t, ids_t, out_a, out_b, pick):
    ids = ids_t[...]
    mine, group = slot_maps(ids, groups, per_group)
    onehot = mine.astype(jnp.bfloat16)
    pick[...] = onehot
    score = scores_t[...]
    total = score[0:1, :]
    for k in range(1, score.shape[0]):
        total = total + score[k : k + 1, :]
    gates = (2.5 * score / total).astype(jnp.bfloat16).astype(jnp.float32)
    width = tok.shape[1]
    lane = lax.broadcasted_iota(jnp.int32, (mine.shape[0], LANES), 1)
    meta = jnp.zeros((mine.shape[0], LANES), jnp.float32)
    for j in range(locals_):
        value = jnp.zeros(mine.shape, jnp.float32)
        for k in range(ids.shape[0]):
            value = value + jnp.where(
                mine & (ids[k : k + 1, :] == group * locals_ + j), gates[k : k + 1, :], 0.0
            )
        meta = jnp.where(lane == j, jnp.sum(value, axis=1, keepdims=True), meta)
    meta = meta.astype(jnp.bfloat16)
    half = mine.shape[0] // 2
    out_a[:, width : width + LANES] = meta[:half]
    out_b[:, width : width + LANES] = meta[half:]
    for j in range(width // LANES):
        cols = slice(j * LANES, (j + 1) * LANES)
        x = tok[:, cols].astype(jnp.float32)
        largest = jnp.max(jnp.abs(x), axis=1, keepdims=True)
        scale = ((largest + 1e-06) / 448.0).astype(jnp.bfloat16).astype(jnp.float32)
        quantized = (x / scale).astype(jnp.bfloat16).astype(jnp.float32)
        restored = (quantized * scale).astype(jnp.bfloat16)
        rows = jnp.dot(onehot, restored, preferred_element_type=jnp.float32).astype(jnp.bfloat16)
        out_a[:, cols] = rows[:half]
        out_b[:, cols] = rows[half:]


def prepare(tokens, gate_scores, expert_ids, groups, locals_):
    count, width = tokens.shape
    per_group = 2 * count // groups
    half = groups * per_group // 2
    return pl.pallas_call(
        functools.partial(prepare_kernel, locals_, groups, per_group),
        out_shape=[
            jax.ShapeDtypeStruct((half, width + LANES), jnp.bfloat16),
            jax.ShapeDtypeStruct((half, width + LANES), jnp.bfloat16),
            jax.ShapeDtypeStruct((2 * half, count), jnp.bfloat16),
        ],
        compiler_params=pltpu.CompilerParams(vmem_limit_bytes=VMEM),
        cost_estimate=pl.CostEstimate(flops=10**9, bytes_accessed=3 * 10**6, transcendentals=0),
    )(tokens, gate_scores.T, expert_ids.T)


def expert_kernel(blocks, local_ref, *refs):
    xs, (wg, wu, wd), outs = refs[:blocks], refs[blocks : blocks + 3], refs[blocks + 3 : 2 * blocks + 3]
    rows, acc = refs[2 * blocks + 3 :]
    step, steps = pl.program_id(0), pl.num_programs(0)
    width = rows.shape[1]
    piece = xs[0].shape[0]

    @pl.when(step == 0)
    def _():
        for b in range(blocks):
            rows[b * piece : (b + 1) * piece, :] = xs[b][:, :width]

    x = rows[...]
    gate = jnp.dot(x, wg[0], preferred_element_type=jnp.float32)
    up = jnp.dot(x, wu[0], preferred_element_type=jnp.float32)
    hidden = (gate / (1.0 + jnp.exp(-gate)) * up).astype(jnp.bfloat16)
    part = jnp.dot(hidden, wd[0], preferred_element_type=jnp.float32)

    @pl.when(step == 0)
    def _():
        acc[...] = part

    @pl.when((step > 0) & (step < steps - 1))
    def _():
        acc[...] += part

    @pl.when(step == steps - 1)
    def _():
        for b in range(blocks):
            meta = xs[b][:, width : width + LANES].astype(jnp.float32)
            lane = lax.broadcasted_iota(jnp.int32, meta.shape, 1)
            weight = jnp.sum(jnp.where(lane == local_ref[0], meta, 0.0), axis=1, keepdims=True)
            own = slice(b * piece, (b + 1) * piece)
            outs[b][...] = ((acc[own, :] + part[own, :]) * weight).astype(jnp.bfloat16)


def experts(xs, local, w_gate, w_up, w_down, tile=256):
    blocks = len(xs)
    piece, wide = xs[0].shape
    width, hidden = w_gate.shape[1:]
    return pl.pallas_call(
        functools.partial(expert_kernel, blocks),
        grid=(hidden // tile,),
        in_specs=[pl.BlockSpec(memory_space=pltpu.SMEM)]
        + [pl.BlockSpec((piece, wide), lambda i: (0, 0))] * blocks
        + [
            pl.BlockSpec((1, width, tile), lambda i: (0, 0, i)),
            pl.BlockSpec((1, width, tile), lambda i: (0, 0, i)),
            pl.BlockSpec((1, tile, width), lambda i: (0, i, 0)),
        ],
        out_specs=[pl.BlockSpec((piece, width), lambda i: (0, 0))] * blocks,
        out_shape=[jax.ShapeDtypeStruct((piece, width), jnp.bfloat16)] * blocks,
        scratch_shapes=[
            pltpu.VMEM((blocks * piece, width), jnp.bfloat16),
            pltpu.VMEM((blocks * piece, width), jnp.float32),
        ],
        compiler_params=pltpu.CompilerParams(
            vmem_limit_bytes=VMEM, dimension_semantics=("arbitrary",)
        ),
        cost_estimate=pl.CostEstimate(
            flops=6 * blocks * piece * width * hidden,
            bytes_accessed=6 * width * hidden,
            transcendentals=blocks * piece * hidden,
        ),
    )(local, *xs, w_gate, w_up, w_down)


def collect_kernel(pick, first, second, out):
    half = first.shape[0]
    dims = (((0,), (0,)), ((), ()))
    total = lax.dot_general(pick[:half, :], first[...], dims, preferred_element_type=jnp.float32)
    total = total + lax.dot_general(
        pick[half:, :], second[...], dims, preferred_element_type=jnp.float32
    )
    out[...] = total.astype(jnp.bfloat16)


def collect(pick, first, second):
    return pl.pallas_call(
        collect_kernel,
        out_shape=jax.ShapeDtypeStruct((pick.shape[1], first.shape[1]), jnp.bfloat16),
        compiler_params=pltpu.CompilerParams(vmem_limit_bytes=VMEM),
        cost_estimate=pl.CostEstimate(flops=3 * 10**8, bytes_accessed=3 * 10**6, transcendentals=0),
    )(pick, first, second)


def per_device(tokens, gate_scores, expert_ids, w_gate, w_up, w_down):
    groups, locals_ = lax.axis_size("node"), lax.axis_size("local")
    local = lax.axis_index("local").astype(jnp.int32).reshape(1)

    def across(block):
        parts = block.reshape(groups, block.shape[0] // groups, block.shape[1])
        return lax.all_to_all(parts, "node", 0, 0, tiled=True).reshape(block.shape)

    def up(block):
        return lax.ppermute(block, "local", [(i, (i + 1) % locals_) for i in range(locals_)])

    def down(block):
        return lax.ppermute(block, "local", [(i, (i - 1) % locals_) for i in range(locals_)])

    def add(*blocks):
        total = blocks[0].astype(jnp.float32)
        for block in blocks[1:]:
            total = total + block.astype(jnp.float32)
        return total.astype(jnp.bfloat16)

    run = functools.partial(experts, local=local, w_gate=w_gate, w_up=w_up, w_down=w_down)

    send_a, send_b, pick = prepare(tokens, gate_scores, expert_ids, groups, locals_)
    own_a = across(send_a)
    below_a, above_a = up(own_a), down(own_a)
    own_b = across(send_b)
    far_a, above_b = up(below_a), down(own_b)
    below_b, far_b = up(own_b), down(above_b)

    own_pa, below_pa, above_pa = run([own_a, below_a, above_a])
    far_pa, own_pb, above_pb = run([far_a, own_b, above_b])
    below_pb, far_pb = run([below_b, far_b])

    back_far_a, back_above_a = down(far_pa), up(above_pa)
    back_near_a, back_far_b = down(add(back_far_a, below_pa)), up(far_pb)
    total_a = add(own_pa, back_above_a, back_near_a)
    back_below_b, back_near_b = down(below_pb), up(add(back_far_b, above_pb))
    final_a = across(total_a)
    final_b = across(add(own_pb, back_below_b, back_near_b))
    return collect(pick, final_a, final_b)


def solution(mesh):
    in_specs = (
        P(("dp", "node", "local"), None),
        P(("dp", "node", "local"), None),
        P(("dp", "node", "local"), None),
        P(("node", "local"), None, None),
        P(("node", "local"), None, None),
        P(("node", "local"), None, None),
    )
    out_specs = P(("dp", "node", "local"), None)
    return jax.shard_map(
        per_device, mesh=mesh, in_specs=in_specs, out_specs=out_specs, check_vma=False
    )
```

time: 325 us -> 206 us (0.63); the launches traced: 322 us -> 206 us
  waiting for transfers between devices: 162 us -> 61.8 us
  blocking collectives: 0 us -> 58.2 us
  Pallas kernels: 0 us -> 55.7 us
  other arithmetic: 51.2 us -> 5.86 us
  local copies, waits for them, and re-layouts: 41.2 us -> 1.93 us
  matrix products: 28.5 us -> 0 us
  starting transfers between devices: 38 us -> 22.3 us
    all_to_all x3 -> x1, waiting for transfers between devices: 162 us -> 10.7 us  [across(): return lax.all_to_all(parts, 'node', 0, 0, tiled=True).reshape(block.shape)]
    all_to_all x0 -> x3, blocking collectives: none -> 58.2 us  [across(): return lax.all_to_all(parts, 'node', 0, 0, tiled=True).reshape(block.shape)]
    pallas_call x0 -> x5, Pallas kernels: none -> 55.7 us  [the longest x3 48.6 us: experts(): pl.pallas_call(functools.partial(expert_kernel, blocks), grid=(hidden //...]
    ppermute x0 -> x12, waiting for transfers between devices: none -> 51.1 us  [the longest x6 37 us: down(): lax.ppermute(block, 'local', [(i, (i - 1) % locals_) for i in range(local...]
    all_to_all x3 -> x1, starting transfers between devices: 38 us -> 3.77 us  [across(): return lax.all_to_all(parts, 'node', 0, 0, tiled=True).reshape(block.shape)]
    dot_general x3 -> x0, matrix products: 28.5 us -> none  [the longest x1 10.1 us: expert_rows(): up_act = jnp.dot(row_block, up_matrix, preferred_element_type=jnp.float32)]
    mul x2 -> x0, local copies, waits for them, and re-layouts: 25.3 us -> none  [restore(): tiles * tile_scale.astype(jnp.float32)[..., None]]
    scatter-add x1 -> x0, other arithmetic: 24.3 us -> none  [per_device(): jax.ops.segment_sum(values.reshape(-1, width), slot_token.reshape(-1), nu...]
  transfers between devices with their start and end apart: 3 -> 13, of which waited for: 2 -> 7; matrix products, arithmetic and copies ran while one was open for 11% -> 3% of each run, Pallas kernels for 0% -> 24%
where the time goes in v1:
time: 206 us
  waiting for transfers between devices  61.8 us (30%)
  blocking collectives  58.2 us (28%)
  Pallas kernels  55.7 us (27%)
  starting transfers between devices  22.3 us (11%)
  other arithmetic  5.86 us (3%)
    all_to_all x3, blocking collectives, across(): return lax.all_to_all(parts, 'node', 0, 0, tiled=True).reshape(block.shape)  58.2 us
    pallas_call x3, Pallas kernels, experts(): pl.pallas_call(functools.partial(expert_kernel, blocks), grid=(hidden //...  48.6 us
    ppermute x6, waiting for transfers between devices, down(): lax.ppermute(block, 'local', [(i, (i - 1) % locals_) for i in range(local...  37 us
    ppermute x6, starting transfers between devices, down(): lax.ppermute(block, 'local', [(i, (i - 1) % locals_) for i in range(local...  14.6 us
    ppermute x6, waiting for transfers between devices, up(): lax.ppermute(block, 'local', [(i, (i + 1) % locals_) for i in range(local...  14.2 us
    all_to_all x1, waiting for transfers between devices, across(): return lax.all_to_all(parts, 'node', 0, 0, tiled=True).reshape(block.shape)  10.7 us
  transfers between devices with their start and end apart: 13, of which 7 were waited for; matrix products, arithmetic and copies ran while one was open for 3% of the time, Pallas kernels for 24%

profile of v1, /device:TPU:0, one launch (start us, length us, event | category | flops | bytes accessed | tf_op | source)
XLA Modules:
  0.0 205.9 jit_solution(6847039443073835832)
XLA Ops:
  0.0 4.1 %shard_map.64 = (bf16[128,3712]{1,0:T(8,128)(2,1)}, bf16[128,3712]{1,0:T(8,128)(2,1)}, bf16[256,128]{1,0:T(8,128)(2,1)}) custom-call(bf16[128,3584]{1,0:T(8,128)(2,1)} %tok.1, f32[4,128]{1,0:T(4,128)} %bitcast.23, s32[4,128]{1,0:T(4,128)} %bitcast.24), custom_call_target="tpu_custom_call" | custom-call | flops 1000000000 | bytes 3000000 | tf_op jit(solution)/shard_map/pallas_call | solution.py:75
  4.1 0.0 copy-start.3
  4.1 24.2 %all_to_all.20 = bf16[16,8,3712]{2,1,0:T(8,128)(2,1)S(1)} all-to-all(bf16[16,8,3712]{2,1,0:T(8,128)(2,1)} %bitcast.22), channel_id=1, replica_groups=mesh['dp'=2,'node'=16,'local'=4] {'node'}, dimensions={0} | all-to-all | bytes 1900544 | tf_op jit(solution)/shard_map/all_to_all | solution.py:179
  28.3 0.0 copy-start.2
  28.3 1.6 collective-permute-start
  29.8 0.0 copy-done.3
  29.8 18.3 %all_to_all.21 = bf16[16,8,3712]{2,1,0:T(8,128)(2,1)S(1)} all-to-all(bf16[16,8,3712]{2,1,0:T(8,128)(2,1)S(1)} %bitcast.21), channel_id=1, replica_groups=mesh['dp'=2,'node'=16,'local'=4] {'node'}, dimensions={0} | all-to-all | bytes 1900544 | tf_op jit(solution)/shard_map/all_to_all | solution.py:179
  48.1 0.0 copy-start.1
  48.1 1.8 collective-permute-start.4
  49.9 1.4 collective-permute-done.refs_1_
  51.3 0.3 collective-permute-start.3
  51.6 2.9 %collective-permute-start.1 = (bf16[128,3712]{1,0:T(8,128)(2,1)S(1)}, bf16[128,3712]{1,0:T(8,128)(2,1)}, u32[]{:S(2)}, u32[]{:S(2)}) collective-permute-start(bf16[128,3712]{1,0:T(8,128)(2,1)S(1)} %bitcast.19), channel_id=1, source_target_pairs={{0,3},{1,0},{2,1},{3,2},{4,7},{5,4},{6,5},{7,6},{8,11},{9,8},{10,9... | collective-permute-start | bytes 2850824 | tf_op jit(solution)/shard_map/ppermute | solution.py:185
  54.5 0.0 collective-permute-start.7
  54.5 17.7 %collective-permute-done.4.refs_2_ = bf16[128,3712]{1,0:T(8,128)(2,1)} collective-permute-done((bf16[128,3712]{1,0:T(8,128)(2,1)S(1)}, bf16[128,3712]{1,0:T(8,128)(2,1)}, u32[]{:S(2)}, u32[]{:S(2)}) %collective-permute-start.4) | collective-permute-done | bytes 950304 | tf_op jit(solution)/shard_map/ppermute | solution.py:185
  72.2 3.0 %collective-permute-start.8 = (bf16[128,3712]{1,0:T(8,128)(2,1)}, bf16[128,3712]{1,0:T(8,128)(2,1)}, u32[]{:S(2)}, u32[]{:S(2)}) collective-permute-start(bf16[128,3712]{1,0:T(8,128)(2,1)} %collective-permute-done.4.refs_2_), channel_id=1, source_target_pairs={{0,3},{1,0},{2,1},{3,2},{4,7},{5,4},{6,5},{7,6},{8,11},{9,8},{10,9... | collective-permute-start | bytes 2850824 | tf_op jit(solution)/shard_map/ppermute | solution.py:185
  75.2 1.6 collective-permute-done.3.refs_0_
  76.8 0.0 copy-done.1
  76.8 17.3 %shard_map.66 = (bf16[128,3584]{1,0:T(8,128)(2,1)}, bf16[128,3584]{1,0:T(8,128)(2,1)}, bf16[128,3584]{1,0:T(8,128)(2,1)}) custom-call(s32[1]{0:T(128)} %bitcast.2.local_ref, bf16[128,3712]{1,0:T(8,128)(2,1)} %collective-permute-done.3.refs_0_, bf16[128,3712]{1,0:T(8,128)(2,1)} %bitcast.17, bf16[128,3712]{1,0:T(8,128)(2,1)} %collective-permute-done.4.refs_2_, ...), custom_call_target="tpu_custom_call" | custom-call | flops 8455716864 | bytes 22020096 | tf_op jit(solution)/shard_map/pallas_call | solution.py:127
  94.1 0.0 copy-done.2
  94.1 0.5 collective-permute-start.5
  94.6 0.0 collective-permute-done.1.refs_2_
  94.7 17.3 %shard_map.65 = (bf16[128,3584]{1,0:T(8,128)(2,1)}, bf16[128,3584]{1,0:T(8,128)(2,1)}, bf16[128,3584]{1,0:T(8,128)(2,1)}) custom-call(s32[1]{0:T(128)} %bitcast.2.local_ref, bf16[128,3712]{1,0:T(8,128)(2,1)} %bitcast.20, bf16[128,3712]{1,0:T(8,128)(2,1)} %collective-permute-done.refs_1_, bf16[128,3712]{1,0:T(8,128)(2,1)} %collective-permute-done.1.refs_2_, ...), custom_call_target="tpu_custom_call" | custom-call | flops 8455716864 | bytes 22020096 | tf_op jit(solution)/shard_map/pallas_call | solution.py:127
  112.0 1.5 collective-permute-start.2
  113.5 0.0 collective-permute-done.7.refs_0_
  113.5 0.0 copy-start.4
  113.5 0.0 collective-permute-done.8.refs_1_
  113.5 1.0 copy-done.4
  114.4 14.0 %shard_map.67 = (bf16[128,3584]{1,0:T(8,128)(2,1)}, bf16[128,3584]{1,0:T(8,128)(2,1)}) custom-call(s32[1]{0:T(128)} %bitcast.2.local_ref, bf16[128,3712]{1,0:T(8,128)(2,1)} %copy-done.4, bf16[128,3712]{1,0:T(8,128)(2,1)} %collective-permute-done.8.refs_1_, bf16[1,3584,1024]{2,1,0:T(8,128)(2,1)} %refs_2_.1, bf16[1,3584,1024]{2,1,0:T(8,128)(2,1)} %refs_3_.5, ...), custom_call_target="tpu_custom_call" | custom-call | flops 5637144576 | bytes 22020096 | tf_op jit(solution)/shard_map/pallas_call | solution.py:127
  128.4 0.0 copy-start.8
  128.4 0.1 collective-permute-start.10
  128.5 3.2 %collective-permute-start.9 = (bf16[128,3584]{1,0:T(8,128)(2,1)}, bf16[128,3584]{1,0:T(8,128)(2,1)S(1)}, u32[]{:S(2)}, u32[]{:S(2)}) collective-permute-start(bf16[128,3584]{1,0:T(8,128)(2,1)} %get-tuple-element.24), channel_id=1, source_target_pairs={{0,3},{1,0},{2,1},{3,2},{4,7},{5,4},{6,5},{7,6},{8,11},{9,8},{10,9... | collective-permute-start | bytes 2752520 | tf_op jit(solution)/shard_map/ppermute | solution.py:185
  131.6 0.9 collective-permute-done.5
  132.6 1.7 add_convert_fusion.3
  134.2 0.0 copy-start.6
  134.3 3.1 %collective-permute-start.6 = (bf16[128,3584]{1,0:T(8,128)(2,1)S(1)}, bf16[128,3584]{1,0:T(8,128)(2,1)S(1)}, u32[]{:S(2)}, u32[]{:S(2)}) collective-permute-start(bf16[128,3584]{1,0:T(8,128)(2,1)S(1)} %add_convert_fusion.3), channel_id=1, source_target_pairs={{0,3},{1,0},{2,1},{3,2},{4,7},{5,4},{6,5},{7,6},{8,11},{9,8},{10,9... | collective-permute-start | bytes 2752520 | tf_op jit(solution)/shard_map/ppermute | solution.py:185
  137.3 11.2 %collective-permute-done.10 = bf16[128,3584]{1,0:T(8,128)(2,1)S(1)} collective-permute-done((bf16[128,3584]{1,0:T(8,128)(2,1)}, bf16[128,3584]{1,0:T(8,128)(2,1)S(1)}, u32[]{:S(2)}, u32[]{:S(2)}) %collective-permute-start.10) | collective-permute-done | bytes 917536 | tf_op jit(solution)/shard_map/ppermute | solution.py:182
  148.6 0.0 copy-done.8
  148.6 1.2 add_convert_fusion.1
  149.7 0.5 collective-permute-start.11
  150.3 0.0 collective-permute-done.2
  150.3 18.3 %collective-permute-done.6 = bf16[128,3584]{1,0:T(8,128)(2,1)S(1)} collective-permute-done((bf16[128,3584]{1,0:T(8,128)(2,1)S(1)}, bf16[128,3584]{1,0:T(8,128)(2,1)S(1)}, u32[]{:S(2)}, u32[]{:S(2)}) %collective-permute-start.6) | collective-permute-done | bytes 917536 | tf_op jit(solution)/shard_map/ppermute | solution.py:185
  168.6 0.0 copy-done.6
  168.6 1.3 fusion
  169.9 0.0 copy-start.5
  169.9 3.8 %all-to-all-start.2 = ((bf16[16,8,3584]{2,1,0:T(8,128)(2,1)}), bf16[16,8,3584]{2,1,0:T(8,128)(2,1)S(1)}, u32[]{:S(2)}, u32[]{:S(2)}) async-start(bf16[16,8,3584]{2,1,0:T(8,128)(2,1)} %fusion), calls=%async_computation.2 | async-start | bytes 1835008 | tf_op jit(solution)/shard_map/all_to_all | solution.py:179
  173.6 0.0 collective-permute-done.9
  173.6 0.0 copy-start.7
  173.7 0.0 collective-permute-done.11
  173.7 0.9 copy-done.7
  174.6 0.0 copy-done.5
  174.6 1.8 fusion.1
  176.4 10.7 %all-to-all-done.2 = bf16[16,8,3584]{2,1,0:T(8,128)(2,1)S(1)} async-done(((bf16[16,8,3584]{2,1,0:T(8,128)(2,1)}), bf16[16,8,3584]{2,1,0:T(8,128)(2,1)S(1)}, u32[]{:S(2)}, u32[]{:S(2)}) %all-to-all-start.2) | async-done | bytes 917536 | tf_op jit(solution)/shard_map/all_to_all | solution.py:179
  187.1 0.0 copy-start
  187.1 15.7 %all_to_all.22 = bf16[16,8,3584]{2,1,0:T(8,128)(2,1)} all-to-all(bf16[16,8,3584]{2,1,0:T(8,128)(2,1)S(1)} %fusion.1), channel_id=1, replica_groups=mesh['dp'=2,'node'=16,'local'=4] {'node'}, dimensions={0} | all-to-all | bytes 1835008 | tf_op jit(solution)/shard_map/all_to_all | solution.py:179
  202.8 0.0 copy-done
  202.8 3.1 %shard_map.68 = bf16[128,3584]{1,0:T(8,128)(2,1)} custom-call(bf16[256,128]{1,0:T(8,128)(2,1)} %get-tuple-element.16.pick, bf16[128,3584]{1,0:T(8,128)(2,1)} %bitcast.13, bf16[128,3584]{1,0:T(8,128)(2,1)} %bitcast.14), custom_call_target="tpu_custom_call" | custom-call | flops 300000000 | bytes 3000000 | tf_op jit(solution)/shard_map/pallas_call | solution.py:165
Async XLA Ops:
  4.1 25.8 %copy-start.3 = (bf16[128,3712]{1,0:T(8,128)(2,1)S(1)}, bf16[128,3712]{1,0:T(8,128)(2,1)}, u32[]{:S(2)}) copy-start(bf16[128,3712]{1,0:T(8,128)(2,1)} %get-tuple-element.20) | copy-start | bytes 2850820
  28.3 65.9 %copy-start.2 = (bf16[16,8,3712]{2,1,0:T(8,128)(2,1)}, bf16[16,8,3712]{2,1,0:T(8,128)(2,1)S(1)}, u32[]{:S(2)}) copy-start(bf16[16,8,3712]{2,1,0:T(8,128)(2,1)S(1)} %all_to_all.20) | copy-start | bytes 2850820
  28.3 23.0 %collective-permute-start = (bf16[128,3712]{1,0:T(8,128)(2,1)S(1)}, bf16[128,3712]{1,0:T(8,128)(2,1)}, u32[]{:S(2)}, u32[]{:S(2)}) collective-permute-start(bf16[128,3712]{1,0:T(8,128)(2,1)S(1)} %bitcast.18), channel_id=1, source_target_pairs={{0,1},{1,2},{2,3},{3,0},{4,5},{5,6},{6,7},{7,4},{8,9},{9,10},{10,1... | collective-permute-start | bytes 2850824 | tf_op jit(solution)/shard_map/ppermute | solution.py:182
  48.1 28.7 %copy-start.1 = (bf16[16,8,3712]{2,1,0:T(8,128)(2,1)}, bf16[16,8,3712]{2,1,0:T(8,128)(2,1)S(1)}, u32[]{:S(2)}) copy-start(bf16[16,8,3712]{2,1,0:T(8,128)(2,1)S(1)} %all_to_all.21) | copy-start | bytes 2850820
  48.1 24.1 %collective-permute-start.4 = (bf16[128,3712]{1,0:T(8,128)(2,1)S(1)}, bf16[128,3712]{1,0:T(8,128)(2,1)}, u32[]{:S(2)}, u32[]{:S(2)}) collective-permute-start(bf16[128,3712]{1,0:T(8,128)(2,1)S(1)} %bitcast.15), channel_id=1, source_target_pairs={{0,3},{1,0},{2,1},{3,2},{4,7},{5,4},{6,5},{7,6},{8,11},{9,8},{10,9... | collective-permute-start | bytes 2850824 | tf_op jit(solution)/shard_map/ppermute | solution.py:185
  51.3 25.5 %collective-permute-start.3 = (bf16[128,3712]{1,0:T(8,128)(2,1)}, bf16[128,3712]{1,0:T(8,128)(2,1)}, u32[]{:S(2)}, u32[]{:S(2)}) collective-permute-start(bf16[128,3712]{1,0:T(8,128)(2,1)} %collective-permute-done.refs_1_), channel_id=1, source_target_pairs={{0,1},{1,2},{2,3},{3,0},{4,5},{5,6},{6,7},{7,4},{8,9},{9,10},{10,1... | collective-permute-start | bytes 2850824 | tf_op jit(solution)/shard_map/ppermute | solution.py:182
  51.6 43.1 %collective-permute-start.1 = (bf16[128,3712]{1,0:T(8,128)(2,1)S(1)}, bf16[128,3712]{1,0:T(8,128)(2,1)}, u32[]{:S(2)}, u32[]{:S(2)}) collective-permute-start(bf16[128,3712]{1,0:T(8,128)(2,1)S(1)} %bitcast.19), channel_id=1, source_target_pairs={{0,3},{1,0},{2,1},{3,2},{4,7},{5,4},{6,5},{7,6},{8,11},{9,8},{10,9... | collective-permute-start | bytes 2850824 | tf_op jit(solution)/shard_map/ppermute | solution.py:185
  54.5 59.0 %collective-permute-start.7 = (bf16[128,3712]{1,0:T(8,128)(2,1)S(1)}, bf16[128,3712]{1,0:T(8,128)(2,1)S(1)}, u32[]{:S(2)}, u32[]{:S(2)}) collective-permute-start(bf16[128,3712]{1,0:T(8,128)(2,1)S(1)} %bitcast.16), channel_id=1, source_target_pairs={{0,1},{1,2},{2,3},{3,0},{4,5},{5,6},{6,7},{7,4},{8,9},{9,10},{10,1... | collective-permute-start | bytes 2850824 | tf_op jit(solution)/shard_map/ppermute | solution.py:182
  72.2 41.3 %collective-permute-start.8 = (bf16[128,3712]{1,0:T(8,128)(2,1)}, bf16[128,3712]{1,0:T(8,128)(2,1)}, u32[]{:S(2)}, u32[]{:S(2)}) collective-permute-start(bf16[128,3712]{1,0:T(8,128)(2,1)} %collective-permute-done.4.refs_2_), channel_id=1, source_target_pairs={{0,3},{1,0},{2,1},{3,2},{4,7},{5,4},{6,5},{7,6},{8,11},{9,8},{10,9... | collective-permute-start | bytes 2850824 | tf_op jit(solution)/shard_map/ppermute | solution.py:185
  94.1 38.5 %collective-permute-start.5 = (bf16[128,3584]{1,0:T(8,128)(2,1)}, bf16[128,3584]{1,0:T(8,128)(2,1)}, u32[]{:S(2)}, u32[]{:S(2)}) collective-permute-start(bf16[128,3584]{1,0:T(8,128)(2,1)} %get-tuple-element.21), channel_id=1, source_target_pairs={{0,3},{1,0},{2,1},{3,2},{4,7},{5,4},{6,5},{7,6},{8,11},{9,8},{10,9... | collective-permute-start | bytes 2752520 | tf_op jit(solution)/shard_map/ppermute | solution.py:185
  112.0 38.3 %collective-permute-start.2 = (bf16[128,3584]{1,0:T(8,128)(2,1)}, bf16[128,3584]{1,0:T(8,128)(2,1)S(1)}, u32[]{:S(2)}, u32[]{:S(2)}) collective-permute-start(bf16[128,3584]{1,0:T(8,128)(2,1)} %get-tuple-element.19), channel_id=1, source_target_pairs={{0,1},{1,2},{2,3},{3,0},{4,5},{5,6},{6,7},{7,4},{8,9},{9,10},{10,1... | collective-permute-start | bytes 2752520 | tf_op jit(solution)/shard_map/ppermute | solution.py:182
  113.5 1.0 copy-start.4
  128.4 20.2 %copy-start.8 = (bf16[128,3584]{1,0:T(8,128)(2,1)S(1)}, bf16[128,3584]{1,0:T(8,128)(2,1)}, u32[]{:S(2)}) copy-start(bf16[128,3584]{1,0:T(8,128)(2,1)} %get-tuple-element.26) | copy-start | bytes 2752516
  128.4 20.2 %collective-permute-start.10 = (bf16[128,3584]{1,0:T(8,128)(2,1)}, bf16[128,3584]{1,0:T(8,128)(2,1)S(1)}, u32[]{:S(2)}, u32[]{:S(2)}) collective-permute-start(bf16[128,3584]{1,0:T(8,128)(2,1)} %get-tuple-element.25), channel_id=1, source_target_pairs={{0,1},{1,2},{2,3},{3,0},{4,5},{5,6},{6,7},{7,4},{8,9},{9,10},{10,1... | collective-permute-start | bytes 2752520 | tf_op jit(solution)/shard_map/ppermute | solution.py:182
  128.5 45.2 %collective-permute-start.9 = (bf16[128,3584]{1,0:T(8,128)(2,1)}, bf16[128,3584]{1,0:T(8,128)(2,1)S(1)}, u32[]{:S(2)}, u32[]{:S(2)}) collective-permute-start(bf16[128,3584]{1,0:T(8,128)(2,1)} %get-tuple-element.24), channel_id=1, source_target_pairs={{0,3},{1,0},{2,1},{3,2},{4,7},{5,4},{6,5},{7,6},{8,11},{9,8},{10,9... | collective-permute-start | bytes 2752520 | tf_op jit(solution)/shard_map/ppermute | solution.py:185
  134.2 34.4 %copy-start.6 = (bf16[128,3584]{1,0:T(8,128)(2,1)S(1)}, bf16[128,3584]{1,0:T(8,128)(2,1)}, u32[]{:S(2)}) copy-start(bf16[128,3584]{1,0:T(8,128)(2,1)} %get-tuple-element.18) | copy-start | bytes 2752516
  134.3 34.4 %collective-permute-start.6 = (bf16[128,3584]{1,0:T(8,128)(2,1)S(1)}, bf16[128,3584]{1,0:T(8,128)(2,1)S(1)}, u32[]{:S(2)}, u32[]{:S(2)}) collective-permute-start(bf16[128,3584]{1,0:T(8,128)(2,1)S(1)} %add_convert_fusion.3), channel_id=1, source_target_pairs={{0,3},{1,0},{2,1},{3,2},{4,7},{5,4},{6,5},{7,6},{8,11},{9,8},{10,9... | collective-permute-start | bytes 2752520 | tf_op jit(solution)/shard_map/ppermute | solution.py:185
  149.7 23.9 %collective-permute-start.11 = (bf16[128,3584]{1,0:T(8,128)(2,1)}, bf16[128,3584]{1,0:T(8,128)(2,1)}, u32[]{:S(2)}, u32[]{:S(2)}) collective-permute-start(bf16[128,3584]{1,0:T(8,128)(2,1)} %add_convert_fusion.1), channel_id=1, source_target_pairs={{0,1},{1,2},{2,3},{3,0},{4,5},{5,6},{6,7},{7,4},{8,9},{9,10},{10,1... | collective-permute-start | bytes 2752520 | tf_op jit(solution)/shard_map/ppermute | solution.py:182
  169.9 4.8 %copy-start.5 = (bf16[128,3584]{1,0:T(8,128)(2,1)S(1)}, bf16[128,3584]{1,0:T(8,128)(2,1)}, u32[]{:S(2)}) copy-start(bf16[128,3584]{1,0:T(8,128)(2,1)} %get-tuple-element.23) | copy-start | bytes 2752516
  169.9 17.2 %all-to-all-start.2 = ((bf16[16,8,3584]{2,1,0:T(8,128)(2,1)}), bf16[16,8,3584]{2,1,0:T(8,128)(2,1)S(1)}, u32[]{:S(2)}, u32[]{:S(2)}) async-start(bf16[16,8,3584]{2,1,0:T(8,128)(2,1)} %fusion), calls=%async_computation.2 | async-start | bytes 1835008 | tf_op jit(solution)/shard_map/all_to_all | solution.py:179
  173.6 1.0 copy-start.7
  187.1 15.7 %copy-start = (bf16[16,8,3584]{2,1,0:T(8,128)(2,1)}, bf16[16,8,3584]{2,1,0:T(8,128)(2,1)S(1)}, u32[]{:S(2)}) copy-start(bf16[16,8,3584]{2,1,0:T(8,128)(2,1)S(1)} %all-to-all-done.2) | copy-start | bytes 2752516

commit v2 on v1

--- a/solution.py
+++ b/solution.py
@@ -10,6 +10,7 @@
 LANES = 128
 PIECE = 128
 VMEM = 60 * 1024 * 1024
+NEAR_TILES = 14
 
 
 def slot_maps(ids_t, groups, per_group):
@@ -85,10 +86,10 @@
 
 
 def expert_kernel(blocks, local_ref, *refs):
-    xs, (wg, wu, wd), outs = refs[:blocks], refs[blocks : blocks + 3], refs[blocks + 3 : 2 * blocks + 3]
-    rows, acc = refs[2 * blocks + 3 :]
+    xs, (wg, wu, wd), refs = refs[:blocks], refs[blocks : blocks + 3], refs[blocks + 3 :]
+    outs, direct, rows, acc = refs[:blocks], refs[blocks], refs[blocks + 1], refs[blocks + 2]
     step, steps = pl.program_id(0), pl.num_programs(0)
-    width = rows.shape[1]
+    width, near = rows.shape[1], outs[0].shape[1]
     piece = xs[0].shape[0]
 
     @pl.when(step == 0)
@@ -117,13 +118,19 @@
             lane = lax.broadcasted_iota(jnp.int32, meta.shape, 1)
             weight = jnp.sum(jnp.where(lane == local_ref[0], meta, 0.0), axis=1, keepdims=True)
             own = slice(b * piece, (b + 1) * piece)
-            outs[b][...] = ((acc[own, :] + part[own, :]) * weight).astype(jnp.bfloat16)
-
-
-def experts(xs, local, w_gate, w_up, w_down, tile=256):
+            value = (acc[own, :] + part[own, :]) * weight
+            outs[b][...] = value[:, :near].astype(jnp.bfloat16)
+            far = value[:, near:]
+            direct[:, b] = far.reshape(direct.shape[0], direct.shape[2], far.shape[1]).astype(
+                jnp.bfloat16
+            )
+
+
+def experts(xs, local, groups, near, w_gate, w_up, w_down, tile=256):
     blocks = len(xs)
     piece, wide = xs[0].shape
     width, hidden = w_gate.shape[1:]
+    direct = (groups, blocks, piece // groups, width - near)
     return pl.pallas_call(
         functools.partial(expert_kernel, blocks),
         grid=(hidden // tile,),
@@ -134,8 +141,10 @@
             pl.BlockSpec((1, width, tile), lambda i: (0, 0, i)),
             pl.BlockSpec((1, tile, width), lambda i: (0, i, 0)),
         ],
-        out_specs=[pl.BlockSpec((piece, width), lambda i: (0, 0))] * blocks,
-        out_shape=[jax.ShapeDtypeStruct((piece, width), jnp.bfloat16)] * blocks,
+        out_specs=[pl.BlockSpec((piece, near), lambda i: (0, 0))] * blocks
+        + [pl.BlockSpec(direct, lambda i: (0, 0, 0, 0))],
+        out_shape=[jax.ShapeDtypeStruct((piece, near), jnp.bfloat16)] * blocks
+        + [jax.ShapeDtypeStruct(direct, jnp.bfloat16)],
         scratch_shapes=[
             pltpu.VMEM((blocks * piece, width), jnp.bfloat16),
             pltpu.VMEM((blocks * piece, width), jnp.float32),
@@ -151,28 +160,55 @@
     )(local, *xs, w_gate, w_up, w_down)
 
 
-def collect_kernel(pick, first, second, out):
-    half = first.shape[0]
-    dims = (((0,), (0,)), ((), ()))
-    total = lax.dot_general(pick[:half, :], first[...], dims, preferred_element_type=jnp.float32)
-    total = total + lax.dot_general(
-        pick[half:, :], second[...], dims, preferred_element_type=jnp.float32
-    )
-    out[...] = total.astype(jnp.bfloat16)
-
-
-def collect(pick, first, second):
+def whole(kernel, shapes, *arrays):
+    moved = sum(x.size * x.dtype.itemsize for x in arrays)
     return pl.pallas_call(
-        collect_kernel,
-        out_shape=jax.ShapeDtypeStruct((pick.shape[1], first.shape[1]), jnp.bfloat16),
+        kernel,
+        out_shape=shapes,
         compiler_params=pltpu.CompilerParams(vmem_limit_bytes=VMEM),
-        cost_estimate=pl.CostEstimate(flops=3 * 10**8, bytes_accessed=3 * 10**6, transcendentals=0),
-    )(pick, first, second)
+        cost_estimate=pl.CostEstimate(flops=10**8, bytes_accessed=3 * moved, transcendentals=0),
+    )(*arrays)
+
+
+def to_tokens(pick, rows):
+    return lax.dot_general(pick, rows, (((0,), (0,)), ((), ())), preferred_element_type=jnp.float32)
+
+
+def scatter_kernel(where, picks, first, second, third, own, below, above, far_lo, far_hi):
+    groups = (first, second, third)
+    width = first.shape[-1]
+    for name, out in (("own", own), ("below", below), ("above", above), ("far", None)):
+        pick = picks[("own", "below", "above", "far").index(name)]
+        total = None
+        for half in range(2):
+            which, place = where[name, half]
+            rows = groups[which][:, place].reshape(PIECE, width)
+            part = to_tokens(pick[half * PIECE : (half + 1) * PIECE, :], rows)
+            total = part if total is None else total + part
+        total = total.astype(jnp.bfloat16)
+        if out is not None:
+            out[...] = total
+        else:
+            far_lo[...] = total[: far_lo.shape[0]]
+            far_hi[...] = total[far_lo.shape[0] :]
+
+
+def collect_kernel(pick, first, second, own, below_lo, below_hi, above_lo, above_hi, out):
+    near = first.shape[1]
+    half = own.shape[0] // 2
+    total = to_tokens(pick[:PIECE, :], first[...]) + to_tokens(pick[PIECE:, :], second[...])
+    out[:, :near] = total.astype(jnp.bfloat16)
+    for place, below, above in ((0, below_lo, above_lo), (half, below_hi, above_hi)):
+        rows = slice(place, place + half)
+        total = own[rows, :].astype(jnp.float32) + below[...].astype(jnp.float32)
+        out[rows, near:] = (total + above[...].astype(jnp.float32)).astype(jnp.bfloat16)
 
 
 def per_device(tokens, gate_scores, expert_ids, w_gate, w_up, w_down):
     groups, locals_ = lax.axis_size("node"), lax.axis_size("local")
     local = lax.axis_index("local").astype(jnp.int32).reshape(1)
+    count, width = tokens.shape
+    near = NEAR_TILES * LANES
 
     def across(block):
         parts = block.reshape(groups, block.shape[0] // groups, block.shape[1])
@@ -190,7 +226,9 @@
             total = total + block.astype(jnp.float32)
         return total.astype(jnp.bfloat16)
 
-    run = functools.partial(experts, local=local, w_gate=w_gate, w_up=w_up, w_down=w_down)
+    run = functools.partial(
+        experts, local=local, groups=groups, near=near, w_gate=w_gate, w_up=w_up, w_down=w_down
+    )
 
     send_a, send_b, pick = prepare(tokens, gate_scores, expert_ids, groups, locals_)
     own_a = across(send_a)
@@ -198,10 +236,16 @@
     own_b = across(send_b)
     far_a, above_b = up(below_a), down(own_b)
     below_b, far_b = up(own_b), down(above_b)
-
-    own_pa, below_pa, above_pa = run([own_a, below_a, above_a])
-    far_pa, own_pb, above_pb = run([far_a, own_b, above_b])
-    below_pb, far_pb = run([below_b, far_b])
+    pick_below, pick_above = up(pick), down(pick)
+    pick_far = up(pick_below)
+
+    own_pa, below_pa, above_pa, first = run([own_a, below_a, above_a])
+    far_a, own_b, above_b, own_pa = lax.optimization_barrier((far_a, own_b, above_b, own_pa))
+    far_pa, own_pb, above_pb, second = run([far_a, own_b, above_b])
+    below_b, far_b, own_pb = lax.optimization_barrier((below_b, far_b, own_pb))
+    below_pb, far_pb, third = run([below_b, far_b])
+
+    home = [lax.all_to_all(x, "node", 0, 0, tiled=True) for x in (first, second, third)]
 
     back_far_a, back_above_a = down(far_pa), up(above_pa)
     back_near_a, back_far_b = down(add(back_far_a, below_pa)), up(far_pb)
@@ -209,7 +253,30 @@
     back_below_b, back_near_b = down(below_pb), up(add(back_far_b, above_pb))
     final_a = across(total_a)
     final_b = across(add(own_pb, back_below_b, back_near_b))
-    return collect(pick, final_a, final_b)
+
+    where = {
+        ("own", 0): (0, 0), ("below", 0): (0, 1), ("above", 0): (0, 2),
+        ("far", 0): (1, 0), ("own", 1): (1, 1), ("above", 1): (1, 2),
+        ("below", 1): (2, 0), ("far", 1): (2, 1),
+    }
+    full = jax.ShapeDtypeStruct((count, width - near), jnp.bfloat16)
+    part = jax.ShapeDtypeStruct((count // 2, width - near), jnp.bfloat16)
+
+    def scatter(p0, p1, p2, p3, *refs):
+        scatter_kernel(where, (p0, p1, p2, p3), *refs)
+
+    own_t, below_t, above_t, far_lo, far_hi = whole(
+        scatter, [full, full, full, part, part], pick, pick_below, pick_above, pick_far, *home
+    )
+    half = count // 2
+    more_lo, more_hi = down(far_lo), up(far_hi)
+    below_hi, above_lo = down(below_t[half:]), up(above_t[:half])
+    below_lo, above_hi = down(add(below_t[:half], more_lo)), up(add(above_t[half:], more_hi))
+    return whole(
+        collect_kernel,
+        jax.ShapeDtypeStruct((count, width), jnp.bfloat16),
+        pick, final_a, final_b, own_t, below_lo, below_hi, above_lo, above_hi,
+    )
 
 
 def solution(mesh):

time: 206 us -> 239 us (1.16)
  starting transfers between devices: 22.3 us -> 70.8 us
  blocking collectives: 58.2 us -> 24.1 us
  waiting for transfers between devices: 61.8 us -> 71.6 us
  Pallas kernels: 55.7 us -> 59.9 us
  local copies, waits for them, and re-layouts: 1.93 us -> 4.94 us
    all_to_all x3 -> x1, blocking collectives: 58.2 us -> 24.1 us  [across(): return lax.all_to_all(parts, 'node', 0, 0, tiled=True).reshape(block.shape)]
    all_to_all x0 -> x3, starting transfers between devices: none -> 18.3 us  [per_device(): lax.all_to_all(x, 'node', 0, 0, tiled=True)]
    all_to_all x1 -> x3, starting transfers between devices: 3.77 us -> 18.1 us  [across(): return lax.all_to_all(parts, 'node', 0, 0, tiled=True).reshape(block.shape)]
    ppermute x6 -> x10, starting transfers between devices: 14.6 us -> 27.4 us  [down(): lax.ppermute(block, 'local', [(i, (i - 1) % locals_) for i in range(local...]
    all_to_all x1 -> x3, waiting for transfers between devices: 10.7 us -> 23.3 us  [across(): return lax.all_to_all(parts, 'node', 0, 0, tiled=True).reshape(block.shape)]
    pallas_call x1 -> x2, Pallas kernels: 3.06 us -> 7.17 us  [whole(): pl.pallas_call(kernel, out_shape=shapes, compiler_params=pltpu.CompilerPa...]
    ppermute x6 -> x11, starting transfers between devices: 3.97 us -> 6.99 us  [up(): lax.ppermute(block, 'local', [(i, (i + 1) % locals_) for i in range(local...]
    ppermute x6 -> x11, waiting for transfers between devices: 14.2 us -> 11.2 us  [up(): lax.ppermute(block, 'local', [(i, (i + 1) % locals_) for i in range(local...]
  transfers between devices with their start and end apart: 13 -> 27, of which waited for: 7 -> 10; matrix products, arithmetic and copies ran while one was open for 3% -> 3% of each run, Pallas kernels for 24% -> 22%
where the time goes in v2:
time: 239 us; the launch traced here: 238 us
  waiting for transfers between devices  71.6 us (30%)
  starting transfers between devices  70.8 us (30%)
  Pallas kernels  59.9 us (25%)
  blocking collectives  24.1 us (10%)
  other arithmetic  6.28 us (3%)
  local copies, waits for them, and re-layouts  4.94 us (2%)
    pallas_call x3, Pallas kernels, experts(): pl.pallas_call(functools.partial(expert_kernel, blocks), grid=(hidden //...  48.7 us
    ppermute x10, waiting for transfers between devices, down(): lax.ppermute(block, 'local', [(i, (i - 1) % locals_) for i in range(local...  37.1 us
    ppermute x10, starting transfers between devices, down(): lax.ppermute(block, 'local', [(i, (i - 1) % locals_) for i in range(local...  27.4 us
    all_to_all x1, blocking collectives, across(): return lax.all_to_all(parts, 'node', 0, 0, tiled=True).reshape(block.shape)  24.1 us
    all_to_all x3, waiting for transfers between devices, across(): return lax.all_to_all(parts, 'node', 0, 0, tiled=True).reshape(block.shape)  23.3 us
    all_to_all x3, starting transfers between devices, per_device(): lax.all_to_all(x, 'node', 0, 0, tiled=True)  18.3 us
    all_to_all x3, starting transfers between devices, across(): return lax.all_to_all(parts, 'node', 0, 0, tiled=True).reshape(block.shape)  18.1 us
    ppermute x11, waiting for transfers between devices, up(): lax.ppermute(block, 'local', [(i, (i + 1) % locals_) for i in range(local...  11.2 us
  transfers between devices with their start and end apart: 27, of which 10 were waited for; matrix products, arithmetic and copies ran while one was open for 3% of the time, Pallas kernels for 22%

profile of v2, /device:TPU:0, one launch (start us, length us, event | category | flops | bytes accessed | tf_op | source)
XLA Modules:
  0.0 237.9 jit_solution(3285792618687117856)
XLA Ops:
  0.0 4.1 %shard_map.64 = (bf16[128,3712]{1,0:T(8,128)(2,1)}, bf16[128,3712]{1,0:T(8,128)(2,1)}, bf16[256,128]{1,0:T(8,128)(2,1)}) custom-call(bf16[128,3584]{1,0:T(8,128)(2,1)} %tok.1, f32[4,128]{1,0:T(4,128)} %bitcast.22, s32[4,128]{1,0:T(4,128)} %bitcast.23), custom_call_target="tpu_custom_call" | custom-call | flops 1000000000 | bytes 3000000 | tf_op jit(solution)/shard_map/pallas_call | solution.py:76
  4.1 24.1 %all_to_all.35 = bf16[16,8,3712]{2,1,0:T(8,128)(2,1)S(1)} all-to-all(bf16[16,8,3712]{2,1,0:T(8,128)(2,1)} %bitcast.21), channel_id=1, replica_groups=mesh['dp'=2,'node'=16,'local'=4] {'node'}, dimensions={0} | all-to-all | bytes 1900544 | tf_op jit(solution)/shard_map/all_to_all | solution.py:215
  28.1 3.6 %all-to-all-start.1 = ((bf16[16,8,3712]{2,1,0:T(8,128)(2,1)}), bf16[16,8,3712]{2,1,0:T(8,128)(2,1)S(1)}, u32[]{:S(2)}, u32[]{:S(2)}) async-start(bf16[16,8,3712]{2,1,0:T(8,128)(2,1)} %bitcast.4), calls=%async_computation.1 | async-start | bytes 1900544 | tf_op jit(solution)/shard_map/all_to_all | solution.py:215
  31.8 1.6 collective-permute-start
  33.4 13.7 %all-to-all-done.1 = bf16[16,8,3712]{2,1,0:T(8,128)(2,1)S(1)} async-done(((bf16[16,8,3712]{2,1,0:T(8,128)(2,1)}), bf16[16,8,3712]{2,1,0:T(8,128)(2,1)S(1)}, u32[]{:S(2)}, u32[]{:S(2)}) %all-to-all-start.1) | async-done | bytes 950304 | tf_op jit(solution)/shard_map/all_to_all | solution.py:215
  47.1 3.0 %collective-permute-start.2 = (bf16[128,3712]{1,0:T(8,128)(2,1)S(1)}, bf16[128,3712]{1,0:T(8,128)(2,1)}, u32[]{:S(2)}, u32[]{:S(2)}) collective-permute-start(bf16[128,3712]{1,0:T(8,128)(2,1)S(1)} %bitcast.15), channel_id=1, source_target_pairs={{0,3},{1,0},{2,1},{3,2},{4,7},{5,4},{6,5},{7,6},{8,11},{9,8},{10,9... | collective-permute-start | bytes 2850824 | tf_op jit(solution)/shard_map/ppermute | solution.py:221
  50.1 0.7 collective-permute-start.3
  50.9 4.0 %collective-permute-done.refs_1_ = bf16[128,3712]{1,0:T(8,128)(2,1)} collective-permute-done((bf16[128,3712]{1,0:T(8,128)(2,1)S(1)}, bf16[128,3712]{1,0:T(8,128)(2,1)}, u32[]{:S(2)}, u32[]{:S(2)}) %collective-permute-start) | collective-permute-done | bytes 950304 | tf_op jit(solution)/shard_map/ppermute | solution.py:218
  54.9 0.3 collective-permute-start.1
  55.2 1.6 collective-permute-start.7
  56.7 14.9 %collective-permute-done.2.refs_2_ = bf16[128,3712]{1,0:T(8,128)(2,1)} collective-permute-done((bf16[128,3712]{1,0:T(8,128)(2,1)S(1)}, bf16[128,3712]{1,0:T(8,128)(2,1)}, u32[]{:S(2)}, u32[]{:S(2)}) %collective-permute-start.2) | collective-permute-done | bytes 950304 | tf_op jit(solution)/shard_map/ppermute | solution.py:221
  71.6 3.8 %collective-permute-start.8 = (bf16[128,3712]{1,0:T(8,128)(2,1)}, bf16[128,3712]{1,0:T(8,128)(2,1)}, u32[]{:S(2)}, u32[]{:S(2)}) collective-permute-start(bf16[128,3712]{1,0:T(8,128)(2,1)} %collective-permute-done.2.refs_2_), channel_id=1, source_target_pairs={{0,3},{1,0},{2,1},{3,2},{4,7},{5,4},{6,5},{7,6},{8,11},{9,8},{10,9... | collective-permute-start | bytes 2850824 | tf_op jit(solution)/shard_map/ppermute | solution.py:221
  75.4 16.6 %collective-permute-done.3.refs_2_ = bf16[128,3712]{1,0:T(8,128)(2,1)} collective-permute-done((bf16[128,3712]{1,0:T(8,128)(2,1)S(1)}, bf16[128,3712]{1,0:T(8,128)(2,1)}, u32[]{:S(2)}, u32[]{:S(2)}) %collective-permute-start.3) | collective-permute-done | bytes 950304 | tf_op jit(solution)/shard_map/ppermute | solution.py:221
  92.0 17.4 %shard_map.65 = (bf16[128,1792]{1,0:T(8,128)(2,1)}, bf16[128,1792]{1,0:T(8,128)(2,1)}, bf16[128,1792]{1,0:T(8,128)(2,1)}, bf16[16,3,8,1792]{3,2,1,0:T(8,128)(2,1)}) custom-call(s32[1]{0:T(128)} %bitcast.6.local_ref, bf16[128,3712]{1,0:T(8,128)(2,1)} %bitcast.20, bf16[128,3712]{1,0:T(8,128)(2,1)} %collective-permute-done.refs_1_, ...), custom_call_target="tpu_custom_call" | custom-call | flops 8455716864 | bytes 22020096 | tf_op jit(solution)/shard_map/pallas_call | solution.py:134
  109.4 3.9 %all-to-all-start.4 = ((bf16[16,3,8,1792]{3,2,1,0:T(8,128)(2,1)}), bf16[16,3,8,1792]{3,2,1,0:T(8,128)(2,1)S(1)}, u32[]{:S(2)}, u32[]{:S(2)}) async-start(bf16[16,3,8,1792]{3,2,1,0:T(8,128)(2,1)} %get-tuple-element.49), calls=%async_computation.4 | async-start | bytes 2752512 | tf_op jit(solution)/shard_map/all_to_all | solution.py:248
  113.3 0.0 collective-permute-done.1.refs_0_
  113.3 17.4 %shard_map.66 = (bf16[128,1792]{1,0:T(8,128)(2,1)}, bf16[128,1792]{1,0:T(8,128)(2,1)}, bf16[128,1792]{1,0:T(8,128)(2,1)}, bf16[16,3,8,1792]{3,2,1,0:T(8,128)(2,1)}) custom-call(s32[1]{0:T(128)} %bitcast.6.local_ref, bf16[128,3712]{1,0:T(8,128)(2,1)} %collective-permute-done.1.refs_0_, bf16[128,3712]{1,0:T(8,128)(2,1)} %bitcast.17, ...), custom_call_target="tpu_custom_call" | custom-call | flops 8455716864 | bytes 22020096 | tf_op jit(solution)/shard_map/pallas_call | solution.py:134
  130.7 0.0 collective-permute-done.7.refs_0_
  130.7 0.0 collective-permute-done.8.refs_1_
  130.7 0.9 copy-done.7
  131.6 13.9 %shard_map.67 = (bf16[128,1792]{1,0:T(8,128)(2,1)}, bf16[128,1792]{1,0:T(8,128)(2,1)}, bf16[16,2,8,1792]{3,2,1,0:T(8,128)(2,1)}) custom-call(s32[1]{0:T(128)} %bitcast.6.local_ref, bf16[128,3712]{1,0:T(8,128)(2,1)} %copy-done.7, bf16[128,3712]{1,0:T(8,128)(2,1)} %collective-permute-done.8.refs_1_, bf16[1,3584,1024]{2,1,0:T(8,128)(2,1)} %refs_2_.1, ...), custom_call_target="tpu_custom_call" | custom-call | flops 5637144576 | bytes 22020096 | tf_op jit(solution)/shard_map/pallas_call | solution.py:134
  145.6 7.1 %all-to-all-start.6 = ((bf16[16,2,8,1792]{3,2,1,0:T(8,128)(2,1)}), bf16[16,2,8,1792]{3,2,1,0:T(8,128)(2,1)S(1)}, u32[]{:S(2)}, u32[]{:S(2)}) async-start(bf16[16,2,8,1792]{3,2,1,0:T(8,128)(2,1)} %get-tuple-element.51), calls=%async_computation.6 | async-start | bytes 1835008 | tf_op jit(solution)/shard_map/all_to_all | solution.py:248
  152.7 3.9 %collective-permute-start.5 = (bf16[128,1792]{1,0:T(8,128)(2,1)S(1)}, bf16[128,1792]{1,0:T(8,128)(2,1)S(1)}, u32[]{:S(2)}, u32[]{:S(2)}) collective-permute-start(bf16[128,1792]{1,0:T(8,128)(2,1)S(1)} %copy-done.22), channel_id=1, source_target_pairs={{0,3},{1,0},{2,1},{3,2},{4,7},{5,4},{6,5},{7,6},{8,11},{9,8},{10,9... | collective-permute-start | bytes 1376264 | tf_op jit(solution)/shard_map/ppermute | solution.py:221
  156.6 0.0 collective-permute-start.12
  156.6 3.2 %collective-permute-start.13 = (bf16[256,128]{1,0:T(8,128)(2,1)S(1)}, bf16[256,128]{1,0:T(8,128)(2,1)S(1)}, u32[]{:S(2)}, u32[]{:S(2)}) collective-permute-start(bf16[256,128]{1,0:T(8,128)(2,1)S(1)} %copy-done.14), channel_id=1, source_target_pairs={{0,3},{1,0},{2,1},{3,2},{4,7},{5,4},{6,5},{7,6},{8,11},{9,8},{10,9... | collective-permute-start | bytes 196616 | tf_op jit(solution)/shard_map/ppermute | solution.py:221
  159.8 3.0 %collective-permute-done.12.p1 = bf16[256,128]{1,0:T(8,128)(2,1)S(1)} collective-permute-done((bf16[256,128]{1,0:T(8,128)(2,1)S(1)}, bf16[256,128]{1,0:T(8,128)(2,1)S(1)}, u32[]{:S(2)}, u32[]{:S(2)}) %collective-permute-start.12) | collective-permute-done | bytes 65568 | tf_op jit(solution)/shard_map/ppermute | solution.py:218
  162.8 0.0 collective-permute-start.14
  162.8 0.0 collective-permute-start.4
  162.8 1.0 collective-permute-start.10
  163.8 0.5 collective-permute-done.5
  164.3 0.8 copy-done.13
  165.1 3.7 %collective-permute-start.9 = (bf16[128,1792]{1,0:T(8,128)(2,1)}, bf16[128,1792]{1,0:T(8,128)(2,1)S(1)}, u32[]{:S(2)}, u32[]{:S(2)}) collective-permute-start(bf16[128,1792]{1,0:T(8,128)(2,1)} %get-tuple-element.46), channel_id=1, source_target_pairs={{0,3},{1,0},{2,1},{3,2},{4,7},{5,4},{6,5},{7,6},{8,11},{9,8},{10,9... | collective-permute-start | bytes 1376264 | tf_op jit(solution)/shard_map/ppermute | solution.py:221
  168.8 0.9 copy-done.2
  169.7 7.3 %all-to-all-start.5 = ((bf16[16,3,8,1792]{3,2,1,0:T(8,128)(2,1)}), bf16[16,3,8,1792]{3,2,1,0:T(8,128)(2,1)S(1)}, u32[]{:S(2)}, u32[]{:S(2)}) async-start(bf16[16,3,8,1792]{3,2,1,0:T(8,128)(2,1)} %get-tuple-element.50), calls=%async_computation.5 | async-start | bytes 2752512 | tf_op jit(solution)/shard_map/all_to_all | solution.py:248
  177.0 1.3 add_convert_fusion.3
  178.4 4.2 %collective-permute-done.10 = bf16[128,1792]{1,0:T(8,128)(2,1)} collective-permute-done((bf16[128,1792]{1,0:T(8,128)(2,1)}, bf16[128,1792]{1,0:T(8,128)(2,1)}, u32[]{:S(2)}, u32[]{:S(2)}) %collective-permute-start.10) | collective-permute-done | bytes 458784 | tf_op jit(solution)/shard_map/ppermute | solution.py:218
  182.6 1.8 collective-permute-start.6
  184.3 1.9 add_convert_fusion.1
  186.3 0.0 collective-permute-done.4
  186.3 0.3 collective-permute-start.11
  186.6 4.5 %collective-permute-done.6 = bf16[128,1792]{1,0:T(8,128)(2,1)S(1)} collective-permute-done((bf16[128,1792]{1,0:T(8,128)(2,1)S(1)}, bf16[128,1792]{1,0:T(8,128)(2,1)S(1)}, u32[]{:S(2)}, u32[]{:S(2)}) %collective-permute-start.6) | collective-permute-done | bytes 458784 | tf_op jit(solution)/shard_map/ppermute | solution.py:221
  191.1 1.9 fusion
  193.0 7.2 %all-to-all-start.2 = ((bf16[16,8,1792]{2,1,0:T(8,128)(2,1)}), bf16[16,8,1792]{2,1,0:T(8,128)(2,1)S(1)}, u32[]{:S(2)}, u32[]{:S(2)}) async-start(bf16[16,8,1792]{2,1,0:T(8,128)(2,1)} %fusion), calls=%async_computation.2 | async-start | bytes 917504 | tf_op jit(solution)/shard_map/all_to_all | solution.py:215
  200.3 0.6 copy-done.20
  200.9 0.6 copy-done.21
  201.5 4.0 %shard_map.68 = (bf16[128,1792]{1,0:T(8,128)(2,1)}, bf16[128,1792]{1,0:T(8,128)(2,1)}, bf16[128,1792]{1,0:T(8,128)(2,1)}, bf16[64,1792]{1,0:T(8,128)(2,1)}, bf16[64,1792]{1,0:T(8,128)(2,1)}) custom-call(bf16[256,128]{1,0:T(8,128)(2,1)} %get-tuple-element.31.p0.pick, bf16[256,128]{1,0:T(8,128)(2,1)} %copy-done.19, bf16[256,128]{1,0:T(8,128)(2,1)} %copy-done.20, ...), custom_call_target="tpu_custom_call" | custom-call | flops 100000000 | bytes 11796480 | tf_op jit(solution)/shard_map/pallas_call | solution.py:165
  205.6 3.5 %collective-permute-start.15 = (bf16[64,1792]{1,0:T(8,128)(2,1)}, bf16[64,1792]{1,0:T(8,128)(2,1)S(1)}, u32[]{:S(2)}, u32[]{:S(2)}) collective-permute-start(bf16[64,1792]{1,0:T(8,128)(2,1)} %get-tuple-element.54), channel_id=1, source_target_pairs={{0,3},{1,0},{2,1},{3,2},{4,7},{5,4},{6,5},{7,6},{8,11},{9,8},{10,9... | collective-permute-start | bytes 688136 | tf_op jit(solution)/shard_map/ppermute | solution.py:221
  209.1 0.9 fusion.1
  210.1 0.1 collective-permute-start.17
  210.2 2.1 collective-permute-start.18
  212.2 0.1 collective-permute-start.19
  212.3 0.6 collective-permute-done.15
  212.9 0.1 add_convert_fusion.5
  213.0 3.7 %collective-permute-start.16 = (bf16[64,1792]{1,0:T(8,128)(2,1)S(1)}, bf16[64,1792]{1,0:T(8,128)(2,1)S(1)}, u32[]{:S(2)}, u32[]{:S(2)}) collective-permute-start(bf16[64,1792]{1,0:T(8,128)(2,1)S(1)} %add_convert_fusion.5), channel_id=1, source_target_pairs={{0,3},{1,0},{2,1},{3,2},{4,7},{5,4},{6,5},{7,6},{8,11},{9,8},{10,9... | collective-permute-start | bytes 688136 | tf_op jit(solution)/shard_map/ppermute | solution.py:221
  216.7 7.2 %all-to-all-start.3 = ((bf16[16,8,1792]{2,1,0:T(8,128)(2,1)}), bf16[16,8,1792]{2,1,0:T(8,128)(2,1)S(1)}, u32[]{:S(2)}, u32[]{:S(2)}) async-start(bf16[16,8,1792]{2,1,0:T(8,128)(2,1)} %fusion.1), calls=%async_computation.3 | async-start | bytes 917504 | tf_op jit(solution)/shard_map/all_to_all | solution.py:215
  223.9 0.1 add_convert_fusion.4
  224.0 0.1 collective-permute-start.20
  224.1 9.6 %all-to-all-done.3 = bf16[16,8,1792]{2,1,0:T(8,128)(2,1)S(1)} async-done(((bf16[16,8,1792]{2,1,0:T(8,128)(2,1)}), bf16[16,8,1792]{2,1,0:T(8,128)(2,1)S(1)}, u32[]{:S(2)}, u32[]{:S(2)}) %all-to-all-start.3) | async-done | bytes 458784 | tf_op jit(solution)/shard_map/all_to_all | solution.py:215
  233.7 0.7 copy-done.4
  234.4 0.1 copy-done.15
  234.5 0.1 copy-done.16
  234.6 0.1 copy-done.17
  234.6 0.1 copy-done.18
  234.7 3.1 %shard_map.69 = bf16[128,3584]{1,0:T(8,128)(2,1)} custom-call(bf16[256,128]{1,0:T(8,128)(2,1)} %get-tuple-element.31.p0.pick, bf16[128,1792]{1,0:T(8,128)(2,1)} %bitcast.13, bf16[128,1792]{1,0:T(8,128)(2,1)} %bitcast.14, bf16[128,1792]{1,0:T(8,128)(2,1)} %get-tuple-element.52.own, bf16[64,1792]{1,0:T(8,128)(2,1)} %copy-done.17, bf16[64,1792]{1,0:T(8,128)(2,1)} %copy-done.15, ...), custom_call_target="tpu_custom_call" | custom-call | flops 100000000 | bytes 7077888 | tf_op jit(solution)/shard_map/pallas_call | solution.py:165
  (53 shorter events, 0.1 us)
Async XLA Ops:
  28.1 63.9 %copy-start.6 = (bf16[16,8,3712]{2,1,0:T(8,128)(2,1)}, bf16[16,8,3712]{2,1,0:T(8,128)(2,1)S(1)}, u32[]{:S(2)}) copy-start(bf16[16,8,3712]{2,1,0:T(8,128)(2,1)S(1)} %all_to_all.35) | copy-start | bytes 2850820
  28.1 19.0 %all-to-all-start.1 = ((bf16[16,8,3712]{2,1,0:T(8,128)(2,1)}), bf16[16,8,3712]{2,1,0:T(8,128)(2,1)S(1)}, u32[]{:S(2)}, u32[]{:S(2)}) async-start(bf16[16,8,3712]{2,1,0:T(8,128)(2,1)} %bitcast.4), calls=%async_computation.1 | async-start | bytes 1900544 | tf_op jit(solution)/shard_map/all_to_all | solution.py:215
  31.8 23.1 %collective-permute-start = (bf16[128,3712]{1,0:T(8,128)(2,1)S(1)}, bf16[128,3712]{1,0:T(8,128)(2,1)}, u32[]{:S(2)}, u32[]{:S(2)}) collective-permute-start(bf16[128,3712]{1,0:T(8,128)(2,1)S(1)} %bitcast.18), channel_id=1, source_target_pairs={{0,1},{1,2},{2,3},{3,0},{4,5},{5,6},{6,7},{7,4},{8,9},{9,10},{10,1... | collective-permute-start | bytes 2850824 | tf_op jit(solution)/shard_map/ppermute | solution.py:218
  47.1 62.3 %copy-start.5 = (bf16[16,8,3712]{2,1,0:T(8,128)(2,1)}, bf16[16,8,3712]{2,1,0:T(8,128)(2,1)S(1)}, u32[]{:S(2)}) copy-start(bf16[16,8,3712]{2,1,0:T(8,128)(2,1)S(1)} %all-to-all-done.1) | copy-start | bytes 2850820
  47.1 24.5 %collective-permute-start.2 = (bf16[128,3712]{1,0:T(8,128)(2,1)S(1)}, bf16[128,3712]{1,0:T(8,128)(2,1)}, u32[]{:S(2)}, u32[]{:S(2)}) collective-permute-start(bf16[128,3712]{1,0:T(8,128)(2,1)S(1)} %bitcast.15), channel_id=1, source_target_pairs={{0,3},{1,0},{2,1},{3,2},{4,7},{5,4},{6,5},{7,6},{8,11},{9,8},{10,9... | collective-permute-start | bytes 2850824 | tf_op jit(solution)/shard_map/ppermute | solution.py:221
  50.1 41.9 %collective-permute-start.3 = (bf16[128,3712]{1,0:T(8,128)(2,1)S(1)}, bf16[128,3712]{1,0:T(8,128)(2,1)}, u32[]{:S(2)}, u32[]{:S(2)}) collective-permute-start(bf16[128,3712]{1,0:T(8,128)(2,1)S(1)} %bitcast.19), channel_id=1, source_target_pairs={{0,3},{1,0},{2,1},{3,2},{4,7},{5,4},{6,5},{7,6},{8,11},{9,8},{10,9... | collective-permute-start | bytes 2850824 | tf_op jit(solution)/shard_map/ppermute | solution.py:221
  54.9 58.4 %collective-permute-start.1 = (bf16[128,3712]{1,0:T(8,128)(2,1)}, bf16[128,3712]{1,0:T(8,128)(2,1)}, u32[]{:S(2)}, u32[]{:S(2)}) collective-permute-start(bf16[128,3712]{1,0:T(8,128)(2,1)} %collective-permute-done.refs_1_), channel_id=1, source_target_pairs={{0,1},{1,2},{2,3},{3,0},{4,5},{5,6},{6,7},{7,4},{8,9},{9,10},{10,1... | collective-permute-start | bytes 2850824 | tf_op jit(solution)/shard_map/ppermute | solution.py:218
  55.2 75.5 %collective-permute-start.7 = (bf16[128,3712]{1,0:T(8,128)(2,1)S(1)}, bf16[128,3712]{1,0:T(8,128)(2,1)S(1)}, u32[]{:S(2)}, u32[]{:S(2)}) collective-permute-start(bf16[128,3712]{1,0:T(8,128)(2,1)S(1)} %bitcast.16), channel_id=1, source_target_pairs={{0,1},{1,2},{2,3},{3,0},{4,5},{5,6},{6,7},{7,4},{8,9},{9,10},{10,1... | collective-permute-start | bytes 2850824 | tf_op jit(solution)/shard_map/ppermute | solution.py:218
  71.6 59.0 %collective-permute-start.8 = (bf16[128,3712]{1,0:T(8,128)(2,1)}, bf16[128,3712]{1,0:T(8,128)(2,1)}, u32[]{:S(2)}, u32[]{:S(2)}) collective-permute-start(bf16[128,3712]{1,0:T(8,128)(2,1)} %collective-permute-done.2.refs_2_), channel_id=1, source_target_pairs={{0,3},{1,0},{2,1},{3,2},{4,7},{5,4},{6,5},{7,6},{8,11},{9,8},{10,9... | collective-permute-start | bytes 2850824 | tf_op jit(solution)/shard_map/ppermute | solution.py:221
  109.4 36.2 %all-to-all-start.4 = ((bf16[16,3,8,1792]{3,2,1,0:T(8,128)(2,1)}), bf16[16,3,8,1792]{3,2,1,0:T(8,128)(2,1)S(1)}, u32[]{:S(2)}, u32[]{:S(2)}) async-start(bf16[16,3,8,1792]{3,2,1,0:T(8,128)(2,1)} %get-tuple-element.49), calls=%async_computation.4 | async-start | bytes 2752512 | tf_op jit(solution)/shard_map/all_to_all | solution.py:248
  130.7 1.0 copy-start.7
  145.6 7.1 %copy-start.22 = (bf16[128,1792]{1,0:T(8,128)(2,1)S(1)}, bf16[128,1792]{1,0:T(8,128)(2,1)}, u32[]{:S(2)}) copy-start(bf16[128,1792]{1,0:T(8,128)(2,1)} %get-tuple-element.40) | copy-start | bytes 1376260
  145.6 11.0 %copy-start.14 = (bf16[256,128]{1,0:T(8,128)(2,1)S(1)}, bf16[256,128]{1,0:T(8,128)(2,1)}, u32[]{:S(2)}) copy-start(bf16[256,128]{1,0:T(8,128)(2,1)} %get-tuple-element.31.p0.pick) | copy-start | bytes 196612
  145.6 24.1 %copy-start = (bf16[16,3,8,1792]{3,2,1,0:T(8,128)(2,1)}, bf16[16,3,8,1792]{3,2,1,0:T(8,128)(2,1)S(1)}, u32[]{:S(2)}) copy-start(bf16[16,3,8,1792]{3,2,1,0:T(8,128)(2,1)S(1)} %all-to-all-done.4.refs_0_) | copy-start | bytes 4128772
  145.6 23.2 %all-to-all-start.6 = ((bf16[16,2,8,1792]{3,2,1,0:T(8,128)(2,1)}), bf16[16,2,8,1792]{3,2,1,0:T(8,128)(2,1)S(1)}, u32[]{:S(2)}, u32[]{:S(2)}) async-start(bf16[16,2,8,1792]{3,2,1,0:T(8,128)(2,1)} %get-tuple-element.51), calls=%async_computation.6 | async-start | bytes 1835008 | tf_op jit(solution)/shard_map/all_to_all | solution.py:248
  152.7 11.6 %collective-permute-start.5 = (bf16[128,1792]{1,0:T(8,128)(2,1)S(1)}, bf16[128,1792]{1,0:T(8,128)(2,1)S(1)}, u32[]{:S(2)}, u32[]{:S(2)}) collective-permute-start(bf16[128,1792]{1,0:T(8,128)(2,1)S(1)} %copy-done.22), channel_id=1, source_target_pairs={{0,3},{1,0},{2,1},{3,2},{4,7},{5,4},{6,5},{7,6},{8,11},{9,8},{10,9... | collective-permute-start | bytes 1376264 | tf_op jit(solution)/shard_map/ppermute | solution.py:221
  156.6 6.2 %collective-permute-start.12 = (bf16[256,128]{1,0:T(8,128)(2,1)S(1)}, bf16[256,128]{1,0:T(8,128)(2,1)S(1)}, u32[]{:S(2)}, u32[]{:S(2)}) collective-permute-start(bf16[256,128]{1,0:T(8,128)(2,1)S(1)} %copy-done.14), channel_id=1, source_target_pairs={{0,1},{1,2},{2,3},{3,0},{4,5},{5,6},{6,7},{7,4},{8,9},{9,10},{10,1... | collective-permute-start | bytes 196616 | tf_op jit(solution)/shard_map/ppermute | solution.py:218
  156.6 43.7 %collective-permute-start.13 = (bf16[256,128]{1,0:T(8,128)(2,1)S(1)}, bf16[256,128]{1,0:T(8,128)(2,1)S(1)}, u32[]{:S(2)}, u32[]{:S(2)}) collective-permute-start(bf16[256,128]{1,0:T(8,128)(2,1)S(1)} %copy-done.14), channel_id=1, source_target_pairs={{0,3},{1,0},{2,1},{3,2},{4,7},{5,4},{6,5},{7,6},{8,11},{9,8},{10,9... | collective-permute-start | bytes 196616 | tf_op jit(solution)/shard_map/ppermute | solution.py:221
  162.8 30.2 %copy-start.19 = (bf16[256,128]{1,0:T(8,128)(2,1)}, bf16[256,128]{1,0:T(8,128)(2,1)S(1)}, u32[]{:S(2)}) copy-start(bf16[256,128]{1,0:T(8,128)(2,1)S(1)} %collective-permute-done.12.p1) | copy-start | bytes 196612
  162.8 37.5 %collective-permute-start.14 = (bf16[256,128]{1,0:T(8,128)(2,1)S(1)}, bf16[256,128]{1,0:T(8,128)(2,1)S(1)}, u32[]{:S(2)}, u32[]{:S(2)}) collective-permute-start(bf16[256,128]{1,0:T(8,128)(2,1)S(1)} %collective-permute-done.12.p1), channel_id=1, source_target_pairs={{0,1},{1,2},{2,3},{3,0},{4,5},{5,6},{6,7},{7,4},{8,9},{9,10},{10,1... | collective-permute-start | bytes 196616 | tf_op jit(solution)/shard_map/ppermute | solution.py:218
  162.8 23.5 %collective-permute-start.4 = (bf16[128,1792]{1,0:T(8,128)(2,1)}, bf16[128,1792]{1,0:T(8,128)(2,1)}, u32[]{:S(2)}, u32[]{:S(2)}) collective-permute-start(bf16[128,1792]{1,0:T(8,128)(2,1)} %get-tuple-element.36), channel_id=1, source_target_pairs={{0,1},{1,2},{2,3},{3,0},{4,5},{5,6},{6,7},{7,4},{8,9},{9,10},{10,1... | collective-permute-start | bytes 1376264 | tf_op jit(solution)/shard_map/ppermute | solution.py:218
  162.8 19.7 %collective-permute-start.10 = (bf16[128,1792]{1,0:T(8,128)(2,1)}, bf16[128,1792]{1,0:T(8,128)(2,1)}, u32[]{:S(2)}, u32[]{:S(2)}) collective-permute-start(bf16[128,1792]{1,0:T(8,128)(2,1)} %get-tuple-element.47), channel_id=1, source_target_pairs={{0,1},{1,2},{2,3},{3,0},{4,5},{5,6},{6,7},{7,4},{8,9},{9,10},{10,1... | collective-permute-start | bytes 1376264 | tf_op jit(solution)/shard_map/ppermute | solution.py:218
  164.3 0.8 copy-start.13
  165.1 44.0 %collective-permute-start.9 = (bf16[128,1792]{1,0:T(8,128)(2,1)}, bf16[128,1792]{1,0:T(8,128)(2,1)S(1)}, u32[]{:S(2)}, u32[]{:S(2)}) collective-permute-start(bf16[128,1792]{1,0:T(8,128)(2,1)} %get-tuple-element.46), channel_id=1, source_target_pairs={{0,3},{1,0},{2,1},{3,2},{4,7},{5,4},{6,5},{7,6},{8,11},{9,8},{10,9... | collective-permute-start | bytes 1376264 | tf_op jit(solution)/shard_map/ppermute | solution.py:221
  168.8 0.9 copy-start.2
  169.7 23.3 %all-to-all-start.5 = ((bf16[16,3,8,1792]{3,2,1,0:T(8,128)(2,1)}), bf16[16,3,8,1792]{3,2,1,0:T(8,128)(2,1)S(1)}, u32[]{:S(2)}, u32[]{:S(2)}) async-start(bf16[16,3,8,1792]{3,2,1,0:T(8,128)(2,1)} %get-tuple-element.50), calls=%async_computation.5 | async-start | bytes 2752512 | tf_op jit(solution)/shard_map/all_to_all | solution.py:248
  177.0 7.3 %copy-start.12 = (bf16[128,1792]{1,0:T(8,128)(2,1)S(1)}, bf16[128,1792]{1,0:T(8,128)(2,1)}, u32[]{:S(2)}) copy-start(bf16[128,1792]{1,0:T(8,128)(2,1)} %get-tuple-element.48) | copy-start | bytes 1376260
  177.0 14.0 %copy-start.9 = (bf16[128,1792]{1,0:T(8,128)(2,1)S(1)}, bf16[128,1792]{1,0:T(8,128)(2,1)}, u32[]{:S(2)}) copy-start(bf16[128,1792]{1,0:T(8,128)(2,1)} %get-tuple-element.35) | copy-start | bytes 1376260
  182.6 8.5 %collective-permute-start.6 = (bf16[128,1792]{1,0:T(8,128)(2,1)S(1)}, bf16[128,1792]{1,0:T(8,128)(2,1)S(1)}, u32[]{:S(2)}, u32[]{:S(2)}) collective-permute-start(bf16[128,1792]{1,0:T(8,128)(2,1)S(1)} %add_convert_fusion.3), channel_id=1, source_target_pairs={{0,3},{1,0},{2,1},{3,2},{4,7},{5,4},{6,5},{7,6},{8,11},{9,8},{10,9... | collective-permute-start | bytes 1376264 | tf_op jit(solution)/shard_map/ppermute | solution.py:221
  186.3 22.8 %collective-permute-start.11 = (bf16[128,1792]{1,0:T(8,128)(2,1)}, bf16[128,1792]{1,0:T(8,128)(2,1)S(1)}, u32[]{:S(2)}, u32[]{:S(2)}) collective-permute-start(bf16[128,1792]{1,0:T(8,128)(2,1)} %add_convert_fusion.1), channel_id=1, source_target_pairs={{0,1},{1,2},{2,3},{3,0},{4,5},{5,6},{6,7},{7,4},{8,9},{9,10},{10,1... | collective-permute-start | bytes 1376264 | tf_op jit(solution)/shard_map/ppermute | solution.py:218
  193.0 7.3 %copy-start.1 = (bf16[16,3,8,1792]{3,2,1,0:T(8,128)(2,1)}, bf16[16,3,8,1792]{3,2,1,0:T(8,128)(2,1)S(1)}, u32[]{:S(2)}) copy-start(bf16[16,3,8,1792]{3,2,1,0:T(8,128)(2,1)S(1)} %all-to-all-done.5.refs_1_) | copy-start | bytes 4128772
  193.0 23.6 %all-to-all-start.2 = ((bf16[16,8,1792]{2,1,0:T(8,128)(2,1)}), bf16[16,8,1792]{2,1,0:T(8,128)(2,1)S(1)}, u32[]{:S(2)}, u32[]{:S(2)}) async-start(bf16[16,8,1792]{2,1,0:T(8,128)(2,1)} %fusion), calls=%async_computation.2 | async-start | bytes 917504 | tf_op jit(solution)/shard_map/all_to_all | solution.py:215
  200.3 8.8 %copy-start.8 = (bf16[128,1792]{1,0:T(8,128)(2,1)S(1)}, bf16[128,1792]{1,0:T(8,128)(2,1)}, u32[]{:S(2)}) copy-start(bf16[128,1792]{1,0:T(8,128)(2,1)} %get-tuple-element.43) | copy-start | bytes 1376260
  200.3 0.6 copy-start.20
  200.9 0.6 copy-start.21
  205.5 4.5 %copy-start.11 = (bf16[128,1792]{1,0:T(8,128)(2,1)S(1)}, bf16[128,1792]{1,0:T(8,128)(2,1)}, u32[]{:S(2)}) copy-start(bf16[128,1792]{1,0:T(8,128)(2,1)} %get-tuple-element.53) | copy-start | bytes 1376260
  205.5 4.6 %copy-start.10 = (bf16[128,1792]{1,0:T(8,128)(2,1)S(1)}, bf16[128,1792]{1,0:T(8,128)(2,1)}, u32[]{:S(2)}) copy-start(bf16[128,1792]{1,0:T(8,128)(2,1)} %get-tuple-element.55) | copy-start | bytes 1376260
  205.5 6.7 %copy-start.23 = (bf16[64,1792]{1,0:T(8,128)(2,1)S(1)}, bf16[64,1792]{1,0:T(8,128)(2,1)}, u32[]{:S(2)}) copy-start(bf16[64,1792]{1,0:T(8,128)(2,1)} %get-tuple-element.56) | copy-start | bytes 688132
  205.6 7.4 %collective-permute-start.15 = (bf16[64,1792]{1,0:T(8,128)(2,1)}, bf16[64,1792]{1,0:T(8,128)(2,1)S(1)}, u32[]{:S(2)}, u32[]{:S(2)}) collective-permute-start(bf16[64,1792]{1,0:T(8,128)(2,1)} %get-tuple-element.54), channel_id=1, source_target_pairs={{0,3},{1,0},{2,1},{3,2},{4,7},{5,4},{6,5},{7,6},{8,11},{9,8},{10,9... | collective-permute-start | bytes 688136 | tf_op jit(solution)/shard_map/ppermute | solution.py:221
  210.1 23.6 %collective-permute-start.17 = (bf16[64,1792]{1,0:T(8,128)(2,1)S(1)}, bf16[64,1792]{1,0:T(8,128)(2,1)S(1)}, u32[]{:S(2)}, u32[]{:S(2)}) collective-permute-start(bf16[64,1792]{1,0:T(8,128)(2,1)S(1)} %slice.13), channel_id=1, source_target_pairs={{0,3},{1,0},{2,1},{3,2},{4,7},{5,4},{6,5},{7,6},{8,11},{9,8},{10,9... | collective-permute-start | bytes 688136 | tf_op jit(solution)/shard_map/ppermute | solution.py:221
  210.2 23.5 %collective-permute-start.18 = (bf16[64,1792]{1,0:T(8,128)(2,1)S(1)}, bf16[64,1792]{1,0:T(8,128)(2,1)S(1)}, u32[]{:S(2)}, u32[]{:S(2)}) collective-permute-start(bf16[64,1792]{1,0:T(8,128)(2,1)S(1)} %slice.14), channel_id=1, source_target_pairs={{0,1},{1,2},{2,3},{3,0},{4,5},{5,6},{6,7},{7,4},{8,9},{9,10},{10,1... | collective-permute-start | bytes 688136 | tf_op jit(solution)/shard_map/ppermute | solution.py:218
  212.2 11.6 %collective-permute-start.19 = (bf16[64,1792]{1,0:T(8,128)(2,1)S(1)}, bf16[64,1792]{1,0:T(8,128)(2,1)S(1)}, u32[]{:S(2)}, u32[]{:S(2)}) collective-permute-start(bf16[64,1792]{1,0:T(8,128)(2,1)S(1)} %copy-done.23), channel_id=1, source_target_pairs={{0,1},{1,2},{2,3},{3,0},{4,5},{5,6},{6,7},{7,4},{8,9},{9,10},{10,1... | collective-permute-start | bytes 688136 | tf_op jit(solution)/shard_map/ppermute | solution.py:218
  213.0 20.7 %collective-permute-start.16 = (bf16[64,1792]{1,0:T(8,128)(2,1)S(1)}, bf16[64,1792]{1,0:T(8,128)(2,1)S(1)}, u32[]{:S(2)}, u32[]{:S(2)}) collective-permute-start(bf16[64,1792]{1,0:T(8,128)(2,1)S(1)} %add_convert_fusion.5), channel_id=1, source_target_pairs={{0,3},{1,0},{2,1},{3,2},{4,7},{5,4},{6,5},{7,6},{8,11},{9,8},{10,9... | collective-permute-start | bytes 688136 | tf_op jit(solution)/shard_map/ppermute | solution.py:221
  216.7 17.0 %copy-start.3 = (bf16[16,8,1792]{2,1,0:T(8,128)(2,1)}, bf16[16,8,1792]{2,1,0:T(8,128)(2,1)S(1)}, u32[]{:S(2)}) copy-start(bf16[16,8,1792]{2,1,0:T(8,128)(2,1)S(1)} %all-to-all-done.2) | copy-start | bytes 1376260
  216.7 17.0 %all-to-all-start.3 = ((bf16[16,8,1792]{2,1,0:T(8,128)(2,1)}), bf16[16,8,1792]{2,1,0:T(8,128)(2,1)S(1)}, u32[]{:S(2)}, u32[]{:S(2)}) async-start(bf16[16,8,1792]{2,1,0:T(8,128)(2,1)} %fusion.1), calls=%async_computation.3 | async-start | bytes 917504 | tf_op jit(solution)/shard_map/all_to_all | solution.py:215
  224.0 9.7 %collective-permute-start.20 = (bf16[64,1792]{1,0:T(8,128)(2,1)S(1)}, bf16[64,1792]{1,0:T(8,128)(2,1)S(1)}, u32[]{:S(2)}, u32[]{:S(2)}) collective-permute-start(bf16[64,1792]{1,0:T(8,128)(2,1)S(1)} %add_convert_fusion.4), channel_id=1, source_target_pairs={{0,1},{1,2},{2,3},{3,0},{4,5},{5,6},{6,7},{7,4},{8,9},{9,10},{10,1... | collective-permute-start | bytes 688136 | tf_op jit(solution)/shard_map/ppermute | solution.py:218
  233.6 0.8 copy-start.4
  233.6 0.9 copy-start.15
  233.7 0.9 copy-start.16
  233.7 1.0 copy-start.17
  233.7 1.0 copy-start.18

commit v3 on v2

v3 whole, which is shorter than its diff:
```python
import functools

import jax
import jax.numpy as jnp
from jax import lax
from jax.experimental import pallas as pl
from jax.experimental.pallas import tpu as pltpu
from jax.sharding import PartitionSpec as P

LANES = 128
PIECE = 128
VMEM = 60 * 1024 * 1024
NEAR_TILES = 16


def slot_maps(ids_t, groups, per_group):
    slots, tokens = groups * per_group, ids_t.shape[1]
    slot = lax.broadcasted_iota(jnp.int32, (slots, tokens), 0)
    group, rank = slot // per_group, slot % per_group
    named = jnp.zeros((slots, tokens), jnp.bool_)
    for k in range(ids_t.shape[0]):
        named = named | (ids_t[k : k + 1, :] // 4 == group)
    before = lax.broadcasted_iota(jnp.int32, (tokens, tokens), 0) < lax.broadcasted_iota(
        jnp.int32, (tokens, tokens), 1
    )
    earlier = jnp.dot(
        named.astype(jnp.bfloat16), before.astype(jnp.bfloat16), preferred_element_type=jnp.float32
    )
    mine = named & (earlier == rank.astype(jnp.float32))
    return mine, group


def prepare_kernel(locals_, groups, per_group, tok, scores_t, ids_t, out, pick):
    ids = ids_t[...]
    mine, group = slot_maps(ids, groups, per_group)
    onehot = mine.astype(jnp.bfloat16)
    pick[...] = onehot
    score = scores_t[...]
    total = score[0:1, :]
    for k in range(1, score.shape[0]):
        total = total + score[k : k + 1, :]
    gates = (2.5 * score / total).astype(jnp.bfloat16).astype(jnp.float32)
    width = tok.shape[1]
    lane = lax.broadcasted_iota(jnp.int32, (mine.shape[0], LANES), 1)
    meta = jnp.zeros((mine.shape[0], LANES), jnp.float32)
    for j in range(locals_):
        value = jnp.zeros(mine.shape, jnp.float32)
        for k in range(ids.shape[0]):
            value = value + jnp.where(
                mine & (ids[k : k + 1, :] == group * locals_ + j), gates[k : k + 1, :], 0.0
            )
        meta = jnp.where(lane == j, jnp.sum(value, axis=1, keepdims=True), meta)
    token = lax.broadcasted_iota(jnp.int32, mine.shape, 1).astype(jnp.float32)
    token = jnp.sum(jnp.where(mine, token, 0.0), axis=1, keepdims=True)
    meta = jnp.where(lane == locals_, token, meta)
    out[:, width : width + LANES] = meta.astype(jnp.bfloat16)
    for j in range(width // LANES):
        cols = slice(j * LANES, (j + 1) * LANES)
        x = tok[:, cols].astype(jnp.float32)
        largest = jnp.max(jnp.abs(x), axis=1, keepdims=True)
        scale = ((largest + 1e-06) / 448.0).astype(jnp.bfloat16).astype(jnp.float32)
        quantized = (x / scale).astype(jnp.bfloat16).astype(jnp.float32)
        restored = (quantized * scale).astype(jnp.bfloat16)
        rows = jnp.dot(onehot, restored, preferred_element_type=jnp.float32)
        out[:, cols] = rows.astype(jnp.bfloat16)


def prepare(tokens, gate_scores, expert_ids, groups, locals_):
    count, width = tokens.shape
    per_group = 2 * count // groups
    slots = groups * per_group
    return pl.pallas_call(
        functools.partial(prepare_kernel, locals_, groups, per_group),
        out_shape=[
            jax.ShapeDtypeStruct((slots, width + LANES), jnp.bfloat16),
            jax.ShapeDtypeStruct((slots, count), jnp.bfloat16),
        ],
        compiler_params=pltpu.CompilerParams(vmem_limit_bytes=VMEM),
        cost_estimate=pl.CostEstimate(flops=10**9, bytes_accessed=3 * 10**6, transcendentals=0),
    )(tokens, gate_scores.T, expert_ids.T)


def expert_kernel(blocks, local_ref, *refs):
    xs, (wg, wu, wd), refs = refs[:blocks], refs[blocks : blocks + 3], refs[blocks + 3 :]
    outs, direct, rows, acc = refs[:blocks], refs[blocks], refs[blocks + 1], refs[blocks + 2]
    step, steps = pl.program_id(0), pl.num_programs(0)
    width, near = rows.shape[1], outs[0].shape[1]
    piece = xs[0].shape[0]

    @pl.when(step == 0)
    def _():
        for b in range(blocks):
            rows[b * piece : (b + 1) * piece, :] = xs[b][:, :width]

    x = rows[...]
    gate = jnp.dot(x, wg[0], preferred_element_type=jnp.float32)
    up = jnp.dot(x, wu[0], preferred_element_type=jnp.float32)
    hidden = (gate / (1.0 + jnp.exp(-gate)) * up).astype(jnp.bfloat16)
    part = jnp.dot(hidden, wd[0], preferred_element_type=jnp.float32)

    @pl.when(step == 0)
    def _():
        acc[...] = part

    @pl.when((step > 0) & (step < steps - 1))
    def _():
        acc[...] += part

    @pl.when(step == steps - 1)
    def _():
        for b in range(blocks):
            meta = xs[b][:, width : width + LANES].astype(jnp.float32)
            lane = lax.broadcasted_iota(jnp.int32, meta.shape, 1)
            weight = jnp.sum(jnp.where(lane == local_ref[0], meta, 0.0), axis=1, keepdims=True)
            own = slice(b * piece, (b + 1) * piece)
            value = (acc[own, :] + part[own, :]) * weight
            outs[b][...] = value[:, :near].astype(jnp.bfloat16)
            far = value[:, near:]
            shape = direct.shape[0], direct.shape[2]
            direct[:, b, :, : far.shape[1]] = far.reshape(*shape, far.shape[1]).astype(jnp.bfloat16)
            direct[:, b, :, far.shape[1] :] = meta.reshape(*shape, LANES).astype(jnp.bfloat16)


def experts(xs, local, groups, near, w_gate, w_up, w_down, tile=256):
    blocks = len(xs)
    piece, wide = xs[0].shape
    width, hidden = w_gate.shape[1:]
    direct = (groups, blocks, piece // groups, width - near + LANES)
    return pl.pallas_call(
        functools.partial(expert_kernel, blocks),
        grid=(hidden // tile,),
        in_specs=[pl.BlockSpec(memory_space=pltpu.SMEM)]
        + [pl.BlockSpec((piece, wide), lambda i: (0, 0))] * blocks
        + [
            pl.BlockSpec((1, width, tile), lambda i: (0, 0, i)),
            pl.BlockSpec((1, width, tile), lambda i: (0, 0, i)),
            pl.BlockSpec((1, tile, width), lambda i: (0, i, 0)),
        ],
        out_specs=[pl.BlockSpec((piece, near), lambda i: (0, 0))] * blocks
        + [pl.BlockSpec(direct, lambda i: (0, 0, 0, 0))],
        out_shape=[jax.ShapeDtypeStruct((piece, near), jnp.bfloat16)] * blocks
        + [jax.ShapeDtypeStruct(direct, jnp.bfloat16)],
        scratch_shapes=[
            pltpu.VMEM((blocks * piece, width), jnp.bfloat16),
            pltpu.VMEM((blocks * piece, width), jnp.float32),
        ],
        compiler_params=pltpu.CompilerParams(
            vmem_limit_bytes=VMEM, dimension_semantics=("arbitrary",)
        ),
        cost_estimate=pl.CostEstimate(
            flops=6 * blocks * piece * width * hidden,
            bytes_accessed=6 * width * hidden,
            transcendentals=blocks * piece * hidden,
        ),
    )(local, *xs, w_gate, w_up, w_down)


def whole(kernel, shapes, *arrays):
    moved = sum(x.size * x.dtype.itemsize for x in arrays)
    return pl.pallas_call(
        kernel,
        out_shape=shapes,
        compiler_params=pltpu.CompilerParams(vmem_limit_bytes=VMEM),
        cost_estimate=pl.CostEstimate(flops=10**8, bytes_accessed=3 * moved, transcendentals=0),
    )(*arrays)


def to_tokens(pick, rows):
    return lax.dot_general(pick, rows, (((0,), (0,)), ((), ())), preferred_element_type=jnp.float32)


def scatter_kernel(where, locals_, first, second, third, own, below, above, far_lo, far_hi):
    groups = (first, second, third)
    count, width = own.shape
    half = count // 2
    for name, out in (("own", own), ("below", below), ("above", above), ("far", None)):
        total = None
        for which, place in where[name]:
            rows = groups[which][:, place].reshape(PIECE, width + LANES)
            meta = rows[:, width:].astype(jnp.float32)
            lane = lax.broadcasted_iota(jnp.int32, meta.shape, 1)
            token = jnp.sum(jnp.where(lane == locals_, meta, 0.0), axis=1, keepdims=True)
            lane = lax.broadcasted_iota(jnp.int32, (PIECE, count), 1)
            pick = (lane.astype(jnp.float32) == token).astype(jnp.bfloat16)
            part = to_tokens(pick, rows[:, :width])
            total = part if total is None else total + part
        total = total.astype(jnp.bfloat16)
        if out is not None:
            out[...] = total
        else:
            far_lo[...] = total[:half]
            far_hi[...] = total[half:]


def pack_kernel(back_a, below_a, below_b, back_b, above_a, above_b, down, up):
    def both(x, y):
        return (x[...].astype(jnp.float32) + y[...].astype(jnp.float32)).astype(jnp.bfloat16)

    down[0] = both(back_a, below_a)
    down[1] = below_b[...]
    up[0] = above_a[...]
    up[1] = both(back_b, above_b)


def total_kernel(own_a, own_b, above, below, out):
    for half, own in enumerate((own_a, own_b)):
        total = own[...].astype(jnp.float32) + above[half].astype(jnp.float32)
        total = total + below[half].astype(jnp.float32)
        shape = out.shape[0], out.shape[2], out.shape[3]
        out[:, half] = total.reshape(shape).astype(jnp.bfloat16)


def join_kernel(below, more_lo, above, more_hi, out_down, out_up):
    half = more_lo.shape[0]

    def plus(x, y):
        return (x.astype(jnp.float32) + y.astype(jnp.float32)).astype(jnp.bfloat16)

    out_down[:half, :] = plus(below[:half, :], more_lo[...])
    out_down[half:, :] = below[half:, :]
    out_up[:half, :] = above[:half, :]
    out_up[half:, :] = plus(above[half:, :], more_hi[...])


def collect_kernel(pick, rows, own, from_above, from_below, out):
    near = rows.shape[1]
    out[:, :near] = to_tokens(pick[...], rows[...]).astype(jnp.bfloat16)
    total = own[...].astype(jnp.float32) + from_above[...].astype(jnp.float32)
    out[:, near:] = (total + from_below[...].astype(jnp.float32)).astype(jnp.bfloat16)


def per_device(tokens, gate_scores, expert_ids, w_gate, w_up, w_down):
    groups, locals_ = lax.axis_size("node"), lax.axis_size("local")
    local = lax.axis_index("local").astype(jnp.int32).reshape(1)
    count, width = tokens.shape
    near = NEAR_TILES * LANES
    tie = lax.optimization_barrier

    def across(block):
        return lax.all_to_all(block, "node", 0, 0, tiled=True)

    def up(block):
        return lax.ppermute(block, "local", [(i, (i + 1) % locals_) for i in range(locals_)])

    def down(block):
        return lax.ppermute(block, "local", [(i, (i - 1) % locals_) for i in range(locals_)])

    def like(*shape):
        return jax.ShapeDtypeStruct(shape, jnp.bfloat16)

    run = functools.partial(
        experts, local=local, groups=groups, near=near, w_gate=w_gate, w_up=w_up, w_down=w_down
    )

    send, pick = prepare(tokens, gate_scores, expert_ids, groups, locals_)
    eight = PIECE // groups
    own = across(send.reshape(groups, 2, eight, width + LANES))
    own_a = own[:, 0].reshape(PIECE, width + LANES)
    own_b = own[:, 1].reshape(PIECE, width + LANES)
    below_a, above_b = up(own_a), down(own_b)
    far_a, far_b = up(below_a), down(above_b)
    last_a, last_b, _, _ = tie((own_a, own_b, far_a, far_b))
    below_b, above_a = up(last_b), down(last_a)

    own_pa, own_pb, first = run([own_a, own_b])
    below_a, above_b, far_a, far_b, first = tie((below_a, above_b, far_a, far_b, first))
    below_pa, above_pb, far_pa, far_pb, second = run([below_a, above_b, far_a, far_b])
    below_b, above_a, second = tie((below_b, above_a, second))
    below_pb, above_pa, third = run([below_b, above_a])

    first = across(first)
    second, first = tie((second, first))
    second = across(second)
    third, second = tie((third, second))
    third = across(third)

    back_a, back_b = down(far_pa), up(far_pb)
    go_down, go_up = whole(
        pack_kernel, [like(2, PIECE, near)] * 2, back_a, below_pa, below_pb, back_b, above_pa, above_pb
    )
    from_above, from_below = down(go_down), up(go_up)
    total = whole(
        total_kernel, like(groups, 2, eight, near), own_pa, own_pb, from_above, from_below
    )
    final = across(total).reshape(2 * PIECE, near)

    where = {
        "own": ((0, 0), (0, 1)), "below": ((1, 0), (2, 0)), "above": ((2, 1), (1, 1)), "far": ((1, 2), (1, 3)),
    }
    full, part = like(count, width - near), like(count // 2, width - near)
    own_t, below_t, above_t, far_lo, far_hi = whole(
        functools.partial(scatter_kernel, where, locals_), [full, full, full, part, part], first, second, third
    )
    more_lo, more_hi = down(far_lo), up(far_hi)
    go_down, go_up = whole(join_kernel, [full, full], below_t, more_lo, above_t, more_hi)
    from_above, from_below = down(go_down), up(go_up)
    return whole(collect_kernel, like(count, width), pick, final, own_t, from_above, from_below)


def solution(mesh):
    in_specs = (
        P(("dp", "node", "local"), None),
        P(("dp", "node", "local"), None),
        P(("dp", "node", "local"), None),
        P(("node", "local"), None, None),
        P(("node", "local"), None, None),
        P(("node", "local"), None, None),
    )
    out_specs = P(("dp", "node", "local"), None)
    return jax.shard_map(
        per_device, mesh=mesh, in_specs=in_specs, out_specs=out_specs, check_vma=False
    )
```

time: 239 us -> 205 us (0.86)
  starting transfers between devices: 70.8 us -> 43.4 us
  waiting for transfers between devices: 71.6 us -> 54.1 us
  blocking collectives: 24.1 us -> 34.2 us
  Pallas kernels: 59.9 us -> 68.7 us
  other arithmetic: 6.28 us -> 0 us
    all_to_all x6 -> x4, waiting for transfers between devices: 23.3 us -> 0.01 us  [across(): return lax.all_to_all(block, 'node', 0, 0, tiled=True)]
    ppermute x10 -> x7, starting transfers between devices: 27.4 us -> 11.9 us  [down(): lax.ppermute(block, 'local', [(i, (i - 1) % locals_) for i in range(local...]
    all_to_all x6 -> x4, starting transfers between devices: 36.4 us -> 25 us  [across(): return lax.all_to_all(block, 'node', 0, 0, tiled=True)]
    all_to_all x1, blocking collectives: 24.1 us -> 34.2 us  [across(): return lax.all_to_all(block, 'node', 0, 0, tiled=True)]
    pallas_call x2 -> x5, Pallas kernels: 7.17 us -> 15.5 us  [whole(): pl.pallas_call(kernel, out_shape=shapes, compiler_params=pltpu.CompilerPa...]
    ppermute x10 -> x7, waiting for transfers between devices: 37.1 us -> 45 us  [down(): lax.ppermute(block, 'local', [(i, (i - 1) % locals_) for i in range(local...]
    convert_element_type x4 -> x0, other arithmetic: 3.4 us -> none  [add(): return total.astype(jnp.bfloat16)]
    reshape x2 -> x0, other arithmetic: 2.88 us -> none  [across(): parts = block.reshape(groups, block.shape[0] // groups, block.shape[1])]
  transfers between devices with their start and end apart: 27 -> 18, of which waited for: 10 -> 9; matrix products, arithmetic and copies ran while one was open for 3% -> 0% of each run, Pallas kernels for 22% -> 30%
where the time goes in v3:
time: 205 us; the launch traced here: 204 us
  Pallas kernels  68.7 us (34%)
  waiting for transfers between devices  54.1 us (26%)
  starting transfers between devices  43.4 us (21%)
  blocking collectives  34.2 us (17%)
  local copies, waits for them, and re-layouts  3.34 us (2%)
    pallas_call x3, Pallas kernels, experts(): pl.pallas_call(functools.partial(expert_kernel, blocks), grid=(hidden //...  49.2 us
    ppermute x7, waiting for transfers between devices, down(): lax.ppermute(block, 'local', [(i, (i - 1) % locals_) for i in range(local...  45 us
    all_to_all x1, blocking collectives, across(): return lax.all_to_all(block, 'node', 0, 0, tiled=True)  34.2 us
    all_to_all x4, starting transfers between devices, across(): return lax.all_to_all(block, 'node', 0, 0, tiled=True)  25 us
    pallas_call x5, Pallas kernels, whole(): pl.pallas_call(kernel, out_shape=shapes, compiler_params=pltpu.CompilerPa...  15.5 us
    ppermute x7, starting transfers between devices, down(): lax.ppermute(block, 'local', [(i, (i - 1) % locals_) for i in range(local...  11.9 us
    ppermute x7, waiting for transfers between devices, up(): lax.ppermute(block, 'local', [(i, (i + 1) % locals_) for i in range(local...  9.17 us
    ppermute x7, starting transfers between devices, up(): lax.ppermute(block, 'local', [(i, (i + 1) % locals_) for i in range(local...  6.51 us
  transfers between devices with their start and end apart: 18, of which 9 were waited for; matrix products, arithmetic and copies ran while one was open for 0% of the time, Pallas kernels for 30%

profile of v3, /device:TPU:0, one launch (start us, length us, event | category | flops | bytes accessed | tf_op | source)
XLA Modules:
  0.0 204.0 jit_solution(13125678202530095146)
XLA Ops:
  0.0 4.1 %shard_map.64 = (bf16[256,3712]{1,0:T(8,128)(2,1)}, bf16[256,128]{1,0:T(8,128)(2,1)}) custom-call(bf16[128,3584]{1,0:T(8,128)(2,1)} %tok.1, f32[4,128]{1,0:T(4,128)} %bitcast.11, s32[4,128]{1,0:T(4,128)} %bitcast.12), custom_call_target="tpu_custom_call" | custom-call | flops 1000000000 | bytes 3000000 | tf_op jit(solution)/shard_map/pallas_call | solution.py:72
  4.1 34.2 %all_to_all.25 = bf16[16,2,8,3712]{3,2,1,0:T(8,128)(2,1)S(1)} all-to-all(bf16[16,2,8,3712]{3,2,1,0:T(8,128)(2,1)} %bitcast.10), channel_id=1, replica_groups=mesh['dp'=2,'node'=16,'local'=4] {'node'}, dimensions={0} | all-to-all | bytes 3801088 | tf_op jit(solution)/shard_map/all_to_all | solution.py:240
  38.3 0.1 slice_bitcast_fusion
  38.4 0.0 copy-start.2
  38.5 0.0 copy-start.3
  38.5 3.1 %collective-permute-start.1 = (bf16[128,3712]{1,0:T(8,128)(2,1)S(1)}, bf16[128,3712]{1,0:T(8,128)(2,1)S(1)}, u32[]{:S(2)}, u32[]{:S(2)}) collective-permute-start(bf16[128,3712]{1,0:T(8,128)(2,1)S(1)} %get-tuple-element.52.refs_1_), channel_id=1, source_target_pairs={{0,3},{1,0},{2,1},{3,2},{4,7},{5,4},{6,5},{7,6},{8,11},{9,8},{10,9... | collective-permute-start | bytes 2850824 | tf_op jit(solution)/shard_map/ppermute | solution.py:246
  41.6 0.0 collective-permute-start
  41.6 19.2 %collective-permute-done.1.refs_1_ = bf16[128,3712]{1,0:T(8,128)(2,1)S(1)} collective-permute-done((bf16[128,3712]{1,0:T(8,128)(2,1)S(1)}, bf16[128,3712]{1,0:T(8,128)(2,1)S(1)}, u32[]{:S(2)}, u32[]{:S(2)}) %collective-permute-start.1) | collective-permute-done | bytes 950304 | tf_op jit(solution)/shard_map/ppermute | solution.py:246
  60.7 3.7 %collective-permute-start.3 = (bf16[128,3712]{1,0:T(8,128)(2,1)S(1)}, bf16[128,3712]{1,0:T(8,128)(2,1)}, u32[]{:S(2)}, u32[]{:S(2)}) collective-permute-start(bf16[128,3712]{1,0:T(8,128)(2,1)S(1)} %collective-permute-done.1.refs_1_), channel_id=1, source_target_pairs={{0,3},{1,0},{2,1},{3,2},{4,7},{5,4},{6,5},{7,6},{8,11},{9,8},{10,9... | collective-permute-start | bytes 2850824 | tf_op jit(solution)/shard_map/ppermute | solution.py:246
  64.4 0.0 collective-permute-done.refs_0_
  64.4 0.0 collective-permute-start.2
  64.4 0.0 copy-done.2
  64.4 0.0 copy-done.3
  64.4 14.0 %shard_map.65 = (bf16[128,2048]{1,0:T(8,128)(2,1)}, bf16[128,2048]{1,0:T(8,128)(2,1)}, bf16[16,2,8,1664]{3,2,1,0:T(8,128)(2,1)}) custom-call(s32[1]{0:T(128)} %bitcast.2.local_ref, bf16[128,3712]{1,0:T(8,128)(2,1)} %copy-done.2, bf16[128,3712]{1,0:T(8,128)(2,1)} %copy-done.3, bf16[1,3584,1024]{2,1,0:T(8,128)(2,1)} %refs_2_.3, ...), custom_call_target="tpu_custom_call" | custom-call | flops 5637144576 | bytes 22020096 | tf_op jit(solution)/shard_map/pallas_call | solution.py:129
  78.4 0.0 copy-done.13
  78.4 4.3 %collective-permute-done.3.refs_3_ = bf16[128,3712]{1,0:T(8,128)(2,1)} collective-permute-done((bf16[128,3712]{1,0:T(8,128)(2,1)S(1)}, bf16[128,3712]{1,0:T(8,128)(2,1)}, u32[]{:S(2)}, u32[]{:S(2)}) %collective-permute-start.3) | collective-permute-done | bytes 950304 | tf_op jit(solution)/shard_map/ppermute | solution.py:246
  82.7 3.7 %collective-permute-done.2.refs_2_ = bf16[128,3712]{1,0:T(8,128)(2,1)} collective-permute-done((bf16[128,3712]{1,0:T(8,128)(2,1)}, bf16[128,3712]{1,0:T(8,128)(2,1)}, u32[]{:S(2)}, u32[]{:S(2)}) %collective-permute-start.2) | collective-permute-done | bytes 950304 | tf_op jit(solution)/shard_map/ppermute | solution.py:243
  86.4 0.0 collective-permute-start.5
  86.4 3.2 %collective-permute-start.6 = (bf16[128,3712]{1,0:T(8,128)(2,1)}, bf16[128,3712]{1,0:T(8,128)(2,1)S(1)}, u32[]{:S(2)}, u32[]{:S(2)}) collective-permute-start(bf16[128,3712]{1,0:T(8,128)(2,1)} %copy-done.2), channel_id=1, source_target_pairs={{0,3},{1,0},{2,1},{3,2},{4,7},{5,4},{6,5},{7,6},{8,11},{9,8},{10,9... | collective-permute-start | bytes 2850824 | tf_op jit(solution)/shard_map/ppermute | solution.py:246
  89.6 4.1 %all-to-all-start.2 = ((bf16[16,2,8,1664]{3,2,1,0:T(8,128)(2,1)}), bf16[16,2,8,1664]{3,2,1,0:T(8,128)(2,1)S(1)}, u32[]{:S(2)}, u32[]{:S(2)}) async-start(bf16[16,2,8,1664]{3,2,1,0:T(8,128)(2,1)} %get-tuple-element.64), calls=%async_computation.2 | async-start | bytes 1703936 | tf_op jit(solution)/shard_map/all_to_all | solution.py:240
  93.8 21.3 %shard_map.66 = (bf16[128,2048]{1,0:T(8,128)(2,1)}, bf16[128,2048]{1,0:T(8,128)(2,1)}, bf16[128,2048]{1,0:T(8,128)(2,1)}, bf16[128,2048]{1,0:T(8,128)(2,1)}, bf16[16,4,8,1664]{3,2,1,0:T(8,128)(2,1)}) custom-call(s32[1]{0:T(128)} %bitcast.2.local_ref, bf16[128,3712]{1,0:T(8,128)(2,1)} %collective-permute-done.refs_0_, bf16[128,3712]{1,0:T(8,128)(2,1)} %copy-done.13, ...), custom_call_target="tpu_custom_call" | custom-call | flops 11274289152 | bytes 22020096 | tf_op jit(solution)/shard_map/pallas_call | solution.py:129
  115.1 0.0 collective-permute-done.5.refs_0_
  115.1 0.0 collective-permute-done.6.refs_1_
  115.1 0.0 copy-start.7
  115.1 0.0 all-to-all-done.2.first
  115.1 0.0 copy-start.4
  115.1 0.9 copy-done.7
  116.1 7.2 %all-to-all-start.3 = ((bf16[16,4,8,1664]{3,2,1,0:T(8,128)(2,1)}), bf16[16,4,8,1664]{3,2,1,0:T(8,128)(2,1)S(1)}, u32[]{:S(2)}, u32[]{:S(2)}) async-start(bf16[16,4,8,1664]{3,2,1,0:T(8,128)(2,1)} %get-tuple-element.67), calls=%async_computation.3 | async-start | bytes 3407872 | tf_op jit(solution)/shard_map/all_to_all | solution.py:240
  123.3 0.3 collective-permute-start.4
  123.5 2.0 collective-permute-start.7
  125.6 0.0 copy-done.6
  125.6 13.9 %shard_map.67 = (bf16[128,2048]{1,0:T(8,128)(2,1)}, bf16[128,2048]{1,0:T(8,128)(2,1)}, bf16[16,2,8,1664]{3,2,1,0:T(8,128)(2,1)}) custom-call(s32[1]{0:T(128)} %bitcast.2.local_ref, bf16[128,3712]{1,0:T(8,128)(2,1)} %copy-done.6, bf16[128,3712]{1,0:T(8,128)(2,1)} %copy-done.7, bf16[1,3584,1024]{2,1,0:T(8,128)(2,1)} %refs_2_.3, ...), custom_call_target="tpu_custom_call" | custom-call | flops 5637144576 | bytes 22020096 | tf_op jit(solution)/shard_map/pallas_call | solution.py:129
  139.5 0.0 copy-done.4
  139.5 0.0 collective-permute-done.4.back_a
  139.5 0.0 copy-start.8
  139.5 0.0 collective-permute-done.7.back_b
  139.5 0.8 copy-done.8
  140.3 3.3 %shard_map.68 = (bf16[2,128,2048]{2,1,0:T(8,128)(2,1)}, bf16[2,128,2048]{2,1,0:T(8,128)(2,1)}) custom-call(bf16[128,2048]{1,0:T(8,128)(2,1)} %copy-done.8, bf16[128,2048]{1,0:T(8,128)(2,1)} %get-tuple-element.51.below_a, bf16[128,2048]{1,0:T(8,128)(2,1)} %get-tuple-element.57.below_b, bf16[128,2048]{1,0:T(8,128)(2,1)} %collective-permute-done.7.back_b, ...), custom_call_target="tpu_custom_call" | custom-call | flops 100000000 | bytes 9437184 | tf_op jit(solution)/shard_map/pallas_call | solution.py:160
  143.7 1.3 collective-permute-start.8
  144.9 0.7 collective-permute-start.9
  145.7 0.0 all-to-all-done.3.second
  145.7 7.0 %all-to-all-start.4 = ((bf16[16,2,8,1664]{3,2,1,0:T(8,128)(2,1)}), bf16[16,2,8,1664]{3,2,1,0:T(8,128)(2,1)S(1)}, u32[]{:S(2)}, u32[]{:S(2)}) async-start(bf16[16,2,8,1664]{3,2,1,0:T(8,128)(2,1)} %get-tuple-element.69), calls=%async_computation.4 | async-start | bytes 1703936 | tf_op jit(solution)/shard_map/all_to_all | solution.py:240
  152.7 11.5 %collective-permute-done.8.above = bf16[2,128,2048]{2,1,0:T(8,128)(2,1)} collective-permute-done((bf16[2,128,2048]{2,1,0:T(8,128)(2,1)}, bf16[2,128,2048]{2,1,0:T(8,128)(2,1)}, u32[]{:S(2)}, u32[]{:S(2)}) %collective-permute-start.8) | collective-permute-done | bytes 1048608 | tf_op jit(solution)/shard_map/ppermute | solution.py:246
  164.2 2.5 %collective-permute-done.9.below = bf16[2,128,2048]{2,1,0:T(8,128)(2,1)} collective-permute-done((bf16[2,128,2048]{2,1,0:T(8,128)(2,1)}, bf16[2,128,2048]{2,1,0:T(8,128)(2,1)}, u32[]{:S(2)}, u32[]{:S(2)}) %collective-permute-start.9) | collective-permute-done | bytes 1048608 | tf_op jit(solution)/shard_map/ppermute | solution.py:243
  166.7 3.2 %shard_map.69 = bf16[16,2,8,2048]{3,2,1,0:T(8,128)(2,1)} custom-call(bf16[128,2048]{1,0:T(8,128)(2,1)} %get-tuple-element.43.own_a, bf16[128,2048]{1,0:T(8,128)(2,1)} %get-tuple-element.44.own_b, bf16[2,128,2048]{2,1,0:T(8,128)(2,1)} %collective-permute-done.8.above, bf16[2,128,2048]{2,1,0:T(8,128)(2,1)} %collective-permute-done.9.below), custom_call_target="tpu_custom_call" | custom-call | flops 100000000 | bytes 9437184 | tf_op jit(solution)/shard_map/pallas_call | solution.py:160
  169.9 0.0 copy-done
  169.9 0.0 all-to-all-done.4.third
  169.9 6.7 %all-to-all-start.1 = ((bf16[16,2,8,2048]{3,2,1,0:T(8,128)(2,1)}), bf16[16,2,8,2048]{3,2,1,0:T(8,128)(2,1)S(1)}, u32[]{:S(2)}, u32[]{:S(2)}) async-start(bf16[16,2,8,2048]{3,2,1,0:T(8,128)(2,1)} %shard_map.69), calls=%async_computation.1 | async-start | bytes 2097152 | tf_op jit(solution)/shard_map/all_to_all | solution.py:240
  176.6 0.0 copy-done.5
  176.7 3.8 %shard_map.70 = (bf16[128,1536]{1,0:T(8,128)(2,1)}, bf16[128,1536]{1,0:T(8,128)(2,1)}, bf16[128,1536]{1,0:T(8,128)(2,1)}, bf16[64,1536]{1,0:T(8,128)(2,1)}, bf16[64,1536]{1,0:T(8,128)(2,1)}) custom-call(bf16[16,2,8,1664]{3,2,1,0:T(8,128)(2,1)} %copy-done.4, bf16[16,4,8,1664]{3,2,1,0:T(8,128)(2,1)} %copy-done, bf16[16,2,8,1664]{3,2,1,0:T(8,128)(2,1)} %copy-done.5), custom_call_target="tpu_custom_call" | custom-call | flops 100000000 | bytes 10223616 | tf_op jit(solution)/shard_map/pallas_call | solution.py:160
  180.4 0.3 collective-permute-start.10
  180.7 1.7 collective-permute-start.11
  182.4 4.1 %collective-permute-done.10.more_lo = bf16[64,1536]{1,0:T(8,128)(2,1)S(1)} collective-permute-done((bf16[64,1536]{1,0:T(8,128)(2,1)}, bf16[64,1536]{1,0:T(8,128)(2,1)S(1)}, u32[]{:S(2)}, u32[]{:S(2)}) %collective-permute-start.10) | collective-permute-done | bytes 196640 | tf_op jit(solution)/shard_map/ppermute | solution.py:246
  186.5 1.7 collective-permute-done.11.more_hi
  188.2 0.0 copy-done.11
  188.2 0.7 copy-done.12
  188.9 2.2 %shard_map.71 = (bf16[128,1536]{1,0:T(8,128)(2,1)}, bf16[128,1536]{1,0:T(8,128)(2,1)}) custom-call(bf16[128,1536]{1,0:T(8,128)(2,1)} %get-tuple-element.71.below, bf16[64,1536]{1,0:T(8,128)(2,1)} %copy-done.11, bf16[128,1536]{1,0:T(8,128)(2,1)} %get-tuple-element.73.above, bf16[64,1536]{1,0:T(8,128)(2,1)} %copy-done.12), custom_call_target="tpu_custom_call" | custom-call | flops 100000000 | bytes 3538944 | tf_op jit(solution)/shard_map/pallas_call | solution.py:160
  191.1 0.0 collective-permute-start.12
  191.1 2.0 collective-permute-start.13
  193.1 0.0 all-to-all-done.1
  193.1 6.0 %collective-permute-done.12.from_above = bf16[128,1536]{1,0:T(8,128)(2,1)S(1)} collective-permute-done((bf16[128,1536]{1,0:T(8,128)(2,1)}, bf16[128,1536]{1,0:T(8,128)(2,1)S(1)}, u32[]{:S(2)}, u32[]{:S(2)}) %collective-permute-start.12) | collective-permute-done | bytes 393248 | tf_op jit(solution)/shard_map/ppermute | solution.py:246
  199.1 1.2 collective-permute-done.13.from_below
  200.3 0.7 copy-done.10
  201.0 3.0 %shard_map.72 = bf16[128,3584]{1,0:T(8,128)(2,1)} custom-call(bf16[256,128]{1,0:T(8,128)(2,1)} %get-tuple-element.41.pick, bf16[256,2048]{1,0:T(8,128)(2,1)} %bitcast.9, bf16[128,1536]{1,0:T(8,128)(2,1)} %get-tuple-element.70.own, bf16[128,1536]{1,0:T(8,128)(2,1)} %copy-done.9, bf16[128,1536]{1,0:T(8,128)(2,1)} %copy-done.10), custom_call_target="tpu_custom_call" | custom-call | flops 100000000 | bytes 6881280 | tf_op jit(solution)/shard_map/pallas_call | solution.py:160
  (11 shorter events, 0.0 us)
Async XLA Ops:
  38.4 26.0 %copy-start.2 = (bf16[128,3712]{1,0:T(8,128)(2,1)}, bf16[128,3712]{1,0:T(8,128)(2,1)S(1)}, u32[]{:S(2)}) copy-start(bf16[128,3712]{1,0:T(8,128)(2,1)S(1)} %get-tuple-element.53.refs_0_) | copy-start | bytes 2850820
  38.5 26.0 %copy-start.3 = (bf16[128,3712]{1,0:T(8,128)(2,1)}, bf16[128,3712]{1,0:T(8,128)(2,1)S(1)}, u32[]{:S(2)}) copy-start(bf16[128,3712]{1,0:T(8,128)(2,1)S(1)} %get-tuple-element.52.refs_1_) | copy-start | bytes 2850820
  38.5 22.3 %collective-permute-start.1 = (bf16[128,3712]{1,0:T(8,128)(2,1)S(1)}, bf16[128,3712]{1,0:T(8,128)(2,1)S(1)}, u32[]{:S(2)}, u32[]{:S(2)}) collective-permute-start(bf16[128,3712]{1,0:T(8,128)(2,1)S(1)} %get-tuple-element.52.refs_1_), channel_id=1, source_target_pairs={{0,3},{1,0},{2,1},{3,2},{4,7},{5,4},{6,5},{7,6},{8,11},{9,8},{10,9... | collective-permute-start | bytes 2850824 | tf_op jit(solution)/shard_map/ppermute | solution.py:246
  41.6 22.9 %collective-permute-start = (bf16[128,3712]{1,0:T(8,128)(2,1)S(1)}, bf16[128,3712]{1,0:T(8,128)(2,1)}, u32[]{:S(2)}, u32[]{:S(2)}) collective-permute-start(bf16[128,3712]{1,0:T(8,128)(2,1)S(1)} %get-tuple-element.53.refs_0_), channel_id=1, source_target_pairs={{0,1},{1,2},{2,3},{3,0},{4,5},{5,6},{6,7},{7,4},{8,9},{9,10},{10,1... | collective-permute-start | bytes 2850824 | tf_op jit(solution)/shard_map/ppermute | solution.py:243
  60.7 17.7 %copy-start.13 = (bf16[128,3712]{1,0:T(8,128)(2,1)}, bf16[128,3712]{1,0:T(8,128)(2,1)S(1)}, u32[]{:S(2)}) copy-start(bf16[128,3712]{1,0:T(8,128)(2,1)S(1)} %collective-permute-done.1.refs_1_) | copy-start | bytes 2850820
  60.7 21.9 %collective-permute-start.3 = (bf16[128,3712]{1,0:T(8,128)(2,1)S(1)}, bf16[128,3712]{1,0:T(8,128)(2,1)}, u32[]{:S(2)}, u32[]{:S(2)}) collective-permute-start(bf16[128,3712]{1,0:T(8,128)(2,1)S(1)} %collective-permute-done.1.refs_1_), channel_id=1, source_target_pairs={{0,3},{1,0},{2,1},{3,2},{4,7},{5,4},{6,5},{7,6},{8,11},{9,8},{10,9... | collective-permute-start | bytes 2850824 | tf_op jit(solution)/shard_map/ppermute | solution.py:246
  64.4 22.0 %collective-permute-start.2 = (bf16[128,3712]{1,0:T(8,128)(2,1)}, bf16[128,3712]{1,0:T(8,128)(2,1)}, u32[]{:S(2)}, u32[]{:S(2)}) collective-permute-start(bf16[128,3712]{1,0:T(8,128)(2,1)} %collective-permute-done.refs_0_), channel_id=1, source_target_pairs={{0,1},{1,2},{2,3},{3,0},{4,5},{5,6},{6,7},{7,4},{8,9},{9,10},{10,1... | collective-permute-start | bytes 2850824 | tf_op jit(solution)/shard_map/ppermute | solution.py:243
  86.4 28.7 %collective-permute-start.5 = (bf16[128,3712]{1,0:T(8,128)(2,1)}, bf16[128,3712]{1,0:T(8,128)(2,1)S(1)}, u32[]{:S(2)}, u32[]{:S(2)}) collective-permute-start(bf16[128,3712]{1,0:T(8,128)(2,1)} %copy-done.3), channel_id=1, source_target_pairs={{0,1},{1,2},{2,3},{3,0},{4,5},{5,6},{6,7},{7,4},{8,9},{9,10},{10,1... | collective-permute-start | bytes 2850824 | tf_op jit(solution)/shard_map/ppermute | solution.py:243
  86.4 28.7 %collective-permute-start.6 = (bf16[128,3712]{1,0:T(8,128)(2,1)}, bf16[128,3712]{1,0:T(8,128)(2,1)S(1)}, u32[]{:S(2)}, u32[]{:S(2)}) collective-permute-start(bf16[128,3712]{1,0:T(8,128)(2,1)} %copy-done.2), channel_id=1, source_target_pairs={{0,3},{1,0},{2,1},{3,2},{4,7},{5,4},{6,5},{7,6},{8,11},{9,8},{10,9... | collective-permute-start | bytes 2850824 | tf_op jit(solution)/shard_map/ppermute | solution.py:246
  89.6 25.5 %all-to-all-start.2 = ((bf16[16,2,8,1664]{3,2,1,0:T(8,128)(2,1)}), bf16[16,2,8,1664]{3,2,1,0:T(8,128)(2,1)S(1)}, u32[]{:S(2)}, u32[]{:S(2)}) async-start(bf16[16,2,8,1664]{3,2,1,0:T(8,128)(2,1)} %get-tuple-element.64), calls=%async_computation.2 | async-start | bytes 1703936 | tf_op jit(solution)/shard_map/all_to_all | solution.py:240
  115.1 10.5 %copy-start.6 = (bf16[128,3712]{1,0:T(8,128)(2,1)}, bf16[128,3712]{1,0:T(8,128)(2,1)S(1)}, u32[]{:S(2)}) copy-start(bf16[128,3712]{1,0:T(8,128)(2,1)S(1)} %collective-permute-done.5.refs_0_) | copy-start | bytes 2850820
  115.1 1.0 copy-start.7
  115.1 24.4 %copy-start.4 = (bf16[16,2,8,1664]{3,2,1,0:T(8,128)(2,1)}, bf16[16,2,8,1664]{3,2,1,0:T(8,128)(2,1)S(1)}, u32[]{:S(2)}) copy-start(bf16[16,2,8,1664]{3,2,1,0:T(8,128)(2,1)S(1)} %all-to-all-done.2.first) | copy-start | bytes 2555908
  116.1 29.6 %all-to-all-start.3 = ((bf16[16,4,8,1664]{3,2,1,0:T(8,128)(2,1)}), bf16[16,4,8,1664]{3,2,1,0:T(8,128)(2,1)S(1)}, u32[]{:S(2)}, u32[]{:S(2)}) async-start(bf16[16,4,8,1664]{3,2,1,0:T(8,128)(2,1)} %get-tuple-element.67), calls=%async_computation.3 | async-start | bytes 3407872 | tf_op jit(solution)/shard_map/all_to_all | solution.py:240
  123.3 16.2 %collective-permute-start.4 = (bf16[128,2048]{1,0:T(8,128)(2,1)}, bf16[128,2048]{1,0:T(8,128)(2,1)S(1)}, u32[]{:S(2)}, u32[]{:S(2)}) collective-permute-start(bf16[128,2048]{1,0:T(8,128)(2,1)} %get-tuple-element.50), channel_id=1, source_target_pairs={{0,3},{1,0},{2,1},{3,2},{4,7},{5,4},{6,5},{7,6},{8,11},{9,8},{10,9... | collective-permute-start | bytes 1572872 | tf_op jit(solution)/shard_map/ppermute | solution.py:246
  123.5 16.0 %collective-permute-start.7 = (bf16[128,2048]{1,0:T(8,128)(2,1)}, bf16[128,2048]{1,0:T(8,128)(2,1)}, u32[]{:S(2)}, u32[]{:S(2)}) collective-permute-start(bf16[128,2048]{1,0:T(8,128)(2,1)} %get-tuple-element.58), channel_id=1, source_target_pairs={{0,1},{1,2},{2,3},{3,0},{4,5},{5,6},{6,7},{7,4},{8,9},{9,10},{10,1... | collective-permute-start | bytes 1572872 | tf_op jit(solution)/shard_map/ppermute | solution.py:243
  139.5 0.8 copy-start.8
  143.7 20.6 %collective-permute-start.8 = (bf16[2,128,2048]{2,1,0:T(8,128)(2,1)}, bf16[2,128,2048]{2,1,0:T(8,128)(2,1)}, u32[]{:S(2)}, u32[]{:S(2)}) collective-permute-start(bf16[2,128,2048]{2,1,0:T(8,128)(2,1)} %get-tuple-element.61), channel_id=1, source_target_pairs={{0,3},{1,0},{2,1},{3,2},{4,7},{5,4},{6,5},{7,6},{8,11},{9,8},{10,9... | collective-permute-start | bytes 3145736 | tf_op jit(solution)/shard_map/ppermute | solution.py:246
  144.9 21.8 %collective-permute-start.9 = (bf16[2,128,2048]{2,1,0:T(8,128)(2,1)}, bf16[2,128,2048]{2,1,0:T(8,128)(2,1)}, u32[]{:S(2)}, u32[]{:S(2)}) collective-permute-start(bf16[2,128,2048]{2,1,0:T(8,128)(2,1)} %get-tuple-element.62), channel_id=1, source_target_pairs={{0,1},{1,2},{2,3},{3,0},{4,5},{5,6},{6,7},{7,4},{8,9},{9,10},{10,1... | collective-permute-start | bytes 3145736 | tf_op jit(solution)/shard_map/ppermute | solution.py:243
  145.7 24.2 %copy-start = (bf16[16,4,8,1664]{3,2,1,0:T(8,128)(2,1)}, bf16[16,4,8,1664]{3,2,1,0:T(8,128)(2,1)S(1)}, u32[]{:S(2)}) copy-start(bf16[16,4,8,1664]{3,2,1,0:T(8,128)(2,1)S(1)} %all-to-all-done.3.second) | copy-start | bytes 5111812
  145.7 24.2 %all-to-all-start.4 = ((bf16[16,2,8,1664]{3,2,1,0:T(8,128)(2,1)}), bf16[16,2,8,1664]{3,2,1,0:T(8,128)(2,1)S(1)}, u32[]{:S(2)}, u32[]{:S(2)}) async-start(bf16[16,2,8,1664]{3,2,1,0:T(8,128)(2,1)} %get-tuple-element.69), calls=%async_computation.4 | async-start | bytes 1703936 | tf_op jit(solution)/shard_map/all_to_all | solution.py:240
  169.9 6.7 %copy-start.5 = (bf16[16,2,8,1664]{3,2,1,0:T(8,128)(2,1)}, bf16[16,2,8,1664]{3,2,1,0:T(8,128)(2,1)S(1)}, u32[]{:S(2)}) copy-start(bf16[16,2,8,1664]{3,2,1,0:T(8,128)(2,1)S(1)} %all-to-all-done.4.third) | copy-start | bytes 2555908
  169.9 23.2 %all-to-all-start.1 = ((bf16[16,2,8,2048]{3,2,1,0:T(8,128)(2,1)}), bf16[16,2,8,2048]{3,2,1,0:T(8,128)(2,1)S(1)}, u32[]{:S(2)}, u32[]{:S(2)}) async-start(bf16[16,2,8,2048]{3,2,1,0:T(8,128)(2,1)} %shard_map.69), calls=%async_computation.1 | async-start | bytes 2097152 | tf_op jit(solution)/shard_map/all_to_all | solution.py:240
  180.4 6.1 %collective-permute-start.10 = (bf16[64,1536]{1,0:T(8,128)(2,1)}, bf16[64,1536]{1,0:T(8,128)(2,1)S(1)}, u32[]{:S(2)}, u32[]{:S(2)}) collective-permute-start(bf16[64,1536]{1,0:T(8,128)(2,1)} %get-tuple-element.72), channel_id=1, source_target_pairs={{0,3},{1,0},{2,1},{3,2},{4,7},{5,4},{6,5},{7,6},{8,11},{9,8},{10,9... | collective-permute-start | bytes 589832 | tf_op jit(solution)/shard_map/ppermute | solution.py:246
  180.7 7.5 %collective-permute-start.11 = (bf16[64,1536]{1,0:T(8,128)(2,1)}, bf16[64,1536]{1,0:T(8,128)(2,1)S(1)}, u32[]{:S(2)}, u32[]{:S(2)}) collective-permute-start(bf16[64,1536]{1,0:T(8,128)(2,1)} %get-tuple-element.74), channel_id=1, source_target_pairs={{0,1},{1,2},{2,3},{3,0},{4,5},{5,6},{6,7},{7,4},{8,9},{9,10},{10,1... | collective-permute-start | bytes 589832 | tf_op jit(solution)/shard_map/ppermute | solution.py:243
  186.5 1.7 copy-start.11
  188.2 0.7 copy-start.12
  191.1 8.0 %collective-permute-start.12 = (bf16[128,1536]{1,0:T(8,128)(2,1)}, bf16[128,1536]{1,0:T(8,128)(2,1)S(1)}, u32[]{:S(2)}, u32[]{:S(2)}) collective-permute-start(bf16[128,1536]{1,0:T(8,128)(2,1)} %get-tuple-element.75), channel_id=1, source_target_pairs={{0,3},{1,0},{2,1},{3,2},{4,7},{5,4},{6,5},{7,6},{8,11},{9,8},{10,9... | collective-permute-start | bytes 1179656 | tf_op jit(solution)/shard_map/ppermute | solution.py:246
  191.1 9.2 %collective-permute-start.13 = (bf16[128,1536]{1,0:T(8,128)(2,1)}, bf16[128,1536]{1,0:T(8,128)(2,1)S(1)}, u32[]{:S(2)}, u32[]{:S(2)}) collective-permute-start(bf16[128,1536]{1,0:T(8,128)(2,1)} %get-tuple-element.76), channel_id=1, source_target_pairs={{0,1},{1,2},{2,3},{3,0},{4,5},{5,6},{6,7},{7,4},{8,9},{9,10},{10,1... | collective-permute-start | bytes 1179656 | tf_op jit(solution)/shard_map/ppermute | solution.py:243
  193.1 7.2 %copy-start.1 = (bf16[16,2,8,2048]{3,2,1,0:T(8,128)(2,1)}, bf16[16,2,8,2048]{3,2,1,0:T(8,128)(2,1)S(1)}, u32[]{:S(2)}) copy-start(bf16[16,2,8,2048]{3,2,1,0:T(8,128)(2,1)S(1)} %all-to-all-done.1) | copy-start | bytes 3145732
  199.1 1.2 copy-start.9
  200.3 0.7 copy-start.10

commit v4 on v3

--- a/solution.py
+++ b/solution.py
@@ -80,8 +80,8 @@
     )(tokens, gate_scores.T, expert_ids.T)
 
 
-def expert_kernel(blocks, local_ref, *refs):
-    xs, (wg, wu, wd), refs = refs[:blocks], refs[blocks : blocks + 3], refs[blocks + 3 :]
+def expert_kernel(blocks, before, local_ref, *refs):
+    xs, (wg, wu, wd), refs = refs[:blocks], refs[blocks : blocks + 3], refs[blocks + 3 + before :]
     outs, direct, rows, acc = refs[:blocks], refs[blocks], refs[blocks + 1], refs[blocks + 2]
     step, steps = pl.program_id(0), pl.num_programs(0)
     width, near = rows.shape[1], outs[0].shape[1]
@@ -121,13 +121,15 @@
             direct[:, b, :, far.shape[1] :] = meta.reshape(*shape, LANES).astype(jnp.bfloat16)
 
 
-def experts(xs, local, groups, near, w_gate, w_up, w_down, tile=256):
+def experts(xs, held, local, groups, near, w_gate, w_up, w_down, tile=256):
     blocks = len(xs)
     piece, wide = xs[0].shape
     width, hidden = w_gate.shape[1:]
+    before = 0 if held is None else 1
     direct = (groups, blocks, piece // groups, width - near + LANES)
+    room = jax.ShapeDtypeStruct((groups, 2 * blocks) + direct[2:], jnp.bfloat16)
     return pl.pallas_call(
-        functools.partial(expert_kernel, blocks),
+        functools.partial(expert_kernel, blocks, before),
         grid=(hidden // tile,),
         in_specs=[pl.BlockSpec(memory_space=pltpu.SMEM)]
         + [pl.BlockSpec((piece, wide), lambda i: (0, 0))] * blocks
@@ -135,11 +137,13 @@
             pl.BlockSpec((1, width, tile), lambda i: (0, 0, i)),
             pl.BlockSpec((1, width, tile), lambda i: (0, 0, i)),
             pl.BlockSpec((1, tile, width), lambda i: (0, i, 0)),
-        ],
+        ]
+        + [pl.BlockSpec(memory_space=pl.ANY)] * before,
         out_specs=[pl.BlockSpec((piece, near), lambda i: (0, 0))] * blocks
-        + [pl.BlockSpec(direct, lambda i: (0, 0, 0, 0))],
+        + [pl.BlockSpec(direct, lambda i: (0, before, 0, 0))],
         out_shape=[jax.ShapeDtypeStruct((piece, near), jnp.bfloat16)] * blocks
-        + [jax.ShapeDtypeStruct(direct, jnp.bfloat16)],
+        + [room],
+        input_output_aliases={blocks + 4: blocks} if before else {},
         scratch_shapes=[
             pltpu.VMEM((blocks * piece, width), jnp.bfloat16),
             pltpu.VMEM((blocks * piece, width), jnp.float32),
@@ -152,7 +156,7 @@
             bytes_accessed=6 * width * hidden,
             transcendentals=blocks * piece * hidden,
         ),
-    )(local, *xs, w_gate, w_up, w_down)
+    )(local, *xs, w_gate, w_up, w_down, *([held] if before else []))
 
 
 def whole(kernel, shapes, *arrays):
@@ -169,8 +173,8 @@
     return lax.dot_general(pick, rows, (((0,), (0,)), ((), ())), preferred_element_type=jnp.float32)
 
 
-def scatter_kernel(where, locals_, first, second, third, own, below, above, far_lo, far_hi):
-    groups = (first, second, third)
+def scatter_kernel(where, locals_, first, second, own, below, above, far_lo, far_hi):
+    groups = (first, second)
     count, width = own.shape
     half = count // 2
     for name, out in (("own", own), ("below", below), ("above", above), ("far", None)):
@@ -258,26 +262,24 @@
     own_a = own[:, 0].reshape(PIECE, width + LANES)
     own_b = own[:, 1].reshape(PIECE, width + LANES)
     below_a, above_b = up(own_a), down(own_b)
+    own_pa, own_pb, first = run([own_a, own_b], None)
+    below_a, above_b, first = tie((below_a, above_b, first))
     far_a, far_b = up(below_a), down(above_b)
-    last_a, last_b, _, _ = tie((own_a, own_b, far_a, far_b))
+    below_pa, above_pb, first = run([below_a, above_b], first)
+    last_a, last_b, far_a, far_b, first = tie((own_a, own_b, far_a, far_b, first))
     below_b, above_a = up(last_b), down(last_a)
-
-    own_pa, own_pb, first = run([own_a, own_b])
-    below_a, above_b, far_a, far_b, first = tie((below_a, above_b, far_a, far_b, first))
-    below_pa, above_pb, far_pa, far_pb, second = run([below_a, above_b, far_a, far_b])
+    far_pa, far_pb, second = run([far_a, far_b], None)
     below_b, above_a, second = tie((below_b, above_a, second))
-    below_pb, above_pa, third = run([below_b, above_a])
+    below_pb, above_pa, second = run([below_b, above_a], second)
 
     first = across(first)
-    second, first = tie((second, first))
-    second = across(second)
-    third, second = tie((third, second))
-    third = across(third)
 
     back_a, back_b = down(far_pa), up(far_pb)
     go_down, go_up = whole(
         pack_kernel, [like(2, PIECE, near)] * 2, back_a, below_pa, below_pb, back_b, above_pa, above_pb
     )
+    second, first, go_down, go_up = tie((second, first, go_down, go_up))
+    second = across(second)
     from_above, from_below = down(go_down), up(go_up)
     total = whole(
         total_kernel, like(groups, 2, eight, near), own_pa, own_pb, from_above, from_below
@@ -285,11 +287,11 @@
     final = across(total).reshape(2 * PIECE, near)
 
     where = {
-        "own": ((0, 0), (0, 1)), "below": ((1, 0), (2, 0)), "above": ((2, 1), (1, 1)), "far": ((1, 2), (1, 3)),
+        "own": ((0, 0), (0, 1)), "below": ((0, 2), (1, 2)), "above": ((1, 3), (0, 3)), "far": ((1, 0), (1, 1)),
     }
     full, part = like(count, width - near), like(count // 2, width - near)
     own_t, below_t, above_t, far_lo, far_hi = whole(
-        functools.partial(scatter_kernel, where, locals_), [full, full, full, part, part], first, second, third
+        functools.partial(scatter_kernel, where, locals_), [full, full, full, part, part], first, second
     )
     more_lo, more_hi = down(far_lo), up(far_hi)
     go_down, go_up = whole(join_kernel, [full, full], below_t, more_lo, above_t, more_hi)

time: 205 us -> 200 us (0.976)
  Pallas kernels: 68.7 us -> 75.8 us
  starting transfers between devices: 43.4 us -> 37.7 us
  waiting for transfers between devices: 54.1 us -> 49.2 us
    ppermute x7, waiting for transfers between devices: 45 us -> 30.2 us  [down(): lax.ppermute(block, 'local', [(i, (i - 1) % locals_) for i in range(local...]
    ppermute x7, waiting for transfers between devices: 9.17 us -> 19 us  [up(): lax.ppermute(block, 'local', [(i, (i + 1) % locals_) for i in range(local...]
    all_to_all x4 -> x3, starting transfers between devices: 25 us -> 18.2 us  [across(): return lax.all_to_all(block, 'node', 0, 0, tiled=True)]
    pallas_call x3 -> x4, Pallas kernels: 49.2 us -> 56 us  [experts(): pl.pallas_call(functools.partial(expert_kernel, blocks, before), grid=(hi...]
    ppermute x7, starting transfers between devices: 11.9 us -> 15.8 us  [down(): lax.ppermute(block, 'local', [(i, (i - 1) % locals_) for i in range(local...]
    ppermute x7, starting transfers between devices: 6.51 us -> 3.76 us  [up(): lax.ppermute(block, 'local', [(i, (i + 1) % locals_) for i in range(local...]
  transfers between devices with their start and end apart: 18 -> 17, of which waited for: 9 -> 11; matrix products, arithmetic and copies ran while one was open for 0% -> 0% of each run, Pallas kernels for 30% -> 34%
where the time goes in v4:
time: 200 us
  Pallas kernels  75.8 us (38%)
  waiting for transfers between devices  49.2 us (25%)
  starting transfers between devices  37.7 us (19%)
  blocking collectives  34.2 us (17%)
  local copies, waits for them, and re-layouts  2.6 us (1%)
    pallas_call x4, Pallas kernels, experts(): pl.pallas_call(functools.partial(expert_kernel, blocks, before), grid=(hi...  56 us
    all_to_all x1, blocking collectives, across(): return lax.all_to_all(block, 'node', 0, 0, tiled=True)  34.2 us
    ppermute x7, waiting for transfers between devices, down(): lax.ppermute(block, 'local', [(i, (i - 1) % locals_) for i in range(local...  30.2 us
    ppermute x7, waiting for transfers between devices, up(): lax.ppermute(block, 'local', [(i, (i + 1) % locals_) for i in range(local...  19 us
    all_to_all x3, starting transfers between devices, across(): return lax.all_to_all(block, 'node', 0, 0, tiled=True)  18.2 us
    ppermute x7, starting transfers between devices, down(): lax.ppermute(block, 'local', [(i, (i - 1) % locals_) for i in range(local...  15.8 us
    pallas_call x5, Pallas kernels, whole(): pl.pallas_call(kernel, out_shape=shapes, compiler_params=pltpu.CompilerPa...  15.7 us
    pallas_call x1, Pallas kernels, prepare(): pl.pallas_call(functools.partial(prepare_kernel, locals_, groups, per_gro...  4.09 us
  transfers between devices with their start and end apart: 17, of which 11 were waited for; matrix products, arithmetic and copies ran while one was open for 0% of the time, Pallas kernels for 34%

profile of v4, /device:TPU:0, one launch (start us, length us, event | category | flops | bytes accessed | tf_op | source)
XLA Modules:
  0.0 199.7 jit_solution(16848823345858105667)
XLA Ops:
  0.0 4.1 %shard_map.64 = (bf16[256,3712]{1,0:T(8,128)(2,1)}, bf16[256,128]{1,0:T(8,128)(2,1)}) custom-call(bf16[128,3584]{1,0:T(8,128)(2,1)} %tok.1, f32[4,128]{1,0:T(4,128)} %bitcast.11, s32[4,128]{1,0:T(4,128)} %bitcast.12), custom_call_target="tpu_custom_call" | custom-call | flops 1000000000 | bytes 3000000 | tf_op jit(solution)/shard_map/pallas_call | solution.py:72
  4.1 34.2 %all_to_all.20 = bf16[16,2,8,3712]{3,2,1,0:T(8,128)(2,1)S(1)} all-to-all(bf16[16,2,8,3712]{3,2,1,0:T(8,128)(2,1)} %bitcast.10), channel_id=1, replica_groups=mesh['dp'=2,'node'=16,'local'=4] {'node'}, dimensions={0} | all-to-all | bytes 3801088 | tf_op jit(solution)/shard_map/all_to_all | solution.py:244
  38.3 0.1 slice_bitcast_fusion
  38.5 0.0 copy-start.3
  38.5 0.0 copy-start.5
  38.5 3.1 %collective-permute-start.1 = (bf16[128,3712]{1,0:T(8,128)(2,1)S(1)}, bf16[128,3712]{1,0:T(8,128)(2,1)}, u32[]{:S(2)}, u32[]{:S(2)}) collective-permute-start(bf16[128,3712]{1,0:T(8,128)(2,1)S(1)} %get-tuple-element.52.refs_1_), channel_id=1, source_target_pairs={{0,3},{1,0},{2,1},{3,2},{4,7},{5,4},{6,5},{7,6},{8,11},{9,8},{10,9... | collective-permute-start | bytes 2850824 | tf_op jit(solution)/shard_map/ppermute | solution.py:250
  41.6 0.0 collective-permute-start
  41.6 0.0 copy-done.3
  41.6 0.0 copy-done.5
  41.6 14.0 %shard_map.65 = (bf16[128,2048]{1,0:T(8,128)(2,1)}, bf16[128,2048]{1,0:T(8,128)(2,1)}, bf16[16,4,8,1664]{3,2,1,0:T(8,128)(2,1)}) custom-call(s32[1]{0:T(128)} %bitcast.2.local_ref, bf16[128,3712]{1,0:T(8,128)(2,1)} %copy-done.3, bf16[128,3712]{1,0:T(8,128)(2,1)} %copy-done.5, bf16[1,3584,1024]{2,1,0:T(8,128)(2,1)} %refs_2_.7, ...), custom_call_target="tpu_custom_call" | custom-call | flops 5637144576 | bytes 22020096 | tf_op jit(solution)/shard_map/pallas_call | solution.py:131
  55.6 5.2 %collective-permute-done.1.refs_1_ = bf16[128,3712]{1,0:T(8,128)(2,1)} collective-permute-done((bf16[128,3712]{1,0:T(8,128)(2,1)S(1)}, bf16[128,3712]{1,0:T(8,128)(2,1)}, u32[]{:S(2)}, u32[]{:S(2)}) %collective-permute-start.1) | collective-permute-done | bytes 950304 | tf_op jit(solution)/shard_map/ppermute | solution.py:250
  60.7 3.5 %collective-permute-done.refs_0_ = bf16[128,3712]{1,0:T(8,128)(2,1)} collective-permute-done((bf16[128,3712]{1,0:T(8,128)(2,1)S(1)}, bf16[128,3712]{1,0:T(8,128)(2,1)}, u32[]{:S(2)}, u32[]{:S(2)}) %collective-permute-start) | collective-permute-done | bytes 950304 | tf_op jit(solution)/shard_map/ppermute | solution.py:247
  64.2 0.0 collective-permute-start.2
  64.3 3.2 %collective-permute-start.3 = (bf16[128,3712]{1,0:T(8,128)(2,1)}, bf16[128,3712]{1,0:T(8,128)(2,1)}, u32[]{:S(2)}, u32[]{:S(2)}) collective-permute-start(bf16[128,3712]{1,0:T(8,128)(2,1)} %collective-permute-done.1.refs_1_), channel_id=1, source_target_pairs={{0,3},{1,0},{2,1},{3,2},{4,7},{5,4},{6,5},{7,6},{8,11},{9,8},{10,9... | collective-permute-start | bytes 2850824 | tf_op jit(solution)/shard_map/ppermute | solution.py:250
  67.5 14.0 %shard_map.66 = (bf16[128,2048]{1,0:T(8,128)(2,1)}, bf16[128,2048]{1,0:T(8,128)(2,1)}, bf16[16,4,8,1664]{3,2,1,0:T(8,128)(2,1)}) custom-call(s32[1]{0:T(128)} %bitcast.2.local_ref, bf16[128,3712]{1,0:T(8,128)(2,1)} %collective-permute-done.refs_0_, bf16[128,3712]{1,0:T(8,128)(2,1)} %collective-permute-done.1.refs_1_, ...), custom_call_target="tpu_custom_call", output_to_operand_aliasing={{2}: (6, {})} | custom-call | flops 5637144576 | bytes 22020096 | tf_op jit(solution)/shard_map/pallas_call | solution.py:131
  81.5 0.0 copy-start.4
  81.5 4.7 %collective-permute-done.2.refs_0_ = bf16[128,3712]{1,0:T(8,128)(2,1)} collective-permute-done((bf16[128,3712]{1,0:T(8,128)(2,1)}, bf16[128,3712]{1,0:T(8,128)(2,1)}, u32[]{:S(2)}, u32[]{:S(2)}) %collective-permute-start.2) | collective-permute-done | bytes 950304 | tf_op jit(solution)/shard_map/ppermute | solution.py:247
  86.2 0.0 collective-permute-done.3.refs_1_
  86.2 4.1 %all-to-all-start.1 = ((bf16[16,4,8,1664]{3,2,1,0:T(8,128)(2,1)}), bf16[16,4,8,1664]{3,2,1,0:T(8,128)(2,1)S(1)}, u32[]{:S(2)}, u32[]{:S(2)}) async-start(bf16[16,4,8,1664]{3,2,1,0:T(8,128)(2,1)} %get-tuple-element.61), calls=%async_computation.1 | async-start | bytes 3407872 | tf_op jit(solution)/shard_map/all_to_all | solution.py:244
  90.4 0.1 collective-permute-start.4
  90.5 0.0 copy-done.4
  90.5 3.2 %collective-permute-start.5 = (bf16[128,3712]{1,0:T(8,128)(2,1)S(1)}, bf16[128,3712]{1,0:T(8,128)(2,1)}, u32[]{:S(2)}, u32[]{:S(2)}) collective-permute-start(bf16[128,3712]{1,0:T(8,128)(2,1)S(1)} %copy-done.4), channel_id=1, source_target_pairs={{0,3},{1,0},{2,1},{3,2},{4,7},{5,4},{6,5},{7,6},{8,11},{9,8},{10,9... | collective-permute-start | bytes 2850824 | tf_op jit(solution)/shard_map/ppermute | solution.py:250
  93.7 14.0 %shard_map.67 = (bf16[128,2048]{1,0:T(8,128)(2,1)}, bf16[128,2048]{1,0:T(8,128)(2,1)}, bf16[16,4,8,1664]{3,2,1,0:T(8,128)(2,1)}) custom-call(s32[1]{0:T(128)} %bitcast.2.local_ref, bf16[128,3712]{1,0:T(8,128)(2,1)} %collective-permute-done.2.refs_0_, bf16[128,3712]{1,0:T(8,128)(2,1)} %collective-permute-done.3.refs_1_, bf16[1,3584,1024]{2,1,0:T(8,128)(2,1)} %refs_2_.7, ...), custom_call_target="tpu_custom_call" | custom-call | flops 5637144576 | bytes 22020096 | tf_op jit(solution)/shard_map/pallas_call | solution.py:131
  107.7 1.7 collective-permute-start.6
  109.5 0.3 collective-permute-start.7
  109.7 4.5 %collective-permute-done.4.refs_0_ = bf16[128,3712]{1,0:T(8,128)(2,1)} collective-permute-done((bf16[128,3712]{1,0:T(8,128)(2,1)}, bf16[128,3712]{1,0:T(8,128)(2,1)}, u32[]{:S(2)}, u32[]{:S(2)}) %collective-permute-start.4) | collective-permute-done | bytes 950304 | tf_op jit(solution)/shard_map/ppermute | solution.py:247
  114.2 1.0 collective-permute-done.5.refs_1_
  115.2 14.0 %shard_map.68 = (bf16[128,2048]{1,0:T(8,128)(2,1)}, bf16[128,2048]{1,0:T(8,128)(2,1)}, bf16[16,4,8,1664]{3,2,1,0:T(8,128)(2,1)}) custom-call(s32[1]{0:T(128)} %bitcast.2.local_ref, bf16[128,3712]{1,0:T(8,128)(2,1)} %collective-permute-done.4.refs_0_, bf16[128,3712]{1,0:T(8,128)(2,1)} %collective-permute-done.5.refs_1_, ...), custom_call_target="tpu_custom_call", output_to_operand_aliasing={{2}: (6, {})} | custom-call | flops 5637144576 | bytes 22020096 | tf_op jit(solution)/shard_map/pallas_call | solution.py:131
  129.2 0.0 collective-permute-done.6.back_a
  129.2 0.0 copy-start.6
  129.2 0.0 collective-permute-done.7.back_b
  129.2 0.0 copy-start.7
  129.2 0.8 copy-done.6
  130.0 0.2 copy-done.7
  130.2 3.4 %shard_map.69 = (bf16[2,128,2048]{2,1,0:T(8,128)(2,1)}, bf16[2,128,2048]{2,1,0:T(8,128)(2,1)}) custom-call(bf16[128,2048]{1,0:T(8,128)(2,1)} %copy-done.6, bf16[128,2048]{1,0:T(8,128)(2,1)} %get-tuple-element.63.below_a, bf16[128,2048]{1,0:T(8,128)(2,1)} %get-tuple-element.64.below_b, bf16[128,2048]{1,0:T(8,128)(2,1)} %copy-done.7, ...), custom_call_target="tpu_custom_call" | custom-call | flops 100000000 | bytes 9437184 | tf_op jit(solution)/shard_map/pallas_call | solution.py:164
  133.6 0.0 all-to-all-done.1.first
  133.6 0.0 copy-start
  133.6 7.2 %all-to-all-start.3 = ((bf16[16,4,8,1664]{3,2,1,0:T(8,128)(2,1)}), bf16[16,4,8,1664]{3,2,1,0:T(8,128)(2,1)S(1)}, u32[]{:S(2)}, u32[]{:S(2)}) async-start(bf16[16,4,8,1664]{3,2,1,0:T(8,128)(2,1)} %get-tuple-element.73), calls=%async_computation.3 | async-start | bytes 3407872 | tf_op jit(solution)/shard_map/all_to_all | solution.py:244
  140.8 3.9 %collective-permute-start.8 = (bf16[2,128,2048]{2,1,0:T(8,128)(2,1)}, bf16[2,128,2048]{2,1,0:T(8,128)(2,1)}, u32[]{:S(2)}, u32[]{:S(2)}) collective-permute-start(bf16[2,128,2048]{2,1,0:T(8,128)(2,1)} %get-tuple-element.70), channel_id=1, source_target_pairs={{0,3},{1,0},{2,1},{3,2},{4,7},{5,4},{6,5},{7,6},{8,11},{9,8},{10,9... | collective-permute-start | bytes 3145736 | tf_op jit(solution)/shard_map/ppermute | solution.py:250
  144.6 0.0 collective-permute-start.9
  144.6 13.3 %collective-permute-done.8.above = bf16[2,128,2048]{2,1,0:T(8,128)(2,1)} collective-permute-done((bf16[2,128,2048]{2,1,0:T(8,128)(2,1)}, bf16[2,128,2048]{2,1,0:T(8,128)(2,1)}, u32[]{:S(2)}, u32[]{:S(2)}) %collective-permute-start.8) | collective-permute-done | bytes 1048608 | tf_op jit(solution)/shard_map/ppermute | solution.py:250
  157.9 3.4 %collective-permute-done.9.below = bf16[2,128,2048]{2,1,0:T(8,128)(2,1)} collective-permute-done((bf16[2,128,2048]{2,1,0:T(8,128)(2,1)}, bf16[2,128,2048]{2,1,0:T(8,128)(2,1)}, u32[]{:S(2)}, u32[]{:S(2)}) %collective-permute-start.9) | collective-permute-done | bytes 1048608 | tf_op jit(solution)/shard_map/ppermute | solution.py:247
  161.3 3.2 %shard_map.70 = bf16[16,2,8,2048]{3,2,1,0:T(8,128)(2,1)} custom-call(bf16[128,2048]{1,0:T(8,128)(2,1)} %get-tuple-element.45.own_a, bf16[128,2048]{1,0:T(8,128)(2,1)} %get-tuple-element.46.own_b, bf16[2,128,2048]{2,1,0:T(8,128)(2,1)} %collective-permute-done.8.above, bf16[2,128,2048]{2,1,0:T(8,128)(2,1)} %collective-permute-done.9.below), custom_call_target="tpu_custom_call" | custom-call | flops 100000000 | bytes 9437184 | tf_op jit(solution)/shard_map/pallas_call | solution.py:164
  164.5 0.0 copy-done
  164.5 0.0 all-to-all-done.3.second
  164.6 6.9 %all-to-all-start.2 = ((bf16[16,2,8,2048]{3,2,1,0:T(8,128)(2,1)}), bf16[16,2,8,2048]{3,2,1,0:T(8,128)(2,1)S(1)}, u32[]{:S(2)}, u32[]{:S(2)}) async-start(bf16[16,2,8,2048]{3,2,1,0:T(8,128)(2,1)} %shard_map.70), calls=%async_computation.2 | async-start | bytes 2097152 | tf_op jit(solution)/shard_map/all_to_all | solution.py:244
  171.4 0.0 copy-done.1
  171.5 3.8 %shard_map.71 = (bf16[128,1536]{1,0:T(8,128)(2,1)}, bf16[128,1536]{1,0:T(8,128)(2,1)}, bf16[128,1536]{1,0:T(8,128)(2,1)}, bf16[64,1536]{1,0:T(8,128)(2,1)}, bf16[64,1536]{1,0:T(8,128)(2,1)}) custom-call(bf16[16,4,8,1664]{3,2,1,0:T(8,128)(2,1)} %copy-done, bf16[16,4,8,1664]{3,2,1,0:T(8,128)(2,1)} %copy-done.1), custom_call_target="tpu_custom_call" | custom-call | flops 100000000 | bytes 10223616 | tf_op jit(solution)/shard_map/pallas_call | solution.py:164
  175.2 0.3 collective-permute-start.10
  175.5 1.7 collective-permute-start.11
  177.3 4.8 %collective-permute-done.10.more_lo = bf16[64,1536]{1,0:T(8,128)(2,1)S(1)} collective-permute-done((bf16[64,1536]{1,0:T(8,128)(2,1)}, bf16[64,1536]{1,0:T(8,128)(2,1)S(1)}, u32[]{:S(2)}, u32[]{:S(2)}) %collective-permute-start.10) | collective-permute-done | bytes 196640 | tf_op jit(solution)/shard_map/ppermute | solution.py:250
  182.1 1.3 collective-permute-done.11.more_hi
  183.4 0.0 copy-done.10
  183.4 0.7 copy-done.11
  184.1 2.2 %shard_map.72 = (bf16[128,1536]{1,0:T(8,128)(2,1)}, bf16[128,1536]{1,0:T(8,128)(2,1)}) custom-call(bf16[128,1536]{1,0:T(8,128)(2,1)} %get-tuple-element.75.below, bf16[64,1536]{1,0:T(8,128)(2,1)} %copy-done.10, bf16[128,1536]{1,0:T(8,128)(2,1)} %get-tuple-element.77.above, bf16[64,1536]{1,0:T(8,128)(2,1)} %copy-done.11), custom_call_target="tpu_custom_call" | custom-call | flops 100000000 | bytes 3538944 | tf_op jit(solution)/shard_map/pallas_call | solution.py:164
  186.3 0.4 collective-permute-start.12
  186.7 1.6 collective-permute-start.13
  188.3 0.0 all-to-all-done.2
  188.4 6.0 %collective-permute-done.12.from_above = bf16[128,1536]{1,0:T(8,128)(2,1)S(1)} collective-permute-done((bf16[128,1536]{1,0:T(8,128)(2,1)}, bf16[128,1536]{1,0:T(8,128)(2,1)S(1)}, u32[]{:S(2)}, u32[]{:S(2)}) %collective-permute-start.12) | collective-permute-done | bytes 393248 | tf_op jit(solution)/shard_map/ppermute | solution.py:250
  194.3 1.6 collective-permute-done.13.from_below
  195.9 0.0 copy-done.2
  195.9 0.0 copy-done.8
  195.9 0.7 copy-done.9
  196.6 3.0 %shard_map.73 = bf16[128,3584]{1,0:T(8,128)(2,1)} custom-call(bf16[256,128]{1,0:T(8,128)(2,1)} %get-tuple-element.43.pick, bf16[256,2048]{1,0:T(8,128)(2,1)} %bitcast.9, bf16[128,1536]{1,0:T(8,128)(2,1)} %get-tuple-element.74.own, bf16[128,1536]{1,0:T(8,128)(2,1)} %copy-done.8, bf16[128,1536]{1,0:T(8,128)(2,1)} %copy-done.9), custom_call_target="tpu_custom_call" | custom-call | flops 100000000 | bytes 6881280 | tf_op jit(solution)/shard_map/pallas_call | solution.py:164
  (6 shorter events, 0.0 us)
Async XLA Ops:
  38.5 3.1 %copy-start.3 = (bf16[128,3712]{1,0:T(8,128)(2,1)}, bf16[128,3712]{1,0:T(8,128)(2,1)S(1)}, u32[]{:S(2)}) copy-start(bf16[128,3712]{1,0:T(8,128)(2,1)S(1)} %get-tuple-element.53.refs_0_) | copy-start | bytes 2850820
  38.5 3.1 %copy-start.5 = (bf16[128,3712]{1,0:T(8,128)(2,1)}, bf16[128,3712]{1,0:T(8,128)(2,1)S(1)}, u32[]{:S(2)}) copy-start(bf16[128,3712]{1,0:T(8,128)(2,1)S(1)} %get-tuple-element.52.refs_1_) | copy-start | bytes 2850820
  38.5 22.3 %collective-permute-start.1 = (bf16[128,3712]{1,0:T(8,128)(2,1)S(1)}, bf16[128,3712]{1,0:T(8,128)(2,1)}, u32[]{:S(2)}, u32[]{:S(2)}) collective-permute-start(bf16[128,3712]{1,0:T(8,128)(2,1)S(1)} %get-tuple-element.52.refs_1_), channel_id=1, source_target_pairs={{0,3},{1,0},{2,1},{3,2},{4,7},{5,4},{6,5},{7,6},{8,11},{9,8},{10,9... | collective-permute-start | bytes 2850824 | tf_op jit(solution)/shard_map/ppermute | solution.py:250
  41.6 22.7 %collective-permute-start = (bf16[128,3712]{1,0:T(8,128)(2,1)S(1)}, bf16[128,3712]{1,0:T(8,128)(2,1)}, u32[]{:S(2)}, u32[]{:S(2)}) collective-permute-start(bf16[128,3712]{1,0:T(8,128)(2,1)S(1)} %get-tuple-element.53.refs_0_), channel_id=1, source_target_pairs={{0,1},{1,2},{2,3},{3,0},{4,5},{5,6},{6,7},{7,4},{8,9},{9,10},{10,1... | collective-permute-start | bytes 2850824 | tf_op jit(solution)/shard_map/ppermute | solution.py:247
  64.2 22.0 %collective-permute-start.2 = (bf16[128,3712]{1,0:T(8,128)(2,1)}, bf16[128,3712]{1,0:T(8,128)(2,1)}, u32[]{:S(2)}, u32[]{:S(2)}) collective-permute-start(bf16[128,3712]{1,0:T(8,128)(2,1)} %collective-permute-done.refs_0_), channel_id=1, source_target_pairs={{0,1},{1,2},{2,3},{3,0},{4,5},{5,6},{6,7},{7,4},{8,9},{9,10},{10,1... | collective-permute-start | bytes 2850824 | tf_op jit(solution)/shard_map/ppermute | solution.py:247
  64.3 22.0 %collective-permute-start.3 = (bf16[128,3712]{1,0:T(8,128)(2,1)}, bf16[128,3712]{1,0:T(8,128)(2,1)}, u32[]{:S(2)}, u32[]{:S(2)}) collective-permute-start(bf16[128,3712]{1,0:T(8,128)(2,1)} %collective-permute-done.1.refs_1_), channel_id=1, source_target_pairs={{0,3},{1,0},{2,1},{3,2},{4,7},{5,4},{6,5},{7,6},{8,11},{9,8},{10,9... | collective-permute-start | bytes 2850824 | tf_op jit(solution)/shard_map/ppermute | solution.py:250
  81.5 9.0 %copy-start.4 = (bf16[128,3712]{1,0:T(8,128)(2,1)S(1)}, bf16[128,3712]{1,0:T(8,128)(2,1)}, u32[]{:S(2)}) copy-start(bf16[128,3712]{1,0:T(8,128)(2,1)} %copy-done.3) | copy-start | bytes 2850820
  86.2 47.4 %all-to-all-start.1 = ((bf16[16,4,8,1664]{3,2,1,0:T(8,128)(2,1)}), bf16[16,4,8,1664]{3,2,1,0:T(8,128)(2,1)S(1)}, u32[]{:S(2)}, u32[]{:S(2)}) async-start(bf16[16,4,8,1664]{3,2,1,0:T(8,128)(2,1)} %get-tuple-element.61), calls=%async_computation.1 | async-start | bytes 3407872 | tf_op jit(solution)/shard_map/all_to_all | solution.py:244
  90.4 23.8 %collective-permute-start.4 = (bf16[128,3712]{1,0:T(8,128)(2,1)}, bf16[128,3712]{1,0:T(8,128)(2,1)}, u32[]{:S(2)}, u32[]{:S(2)}) collective-permute-start(bf16[128,3712]{1,0:T(8,128)(2,1)} %copy-done.5), channel_id=1, source_target_pairs={{0,1},{1,2},{2,3},{3,0},{4,5},{5,6},{6,7},{7,4},{8,9},{9,10},{10,1... | collective-permute-start | bytes 2850824 | tf_op jit(solution)/shard_map/ppermute | solution.py:247
  90.5 24.7 %collective-permute-start.5 = (bf16[128,3712]{1,0:T(8,128)(2,1)S(1)}, bf16[128,3712]{1,0:T(8,128)(2,1)}, u32[]{:S(2)}, u32[]{:S(2)}) collective-permute-start(bf16[128,3712]{1,0:T(8,128)(2,1)S(1)} %copy-done.4), channel_id=1, source_target_pairs={{0,3},{1,0},{2,1},{3,2},{4,7},{5,4},{6,5},{7,6},{8,11},{9,8},{10,9... | collective-permute-start | bytes 2850824 | tf_op jit(solution)/shard_map/ppermute | solution.py:250
  107.7 21.5 %collective-permute-start.6 = (bf16[128,2048]{1,0:T(8,128)(2,1)}, bf16[128,2048]{1,0:T(8,128)(2,1)S(1)}, u32[]{:S(2)}, u32[]{:S(2)}) collective-permute-start(bf16[128,2048]{1,0:T(8,128)(2,1)} %get-tuple-element.62), channel_id=1, source_target_pairs={{0,3},{1,0},{2,1},{3,2},{4,7},{5,4},{6,5},{7,6},{8,11},{9,8},{10,9... | collective-permute-start | bytes 1572872 | tf_op jit(solution)/shard_map/ppermute | solution.py:250
  109.5 19.7 %collective-permute-start.7 = (bf16[128,2048]{1,0:T(8,128)(2,1)}, bf16[128,2048]{1,0:T(8,128)(2,1)S(1)}, u32[]{:S(2)}, u32[]{:S(2)}) collective-permute-start(bf16[128,2048]{1,0:T(8,128)(2,1)} %get-tuple-element.65), channel_id=1, source_target_pairs={{0,1},{1,2},{2,3},{3,0},{4,5},{5,6},{6,7},{7,4},{8,9},{9,10},{10,1... | collective-permute-start | bytes 1572872 | tf_op jit(solution)/shard_map/ppermute | solution.py:247
  129.2 0.9 copy-start.6
  129.2 1.0 copy-start.7
  133.6 30.9 %copy-start = (bf16[16,4,8,1664]{3,2,1,0:T(8,128)(2,1)}, bf16[16,4,8,1664]{3,2,1,0:T(8,128)(2,1)S(1)}, u32[]{:S(2)}) copy-start(bf16[16,4,8,1664]{3,2,1,0:T(8,128)(2,1)S(1)} %all-to-all-done.1.first) | copy-start | bytes 5111812
  133.6 30.9 %all-to-all-start.3 = ((bf16[16,4,8,1664]{3,2,1,0:T(8,128)(2,1)}), bf16[16,4,8,1664]{3,2,1,0:T(8,128)(2,1)S(1)}, u32[]{:S(2)}, u32[]{:S(2)}) async-start(bf16[16,4,8,1664]{3,2,1,0:T(8,128)(2,1)} %get-tuple-element.73), calls=%async_computation.3 | async-start | bytes 3407872 | tf_op jit(solution)/shard_map/all_to_all | solution.py:244
  140.8 17.1 %collective-permute-start.8 = (bf16[2,128,2048]{2,1,0:T(8,128)(2,1)}, bf16[2,128,2048]{2,1,0:T(8,128)(2,1)}, u32[]{:S(2)}, u32[]{:S(2)}) collective-permute-start(bf16[2,128,2048]{2,1,0:T(8,128)(2,1)} %get-tuple-element.70), channel_id=1, source_target_pairs={{0,3},{1,0},{2,1},{3,2},{4,7},{5,4},{6,5},{7,6},{8,11},{9,8},{10,9... | collective-permute-start | bytes 3145736 | tf_op jit(solution)/shard_map/ppermute | solution.py:250
  144.6 16.7 %collective-permute-start.9 = (bf16[2,128,2048]{2,1,0:T(8,128)(2,1)}, bf16[2,128,2048]{2,1,0:T(8,128)(2,1)}, u32[]{:S(2)}, u32[]{:S(2)}) collective-permute-start(bf16[2,128,2048]{2,1,0:T(8,128)(2,1)} %get-tuple-element.71), channel_id=1, source_target_pairs={{0,1},{1,2},{2,3},{3,0},{4,5},{5,6},{6,7},{7,4},{8,9},{9,10},{10,1... | collective-permute-start | bytes 3145736 | tf_op jit(solution)/shard_map/ppermute | solution.py:247
  164.5 6.9 %copy-start.1 = (bf16[16,4,8,1664]{3,2,1,0:T(8,128)(2,1)}, bf16[16,4,8,1664]{3,2,1,0:T(8,128)(2,1)S(1)}, u32[]{:S(2)}) copy-start(bf16[16,4,8,1664]{3,2,1,0:T(8,128)(2,1)S(1)} %all-to-all-done.3.second) | copy-start | bytes 5111812
  164.6 23.8 %all-to-all-start.2 = ((bf16[16,2,8,2048]{3,2,1,0:T(8,128)(2,1)}), bf16[16,2,8,2048]{3,2,1,0:T(8,128)(2,1)S(1)}, u32[]{:S(2)}, u32[]{:S(2)}) async-start(bf16[16,2,8,2048]{3,2,1,0:T(8,128)(2,1)} %shard_map.70), calls=%async_computation.2 | async-start | bytes 2097152 | tf_op jit(solution)/shard_map/all_to_all | solution.py:244
  175.2 6.9 %collective-permute-start.10 = (bf16[64,1536]{1,0:T(8,128)(2,1)}, bf16[64,1536]{1,0:T(8,128)(2,1)S(1)}, u32[]{:S(2)}, u32[]{:S(2)}) collective-permute-start(bf16[64,1536]{1,0:T(8,128)(2,1)} %get-tuple-element.76), channel_id=1, source_target_pairs={{0,3},{1,0},{2,1},{3,2},{4,7},{5,4},{6,5},{7,6},{8,11},{9,8},{10,9... | collective-permute-start | bytes 589832 | tf_op jit(solution)/shard_map/ppermute | solution.py:250
  175.5 7.9 %collective-permute-start.11 = (bf16[64,1536]{1,0:T(8,128)(2,1)}, bf16[64,1536]{1,0:T(8,128)(2,1)S(1)}, u32[]{:S(2)}, u32[]{:S(2)}) collective-permute-start(bf16[64,1536]{1,0:T(8,128)(2,1)} %get-tuple-element.78), channel_id=1, source_target_pairs={{0,1},{1,2},{2,3},{3,0},{4,5},{5,6},{6,7},{7,4},{8,9},{9,10},{10,1... | collective-permute-start | bytes 589832 | tf_op jit(solution)/shard_map/ppermute | solution.py:247
  182.1 1.3 copy-start.10
  183.4 0.7 copy-start.11
  186.3 8.0 %collective-permute-start.12 = (bf16[128,1536]{1,0:T(8,128)(2,1)}, bf16[128,1536]{1,0:T(8,128)(2,1)S(1)}, u32[]{:S(2)}, u32[]{:S(2)}) collective-permute-start(bf16[128,1536]{1,0:T(8,128)(2,1)} %get-tuple-element.79), channel_id=1, source_target_pairs={{0,3},{1,0},{2,1},{3,2},{4,7},{5,4},{6,5},{7,6},{8,11},{9,8},{10,9... | collective-permute-start | bytes 1179656 | tf_op jit(solution)/shard_map/ppermute | solution.py:250
  186.7 9.2 %collective-permute-start.13 = (bf16[128,1536]{1,0:T(8,128)(2,1)}, bf16[128,1536]{1,0:T(8,128)(2,1)S(1)}, u32[]{:S(2)}, u32[]{:S(2)}) collective-permute-start(bf16[128,1536]{1,0:T(8,128)(2,1)} %get-tuple-element.80), channel_id=1, source_target_pairs={{0,1},{1,2},{2,3},{3,0},{4,5},{5,6},{6,7},{7,4},{8,9},{9,10},{10,1... | collective-permute-start | bytes 1179656 | tf_op jit(solution)/shard_map/ppermute | solution.py:247
  188.4 7.6 %copy-start.2 = (bf16[16,2,8,2048]{3,2,1,0:T(8,128)(2,1)}, bf16[16,2,8,2048]{3,2,1,0:T(8,128)(2,1)S(1)}, u32[]{:S(2)}) copy-start(bf16[16,2,8,2048]{3,2,1,0:T(8,128)(2,1)S(1)} %all-to-all-done.2) | copy-start | bytes 3145732
  194.3 1.6 copy-start.8
  195.9 0.7 copy-start.9

commit v5 on v1

--- a/solution.py
+++ b/solution.py
@@ -52,6 +52,9 @@
                 mine & (ids[k : k + 1, :] == group * locals_ + j), gates[k : k + 1, :], 0.0
             )
         meta = jnp.where(lane == j, jnp.sum(value, axis=1, keepdims=True), meta)
+    token = lax.broadcasted_iota(jnp.int32, mine.shape, 1).astype(jnp.float32)
+    token = jnp.sum(jnp.where(mine, token, 0.0), axis=1, keepdims=True)
+    meta = jnp.where(lane == locals_, token, meta)
     meta = meta.astype(jnp.bfloat16)
     half = mine.shape[0] // 2
     out_a[:, width : width + LANES] = meta[:half]
@@ -71,13 +74,13 @@
 def prepare(tokens, gate_scores, expert_ids, groups, locals_):
     count, width = tokens.shape
     per_group = 2 * count // groups
-    half = groups * per_group // 2
+    slots = groups * per_group
     return pl.pallas_call(
         functools.partial(prepare_kernel, locals_, groups, per_group),
         out_shape=[
-            jax.ShapeDtypeStruct((half, width + LANES), jnp.bfloat16),
-            jax.ShapeDtypeStruct((half, width + LANES), jnp.bfloat16),
-            jax.ShapeDtypeStruct((2 * half, count), jnp.bfloat16),
+            jax.ShapeDtypeStruct((slots // 2, width + LANES), jnp.bfloat16),
+            jax.ShapeDtypeStruct((slots // 2, width + LANES), jnp.bfloat16),
+            jax.ShapeDtypeStruct((slots, count), jnp.bfloat16),
         ],
         compiler_params=pltpu.CompilerParams(vmem_limit_bytes=VMEM),
         cost_estimate=pl.CostEstimate(flops=10**9, bytes_accessed=3 * 10**6, transcendentals=0),
@@ -85,8 +88,8 @@
 
 
 def expert_kernel(blocks, local_ref, *refs):
-    xs, (wg, wu, wd), outs = refs[:blocks], refs[blocks : blocks + 3], refs[blocks + 3 : 2 * blocks + 3]
-    rows, acc = refs[2 * blocks + 3 :]
+    xs, (wg, wu, wd), outs = refs[:blocks], refs[blocks : blocks + 3], refs[blocks + 3 : -2]
+    rows, acc = refs[-2:]
     step, steps = pl.program_id(0), pl.num_programs(0)
     width = rows.shape[1]
     piece = xs[0].shape[0]
@@ -113,17 +116,21 @@
     @pl.when(step == steps - 1)
     def _():
         for b in range(blocks):
-            meta = xs[b][:, width : width + LANES].astype(jnp.float32)
+            meta = xs[b][:, width : width + LANES]
             lane = lax.broadcasted_iota(jnp.int32, meta.shape, 1)
-            weight = jnp.sum(jnp.where(lane == local_ref[0], meta, 0.0), axis=1, keepdims=True)
+            weight = jnp.where(lane == local_ref[0], meta.astype(jnp.float32), 0.0)
+            weight = jnp.sum(weight, axis=1, keepdims=True)
             own = slice(b * piece, (b + 1) * piece)
-            outs[b][...] = ((acc[own, :] + part[own, :]) * weight).astype(jnp.bfloat16)
-
-
-def experts(xs, local, w_gate, w_up, w_down, tile=256):
+            outs[b][:, :width] = ((acc[own, :] + part[own, :]) * weight).astype(jnp.bfloat16)
+            if outs[b].shape[1] > width:
+                outs[b][:, width:] = meta
+
+
+def experts(xs, marked, local, w_gate, w_up, w_down, tile=256):
     blocks = len(xs)
     piece, wide = xs[0].shape
     width, hidden = w_gate.shape[1:]
+    wides = [wide if b in marked else width for b in range(blocks)]
     return pl.pallas_call(
         functools.partial(expert_kernel, blocks),
         grid=(hidden // tile,),
@@ -134,8 +141,8 @@
             pl.BlockSpec((1, width, tile), lambda i: (0, 0, i)),
             pl.BlockSpec((1, tile, width), lambda i: (0, i, 0)),
         ],
-        out_specs=[pl.BlockSpec((piece, width), lambda i: (0, 0))] * blocks,
-        out_shape=[jax.ShapeDtypeStruct((piece, width), jnp.bfloat16)] * blocks,
+        out_specs=[pl.BlockSpec((piece, w), lambda i: (0, 0)) for w in wides],
+        out_shape=[jax.ShapeDtypeStruct((piece, w), jnp.bfloat16) for w in wides],
         scratch_shapes=[
             pltpu.VMEM((blocks * piece, width), jnp.bfloat16),
             pltpu.VMEM((blocks * piece, width), jnp.float32),
@@ -151,38 +158,55 @@
     )(local, *xs, w_gate, w_up, w_down)
 
 
-def collect_kernel(pick, first, second, out):
-    half = first.shape[0]
-    dims = (((0,), (0,)), ((), ()))
-    total = lax.dot_general(pick[:half, :], first[...], dims, preferred_element_type=jnp.float32)
-    total = total + lax.dot_general(
-        pick[half:, :], second[...], dims, preferred_element_type=jnp.float32
-    )
+def whole(kernel, shapes, *arrays):
+    moved = sum(x.size * x.dtype.itemsize for x in arrays)
+    return pl.pallas_call(
+        kernel,
+        out_shape=shapes,
+        compiler_params=pltpu.CompilerParams(vmem_limit_bytes=VMEM),
+        cost_estimate=pl.CostEstimate(flops=10**8, bytes_accessed=3 * moved, transcendentals=0),
+    )(*arrays)
+
+
+def to_tokens(pick, rows):
+    return lax.dot_general(pick, rows, (((0,), (0,)), ((), ())), preferred_element_type=jnp.float32)
+
+
+def scatter_kernel(locals_, first, second, out):
+    count, width = out.shape
+    total = None
+    for rows in (first, second):
+        meta = rows[:, width:].astype(jnp.float32)
+        lane = lax.broadcasted_iota(jnp.int32, meta.shape, 1)
+        token = jnp.sum(jnp.where(lane == locals_, meta, 0.0), axis=1, keepdims=True)
+        lane = lax.broadcasted_iota(jnp.int32, (rows.shape[0], count), 1)
+        part = to_tokens((lane.astype(jnp.float32) == token).astype(jnp.bfloat16), rows[:, :width])
+        total = part if total is None else total + part
     out[...] = total.astype(jnp.bfloat16)
 
 
-def collect(pick, first, second):
-    return pl.pallas_call(
-        collect_kernel,
-        out_shape=jax.ShapeDtypeStruct((pick.shape[1], first.shape[1]), jnp.bfloat16),
-        compiler_params=pltpu.CompilerParams(vmem_limit_bytes=VMEM),
-        cost_estimate=pl.CostEstimate(flops=3 * 10**8, bytes_accessed=3 * 10**6, transcendentals=0),
-    )(pick, first, second)
+def collect_kernel(pick, first, second, far, out):
+    total = to_tokens(pick[:PIECE, :], first[...]) + to_tokens(pick[PIECE:, :], second[...])
+    out[...] = (total + far[...].astype(jnp.float32)).astype(jnp.bfloat16)
 
 
 def per_device(tokens, gate_scores, expert_ids, w_gate, w_up, w_down):
     groups, locals_ = lax.axis_size("node"), lax.axis_size("local")
     local = lax.axis_index("local").astype(jnp.int32).reshape(1)
+    tie = lax.optimization_barrier
 
     def across(block):
         parts = block.reshape(groups, block.shape[0] // groups, block.shape[1])
         return lax.all_to_all(parts, "node", 0, 0, tiled=True).reshape(block.shape)
 
+    def shift(block, by):
+        return lax.ppermute(block, "local", [(i, (i + by) % locals_) for i in range(locals_)])
+
     def up(block):
-        return lax.ppermute(block, "local", [(i, (i + 1) % locals_) for i in range(locals_)])
+        return shift(block, 1)
 
     def down(block):
-        return lax.ppermute(block, "local", [(i, (i - 1) % locals_) for i in range(locals_)])
+        return shift(block, -1)
 
     def add(*blocks):
         total = blocks[0].astype(jnp.float32)
@@ -195,21 +219,30 @@
     send_a, send_b, pick = prepare(tokens, gate_scores, expert_ids, groups, locals_)
     own_a = across(send_a)
     below_a, above_a = up(own_a), down(own_a)
+    send_b, _ = tie((send_b, own_a))
     own_b = across(send_b)
-    far_a, above_b = up(below_a), down(own_b)
-    below_b, far_b = up(own_b), down(above_b)
-
-    own_pa, below_pa, above_pa = run([own_a, below_a, above_a])
-    far_pa, own_pb, above_pb = run([far_a, own_b, above_b])
-    below_pb, far_pb = run([below_b, far_b])
-
-    back_far_a, back_above_a = down(far_pa), up(above_pa)
-    back_near_a, back_far_b = down(add(back_far_a, below_pa)), up(far_pb)
-    total_a = add(own_pa, back_above_a, back_near_a)
-    back_below_b, back_near_b = down(below_pb), up(add(back_far_b, above_pb))
-    final_a = across(total_a)
-    final_b = across(add(own_pb, back_below_b, back_near_b))
-    return collect(pick, final_a, final_b)
+    own_pa, own_pb = run([own_a, own_b], ())
+    below_a, above_a, next_b, own_pa = tie((below_a, above_a, own_b, own_pa))
+    far_a, above_b = up(below_a), down(next_b)
+    below_pa, above_pa = run([below_a, above_a], ())
+    far_a, above_b, last_b, below_pa = tie((far_a, above_b, next_b, below_pa))
+    below_b, far_b = up(last_b), down(above_b)
+    far_pa, above_pb = run([far_a, above_b], (0,))
+    below_b, far_b, above_pb = tie((below_b, far_b, above_pb))
+    below_pb, far_pb = run([below_b, far_b], (1,))
+
+    home_a, home_b = across(far_pa), across(far_pb)
+    far = whole(
+        functools.partial(scatter_kernel, locals_),
+        jax.ShapeDtypeStruct(tokens.shape, jnp.bfloat16), home_a, home_b,
+    )
+    far = shift(far, locals_ // 2)
+
+    final_a = across(add(own_pa, down(below_pa), up(above_pa)))
+    final_b = across(add(own_pb, down(below_pb), up(above_pb)))
+    return whole(
+        collect_kernel, jax.ShapeDtypeStruct(tokens.shape, jnp.bfloat16), pick, final_a, final_b, far
+    )
 
 
 def solution(mesh):

time: 206 us -> 183 us (0.89)
  waiting for transfers between devices: 61.8 us -> 34.4 us
  blocking collectives: 58.2 us -> 39.6 us
  starting transfers between devices: 22.3 us -> 35.1 us
  Pallas kernels: 55.7 us -> 66.5 us
    ppermute x12 -> x11, waiting for transfers between devices: 51.1 us -> 5.3 us  [shift(): lax.ppermute(block, 'local', [(i, (i + by) % locals_) for i in range(loca...]
    all_to_all x3 -> x2, blocking collectives: 58.2 us -> 39.6 us  [across(): return lax.all_to_all(parts, 'node', 0, 0, tiled=True).reshape(block.shape)]
    all_to_all x1 -> x4, waiting for transfers between devices: 10.7 us -> 29.1 us  [across(): return lax.all_to_all(parts, 'node', 0, 0, tiled=True).reshape(block.shape)]
    all_to_all x1 -> x4, starting transfers between devices: 3.77 us -> 18.7 us  [across(): return lax.all_to_all(parts, 'node', 0, 0, tiled=True).reshape(block.shape)]
    pallas_call x3 -> x4, Pallas kernels: 48.6 us -> 55.9 us  [experts(): pl.pallas_call(functools.partial(expert_kernel, blocks), grid=(hidden //...]
    pallas_call x1 -> x2, Pallas kernels: 3.06 us -> 6.55 us  [whole(): pl.pallas_call(kernel, out_shape=shapes, compiler_params=pltpu.CompilerPa...]
    convert_element_type x2 -> x0, other arithmetic: 2.82 us -> none  [add(): return total.astype(jnp.bfloat16)]
    ppermute x12 -> x11, starting transfers between devices: 18.5 us -> 16.3 us  [shift(): lax.ppermute(block, 'local', [(i, (i + by) % locals_) for i in range(loca...]
  transfers between devices with their start and end apart: 13 -> 15, of which waited for: 7 -> 6; matrix products, arithmetic and copies ran while one was open for 3% -> 2% of each run, Pallas kernels for 24% -> 32%
where the time goes in v5:
time: 183 us; the launch traced here: 182 us
  Pallas kernels  66.5 us (36%)
  blocking collectives  39.6 us (22%)
  starting transfers between devices  35.1 us (19%)
  waiting for transfers between devices  34.4 us (19%)
  other arithmetic  4.5 us (2%)
  local copies, waits for them, and re-layouts  1.9 us (1%)
    pallas_call x4, Pallas kernels, experts(): pl.pallas_call(functools.partial(expert_kernel, blocks), grid=(hidden //...  55.9 us
    all_to_all x2, blocking collectives, across(): return lax.all_to_all(parts, 'node', 0, 0, tiled=True).reshape(block.shape)  39.6 us
    all_to_all x4, waiting for transfers between devices, across(): return lax.all_to_all(parts, 'node', 0, 0, tiled=True).reshape(block.shape)  29.1 us
    all_to_all x4, starting transfers between devices, across(): return lax.all_to_all(parts, 'node', 0, 0, tiled=True).reshape(block.shape)  18.7 us
    ppermute x11, starting transfers between devices, shift(): lax.ppermute(block, 'local', [(i, (i + by) % locals_) for i in range(loca...  16.3 us
    pallas_call x2, Pallas kernels, whole(): pl.pallas_call(kernel, out_shape=shapes, compiler_params=pltpu.CompilerPa...  6.55 us
    ppermute x11, waiting for transfers between devices, shift(): lax.ppermute(block, 'local', [(i, (i + by) % locals_) for i in range(loca...  5.3 us
    reshape x2, other arithmetic, across(): parts = block.reshape(groups, block.shape[0] // groups, block.shape[1])  4.5 us
  transfers between devices with their start and end apart: 15, of which 6 were waited for; matrix products, arithmetic and copies ran while one was open for 2% of the time, Pallas kernels for 32%

profile of v5, /device:TPU:0, one launch (start us, length us, event | category | flops | bytes accessed | tf_op | source)
XLA Modules:
  0.0 182.1 jit_solution(16027290159285543896)
XLA Ops:
  0.0 4.1 %shard_map.64 = (bf16[128,3712]{1,0:T(8,128)(2,1)}, bf16[128,3712]{1,0:T(8,128)(2,1)}, bf16[256,128]{1,0:T(8,128)(2,1)}) custom-call(bf16[128,3584]{1,0:T(8,128)(2,1)} %tok.1, f32[4,128]{1,0:T(4,128)} %bitcast.30, s32[4,128]{1,0:T(4,128)} %bitcast.31), custom_call_target="tpu_custom_call" | custom-call | flops 1000000000 | bytes 3000000 | tf_op jit(solution)/shard_map/pallas_call | solution.py:78
  4.1 24.1 %all_to_all.30 = bf16[16,8,3712]{2,1,0:T(8,128)(2,1)S(1)} all-to-all(bf16[16,8,3712]{2,1,0:T(8,128)(2,1)} %bitcast.29), channel_id=1, replica_groups=mesh['dp'=2,'node'=16,'local'=4] {'node'}, dimensions={0} | all-to-all | bytes 1900544 | tf_op jit(solution)/shard_map/all_to_all | solution.py:200
  28.1 0.0 copy-start.4
  28.1 3.6 %all-to-all-start.1 = ((bf16[16,8,3712]{2,1,0:T(8,128)(2,1)}), bf16[16,8,3712]{2,1,0:T(8,128)(2,1)S(1)}, u32[]{:S(2)}, u32[]{:S(2)}) async-start(bf16[16,8,3712]{2,1,0:T(8,128)(2,1)} %bitcast.4), calls=%async_computation.1 | async-start | bytes 1900544 | tf_op jit(solution)/shard_map/all_to_all | solution.py:200
  31.8 1.6 collective-permute-start
  33.4 1.7 collective-permute-start.1
  35.1 12.0 %all-to-all-done.1 = bf16[16,8,3712]{2,1,0:T(8,128)(2,1)S(1)} async-done(((bf16[16,8,3712]{2,1,0:T(8,128)(2,1)}), bf16[16,8,3712]{2,1,0:T(8,128)(2,1)S(1)}, u32[]{:S(2)}, u32[]{:S(2)}) %all-to-all-start.1) | async-done | bytes 950304 | tf_op jit(solution)/shard_map/all_to_all | solution.py:200
  47.1 0.0 copy-start.2
  47.1 0.0 copy-done.4
  47.1 0.9 copy-done.2
  48.1 14.0 %shard_map.65 = (bf16[128,3584]{1,0:T(8,128)(2,1)}, bf16[128,3584]{1,0:T(8,128)(2,1)}) custom-call(s32[1]{0:T(128)} %bitcast.6.local_ref, bf16[128,3712]{1,0:T(8,128)(2,1)} %bitcast.24, bf16[128,3712]{1,0:T(8,128)(2,1)} %bitcast.19, bf16[1,3584,1024]{2,1,0:T(8,128)(2,1)} %refs_2_.7, bf16[1,3584,1024]{2,1,0:T(8,128)(2,1)} %refs_3_.7, ...), custom_call_target="tpu_custom_call" | custom-call | flops 5637144576 | bytes 22020096 | tf_op jit(solution)/shard_map/pallas_call | solution.py:134
  62.1 0.0 collective-permute-done.refs_0_
  62.1 0.0 collective-permute-done.1.refs_1_
  62.1 0.0 copy-start.8
  62.1 0.9 copy-done.8
  63.0 0.0 copy-start.3
  63.0 1.6 collective-permute-start.2
  64.6 1.7 collective-permute-start.3
  66.2 13.9 %shard_map.66 = (bf16[128,3584]{1,0:T(8,128)(2,1)}, bf16[128,3584]{1,0:T(8,128)(2,1)}) custom-call(s32[1]{0:T(128)} %bitcast.6.local_ref, bf16[128,3712]{1,0:T(8,128)(2,1)} %collective-permute-done.refs_0_, bf16[128,3712]{1,0:T(8,128)(2,1)} %copy-done.8, bf16[1,3584,1024]{2,1,0:T(8,128)(2,1)} %refs_2_.7, bf16[1,3584,1024]{2,1,0:T(8,128)(2,1)} %refs_3_.7, ...), custom_call_target="tpu_custom_call" | custom-call | flops 5637144576 | bytes 22020096 | tf_op jit(solution)/shard_map/pallas_call | solution.py:134
  80.2 4.8 %collective-permute-done.2.refs_0_ = bf16[128,3712]{1,0:T(8,128)(2,1)S(1)} collective-permute-done((bf16[128,3712]{1,0:T(8,128)(2,1)}, bf16[128,3712]{1,0:T(8,128)(2,1)S(1)}, u32[]{:S(2)}, u32[]{:S(2)}) %collective-permute-start.2) | collective-permute-done | bytes 950304 | tf_op jit(solution)/shard_map/ppermute | solution.py:203
  84.9 0.0 copy-start.7
  84.9 0.0 collective-permute-done.3.refs_1_
  85.0 0.0 copy-start.6
  85.0 0.0 copy-done.3
  85.0 1.6 collective-permute-start.6
  86.6 1.7 collective-permute-start.7
  88.3 0.4 collective-permute-start.5
  88.6 2.9 %collective-permute-start.4 = (bf16[128,3584]{1,0:T(8,128)(2,1)}, bf16[128,3584]{1,0:T(8,128)(2,1)}, u32[]{:S(2)}, u32[]{:S(2)}) collective-permute-start(bf16[128,3584]{1,0:T(8,128)(2,1)} %get-tuple-element.38), channel_id=1, source_target_pairs={{0,3},{1,0},{2,1},{3,2},{4,7},{5,4},{6,5},{7,6},{8,11},{9,8},{10,9... | collective-permute-start | bytes 2752520 | tf_op jit(solution)/shard_map/ppermute | solution.py:203
  91.5 0.0 copy-done.7
  91.5 0.0 copy-done.6
  91.5 14.0 %shard_map.67 = (bf16[128,3712]{1,0:T(8,128)(2,1)}, bf16[128,3584]{1,0:T(8,128)(2,1)}) custom-call(s32[1]{0:T(128)} %bitcast.6.local_ref, bf16[128,3712]{1,0:T(8,128)(2,1)} %copy-done.7, bf16[128,3712]{1,0:T(8,128)(2,1)} %copy-done.6, bf16[1,3584,1024]{2,1,0:T(8,128)(2,1)} %refs_2_.7, bf16[1,3584,1024]{2,1,0:T(8,128)(2,1)} %refs_3_.7, ...), custom_call_target="tpu_custom_call" | custom-call | flops 5637144576 | bytes 22020096 | tf_op jit(solution)/shard_map/pallas_call | solution.py:134
  105.5 4.7 %all-to-all-start.4 = ((bf16[16,8,3712]{2,1,0:T(8,128)(2,1)}), bf16[16,8,3712]{2,1,0:T(8,128)(2,1)S(1)}, u32[]{:S(2)}, u32[]{:S(2)}) async-start(bf16[16,8,3712]{2,1,0:T(8,128)(2,1)} %bitcast.28), calls=%async_computation.4 | async-start | bytes 1900544 | tf_op jit(solution)/shard_map/all_to_all | solution.py:200
  110.2 0.1 collective-permute-done.6.refs_0_
  110.3 0.4 collective-permute-done.7.refs_1_
  110.7 1.2 collective-permute-start.9
  111.9 14.0 %shard_map.68 = (bf16[128,3584]{1,0:T(8,128)(2,1)}, bf16[128,3712]{1,0:T(8,128)(2,1)}) custom-call(s32[1]{0:T(128)} %bitcast.6.local_ref, bf16[128,3712]{1,0:T(8,128)(2,1)} %collective-permute-done.6.refs_0_, bf16[128,3712]{1,0:T(8,128)(2,1)} %collective-permute-done.7.refs_1_, bf16[1,3584,1024]{2,1,0:T(8,128)(2,1)} %refs_2_.7, ...), custom_call_target="tpu_custom_call" | custom-call | flops 5637144576 | bytes 22020096 | tf_op jit(solution)/shard_map/pallas_call | solution.py:134
  125.9 0.0 copy-start.10
  125.9 2.0 %collective-permute-start.8 = (bf16[128,3584]{1,0:T(8,128)(2,1)}, bf16[128,3584]{1,0:T(8,128)(2,1)}, u32[]{:S(2)}, u32[]{:S(2)}) collective-permute-start(bf16[128,3584]{1,0:T(8,128)(2,1)} %get-tuple-element.47), channel_id=1, source_target_pairs={{0,3},{1,0},{2,1},{3,2},{4,7},{5,4},{6,5},{7,6},{8,11},{9,8},{10,9... | collective-permute-start | bytes 2752520 | tf_op jit(solution)/shard_map/ppermute | solution.py:203
  127.9 0.0 all-to-all-done.4
  127.9 0.0 copy-start
  127.9 6.8 %all-to-all-start.5 = ((bf16[16,8,3712]{2,1,0:T(8,128)(2,1)}), bf16[16,8,3712]{2,1,0:T(8,128)(2,1)S(1)}, u32[]{:S(2)}, u32[]{:S(2)}) async-start(bf16[16,8,3712]{2,1,0:T(8,128)(2,1)} %bitcast.27), calls=%async_computation.5 | async-start | bytes 1900544 | tf_op jit(solution)/shard_map/all_to_all | solution.py:200
  134.7 0.0 collective-permute-done.5
  134.7 0.0 collective-permute-done.4
  134.7 0.0 copy-done.10
  134.8 2.7 %fusion = bf16[16,8,3584]{2,1,0:T(8,128)(2,1)} fusion(bf16[128,3584]{1,0:T(8,128)(2,1)} %collective-permute-done.5, bf16[128,3584]{1,0:T(8,128)(2,1)} %collective-permute-done.4, bf16[128,3584]{1,0:T(8,128)(2,1)S(1)} %copy-done.10), kind=kLoop, calls=%fused_computation.2 | loop fusion | flops 2752512 | bytes 3670016 | tf_op jit(solution)/shard_map/reshape | solution.py:199
  137.5 0.0 copy-done
  137.5 9.6 %all-to-all-done.5 = bf16[16,8,3712]{2,1,0:T(8,128)(2,1)S(1)} async-done(((bf16[16,8,3712]{2,1,0:T(8,128)(2,1)}), bf16[16,8,3712]{2,1,0:T(8,128)(2,1)S(1)}, u32[]{:S(2)}, u32[]{:S(2)}) %all-to-all-start.5) | async-done | bytes 950304 | tf_op jit(solution)/shard_map/all_to_all | solution.py:200
  147.1 0.0 copy-start.1
  147.1 3.6 %all-to-all-start.2 = ((bf16[16,8,3584]{2,1,0:T(8,128)(2,1)}), bf16[16,8,3584]{2,1,0:T(8,128)(2,1)S(1)}, u32[]{:S(2)}, u32[]{:S(2)}) async-start(bf16[16,8,3584]{2,1,0:T(8,128)(2,1)} %fusion), calls=%async_computation.2 | async-start | bytes 1835008 | tf_op jit(solution)/shard_map/all_to_all | solution.py:200
  150.8 0.0 copy-start.9
  150.8 0.0 copy-done.1
  150.8 3.2 %shard_map.69 = bf16[128,3584]{1,0:T(8,128)(2,1)} custom-call(bf16[128,3712]{1,0:T(8,128)(2,1)} %bitcast.17, bf16[128,3712]{1,0:T(8,128)(2,1)} %bitcast.18), custom_call_target="tpu_custom_call" | custom-call | flops 100000000 | bytes 5701632 | tf_op jit(solution)/shard_map/pallas_call | solution.py:163
  154.0 0.0 collective-permute-start.10
  154.0 0.0 collective-permute-done.9
  154.0 0.0 collective-permute-done.8
  154.0 0.0 copy-done.9
  154.0 1.8 fusion.1
  155.8 7.4 %all-to-all-done.2 = bf16[16,8,3584]{2,1,0:T(8,128)(2,1)S(1)} async-done(((bf16[16,8,3584]{2,1,0:T(8,128)(2,1)}), bf16[16,8,3584]{2,1,0:T(8,128)(2,1)S(1)}, u32[]{:S(2)}, u32[]{:S(2)}) %all-to-all-start.2) | async-done | bytes 917536 | tf_op jit(solution)/shard_map/all_to_all | solution.py:200
  163.2 0.0 copy-start.5
  163.2 15.6 %all_to_all.31 = bf16[16,8,3584]{2,1,0:T(8,128)(2,1)} all-to-all(bf16[16,8,3584]{2,1,0:T(8,128)(2,1)S(1)} %fusion.1), channel_id=1, replica_groups=mesh['dp'=2,'node'=16,'local'=4] {'node'}, dimensions={0} | all-to-all | bytes 1835008 | tf_op jit(solution)/shard_map/all_to_all | solution.py:200
  178.8 0.0 collective-permute-done.10.far
  178.8 0.0 copy-done.5
  178.8 3.3 %shard_map.70 = bf16[128,3584]{1,0:T(8,128)(2,1)} custom-call(bf16[256,128]{1,0:T(8,128)(2,1)} %get-tuple-element.28.pick, bf16[128,3584]{1,0:T(8,128)(2,1)} %bitcast.25, bf16[128,3584]{1,0:T(8,128)(2,1)} %bitcast.26, bf16[128,3584]{1,0:T(8,128)(2,1)} %collective-permute-done.10.far), custom_call_target="tpu_custom_call" | custom-call | flops 100000000 | bytes 8454144 | tf_op jit(solution)/shard_map/pallas_call | solution.py:163
Async XLA Ops:
  28.1 19.0 %copy-start.4 = (bf16[16,8,3712]{2,1,0:T(8,128)(2,1)}, bf16[16,8,3712]{2,1,0:T(8,128)(2,1)S(1)}, u32[]{:S(2)}) copy-start(bf16[16,8,3712]{2,1,0:T(8,128)(2,1)S(1)} %all_to_all.30) | copy-start | bytes 2850820
  28.1 19.0 %all-to-all-start.1 = ((bf16[16,8,3712]{2,1,0:T(8,128)(2,1)}), bf16[16,8,3712]{2,1,0:T(8,128)(2,1)S(1)}, u32[]{:S(2)}, u32[]{:S(2)}) async-start(bf16[16,8,3712]{2,1,0:T(8,128)(2,1)} %bitcast.4), calls=%async_computation.1 | async-start | bytes 1900544 | tf_op jit(solution)/shard_map/all_to_all | solution.py:200
  31.8 30.3 %collective-permute-start = (bf16[128,3712]{1,0:T(8,128)(2,1)S(1)}, bf16[128,3712]{1,0:T(8,128)(2,1)}, u32[]{:S(2)}, u32[]{:S(2)}) collective-permute-start(bf16[128,3712]{1,0:T(8,128)(2,1)S(1)} %bitcast.22), channel_id=1, source_target_pairs={{0,1},{1,2},{2,3},{3,0},{4,5},{5,6},{6,7},{7,4},{8,9},{9,10},{10,1... | collective-permute-start | bytes 2850824 | tf_op jit(solution)/shard_map/ppermute | solution.py:203
  33.4 28.6 %collective-permute-start.1 = (bf16[128,3712]{1,0:T(8,128)(2,1)S(1)}, bf16[128,3712]{1,0:T(8,128)(2,1)S(1)}, u32[]{:S(2)}, u32[]{:S(2)}) collective-permute-start(bf16[128,3712]{1,0:T(8,128)(2,1)S(1)} %bitcast.23), channel_id=1, source_target_pairs={{0,3},{1,0},{2,1},{3,2},{4,7},{5,4},{6,5},{7,6},{8,11},{9,8},{10,9... | collective-permute-start | bytes 2850824 | tf_op jit(solution)/shard_map/ppermute | solution.py:203
  47.1 0.9 copy-start.2
  62.1 0.9 copy-start.8
  63.0 22.0 %copy-start.3 = (bf16[16,8,3712]{2,1,0:T(8,128)(2,1)S(1)}, bf16[16,8,3712]{2,1,0:T(8,128)(2,1)}, u32[]{:S(2)}) copy-start(bf16[16,8,3712]{2,1,0:T(8,128)(2,1)} %copy-done.2) | copy-start | bytes 2850820
  63.0 21.9 %collective-permute-start.2 = (bf16[128,3712]{1,0:T(8,128)(2,1)}, bf16[128,3712]{1,0:T(8,128)(2,1)S(1)}, u32[]{:S(2)}, u32[]{:S(2)}) collective-permute-start(bf16[128,3712]{1,0:T(8,128)(2,1)} %collective-permute-done.refs_0_), channel_id=1, source_target_pairs={{0,1},{1,2},{2,3},{3,0},{4,5},{5,6},{6,7},{7,4},{8,9},{9,10},{10,1... | collective-permute-start | bytes 2850824 | tf_op jit(solution)/shard_map/ppermute | solution.py:203
  64.6 20.4 %collective-permute-start.3 = (bf16[128,3712]{1,0:T(8,128)(2,1)}, bf16[128,3712]{1,0:T(8,128)(2,1)S(1)}, u32[]{:S(2)}, u32[]{:S(2)}) collective-permute-start(bf16[128,3712]{1,0:T(8,128)(2,1)} %bitcast.20), channel_id=1, source_target_pairs={{0,3},{1,0},{2,1},{3,2},{4,7},{5,4},{6,5},{7,6},{8,11},{9,8},{10,9... | collective-permute-start | bytes 2850824 | tf_op jit(solution)/shard_map/ppermute | solution.py:203
  84.9 6.6 %copy-start.7 = (bf16[128,3712]{1,0:T(8,128)(2,1)}, bf16[128,3712]{1,0:T(8,128)(2,1)S(1)}, u32[]{:S(2)}) copy-start(bf16[128,3712]{1,0:T(8,128)(2,1)S(1)} %collective-permute-done.2.refs_0_) | copy-start | bytes 2850820
  85.0 6.5 %copy-start.6 = (bf16[128,3712]{1,0:T(8,128)(2,1)}, bf16[128,3712]{1,0:T(8,128)(2,1)S(1)}, u32[]{:S(2)}) copy-start(bf16[128,3712]{1,0:T(8,128)(2,1)S(1)} %collective-permute-done.3.refs_1_) | copy-start | bytes 2850820
  85.0 25.4 %collective-permute-start.6 = (bf16[128,3712]{1,0:T(8,128)(2,1)S(1)}, bf16[128,3712]{1,0:T(8,128)(2,1)}, u32[]{:S(2)}, u32[]{:S(2)}) collective-permute-start(bf16[128,3712]{1,0:T(8,128)(2,1)S(1)} %bitcast.21), channel_id=1, source_target_pairs={{0,1},{1,2},{2,3},{3,0},{4,5},{5,6},{6,7},{7,4},{8,9},{9,10},{10,1... | collective-permute-start | bytes 2850824 | tf_op jit(solution)/shard_map/ppermute | solution.py:203
  86.6 24.1 %collective-permute-start.7 = (bf16[128,3712]{1,0:T(8,128)(2,1)S(1)}, bf16[128,3712]{1,0:T(8,128)(2,1)}, u32[]{:S(2)}, u32[]{:S(2)}) collective-permute-start(bf16[128,3712]{1,0:T(8,128)(2,1)S(1)} %collective-permute-done.3.refs_1_), channel_id=1, source_target_pairs={{0,3},{1,0},{2,1},{3,2},{4,7},{5,4},{6,5},{7,6},{8,11},{9,8},{10,9... | collective-permute-start | bytes 2850824 | tf_op jit(solution)/shard_map/ppermute | solution.py:203
  88.3 46.5 %collective-permute-start.5 = (bf16[128,3584]{1,0:T(8,128)(2,1)}, bf16[128,3584]{1,0:T(8,128)(2,1)}, u32[]{:S(2)}, u32[]{:S(2)}) collective-permute-start(bf16[128,3584]{1,0:T(8,128)(2,1)} %get-tuple-element.39), channel_id=1, source_target_pairs={{0,1},{1,2},{2,3},{3,0},{4,5},{5,6},{6,7},{7,4},{8,9},{9,10},{10,1... | collective-permute-start | bytes 2752520 | tf_op jit(solution)/shard_map/ppermute | solution.py:203
  88.6 46.1 %collective-permute-start.4 = (bf16[128,3584]{1,0:T(8,128)(2,1)}, bf16[128,3584]{1,0:T(8,128)(2,1)}, u32[]{:S(2)}, u32[]{:S(2)}) collective-permute-start(bf16[128,3584]{1,0:T(8,128)(2,1)} %get-tuple-element.38), channel_id=1, source_target_pairs={{0,3},{1,0},{2,1},{3,2},{4,7},{5,4},{6,5},{7,6},{8,11},{9,8},{10,9... | collective-permute-start | bytes 2752520 | tf_op jit(solution)/shard_map/ppermute | solution.py:203
  105.5 22.4 %all-to-all-start.4 = ((bf16[16,8,3712]{2,1,0:T(8,128)(2,1)}), bf16[16,8,3712]{2,1,0:T(8,128)(2,1)S(1)}, u32[]{:S(2)}, u32[]{:S(2)}) async-start(bf16[16,8,3712]{2,1,0:T(8,128)(2,1)} %bitcast.28), calls=%async_computation.4 | async-start | bytes 1900544 | tf_op jit(solution)/shard_map/all_to_all | solution.py:200
  110.7 43.3 %collective-permute-start.9 = (bf16[128,3584]{1,0:T(8,128)(2,1)}, bf16[128,3584]{1,0:T(8,128)(2,1)}, u32[]{:S(2)}, u32[]{:S(2)}) collective-permute-start(bf16[128,3584]{1,0:T(8,128)(2,1)} %get-tuple-element.48), channel_id=1, source_target_pairs={{0,1},{1,2},{2,3},{3,0},{4,5},{5,6},{6,7},{7,4},{8,9},{9,10},{10,1... | collective-permute-start | bytes 2752520 | tf_op jit(solution)/shard_map/ppermute | solution.py:203
  125.9 8.8 %copy-start.10 = (bf16[128,3584]{1,0:T(8,128)(2,1)S(1)}, bf16[128,3584]{1,0:T(8,128)(2,1)}, u32[]{:S(2)}) copy-start(bf16[128,3584]{1,0:T(8,128)(2,1)} %get-tuple-element.33) | copy-start | bytes 2752516
  125.9 28.1 %collective-permute-start.8 = (bf16[128,3584]{1,0:T(8,128)(2,1)}, bf16[128,3584]{1,0:T(8,128)(2,1)}, u32[]{:S(2)}, u32[]{:S(2)}) collective-permute-start(bf16[128,3584]{1,0:T(8,128)(2,1)} %get-tuple-element.47), channel_id=1, source_target_pairs={{0,3},{1,0},{2,1},{3,2},{4,7},{5,4},{6,5},{7,6},{8,11},{9,8},{10,9... | collective-permute-start | bytes 2752520 | tf_op jit(solution)/shard_map/ppermute | solution.py:203
  127.9 9.6 %copy-start = (bf16[16,8,3712]{2,1,0:T(8,128)(2,1)}, bf16[16,8,3712]{2,1,0:T(8,128)(2,1)S(1)}, u32[]{:S(2)}) copy-start(bf16[16,8,3712]{2,1,0:T(8,128)(2,1)S(1)} %all-to-all-done.4) | copy-start | bytes 2850820
  127.9 19.2 %all-to-all-start.5 = ((bf16[16,8,3712]{2,1,0:T(8,128)(2,1)}), bf16[16,8,3712]{2,1,0:T(8,128)(2,1)S(1)}, u32[]{:S(2)}, u32[]{:S(2)}) async-start(bf16[16,8,3712]{2,1,0:T(8,128)(2,1)} %bitcast.27), calls=%async_computation.5 | async-start | bytes 1900544 | tf_op jit(solution)/shard_map/all_to_all | solution.py:200
  147.1 3.7 %copy-start.1 = (bf16[16,8,3712]{2,1,0:T(8,128)(2,1)}, bf16[16,8,3712]{2,1,0:T(8,128)(2,1)S(1)}, u32[]{:S(2)}) copy-start(bf16[16,8,3712]{2,1,0:T(8,128)(2,1)S(1)} %all-to-all-done.5) | copy-start | bytes 2850820
  147.1 16.1 %all-to-all-start.2 = ((bf16[16,8,3584]{2,1,0:T(8,128)(2,1)}), bf16[16,8,3584]{2,1,0:T(8,128)(2,1)S(1)}, u32[]{:S(2)}, u32[]{:S(2)}) async-start(bf16[16,8,3584]{2,1,0:T(8,128)(2,1)} %fusion), calls=%async_computation.2 | async-start | bytes 1835008 | tf_op jit(solution)/shard_map/all_to_all | solution.py:200
  150.8 3.2 %copy-start.9 = (bf16[128,3584]{1,0:T(8,128)(2,1)S(1)}, bf16[128,3584]{1,0:T(8,128)(2,1)}, u32[]{:S(2)}) copy-start(bf16[128,3584]{1,0:T(8,128)(2,1)} %get-tuple-element.40) | copy-start | bytes 2752516
  154.0 24.8 %collective-permute-start.10 = (bf16[128,3584]{1,0:T(8,128)(2,1)}, bf16[128,3584]{1,0:T(8,128)(2,1)}, u32[]{:S(2)}, u32[]{:S(2)}) collective-permute-start(bf16[128,3584]{1,0:T(8,128)(2,1)} %shard_map.69), channel_id=1, source_target_pairs={{0,2},{1,3},{2,0},{3,1},{4,6},{5,7},{6,4},{7,5},{8,10},{9,11},{10,... | collective-permute-start | bytes 2752520 | tf_op jit(solution)/shard_map/ppermute | solution.py:203
  163.2 15.6 %copy-start.5 = (bf16[16,8,3584]{2,1,0:T(8,128)(2,1)}, bf16[16,8,3584]{2,1,0:T(8,128)(2,1)S(1)}, u32[]{:S(2)}) copy-start(bf16[16,8,3584]{2,1,0:T(8,128)(2,1)S(1)} %all-to-all-done.2) | copy-start | bytes 2752516

commit v6 on v5

--- a/solution.py
+++ b/solution.py
@@ -64,7 +64,7 @@
         x = tok[:, cols].astype(jnp.float32)
         largest = jnp.max(jnp.abs(x), axis=1, keepdims=True)
         scale = ((largest + 1e-06) / 448.0).astype(jnp.bfloat16).astype(jnp.float32)
-        quantized = (x / scale).astype(jnp.bfloat16).astype(jnp.float32)
+        quantized = (x * (1.0 / scale)).astype(jnp.bfloat16).astype(jnp.float32)
         restored = (quantized * scale).astype(jnp.bfloat16)
         rows = jnp.dot(onehot, restored, preferred_element_type=jnp.float32).astype(jnp.bfloat16)
         out_a[:, cols] = rows[:half]
@@ -190,6 +190,23 @@
     out[...] = (total + far[...].astype(jnp.float32)).astype(jnp.bfloat16)
 
 
+def collect(pick, first, second, far, steps=4):
+    count, width = far.shape
+    cut = width // steps
+    block = pl.BlockSpec((count, cut), lambda i: (0, i))
+    return pl.pallas_call(
+        collect_kernel,
+        grid=(steps,),
+        in_specs=[pl.BlockSpec(pick.shape, lambda i: (0, 0)), block, block, block],
+        out_specs=block,
+        out_shape=jax.ShapeDtypeStruct((count, width), jnp.bfloat16),
+        compiler_params=pltpu.CompilerParams(vmem_limit_bytes=VMEM),
+        cost_estimate=pl.CostEstimate(
+            flops=4 * pick.size * width, bytes_accessed=8 * far.size, transcendentals=0
+        ),
+    )(pick, first, second, far)
+
+
 def per_device(tokens, gate_scores, expert_ids, w_gate, w_up, w_down):
     groups, locals_ = lax.axis_size("node"), lax.axis_size("local")
     local = lax.axis_index("local").astype(jnp.int32).reshape(1)
@@ -221,15 +238,18 @@
     below_a, above_a = up(own_a), down(own_a)
     send_b, _ = tie((send_b, own_a))
     own_b = across(send_b)
-    own_pa, own_pb = run([own_a, own_b], ())
+    [own_pa] = run([own_a], ())
     below_a, above_a, next_b, own_pa = tie((below_a, above_a, own_b, own_pa))
     far_a, above_b = up(below_a), down(next_b)
     below_pa, above_pa = run([below_a, above_a], ())
     far_a, above_b, last_b, below_pa = tie((far_a, above_b, next_b, below_pa))
     below_b, far_b = up(last_b), down(above_b)
     far_pa, above_pb = run([far_a, above_b], (0,))
+    below_pa, above_pa, far_pa = tie((below_pa, above_pa, far_pa))
     below_b, far_b, above_pb = tie((below_b, far_b, above_pb))
     below_pb, far_pb = run([below_b, far_b], (1,))
+    last_b, far_pb = tie((last_b, far_pb))
+    [own_pb] = run([last_b], ())
 
     home_a, home_b = across(far_pa), across(far_pb)
     far = whole(
@@ -240,9 +260,7 @@
 
     final_a = across(add(own_pa, down(below_pa), up(above_pa)))
     final_b = across(add(own_pb, down(below_pb), up(above_pb)))
-    return whole(
-        collect_kernel, jax.ShapeDtypeStruct(tokens.shape, jnp.bfloat16), pick, final_a, final_b, far
-    )
+    return collect(pick, final_a, final_b, far)
 
 
 def solution(mesh):

time: 183 us -> 177 us (0.967)
  waiting for transfers between devices: 34.4 us -> 16.9 us
  Pallas kernels: 66.5 us -> 76.6 us
  starting transfers between devices: 35.1 us -> 38.5 us
  local copies, waits for them, and re-layouts: 1.9 us -> 0.04 us
    all_to_all x4, waiting for transfers between devices: 29.1 us -> 11 us  [across(): return lax.all_to_all(parts, 'node', 0, 0, tiled=True).reshape(block.shape)]
    pallas_call x4 -> x5, Pallas kernels: 55.9 us -> 64.8 us  [experts(): pl.pallas_call(functools.partial(expert_kernel, blocks), grid=(hidden //...]
    pallas_call x0 -> x1, Pallas kernels: none -> 4.44 us  [collect(): pl.pallas_call(collect_kernel, grid=(steps,), in_specs=[pl.BlockSpec(pick...]
    pallas_call x2 -> x1, Pallas kernels: 6.55 us -> 3.24 us  [whole(): pl.pallas_call(kernel, out_shape=shapes, compiler_params=pltpu.CompilerPa...]
    all_to_all x4, starting transfers between devices: 18.7 us -> 22 us  [across(): return lax.all_to_all(parts, 'node', 0, 0, tiled=True).reshape(block.shape)]
    unnamed x22 -> x20, local copies, waits for them, and re-layouts: 1.9 us -> 0.04 us
  transfers between devices with their start and end apart: 15 -> 15, of which waited for: 6 -> 5; matrix products, arithmetic and copies ran while one was open for 2% -> 3% of each run, Pallas kernels for 32% -> 39%
where the time goes in v6:
time: 177 us; the launch traced here: 176 us
  Pallas kernels  76.6 us (43%)
  blocking collectives  39.6 us (22%)
  starting transfers between devices  38.5 us (22%)
  waiting for transfers between devices  16.9 us (10%)
  other arithmetic  4.5 us (3%)
    pallas_call x5, Pallas kernels, experts(): pl.pallas_call(functools.partial(expert_kernel, blocks), grid=(hidden //...  64.8 us
    all_to_all x2, blocking collectives, across(): return lax.all_to_all(parts, 'node', 0, 0, tiled=True).reshape(block.shape)  39.6 us
    all_to_all x4, starting transfers between devices, across(): return lax.all_to_all(parts, 'node', 0, 0, tiled=True).reshape(block.shape)  22 us
    ppermute x11, starting transfers between devices, shift(): lax.ppermute(block, 'local', [(i, (i + by) % locals_) for i in range(loca...  16.5 us
    all_to_all x4, waiting for transfers between devices, across(): return lax.all_to_all(parts, 'node', 0, 0, tiled=True).reshape(block.shape)  11 us
    ppermute x11, waiting for transfers between devices, shift(): lax.ppermute(block, 'local', [(i, (i + by) % locals_) for i in range(loca...  5.88 us
    reshape x2, other arithmetic, across(): parts = block.reshape(groups, block.shape[0] // groups, block.shape[1])  4.5 us
    pallas_call x1, Pallas kernels, collect(): pl.pallas_call(collect_kernel, grid=(steps,), in_specs=[pl.BlockSpec(pick...  4.44 us
  transfers between devices with their start and end apart: 15, of which 5 were waited for; matrix products, arithmetic and copies ran while one was open for 3% of the time, Pallas kernels for 39%

profile of v6, /device:TPU:0, one launch (start us, length us, event | category | flops | bytes accessed | tf_op | source)
XLA Modules:
  0.0 176.3 jit_solution(13693277017700936455)
XLA Ops:
  0.0 4.1 %shard_map.64 = (bf16[128,3712]{1,0:T(8,128)(2,1)}, bf16[128,3712]{1,0:T(8,128)(2,1)}, bf16[256,128]{1,0:T(8,128)(2,1)}) custom-call(bf16[128,3584]{1,0:T(8,128)(2,1)} %tok.1, f32[4,128]{1,0:T(4,128)} %bitcast.30, s32[4,128]{1,0:T(4,128)} %bitcast.31), custom_call_target="tpu_custom_call" | custom-call | flops 1000000000 | bytes 3000000 | tf_op jit(solution)/shard_map/pallas_call | solution.py:78
  4.1 24.1 %all_to_all.30 = bf16[16,8,3712]{2,1,0:T(8,128)(2,1)S(1)} all-to-all(bf16[16,8,3712]{2,1,0:T(8,128)(2,1)} %bitcast.29), channel_id=1, replica_groups=mesh['dp'=2,'node'=16,'local'=4] {'node'}, dimensions={0} | all-to-all | bytes 1900544 | tf_op jit(solution)/shard_map/all_to_all | solution.py:217
  28.2 0.0 copy-start.3
  28.2 1.6 collective-permute-start
  29.7 1.7 collective-permute-start.1
  31.4 3.6 %all-to-all-start.1 = ((bf16[16,8,3712]{2,1,0:T(8,128)(2,1)}), bf16[16,8,3712]{2,1,0:T(8,128)(2,1)S(1)}, u32[]{:S(2)}, u32[]{:S(2)}) async-start(bf16[16,8,3712]{2,1,0:T(8,128)(2,1)} %bitcast.4), calls=%async_computation.1 | async-start | bytes 1900544 | tf_op jit(solution)/shard_map/all_to_all | solution.py:217
  35.0 0.0 copy-done.3
  35.1 11.3 %shard_map.65 = bf16[128,3584]{1,0:T(8,128)(2,1)} custom-call(s32[1]{0:T(128)} %bitcast.6.local_ref, bf16[128,3712]{1,0:T(8,128)(2,1)} %bitcast.24, bf16[1,3584,1024]{2,1,0:T(8,128)(2,1)} %refs_1_.3, bf16[1,3584,1024]{2,1,0:T(8,128)(2,1)} %refs_2_.9, bf16[1,1024,3584]{2,1,0:T(8,128)(2,1)} %refs_3_.9), custom_call_target="tpu_custom_call" | custom-call | flops 2818572288 | bytes 22020096 | tf_op jit(solution)/shard_map/pallas_call | solution.py:134
  46.4 3.6 %all-to-all-done.1 = bf16[16,8,3712]{2,1,0:T(8,128)(2,1)S(1)} async-done(((bf16[16,8,3712]{2,1,0:T(8,128)(2,1)}), bf16[16,8,3712]{2,1,0:T(8,128)(2,1)S(1)}, u32[]{:S(2)}, u32[]{:S(2)}) %all-to-all-start.1) | async-done | bytes 950304 | tf_op jit(solution)/shard_map/all_to_all | solution.py:217
  50.0 0.0 copy-start
  50.0 1.1 collective-permute-done.refs_0_
  51.1 0.0 copy-start.7
  51.1 0.1 collective-permute-done.1.refs_1_
  51.2 1.6 collective-permute-start.2
  52.8 1.7 collective-permute-start.3
  54.4 0.0 copy-done.7
  54.5 14.0 %shard_map.66 = (bf16[128,3584]{1,0:T(8,128)(2,1)}, bf16[128,3584]{1,0:T(8,128)(2,1)}) custom-call(s32[1]{0:T(128)} %bitcast.6.local_ref, bf16[128,3712]{1,0:T(8,128)(2,1)} %copy-done.7, bf16[128,3712]{1,0:T(8,128)(2,1)} %collective-permute-done.1.refs_1_, bf16[1,3584,1024]{2,1,0:T(8,128)(2,1)} %refs_1_.3, bf16[1,3584,1024]{2,1,0:T(8,128)(2,1)} %refs_2_.9, ...), custom_call_target="tpu_custom_call" | custom-call | flops 5637144576 | bytes 22020096 | tf_op jit(solution)/shard_map/pallas_call | solution.py:134
  68.5 4.6 %collective-permute-done.2.refs_0_ = bf16[128,3712]{1,0:T(8,128)(2,1)S(1)} collective-permute-done((bf16[128,3712]{1,0:T(8,128)(2,1)S(1)}, bf16[128,3712]{1,0:T(8,128)(2,1)S(1)}, u32[]{:S(2)}, u32[]{:S(2)}) %collective-permute-start.2) | collective-permute-done | bytes 950304 | tf_op jit(solution)/shard_map/ppermute | solution.py:220
  73.1 0.0 copy-start.9
  73.1 0.0 collective-permute-done.3.refs_1_
  73.1 0.0 copy-done
  73.1 1.3 collective-permute-start.6
  74.3 2.1 %collective-permute-start.7 = (bf16[128,3712]{1,0:T(8,128)(2,1)}, bf16[128,3712]{1,0:T(8,128)(2,1)}, u32[]{:S(2)}, u32[]{:S(2)}) collective-permute-start(bf16[128,3712]{1,0:T(8,128)(2,1)} %collective-permute-done.3.refs_1_), channel_id=1, source_target_pairs={{0,3},{1,0},{2,1},{3,2},{4,7},{5,4},{6,5},{7,6},{8,11},{9,8},{10,9... | collective-permute-start | bytes 2850824 | tf_op jit(solution)/shard_map/ppermute | solution.py:220
  76.4 0.0 copy-done.9
  76.4 14.0 %shard_map.67 = (bf16[128,3712]{1,0:T(8,128)(2,1)}, bf16[128,3584]{1,0:T(8,128)(2,1)}) custom-call(s32[1]{0:T(128)} %bitcast.6.local_ref, bf16[128,3712]{1,0:T(8,128)(2,1)} %copy-done.9, bf16[128,3712]{1,0:T(8,128)(2,1)} %collective-permute-done.3.refs_1_, bf16[1,3584,1024]{2,1,0:T(8,128)(2,1)} %refs_1_.3, bf16[1,3584,1024]{2,1,0:T(8,128)(2,1)} %refs_2_.9, ...), custom_call_target="tpu_custom_call" | custom-call | flops 5637144576 | bytes 22020096 | tf_op jit(solution)/shard_map/pallas_call | solution.py:134
  90.4 0.0 collective-permute-start.5
  90.4 3.2 %collective-permute-start.4 = (bf16[128,3584]{1,0:T(8,128)(2,1)}, bf16[128,3584]{1,0:T(8,128)(2,1)}, u32[]{:S(2)}, u32[]{:S(2)}) collective-permute-start(bf16[128,3584]{1,0:T(8,128)(2,1)} %get-tuple-element.45), channel_id=1, source_target_pairs={{0,3},{1,0},{2,1},{3,2},{4,7},{5,4},{6,5},{7,6},{8,11},{9,8},{10,9... | collective-permute-start | bytes 2752520 | tf_op jit(solution)/shard_map/ppermute | solution.py:220
  93.6 4.0 %all-to-all-start.4 = ((bf16[16,8,3712]{2,1,0:T(8,128)(2,1)}), bf16[16,8,3712]{2,1,0:T(8,128)(2,1)S(1)}, u32[]{:S(2)}, u32[]{:S(2)}) async-start(bf16[16,8,3712]{2,1,0:T(8,128)(2,1)} %bitcast.27), calls=%async_computation.4 | async-start | bytes 1900544 | tf_op jit(solution)/shard_map/all_to_all | solution.py:217
  97.6 0.0 collective-permute-done.6.refs_0_
  97.6 0.0 copy-start.8
  97.6 0.0 collective-permute-done.7.refs_1_
  97.7 2.5 %collective-permute-start.9 = (bf16[128,3584]{1,0:T(8,128)(2,1)}, bf16[128,3584]{1,0:T(8,128)(2,1)}, u32[]{:S(2)}, u32[]{:S(2)}) collective-permute-start(bf16[128,3584]{1,0:T(8,128)(2,1)} %get-tuple-element.54), channel_id=1, source_target_pairs={{0,1},{1,2},{2,3},{3,0},{4,5},{5,6},{6,7},{7,4},{8,9},{9,10},{10,1... | collective-permute-start | bytes 2752520 | tf_op jit(solution)/shard_map/ppermute | solution.py:220
  100.2 0.0 copy-done.8
  100.2 14.0 %shard_map.68 = (bf16[128,3584]{1,0:T(8,128)(2,1)}, bf16[128,3712]{1,0:T(8,128)(2,1)}) custom-call(s32[1]{0:T(128)} %bitcast.6.local_ref, bf16[128,3712]{1,0:T(8,128)(2,1)} %copy-done.8, bf16[128,3712]{1,0:T(8,128)(2,1)} %collective-permute-done.7.refs_1_, bf16[1,3584,1024]{2,1,0:T(8,128)(2,1)} %refs_1_.3, bf16[1,3584,1024]{2,1,0:T(8,128)(2,1)} %refs_2_.9, ...), custom_call_target="tpu_custom_call" | custom-call | flops 5637144576 | bytes 22020096 | tf_op jit(solution)/shard_map/pallas_call | solution.py:134
  114.2 0.0 copy-start.5
  114.2 0.9 collective-permute-start.8
  115.1 0.0 all-to-all-done.4
  115.1 0.0 copy-start.1
  115.1 7.2 %all-to-all-start.5 = ((bf16[16,8,3712]{2,1,0:T(8,128)(2,1)}), bf16[16,8,3712]{2,1,0:T(8,128)(2,1)S(1)}, u32[]{:S(2)}, u32[]{:S(2)}) async-start(bf16[16,8,3712]{2,1,0:T(8,128)(2,1)} %bitcast.28), calls=%async_computation.5 | async-start | bytes 1900544 | tf_op jit(solution)/shard_map/all_to_all | solution.py:217
  122.4 0.0 collective-permute-done.5
  122.4 0.0 collective-permute-done.4
  122.4 0.0 copy-done.5
  122.4 2.7 %fusion = bf16[16,8,3584]{2,1,0:T(8,128)(2,1)} fusion(bf16[128,3584]{1,0:T(8,128)(2,1)} %collective-permute-done.5, bf16[128,3584]{1,0:T(8,128)(2,1)} %collective-permute-done.4, bf16[128,3584]{1,0:T(8,128)(2,1)S(1)} %copy-done.5), kind=kLoop, calls=%fused_computation.2 | loop fusion | flops 2752512 | bytes 3670016 | tf_op jit(solution)/shard_map/reshape | solution.py:216
  125.1 0.0 copy-done.1
  125.1 11.4 %shard_map.69 = bf16[128,3584]{1,0:T(8,128)(2,1)} custom-call(s32[1]{0:T(128)} %bitcast.6.local_ref, bf16[128,3712]{1,0:T(8,128)(2,1)} %bitcast.19, bf16[1,3584,1024]{2,1,0:T(8,128)(2,1)} %refs_1_.3, bf16[1,3584,1024]{2,1,0:T(8,128)(2,1)} %refs_2_.9, bf16[1,1024,3584]{2,1,0:T(8,128)(2,1)} %refs_3_.9), custom_call_target="tpu_custom_call" | custom-call | flops 2818572288 | bytes 22020096 | tf_op jit(solution)/shard_map/pallas_call | solution.py:134
  136.5 0.0 all-to-all-done.5
  136.5 0.0 copy-start.2
  136.5 7.2 %all-to-all-start.2 = ((bf16[16,8,3584]{2,1,0:T(8,128)(2,1)}), bf16[16,8,3584]{2,1,0:T(8,128)(2,1)S(1)}, u32[]{:S(2)}, u32[]{:S(2)}) async-start(bf16[16,8,3584]{2,1,0:T(8,128)(2,1)} %fusion), calls=%async_computation.2 | async-start | bytes 1835008 | tf_op jit(solution)/shard_map/all_to_all | solution.py:217
  143.8 0.0 copy-start.6
  143.8 0.0 copy-done.2
  143.8 3.2 %shard_map.70 = bf16[128,3584]{1,0:T(8,128)(2,1)} custom-call(bf16[128,3712]{1,0:T(8,128)(2,1)} %bitcast.20, bf16[128,3712]{1,0:T(8,128)(2,1)} %bitcast.21), custom_call_target="tpu_custom_call" | custom-call | flops 100000000 | bytes 5701632 | tf_op jit(solution)/shard_map/pallas_call | solution.py:163
  147.0 0.0 collective-permute-start.10
  147.0 0.0 collective-permute-done.9
  147.0 0.0 collective-permute-done.8
  147.0 0.0 copy-done.6
  147.1 1.8 %fusion.1 = bf16[16,8,3584]{2,1,0:T(8,128)(2,1)S(1)} fusion(bf16[128,3584]{1,0:T(8,128)(2,1)} %collective-permute-done.9, bf16[128,3584]{1,0:T(8,128)(2,1)} %collective-permute-done.8, bf16[128,3584]{1,0:T(8,128)(2,1)S(1)} %copy-done.6), kind=kLoop, calls=%fused_computation.3 | loop fusion | flops 2752512 | bytes 3670016 | tf_op jit(solution)/shard_map/reshape | solution.py:216
  148.8 7.4 %all-to-all-done.2 = bf16[16,8,3584]{2,1,0:T(8,128)(2,1)S(1)} async-done(((bf16[16,8,3584]{2,1,0:T(8,128)(2,1)}), bf16[16,8,3584]{2,1,0:T(8,128)(2,1)S(1)}, u32[]{:S(2)}, u32[]{:S(2)}) %all-to-all-start.2) | async-done | bytes 917536 | tf_op jit(solution)/shard_map/all_to_all | solution.py:217
  156.2 0.0 copy-start.4
  156.2 15.6 %all_to_all.31 = bf16[16,8,3584]{2,1,0:T(8,128)(2,1)} all-to-all(bf16[16,8,3584]{2,1,0:T(8,128)(2,1)S(1)} %fusion.1), channel_id=1, replica_groups=mesh['dp'=2,'node'=16,'local'=4] {'node'}, dimensions={0} | all-to-all | bytes 1835008 | tf_op jit(solution)/shard_map/all_to_all | solution.py:217
  171.8 0.0 collective-permute-done.10.far
  171.8 0.0 copy-done.4
  171.8 4.4 %shard_map.71 = bf16[128,3584]{1,0:T(8,128)(2,1)} custom-call(bf16[256,128]{1,0:T(8,128)(2,1)} %get-tuple-element.31.pick, bf16[128,3584]{1,0:T(8,128)(2,1)} %bitcast.25, bf16[128,3584]{1,0:T(8,128)(2,1)} %bitcast.26, bf16[128,3584]{1,0:T(8,128)(2,1)} %collective-permute-done.10.far), custom_call_target="tpu_custom_call" | custom-call | flops 469762048 | bytes 3670016 | tf_op jit(solution)/shard_map/pallas_call | solution.py:197
Async XLA Ops:
  28.2 6.9 %copy-start.3 = (bf16[16,8,3712]{2,1,0:T(8,128)(2,1)}, bf16[16,8,3712]{2,1,0:T(8,128)(2,1)S(1)}, u32[]{:S(2)}) copy-start(bf16[16,8,3712]{2,1,0:T(8,128)(2,1)S(1)} %all_to_all.30) | copy-start | bytes 2850820
  28.2 22.9 %collective-permute-start = (bf16[128,3712]{1,0:T(8,128)(2,1)S(1)}, bf16[128,3712]{1,0:T(8,128)(2,1)S(1)}, u32[]{:S(2)}, u32[]{:S(2)}) collective-permute-start(bf16[128,3712]{1,0:T(8,128)(2,1)S(1)} %bitcast.22), channel_id=1, source_target_pairs={{0,1},{1,2},{2,3},{3,0},{4,5},{5,6},{6,7},{7,4},{8,9},{9,10},{10,1... | collective-permute-start | bytes 2850824 | tf_op jit(solution)/shard_map/ppermute | solution.py:220
  29.7 21.5 %collective-permute-start.1 = (bf16[128,3712]{1,0:T(8,128)(2,1)S(1)}, bf16[128,3712]{1,0:T(8,128)(2,1)}, u32[]{:S(2)}, u32[]{:S(2)}) collective-permute-start(bf16[128,3712]{1,0:T(8,128)(2,1)S(1)} %bitcast.23), channel_id=1, source_target_pairs={{0,3},{1,0},{2,1},{3,2},{4,7},{5,4},{6,5},{7,6},{8,11},{9,8},{10,9... | collective-permute-start | bytes 2850824 | tf_op jit(solution)/shard_map/ppermute | solution.py:220
  31.4 18.6 %all-to-all-start.1 = ((bf16[16,8,3712]{2,1,0:T(8,128)(2,1)}), bf16[16,8,3712]{2,1,0:T(8,128)(2,1)S(1)}, u32[]{:S(2)}, u32[]{:S(2)}) async-start(bf16[16,8,3712]{2,1,0:T(8,128)(2,1)} %bitcast.4), calls=%async_computation.1 | async-start | bytes 1900544 | tf_op jit(solution)/shard_map/all_to_all | solution.py:217
  50.0 23.1 %copy-start = (bf16[16,8,3712]{2,1,0:T(8,128)(2,1)}, bf16[16,8,3712]{2,1,0:T(8,128)(2,1)S(1)}, u32[]{:S(2)}) copy-start(bf16[16,8,3712]{2,1,0:T(8,128)(2,1)S(1)} %all-to-all-done.1) | copy-start | bytes 2850820
  51.1 3.4 %copy-start.7 = (bf16[128,3712]{1,0:T(8,128)(2,1)}, bf16[128,3712]{1,0:T(8,128)(2,1)S(1)}, u32[]{:S(2)}) copy-start(bf16[128,3712]{1,0:T(8,128)(2,1)S(1)} %collective-permute-done.refs_0_) | copy-start | bytes 2850820
  51.2 21.9 %collective-permute-start.2 = (bf16[128,3712]{1,0:T(8,128)(2,1)S(1)}, bf16[128,3712]{1,0:T(8,128)(2,1)S(1)}, u32[]{:S(2)}, u32[]{:S(2)}) collective-permute-start(bf16[128,3712]{1,0:T(8,128)(2,1)S(1)} %collective-permute-done.refs_0_), channel_id=1, source_target_pairs={{0,1},{1,2},{2,3},{3,0},{4,5},{5,6},{6,7},{7,4},{8,9},{9,10},{10,1... | collective-permute-start | bytes 2850824 | tf_op jit(solution)/shard_map/ppermute | solution.py:220
  52.8 20.3 %collective-permute-start.3 = (bf16[128,3712]{1,0:T(8,128)(2,1)S(1)}, bf16[128,3712]{1,0:T(8,128)(2,1)}, u32[]{:S(2)}, u32[]{:S(2)}) collective-permute-start(bf16[128,3712]{1,0:T(8,128)(2,1)S(1)} %bitcast.17), channel_id=1, source_target_pairs={{0,3},{1,0},{2,1},{3,2},{4,7},{5,4},{6,5},{7,6},{8,11},{9,8},{10,9... | collective-permute-start | bytes 2850824 | tf_op jit(solution)/shard_map/ppermute | solution.py:220
  73.1 3.3 %copy-start.9 = (bf16[128,3712]{1,0:T(8,128)(2,1)}, bf16[128,3712]{1,0:T(8,128)(2,1)S(1)}, u32[]{:S(2)}) copy-start(bf16[128,3712]{1,0:T(8,128)(2,1)S(1)} %collective-permute-done.2.refs_0_) | copy-start | bytes 2850820
  73.1 24.5 %collective-permute-start.6 = (bf16[128,3712]{1,0:T(8,128)(2,1)S(1)}, bf16[128,3712]{1,0:T(8,128)(2,1)S(1)}, u32[]{:S(2)}, u32[]{:S(2)}) collective-permute-start(bf16[128,3712]{1,0:T(8,128)(2,1)S(1)} %bitcast.18), channel_id=1, source_target_pairs={{0,1},{1,2},{2,3},{3,0},{4,5},{5,6},{6,7},{7,4},{8,9},{9,10},{10,1... | collective-permute-start | bytes 2850824 | tf_op jit(solution)/shard_map/ppermute | solution.py:220
  74.3 23.3 %collective-permute-start.7 = (bf16[128,3712]{1,0:T(8,128)(2,1)}, bf16[128,3712]{1,0:T(8,128)(2,1)}, u32[]{:S(2)}, u32[]{:S(2)}) collective-permute-start(bf16[128,3712]{1,0:T(8,128)(2,1)} %collective-permute-done.3.refs_1_), channel_id=1, source_target_pairs={{0,3},{1,0},{2,1},{3,2},{4,7},{5,4},{6,5},{7,6},{8,11},{9,8},{10,9... | collective-permute-start | bytes 2850824 | tf_op jit(solution)/shard_map/ppermute | solution.py:220
  90.4 32.0 %collective-permute-start.5 = (bf16[128,3584]{1,0:T(8,128)(2,1)}, bf16[128,3584]{1,0:T(8,128)(2,1)}, u32[]{:S(2)}, u32[]{:S(2)}) collective-permute-start(bf16[128,3584]{1,0:T(8,128)(2,1)} %get-tuple-element.46), channel_id=1, source_target_pairs={{0,1},{1,2},{2,3},{3,0},{4,5},{5,6},{6,7},{7,4},{8,9},{9,10},{10,1... | collective-permute-start | bytes 2752520 | tf_op jit(solution)/shard_map/ppermute | solution.py:220
  90.4 32.0 %collective-permute-start.4 = (bf16[128,3584]{1,0:T(8,128)(2,1)}, bf16[128,3584]{1,0:T(8,128)(2,1)}, u32[]{:S(2)}, u32[]{:S(2)}) collective-permute-start(bf16[128,3584]{1,0:T(8,128)(2,1)} %get-tuple-element.45), channel_id=1, source_target_pairs={{0,3},{1,0},{2,1},{3,2},{4,7},{5,4},{6,5},{7,6},{8,11},{9,8},{10,9... | collective-permute-start | bytes 2752520 | tf_op jit(solution)/shard_map/ppermute | solution.py:220
  93.6 21.5 %all-to-all-start.4 = ((bf16[16,8,3712]{2,1,0:T(8,128)(2,1)}), bf16[16,8,3712]{2,1,0:T(8,128)(2,1)S(1)}, u32[]{:S(2)}, u32[]{:S(2)}) async-start(bf16[16,8,3712]{2,1,0:T(8,128)(2,1)} %bitcast.27), calls=%async_computation.4 | async-start | bytes 1900544 | tf_op jit(solution)/shard_map/all_to_all | solution.py:217
  97.6 2.6 %copy-start.8 = (bf16[128,3712]{1,0:T(8,128)(2,1)}, bf16[128,3712]{1,0:T(8,128)(2,1)S(1)}, u32[]{:S(2)}) copy-start(bf16[128,3712]{1,0:T(8,128)(2,1)S(1)} %collective-permute-done.6.refs_0_) | copy-start | bytes 2850820
  97.7 49.4 %collective-permute-start.9 = (bf16[128,3584]{1,0:T(8,128)(2,1)}, bf16[128,3584]{1,0:T(8,128)(2,1)}, u32[]{:S(2)}, u32[]{:S(2)}) collective-permute-start(bf16[128,3584]{1,0:T(8,128)(2,1)} %get-tuple-element.54), channel_id=1, source_target_pairs={{0,1},{1,2},{2,3},{3,0},{4,5},{5,6},{6,7},{7,4},{8,9},{9,10},{10,1... | collective-permute-start | bytes 2752520 | tf_op jit(solution)/shard_map/ppermute | solution.py:220
  114.2 8.1 %copy-start.5 = (bf16[128,3584]{1,0:T(8,128)(2,1)S(1)}, bf16[128,3584]{1,0:T(8,128)(2,1)}, u32[]{:S(2)}) copy-start(bf16[128,3584]{1,0:T(8,128)(2,1)} %shard_map.65) | copy-start | bytes 2752516
  114.2 32.8 %collective-permute-start.8 = (bf16[128,3584]{1,0:T(8,128)(2,1)}, bf16[128,3584]{1,0:T(8,128)(2,1)}, u32[]{:S(2)}, u32[]{:S(2)}) collective-permute-start(bf16[128,3584]{1,0:T(8,128)(2,1)} %get-tuple-element.53), channel_id=1, source_target_pairs={{0,3},{1,0},{2,1},{3,2},{4,7},{5,4},{6,5},{7,6},{8,11},{9,8},{10,9... | collective-permute-start | bytes 2752520 | tf_op jit(solution)/shard_map/ppermute | solution.py:220
  115.1 10.0 %copy-start.1 = (bf16[16,8,3712]{2,1,0:T(8,128)(2,1)}, bf16[16,8,3712]{2,1,0:T(8,128)(2,1)S(1)}, u32[]{:S(2)}) copy-start(bf16[16,8,3712]{2,1,0:T(8,128)(2,1)S(1)} %all-to-all-done.4) | copy-start | bytes 2850820
  115.1 21.4 %all-to-all-start.5 = ((bf16[16,8,3712]{2,1,0:T(8,128)(2,1)}), bf16[16,8,3712]{2,1,0:T(8,128)(2,1)S(1)}, u32[]{:S(2)}, u32[]{:S(2)}) async-start(bf16[16,8,3712]{2,1,0:T(8,128)(2,1)} %bitcast.28), calls=%async_computation.5 | async-start | bytes 1900544 | tf_op jit(solution)/shard_map/all_to_all | solution.py:217
  136.5 7.3 %copy-start.2 = (bf16[16,8,3712]{2,1,0:T(8,128)(2,1)}, bf16[16,8,3712]{2,1,0:T(8,128)(2,1)S(1)}, u32[]{:S(2)}) copy-start(bf16[16,8,3712]{2,1,0:T(8,128)(2,1)S(1)} %all-to-all-done.5) | copy-start | bytes 2850820
  136.5 19.7 %all-to-all-start.2 = ((bf16[16,8,3584]{2,1,0:T(8,128)(2,1)}), bf16[16,8,3584]{2,1,0:T(8,128)(2,1)S(1)}, u32[]{:S(2)}, u32[]{:S(2)}) async-start(bf16[16,8,3584]{2,1,0:T(8,128)(2,1)} %fusion), calls=%async_computation.2 | async-start | bytes 1835008 | tf_op jit(solution)/shard_map/all_to_all | solution.py:217
  143.8 3.3 %copy-start.6 = (bf16[128,3584]{1,0:T(8,128)(2,1)S(1)}, bf16[128,3584]{1,0:T(8,128)(2,1)}, u32[]{:S(2)}) copy-start(bf16[128,3584]{1,0:T(8,128)(2,1)} %shard_map.69) | copy-start | bytes 2752516
  147.0 24.8 %collective-permute-start.10 = (bf16[128,3584]{1,0:T(8,128)(2,1)}, bf16[128,3584]{1,0:T(8,128)(2,1)}, u32[]{:S(2)}, u32[]{:S(2)}) collective-permute-start(bf16[128,3584]{1,0:T(8,128)(2,1)} %shard_map.70), channel_id=1, source_target_pairs={{0,2},{1,3},{2,0},{3,1},{4,6},{5,7},{6,4},{7,5},{8,10},{9,11},{10,... | collective-permute-start | bytes 2752520 | tf_op jit(solution)/shard_map/ppermute | solution.py:220
  156.2 15.6 %copy-start.4 = (bf16[16,8,3584]{2,1,0:T(8,128)(2,1)}, bf16[16,8,3584]{2,1,0:T(8,128)(2,1)S(1)}, u32[]{:S(2)}) copy-start(bf16[16,8,3584]{2,1,0:T(8,128)(2,1)S(1)} %all-to-all-done.2) | copy-start | bytes 2752516

commit v7 on v5

--- a/solution.py
+++ b/solution.py
@@ -64,7 +64,7 @@
         x = tok[:, cols].astype(jnp.float32)
         largest = jnp.max(jnp.abs(x), axis=1, keepdims=True)
         scale = ((largest + 1e-06) / 448.0).astype(jnp.bfloat16).astype(jnp.float32)
-        quantized = (x / scale).astype(jnp.bfloat16).astype(jnp.float32)
+        quantized = (x * (1.0 / scale)).astype(jnp.bfloat16).astype(jnp.float32)
         restored = (quantized * scale).astype(jnp.bfloat16)
         rows = jnp.dot(onehot, restored, preferred_element_type=jnp.float32).astype(jnp.bfloat16)
         out_a[:, cols] = rows[:half]
@@ -87,43 +87,69 @@
     )(tokens, gate_scores.T, expert_ids.T)
 
 
-def expert_kernel(blocks, local_ref, *refs):
-    xs, (wg, wu, wd), outs = refs[:blocks], refs[blocks : blocks + 3], refs[blocks + 3 : -2]
-    rows, acc = refs[-2:]
-    step, steps = pl.program_id(0), pl.num_programs(0)
-    width = rows.shape[1]
+def expert_kernel(blocks, tile, local_ref, *refs):
+    xs, weights, outs = refs[:blocks], refs[blocks : blocks + 3], refs[blocks + 3 : 2 * blocks + 3]
+    rows, acc, done, wg, wu, wd, arrived, left, held = refs[2 * blocks + 3 :]
+    width = acc.shape[1]
     piece = xs[0].shape[0]
 
-    @pl.when(step == 0)
-    def _():
-        for b in range(blocks):
-            rows[b * piece : (b + 1) * piece, :] = xs[b][:, :width]
-
-    x = rows[...]
-    gate = jnp.dot(x, wg[0], preferred_element_type=jnp.float32)
-    up = jnp.dot(x, wu[0], preferred_element_type=jnp.float32)
-    hidden = (gate / (1.0 + jnp.exp(-gate)) * up).astype(jnp.bfloat16)
-    part = jnp.dot(hidden, wd[0], preferred_element_type=jnp.float32)
-
-    @pl.when(step == 0)
-    def _():
-        acc[...] = part
-
-    @pl.when((step > 0) & (step < steps - 1))
-    def _():
-        acc[...] += part
-
-    @pl.when(step == steps - 1)
-    def _():
-        for b in range(blocks):
-            meta = xs[b][:, width : width + LANES]
-            lane = lax.broadcasted_iota(jnp.int32, meta.shape, 1)
-            weight = jnp.where(lane == local_ref[0], meta.astype(jnp.float32), 0.0)
-            weight = jnp.sum(weight, axis=1, keepdims=True)
-            own = slice(b * piece, (b + 1) * piece)
-            outs[b][:, :width] = ((acc[own, :] + part[own, :]) * weight).astype(jnp.bfloat16)
-            if outs[b].shape[1] > width:
-                outs[b][:, width:] = meta
+    def own(b):
+        return pl.ds(b * piece, piece)
+
+    loads = [pltpu.make_async_copy(xs[b], rows.at[own(b)], arrived.at[b]) for b in range(blocks)]
+    for load in loads:
+        load.start()
+
+    def weight_tiles(i):
+        cols = pl.ds(pl.multiple_of(i * tile, tile), tile)
+        places = (0, slice(None), cols), (0, slice(None), cols), (0, cols, slice(None))
+        return [
+            pltpu.make_async_copy(source.at[place], target.at[place[1:]], held.at[which, i])
+            for which, (source, target, place) in enumerate(zip(weights, (wg, wu, wd), places))
+        ]
+
+    steps = wg.shape[1] // tile
+    for i in range(steps):
+        for copy in weight_tiles(i):
+            copy.start()
+    for load in loads:
+        load.wait()
+
+    def step(i, carry):
+        cols = pl.ds(pl.multiple_of(i * tile, tile), tile)
+        for copy in weight_tiles(i):
+            copy.wait()
+        x = rows[:, :width]
+        gate = jnp.dot(x, wg[:, cols], preferred_element_type=jnp.float32)
+        up = jnp.dot(x, wu[:, cols], preferred_element_type=jnp.float32)
+        hidden = (gate / (1.0 + jnp.exp(-gate)) * up).astype(jnp.bfloat16)
+        part = jnp.dot(hidden, wd[cols, :], preferred_element_type=jnp.float32)
+
+        @pl.when(i == 0)
+        def _():
+            acc[...] = part
+
+        @pl.when(i > 0)
+        def _():
+            acc[...] += part
+
+        return carry
+
+    lax.fori_loop(0, steps, step, 0)
+    stores = []
+    for b in range(blocks):
+        meta = rows[own(b), width:]
+        lane = lax.broadcasted_iota(jnp.int32, meta.shape, 1)
+        weight = jnp.where(lane == local_ref[0], meta.astype(jnp.float32), 0.0)
+        weight = jnp.sum(weight, axis=1, keepdims=True)
+        done[own(b), :width] = (acc[own(b), :] * weight).astype(jnp.bfloat16)
+        done[own(b), width:] = meta
+        stores.append(
+            pltpu.make_async_copy(done.at[own(b), pl.ds(0, outs[b].shape[1])], outs[b], left.at[b])
+        )
+        stores[-1].start()
+    for store in stores:
+        store.wait()
 
 
 def experts(xs, marked, local, w_gate, w_up, w_down, tile=256):
@@ -131,25 +157,26 @@
     piece, wide = xs[0].shape
     width, hidden = w_gate.shape[1:]
     wides = [wide if b in marked else width for b in range(blocks)]
+    anywhere = pl.BlockSpec(memory_space=pl.ANY)
     return pl.pallas_call(
-        functools.partial(expert_kernel, blocks),
-        grid=(hidden // tile,),
+        functools.partial(expert_kernel, blocks, tile),
         in_specs=[pl.BlockSpec(memory_space=pltpu.SMEM)]
-        + [pl.BlockSpec((piece, wide), lambda i: (0, 0))] * blocks
-        + [
-            pl.BlockSpec((1, width, tile), lambda i: (0, 0, i)),
-            pl.BlockSpec((1, width, tile), lambda i: (0, 0, i)),
-            pl.BlockSpec((1, tile, width), lambda i: (0, i, 0)),
-        ],
-        out_specs=[pl.BlockSpec((piece, w), lambda i: (0, 0)) for w in wides],
+        + [anywhere] * blocks
+        + [anywhere] * 3,
+        out_specs=[anywhere] * blocks,
         out_shape=[jax.ShapeDtypeStruct((piece, w), jnp.bfloat16) for w in wides],
         scratch_shapes=[
-            pltpu.VMEM((blocks * piece, width), jnp.bfloat16),
+            pltpu.VMEM((blocks * piece, wide), jnp.bfloat16),
             pltpu.VMEM((blocks * piece, width), jnp.float32),
+            pltpu.VMEM((blocks * piece, wide), jnp.bfloat16),
+            pltpu.VMEM((width, hidden), jnp.bfloat16),
+            pltpu.VMEM((width, hidden), jnp.bfloat16),
+            pltpu.VMEM((hidden, width), jnp.bfloat16),
+            pltpu.SemaphoreType.DMA((blocks,)),
+            pltpu.SemaphoreType.DMA((blocks,)),
+            pltpu.SemaphoreType.DMA((3, hidden // tile)),
         ],
-        compiler_params=pltpu.CompilerParams(
-            vmem_limit_bytes=VMEM, dimension_semantics=("arbitrary",)
-        ),
+        compiler_params=pltpu.CompilerParams(vmem_limit_bytes=VMEM),
         cost_estimate=pl.CostEstimate(
             flops=6 * blocks * piece * width * hidden,
             bytes_accessed=6 * width * hidden,
@@ -221,17 +248,22 @@
     below_a, above_a = up(own_a), down(own_a)
     send_b, _ = tie((send_b, own_a))
     own_b = across(send_b)
-    own_pa, own_pb = run([own_a, own_b], ())
+    [own_pa] = run([own_a], ())
     below_a, above_a, next_b, own_pa = tie((below_a, above_a, own_b, own_pa))
     far_a, above_b = up(below_a), down(next_b)
     below_pa, above_pa = run([below_a, above_a], ())
     far_a, above_b, last_b, below_pa = tie((far_a, above_b, next_b, below_pa))
     below_b, far_b = up(last_b), down(above_b)
     far_pa, above_pb = run([far_a, above_b], (0,))
+    below_pa, above_pa, far_pa = tie((below_pa, above_pa, far_pa))
     below_b, far_b, above_pb = tie((below_b, far_b, above_pb))
     below_pb, far_pb = run([below_b, far_b], (1,))
 
-    home_a, home_b = across(far_pa), across(far_pb)
+    home_a = across(far_pa)
+    above_pb, below_pb, far_pb, home_a = tie((above_pb, below_pb, far_pb, home_a))
+    home_b = across(far_pb)
+    last_b, home_b = tie((last_b, home_b))
+    [own_pb] = run([last_b], ())
     far = whole(
         functools.partial(scatter_kernel, locals_),
         jax.ShapeDtypeStruct(tokens.shape, jnp.bfloat16), home_a, home_b,
@@ -240,9 +272,8 @@
 
     final_a = across(add(own_pa, down(below_pa), up(above_pa)))
     final_b = across(add(own_pb, down(below_pb), up(above_pb)))
-    return whole(
-        collect_kernel, jax.ShapeDtypeStruct(tokens.shape, jnp.bfloat16), pick, final_a, final_b, far
-    )
+    near = [pltpu.with_memory_space_constraint(x, pltpu.VMEM) for x in (final_a, final_b, far)]
+    return whole(collect_kernel, jax.ShapeDtypeStruct(tokens.shape, jnp.bfloat16), pick, *near)
 
 
 def solution(mesh):

time: 183 us -> 189 us (1.033)
  Pallas kernels: 66.5 us -> 88 us
  waiting for transfers between devices: 34.4 us -> 14.2 us
  blocking collectives: 39.6 us -> 43.5 us
    pallas_call x4 -> x5, Pallas kernels: 55.9 us -> 78.4 us  [experts(): pl.pallas_call(functools.partial(expert_kernel, blocks, tile), in_specs=[...]
    all_to_all x4, waiting for transfers between devices: 29.1 us -> 11.5 us  [across(): return lax.all_to_all(parts, 'node', 0, 0, tiled=True).reshape(block.shape)]
    all_to_all x2, blocking collectives: 39.6 us -> 43.5 us  [across(): return lax.all_to_all(parts, 'node', 0, 0, tiled=True).reshape(block.shape)]
    ppermute x11, waiting for transfers between devices: 5.3 us -> 2.68 us  [shift(): lax.ppermute(block, 'local', [(i, (i + by) % locals_) for i in range(loca...]
  transfers between devices with their start and end apart: 15 -> 15, of which waited for: 6 -> 5; matrix products, arithmetic and copies ran while one was open for 2% -> 3% of each run, Pallas kernels for 32% -> 43%
where the time goes in v7:
time: 189 us; the launch traced here: 188 us
  Pallas kernels  88 us (47%)
  blocking collectives  43.5 us (23%)
  starting transfers between devices  35.5 us (19%)
  waiting for transfers between devices  14.2 us (8%)
  other arithmetic  5.72 us (3%)
    pallas_call x5, Pallas kernels, experts(): pl.pallas_call(functools.partial(expert_kernel, blocks, tile), in_specs=[...  78.4 us
    all_to_all x2, blocking collectives, across(): return lax.all_to_all(parts, 'node', 0, 0, tiled=True).reshape(block.shape)  43.5 us
    all_to_all x4, starting transfers between devices, across(): return lax.all_to_all(parts, 'node', 0, 0, tiled=True).reshape(block.shape)  19.1 us
    ppermute x11, starting transfers between devices, shift(): lax.ppermute(block, 'local', [(i, (i + by) % locals_) for i in range(loca...  16.4 us
    all_to_all x4, waiting for transfers between devices, across(): return lax.all_to_all(parts, 'node', 0, 0, tiled=True).reshape(block.shape)  11.5 us
    reshape x2, other arithmetic, across(): parts = block.reshape(groups, block.shape[0] // groups, block.shape[1])  5.72 us
    pallas_call x2, Pallas kernels, whole(): pl.pallas_call(kernel, out_shape=shapes, compiler_params=pltpu.CompilerPa...  5.56 us
    pallas_call x1, Pallas kernels, prepare(): pl.pallas_call(functools.partial(prepare_kernel, locals_, groups, per_gro...  4.09 us
  transfers between devices with their start and end apart: 15, of which 5 were waited for; matrix products, arithmetic and copies ran while one was open for 3% of the time, Pallas kernels for 43%

profile of v7, /device:TPU:0, one launch (start us, length us, event | category | flops | bytes accessed | tf_op | source)
XLA Modules:
  0.0 188.2 jit_solution(4962289762830414340)
XLA Ops:
  0.0 4.1 %shard_map.64 = (bf16[128,3712]{1,0:T(8,128)(2,1)}, bf16[128,3712]{1,0:T(8,128)(2,1)}, bf16[256,128]{1,0:T(8,128)(2,1)}) custom-call(bf16[128,3584]{1,0:T(8,128)(2,1)} %tok.1, f32[4,128]{1,0:T(4,128)} %bitcast.30, s32[4,128]{1,0:T(4,128)} %bitcast.31), custom_call_target="tpu_custom_call" | custom-call | flops 1000000000 | bytes 3000000 | tf_op jit(solution)/shard_map/pallas_call | solution.py:78
  4.1 24.1 %all_to_all.30 = bf16[16,8,3712]{2,1,0:T(8,128)(2,1)S(1)} all-to-all(bf16[16,8,3712]{2,1,0:T(8,128)(2,1)} %bitcast.29), channel_id=1, replica_groups=mesh['dp'=2,'node'=16,'local'=4] {'node'}, dimensions={0} | all-to-all | bytes 1900544 | tf_op jit(solution)/shard_map/all_to_all | solution.py:227
  28.2 0.0 copy-start.2
  28.2 1.6 collective-permute-start
  29.7 1.7 collective-permute-start.1
  31.4 3.6 %all-to-all-start.1 = ((bf16[16,8,3712]{2,1,0:T(8,128)(2,1)}), bf16[16,8,3712]{2,1,0:T(8,128)(2,1)S(1)}, u32[]{:S(2)}, u32[]{:S(2)}) async-start(bf16[16,8,3712]{2,1,0:T(8,128)(2,1)} %bitcast.4), calls=%async_computation.1 | async-start | bytes 1900544 | tf_op jit(solution)/shard_map/all_to_all | solution.py:227
  35.0 0.0 copy-done.2
  35.1 13.3 %shard_map.65 = bf16[128,3584]{1,0:T(8,128)(2,1)} custom-call(s32[1]{0:T(128)} %bitcast.6.local_ref, bf16[128,3712]{1,0:T(8,128)(2,1)} %bitcast.25, bf16[1,3584,1024]{2,1,0:T(8,128)(2,1)} %refs_1_.3, bf16[1,3584,1024]{2,1,0:T(8,128)(2,1)} %refs_2_.9, bf16[1,1024,3584]{2,1,0:T(8,128)(2,1)} %refs_3_.9), custom_call_target="tpu_custom_call" | custom-call | flops 2818572288 | bytes 22020096 | tf_op jit(solution)/shard_map/pallas_call | solution.py:161
  48.4 1.6 all-to-all-done.1
  50.0 0.0 copy-start
  50.0 1.1 collective-permute-done.refs_0_
  51.1 0.0 copy-start.5
  51.1 0.1 collective-permute-done.1.refs_1_
  51.2 1.6 collective-permute-start.2
  52.8 1.7 collective-permute-start.3
  54.4 0.0 copy-done.5
  54.4 17.2 %shard_map.66 = (bf16[128,3584]{1,0:T(8,128)(2,1)}, bf16[128,3584]{1,0:T(8,128)(2,1)}) custom-call(s32[1]{0:T(128)} %bitcast.6.local_ref, bf16[128,3712]{1,0:T(8,128)(2,1)} %copy-done.5, bf16[128,3712]{1,0:T(8,128)(2,1)} %collective-permute-done.1.refs_1_, bf16[1,3584,1024]{2,1,0:T(8,128)(2,1)} %refs_1_.3, bf16[1,3584,1024]{2,1,0:T(8,128)(2,1)} %refs_2_.9, ...), custom_call_target="tpu_custom_call" | custom-call | flops 5637144576 | bytes 22020096 | tf_op jit(solution)/shard_map/pallas_call | solution.py:161
  71.6 1.5 collective-permute-done.2.refs_0_
  73.1 0.0 copy-start.7
  73.1 0.0 collective-permute-done.3.refs_1_
  73.1 0.0 copy-done
  73.1 1.3 collective-permute-start.6
  74.3 2.1 %collective-permute-start.7 = (bf16[128,3712]{1,0:T(8,128)(2,1)}, bf16[128,3712]{1,0:T(8,128)(2,1)}, u32[]{:S(2)}, u32[]{:S(2)}) collective-permute-start(bf16[128,3712]{1,0:T(8,128)(2,1)} %collective-permute-done.3.refs_1_), channel_id=1, source_target_pairs={{0,3},{1,0},{2,1},{3,2},{4,7},{5,4},{6,5},{7,6},{8,11},{9,8},{10,9... | collective-permute-start | bytes 2850824 | tf_op jit(solution)/shard_map/ppermute | solution.py:230
  76.4 0.0 copy-done.7
  76.4 17.2 %shard_map.67 = (bf16[128,3712]{1,0:T(8,128)(2,1)}, bf16[128,3584]{1,0:T(8,128)(2,1)}) custom-call(s32[1]{0:T(128)} %bitcast.6.local_ref, bf16[128,3712]{1,0:T(8,128)(2,1)} %copy-done.7, bf16[128,3712]{1,0:T(8,128)(2,1)} %collective-permute-done.3.refs_1_, bf16[1,3584,1024]{2,1,0:T(8,128)(2,1)} %refs_1_.3, bf16[1,3584,1024]{2,1,0:T(8,128)(2,1)} %refs_2_.9, ...), custom_call_target="tpu_custom_call" | custom-call | flops 5637144576 | bytes 22020096 | tf_op jit(solution)/shard_map/pallas_call | solution.py:161
  93.6 0.1 collective-permute-start.5
  93.7 3.2 %collective-permute-start.4 = (bf16[128,3584]{1,0:T(8,128)(2,1)}, bf16[128,3584]{1,0:T(8,128)(2,1)}, u32[]{:S(2)}, u32[]{:S(2)}) collective-permute-start(bf16[128,3584]{1,0:T(8,128)(2,1)} %get-tuple-element.49), channel_id=1, source_target_pairs={{0,3},{1,0},{2,1},{3,2},{4,7},{5,4},{6,5},{7,6},{8,11},{9,8},{10,9... | collective-permute-start | bytes 2752520 | tf_op jit(solution)/shard_map/ppermute | solution.py:230
  96.9 4.7 %all-to-all-start.3 = ((bf16[16,8,3712]{2,1,0:T(8,128)(2,1)}), bf16[16,8,3712]{2,1,0:T(8,128)(2,1)S(1)}, u32[]{:S(2)}, u32[]{:S(2)}) async-start(bf16[16,8,3712]{2,1,0:T(8,128)(2,1)} %bitcast.28), calls=%async_computation.3 | async-start | bytes 1900544 | tf_op jit(solution)/shard_map/all_to_all | solution.py:227
  101.6 0.0 collective-permute-done.6.refs_0_
  101.6 0.0 copy-start.6
  101.6 0.0 collective-permute-done.7.refs_1_
  101.6 0.9 copy-done.6
  102.6 17.3 %shard_map.68 = (bf16[128,3584]{1,0:T(8,128)(2,1)}, bf16[128,3712]{1,0:T(8,128)(2,1)}) custom-call(s32[1]{0:T(128)} %bitcast.6.local_ref, bf16[128,3712]{1,0:T(8,128)(2,1)} %copy-done.6, bf16[128,3712]{1,0:T(8,128)(2,1)} %collective-permute-done.7.refs_1_, bf16[1,3584,1024]{2,1,0:T(8,128)(2,1)} %refs_1_.3, bf16[1,3584,1024]{2,1,0:T(8,128)(2,1)} %refs_2_.9, ...), custom_call_target="tpu_custom_call" | custom-call | flops 5637144576 | bytes 22020096 | tf_op jit(solution)/shard_map/pallas_call | solution.py:161
  119.9 0.0 copy-start.4
  119.9 0.0 all-to-all-done.3
  119.9 0.0 copy-start.1
  119.9 0.1 collective-permute-start.9
  120.0 3.2 %collective-permute-start.8 = (bf16[128,3584]{1,0:T(8,128)(2,1)}, bf16[128,3584]{1,0:T(8,128)(2,1)}, u32[]{:S(2)}, u32[]{:S(2)}) collective-permute-start(bf16[128,3584]{1,0:T(8,128)(2,1)} %get-tuple-element.61), channel_id=1, source_target_pairs={{0,3},{1,0},{2,1},{3,2},{4,7},{5,4},{6,5},{7,6},{8,11},{9,8},{10,9... | collective-permute-start | bytes 2752520 | tf_op jit(solution)/shard_map/ppermute | solution.py:230
  123.2 7.2 %all-to-all-start.4 = ((bf16[16,8,3712]{2,1,0:T(8,128)(2,1)}), bf16[16,8,3712]{2,1,0:T(8,128)(2,1)S(1)}, u32[]{:S(2)}, u32[]{:S(2)}) async-start(bf16[16,8,3712]{2,1,0:T(8,128)(2,1)} %bitcast.27), calls=%async_computation.4 | async-start | bytes 1900544 | tf_op jit(solution)/shard_map/all_to_all | solution.py:227
  130.4 0.0 collective-permute-done.5
  130.4 0.0 collective-permute-done.4
  130.4 0.0 copy-done.4
  130.4 2.7 %fusion = bf16[16,8,3584]{2,1,0:T(8,128)(2,1)} fusion(bf16[128,3584]{1,0:T(8,128)(2,1)} %collective-permute-done.5, bf16[128,3584]{1,0:T(8,128)(2,1)} %collective-permute-done.4, bf16[128,3584]{1,0:T(8,128)(2,1)S(1)} %copy-done.4), kind=kLoop, calls=%fused_computation.2 | loop fusion | flops 2752512 | bytes 3670016 | tf_op jit(solution)/shard_map/reshape | solution.py:226
  133.2 0.0 copy-done.1
  133.2 9.9 %all-to-all-done.4 = bf16[16,8,3712]{2,1,0:T(8,128)(2,1)S(1)} async-done(((bf16[16,8,3712]{2,1,0:T(8,128)(2,1)}), bf16[16,8,3712]{2,1,0:T(8,128)(2,1)S(1)}, u32[]{:S(2)}, u32[]{:S(2)}) %all-to-all-start.4) | async-done | bytes 950304 | tf_op jit(solution)/shard_map/all_to_all | solution.py:227
  143.1 0.0 copy-start.3
  143.1 3.6 %all-to-all-start.2 = ((bf16[16,8,3584]{2,1,0:T(8,128)(2,1)}), bf16[16,8,3584]{2,1,0:T(8,128)(2,1)S(1)}, u32[]{:S(2)}, u32[]{:S(2)}) async-start(bf16[16,8,3584]{2,1,0:T(8,128)(2,1)} %fusion), calls=%async_computation.2 | async-start | bytes 1835008 | tf_op jit(solution)/shard_map/all_to_all | solution.py:227
  146.7 0.0 copy-done.3
  146.8 3.1 %shard_map.70 = bf16[128,3584]{1,0:T(8,128)(2,1)} custom-call(bf16[128,3712]{1,0:T(8,128)(2,1)} %bitcast.22, bf16[128,3712]{1,0:T(8,128)(2,1)} %bitcast.26), custom_call_target="tpu_custom_call" | custom-call | flops 100000000 | bytes 5701632 | tf_op jit(solution)/shard_map/pallas_call | solution.py:190
  149.9 0.0 collective-permute-start.10
  149.9 13.3 %shard_map.69 = bf16[128,3584]{1,0:T(8,128)(2,1)} custom-call(s32[1]{0:T(128)} %bitcast.6.local_ref, bf16[128,3712]{1,0:T(8,128)(2,1)} %bitcast.21, bf16[1,3584,1024]{2,1,0:T(8,128)(2,1)} %refs_1_.3, bf16[1,3584,1024]{2,1,0:T(8,128)(2,1)} %refs_2_.9, bf16[1,1024,3584]{2,1,0:T(8,128)(2,1)} %refs_3_.9), custom_call_target="tpu_custom_call" | custom-call | flops 2818572288 | bytes 22020096 | tf_op jit(solution)/shard_map/pallas_call | solution.py:161
  163.2 0.0 collective-permute-done.9
  163.3 0.0 collective-permute-done.8
  163.3 3.0 %fusion.1 = bf16[16,8,3584]{2,1,0:T(8,128)(2,1)} fusion(bf16[128,3584]{1,0:T(8,128)(2,1)} %collective-permute-done.9, bf16[128,3584]{1,0:T(8,128)(2,1)} %collective-permute-done.8, bf16[128,3584]{1,0:T(8,128)(2,1)} %shard_map.69), kind=kLoop, calls=%fused_computation.3 | loop fusion | flops 2752512 | bytes 3670016 | tf_op jit(solution)/shard_map/reshape | solution.py:226
  166.3 0.0 all-to-all-done.2
  166.3 19.4 %all_to_all.31 = bf16[16,8,3584]{2,1,0:T(8,128)(2,1)S(1)} all-to-all(bf16[16,8,3584]{2,1,0:T(8,128)(2,1)} %fusion.1), channel_id=1, replica_groups=mesh['dp'=2,'node'=16,'local'=4] {'node'}, dimensions={0} | all-to-all | bytes 1835008 | tf_op jit(solution)/shard_map/all_to_all | solution.py:227
  185.7 0.0 collective-permute-done.10.far
  185.7 2.4 %shard_map.71 = bf16[128,3584]{1,0:T(8,128)(2,1)} custom-call(bf16[256,128]{1,0:T(8,128)(2,1)} %get-tuple-element.35.pick, bf16[128,3584]{1,0:T(8,128)(2,1)S(1)} %bitcast.17, bf16[128,3584]{1,0:T(8,128)(2,1)S(1)} %bitcast.18, bf16[128,3584]{1,0:T(8,128)(2,1)S(1)} %collective-permute-done.10.far), custom_call_target="tpu_custom_call" | custom-call | flops 100000000 | bytes 8454144 | tf_op jit(solution)/shard_map/pallas_call | solution.py:190
Async XLA Ops:
  28.2 6.9 %copy-start.2 = (bf16[16,8,3712]{2,1,0:T(8,128)(2,1)}, bf16[16,8,3712]{2,1,0:T(8,128)(2,1)S(1)}, u32[]{:S(2)}) copy-start(bf16[16,8,3712]{2,1,0:T(8,128)(2,1)S(1)} %all_to_all.30) | copy-start | bytes 2850820
  28.2 22.9 %collective-permute-start = (bf16[128,3712]{1,0:T(8,128)(2,1)S(1)}, bf16[128,3712]{1,0:T(8,128)(2,1)S(1)}, u32[]{:S(2)}, u32[]{:S(2)}) collective-permute-start(bf16[128,3712]{1,0:T(8,128)(2,1)S(1)} %bitcast.23), channel_id=1, source_target_pairs={{0,1},{1,2},{2,3},{3,0},{4,5},{5,6},{6,7},{7,4},{8,9},{9,10},{10,1... | collective-permute-start | bytes 2850824 | tf_op jit(solution)/shard_map/ppermute | solution.py:230
  29.7 21.5 %collective-permute-start.1 = (bf16[128,3712]{1,0:T(8,128)(2,1)S(1)}, bf16[128,3712]{1,0:T(8,128)(2,1)}, u32[]{:S(2)}, u32[]{:S(2)}) collective-permute-start(bf16[128,3712]{1,0:T(8,128)(2,1)S(1)} %bitcast.24), channel_id=1, source_target_pairs={{0,3},{1,0},{2,1},{3,2},{4,7},{5,4},{6,5},{7,6},{8,11},{9,8},{10,9... | collective-permute-start | bytes 2850824 | tf_op jit(solution)/shard_map/ppermute | solution.py:230
  31.4 18.6 %all-to-all-start.1 = ((bf16[16,8,3712]{2,1,0:T(8,128)(2,1)}), bf16[16,8,3712]{2,1,0:T(8,128)(2,1)S(1)}, u32[]{:S(2)}, u32[]{:S(2)}) async-start(bf16[16,8,3712]{2,1,0:T(8,128)(2,1)} %bitcast.4), calls=%async_computation.1 | async-start | bytes 1900544 | tf_op jit(solution)/shard_map/all_to_all | solution.py:227
  50.0 23.1 %copy-start = (bf16[16,8,3712]{2,1,0:T(8,128)(2,1)}, bf16[16,8,3712]{2,1,0:T(8,128)(2,1)S(1)}, u32[]{:S(2)}) copy-start(bf16[16,8,3712]{2,1,0:T(8,128)(2,1)S(1)} %all-to-all-done.1) | copy-start | bytes 2850820
  51.1 3.4 %copy-start.5 = (bf16[128,3712]{1,0:T(8,128)(2,1)}, bf16[128,3712]{1,0:T(8,128)(2,1)S(1)}, u32[]{:S(2)}) copy-start(bf16[128,3712]{1,0:T(8,128)(2,1)S(1)} %collective-permute-done.refs_0_) | copy-start | bytes 2850820
  51.2 21.9 %collective-permute-start.2 = (bf16[128,3712]{1,0:T(8,128)(2,1)S(1)}, bf16[128,3712]{1,0:T(8,128)(2,1)S(1)}, u32[]{:S(2)}, u32[]{:S(2)}) collective-permute-start(bf16[128,3712]{1,0:T(8,128)(2,1)S(1)} %collective-permute-done.refs_0_), channel_id=1, source_target_pairs={{0,1},{1,2},{2,3},{3,0},{4,5},{5,6},{6,7},{7,4},{8,9},{9,10},{10,1... | collective-permute-start | bytes 2850824 | tf_op jit(solution)/shard_map/ppermute | solution.py:230
  52.8 20.3 %collective-permute-start.3 = (bf16[128,3712]{1,0:T(8,128)(2,1)S(1)}, bf16[128,3712]{1,0:T(8,128)(2,1)}, u32[]{:S(2)}, u32[]{:S(2)}) collective-permute-start(bf16[128,3712]{1,0:T(8,128)(2,1)S(1)} %bitcast.19), channel_id=1, source_target_pairs={{0,3},{1,0},{2,1},{3,2},{4,7},{5,4},{6,5},{7,6},{8,11},{9,8},{10,9... | collective-permute-start | bytes 2850824 | tf_op jit(solution)/shard_map/ppermute | solution.py:230
  73.1 3.3 %copy-start.7 = (bf16[128,3712]{1,0:T(8,128)(2,1)}, bf16[128,3712]{1,0:T(8,128)(2,1)S(1)}, u32[]{:S(2)}) copy-start(bf16[128,3712]{1,0:T(8,128)(2,1)S(1)} %collective-permute-done.2.refs_0_) | copy-start | bytes 2850820
  73.1 28.5 %collective-permute-start.6 = (bf16[128,3712]{1,0:T(8,128)(2,1)S(1)}, bf16[128,3712]{1,0:T(8,128)(2,1)S(1)}, u32[]{:S(2)}, u32[]{:S(2)}) collective-permute-start(bf16[128,3712]{1,0:T(8,128)(2,1)S(1)} %bitcast.20), channel_id=1, source_target_pairs={{0,1},{1,2},{2,3},{3,0},{4,5},{5,6},{6,7},{7,4},{8,9},{9,10},{10,1... | collective-permute-start | bytes 2850824 | tf_op jit(solution)/shard_map/ppermute | solution.py:230
  74.3 27.3 %collective-permute-start.7 = (bf16[128,3712]{1,0:T(8,128)(2,1)}, bf16[128,3712]{1,0:T(8,128)(2,1)}, u32[]{:S(2)}, u32[]{:S(2)}) collective-permute-start(bf16[128,3712]{1,0:T(8,128)(2,1)} %collective-permute-done.3.refs_1_), channel_id=1, source_target_pairs={{0,3},{1,0},{2,1},{3,2},{4,7},{5,4},{6,5},{7,6},{8,11},{9,8},{10,9... | collective-permute-start | bytes 2850824 | tf_op jit(solution)/shard_map/ppermute | solution.py:230
  93.6 36.8 %collective-permute-start.5 = (bf16[128,3584]{1,0:T(8,128)(2,1)}, bf16[128,3584]{1,0:T(8,128)(2,1)}, u32[]{:S(2)}, u32[]{:S(2)}) collective-permute-start(bf16[128,3584]{1,0:T(8,128)(2,1)} %get-tuple-element.50), channel_id=1, source_target_pairs={{0,1},{1,2},{2,3},{3,0},{4,5},{5,6},{6,7},{7,4},{8,9},{9,10},{10,1... | collective-permute-start | bytes 2752520 | tf_op jit(solution)/shard_map/ppermute | solution.py:230
  93.7 36.7 %collective-permute-start.4 = (bf16[128,3584]{1,0:T(8,128)(2,1)}, bf16[128,3584]{1,0:T(8,128)(2,1)}, u32[]{:S(2)}, u32[]{:S(2)}) collective-permute-start(bf16[128,3584]{1,0:T(8,128)(2,1)} %get-tuple-element.49), channel_id=1, source_target_pairs={{0,3},{1,0},{2,1},{3,2},{4,7},{5,4},{6,5},{7,6},{8,11},{9,8},{10,9... | collective-permute-start | bytes 2752520 | tf_op jit(solution)/shard_map/ppermute | solution.py:230
  96.9 23.0 %all-to-all-start.3 = ((bf16[16,8,3712]{2,1,0:T(8,128)(2,1)}), bf16[16,8,3712]{2,1,0:T(8,128)(2,1)S(1)}, u32[]{:S(2)}, u32[]{:S(2)}) async-start(bf16[16,8,3712]{2,1,0:T(8,128)(2,1)} %bitcast.28), calls=%async_computation.3 | async-start | bytes 1900544 | tf_op jit(solution)/shard_map/all_to_all | solution.py:227
  101.6 0.9 copy-start.6
  119.9 10.6 %copy-start.4 = (bf16[128,3584]{1,0:T(8,128)(2,1)S(1)}, bf16[128,3584]{1,0:T(8,128)(2,1)}, u32[]{:S(2)}) copy-start(bf16[128,3584]{1,0:T(8,128)(2,1)} %shard_map.65) | copy-start | bytes 2752516
  119.9 13.3 %copy-start.1 = (bf16[16,8,3712]{2,1,0:T(8,128)(2,1)}, bf16[16,8,3712]{2,1,0:T(8,128)(2,1)S(1)}, u32[]{:S(2)}) copy-start(bf16[16,8,3712]{2,1,0:T(8,128)(2,1)S(1)} %all-to-all-done.3) | copy-start | bytes 2850820
  119.9 43.3 %collective-permute-start.9 = (bf16[128,3584]{1,0:T(8,128)(2,1)}, bf16[128,3584]{1,0:T(8,128)(2,1)}, u32[]{:S(2)}, u32[]{:S(2)}) collective-permute-start(bf16[128,3584]{1,0:T(8,128)(2,1)} %get-tuple-element.62), channel_id=1, source_target_pairs={{0,1},{1,2},{2,3},{3,0},{4,5},{5,6},{6,7},{7,4},{8,9},{9,10},{10,1... | collective-permute-start | bytes 2752520 | tf_op jit(solution)/shard_map/ppermute | solution.py:230
  120.0 43.3 %collective-permute-start.8 = (bf16[128,3584]{1,0:T(8,128)(2,1)}, bf16[128,3584]{1,0:T(8,128)(2,1)}, u32[]{:S(2)}, u32[]{:S(2)}) collective-permute-start(bf16[128,3584]{1,0:T(8,128)(2,1)} %get-tuple-element.61), channel_id=1, source_target_pairs={{0,3},{1,0},{2,1},{3,2},{4,7},{5,4},{6,5},{7,6},{8,11},{9,8},{10,9... | collective-permute-start | bytes 2752520 | tf_op jit(solution)/shard_map/ppermute | solution.py:230
  123.2 19.9 %all-to-all-start.4 = ((bf16[16,8,3712]{2,1,0:T(8,128)(2,1)}), bf16[16,8,3712]{2,1,0:T(8,128)(2,1)S(1)}, u32[]{:S(2)}, u32[]{:S(2)}) async-start(bf16[16,8,3712]{2,1,0:T(8,128)(2,1)} %bitcast.27), calls=%async_computation.4 | async-start | bytes 1900544 | tf_op jit(solution)/shard_map/all_to_all | solution.py:227
  143.1 3.6 %copy-start.3 = (bf16[16,8,3712]{2,1,0:T(8,128)(2,1)}, bf16[16,8,3712]{2,1,0:T(8,128)(2,1)S(1)}, u32[]{:S(2)}) copy-start(bf16[16,8,3712]{2,1,0:T(8,128)(2,1)S(1)} %all-to-all-done.4) | copy-start | bytes 2850820
  143.1 23.2 %all-to-all-start.2 = ((bf16[16,8,3584]{2,1,0:T(8,128)(2,1)}), bf16[16,8,3584]{2,1,0:T(8,128)(2,1)S(1)}, u32[]{:S(2)}, u32[]{:S(2)}) async-start(bf16[16,8,3584]{2,1,0:T(8,128)(2,1)} %fusion), calls=%async_computation.2 | async-start | bytes 1835008 | tf_op jit(solution)/shard_map/all_to_all | solution.py:227
  149.9 35.8 %collective-permute-start.10 = (bf16[128,3584]{1,0:T(8,128)(2,1)}, bf16[128,3584]{1,0:T(8,128)(2,1)S(1)}, u32[]{:S(2)}, u32[]{:S(2)}) collective-permute-start(bf16[128,3584]{1,0:T(8,128)(2,1)} %shard_map.70), channel_id=1, source_target_pairs={{0,2},{1,3},{2,0},{3,1},{4,6},{5,7},{6,4},{7,5},{8,10},{9,11},{10,... | collective-permute-start | bytes 2752520 | tf_op jit(solution)/shard_map/ppermute | solution.py:230

commit v8 on v5

--- a/solution.py
+++ b/solution.py
@@ -59,13 +59,16 @@
     half = mine.shape[0] // 2
     out_a[:, width : width + LANES] = meta[:half]
     out_b[:, width : width + LANES] = meta[half:]
-    for j in range(width // LANES):
-        cols = slice(j * LANES, (j + 1) * LANES)
-        x = tok[:, cols].astype(jnp.float32)
-        largest = jnp.max(jnp.abs(x), axis=1, keepdims=True)
-        scale = ((largest + 1e-06) / 448.0).astype(jnp.bfloat16).astype(jnp.float32)
-        quantized = (x / scale).astype(jnp.bfloat16).astype(jnp.float32)
-        restored = (quantized * scale).astype(jnp.bfloat16)
+    for start in range(0, width, 4 * LANES):
+        restored = []
+        for place in range(start, start + 4 * LANES, LANES):
+            x = tok[:, place : place + LANES].astype(jnp.float32)
+            largest = jnp.max(jnp.abs(x), axis=1, keepdims=True)
+            scale = ((largest + 1e-06) / 448.0).astype(jnp.bfloat16).astype(jnp.float32)
+            quantized = (x * (1.0 / scale)).astype(jnp.bfloat16).astype(jnp.float32)
+            restored.append((quantized * scale).astype(jnp.bfloat16))
+        cols = slice(start, start + 4 * LANES)
+        restored = jnp.concatenate(restored, axis=1)
         rows = jnp.dot(onehot, restored, preferred_element_type=jnp.float32).astype(jnp.bfloat16)
         out_a[:, cols] = rows[:half]
         out_b[:, cols] = rows[half:]
@@ -221,17 +224,20 @@
     below_a, above_a = up(own_a), down(own_a)
     send_b, _ = tie((send_b, own_a))
     own_b = across(send_b)
-    own_pa, own_pb = run([own_a, own_b], ())
+    [own_pa] = run([own_a], ())
     below_a, above_a, next_b, own_pa = tie((below_a, above_a, own_b, own_pa))
     far_a, above_b = up(below_a), down(next_b)
-    below_pa, above_pa = run([below_a, above_a], ())
+    below_pa, above_pa, own_pb = run([below_a, above_a, next_b], ())
     far_a, above_b, last_b, below_pa = tie((far_a, above_b, next_b, below_pa))
     below_b, far_b = up(last_b), down(above_b)
     far_pa, above_pb = run([far_a, above_b], (0,))
+    below_pa, above_pa, far_pa = tie((below_pa, above_pa, far_pa))
     below_b, far_b, above_pb = tie((below_b, far_b, above_pb))
     below_pb, far_pb = run([below_b, far_b], (1,))
 
-    home_a, home_b = across(far_pa), across(far_pb)
+    home_a = across(far_pa)
+    above_pb, below_pb, far_pb, home_a = tie((above_pb, below_pb, far_pb, home_a))
+    home_b = across(far_pb)
     far = whole(
         functools.partial(scatter_kernel, locals_),
         jax.ShapeDtypeStruct(tokens.shape, jnp.bfloat16), home_a, home_b,
@@ -240,9 +246,8 @@
 
     final_a = across(add(own_pa, down(below_pa), up(above_pa)))
     final_b = across(add(own_pb, down(below_pb), up(above_pb)))
-    return whole(
-        collect_kernel, jax.ShapeDtypeStruct(tokens.shape, jnp.bfloat16), pick, final_a, final_b, far
-    )
+    near = [pltpu.with_memory_space_constraint(x, pltpu.VMEM) for x in (final_a, final_b, far)]
+    return whole(collect_kernel, jax.ShapeDtypeStruct(tokens.shape, jnp.bfloat16), pick, *near)
 
 
 def solution(mesh):

time: 183 us -> 172 us (0.940)
  waiting for transfers between devices: 34.4 us -> 23.3 us
    all_to_all x4, waiting for transfers between devices: 29.1 us -> 19.9 us  [across(): return lax.all_to_all(parts, 'node', 0, 0, tiled=True).reshape(block.shape)]
    ppermute x11, waiting for transfers between devices: 5.3 us -> 3.39 us  [shift(): lax.ppermute(block, 'local', [(i, (i + by) % locals_) for i in range(loca...]
  transfers between devices with their start and end apart: 15 -> 15, of which waited for: 6 -> 6; matrix products, arithmetic and copies ran while one was open for 2% -> 3% of each run, Pallas kernels for 32% -> 35%
where the time goes in v8:
time: 172 us; the launch traced here: 171 us
  Pallas kernels  66.1 us (38%)
  blocking collectives  39.9 us (23%)
  starting transfers between devices  34.2 us (20%)
  waiting for transfers between devices  23.3 us (14%)
  other arithmetic  5.69 us (3%)
  local copies, waits for them, and re-layouts  1.92 us (1%)
    pallas_call x4, Pallas kernels, experts(): pl.pallas_call(functools.partial(expert_kernel, blocks), grid=(hidden //...  56.5 us
    all_to_all x2, blocking collectives, across(): return lax.all_to_all(parts, 'node', 0, 0, tiled=True).reshape(block.shape)  39.9 us
    all_to_all x4, waiting for transfers between devices, across(): return lax.all_to_all(parts, 'node', 0, 0, tiled=True).reshape(block.shape)  19.9 us
    all_to_all x4, starting transfers between devices, across(): return lax.all_to_all(parts, 'node', 0, 0, tiled=True).reshape(block.shape)  17.9 us
    ppermute x11, starting transfers between devices, shift(): lax.ppermute(block, 'local', [(i, (i + by) % locals_) for i in range(loca...  16.3 us
    reshape x2, other arithmetic, across(): parts = block.reshape(groups, block.shape[0] // groups, block.shape[1])  5.69 us
    pallas_call x2, Pallas kernels, whole(): pl.pallas_call(kernel, out_shape=shapes, compiler_params=pltpu.CompilerPa...  5.57 us
    pallas_call x1, Pallas kernels, prepare(): pl.pallas_call(functools.partial(prepare_kernel, locals_, groups, per_gro...  3.98 us
  transfers between devices with their start and end apart: 15, of which 6 were waited for; matrix products, arithmetic and copies ran while one was open for 3% of the time, Pallas kernels for 35%

profile of v8, /device:TPU:0, one launch (start us, length us, event | category | flops | bytes accessed | tf_op | source)
XLA Modules:
  0.0 171.2 jit_solution(5412668405271940560)
XLA Ops:
  0.0 4.0 %shard_map.64 = (bf16[128,3712]{1,0:T(8,128)(2,1)}, bf16[128,3712]{1,0:T(8,128)(2,1)}, bf16[256,128]{1,0:T(8,128)(2,1)}) custom-call(bf16[128,3584]{1,0:T(8,128)(2,1)} %tok.1, f32[4,128]{1,0:T(4,128)} %bitcast.30, s32[4,128]{1,0:T(4,128)} %bitcast.31), custom_call_target="tpu_custom_call" | custom-call | flops 1000000000 | bytes 3000000 | tf_op jit(solution)/shard_map/pallas_call | solution.py:81
  4.0 24.1 %all_to_all.30 = bf16[16,8,3712]{2,1,0:T(8,128)(2,1)S(1)} all-to-all(bf16[16,8,3712]{2,1,0:T(8,128)(2,1)} %bitcast.29), channel_id=1, replica_groups=mesh['dp'=2,'node'=16,'local'=4] {'node'}, dimensions={0} | all-to-all | bytes 1900544 | tf_op jit(solution)/shard_map/all_to_all | solution.py:203
  28.0 0.0 copy-start.1
  28.0 1.6 collective-permute-start
  29.6 1.7 collective-permute-start.1
  31.3 3.6 %all-to-all-start.1 = ((bf16[16,8,3712]{2,1,0:T(8,128)(2,1)}), bf16[16,8,3712]{2,1,0:T(8,128)(2,1)S(1)}, u32[]{:S(2)}, u32[]{:S(2)}) async-start(bf16[16,8,3712]{2,1,0:T(8,128)(2,1)} %bitcast.4), calls=%async_computation.1 | async-start | bytes 1900544 | tf_op jit(solution)/shard_map/all_to_all | solution.py:203
  34.9 0.0 copy-done.1
  34.9 11.3 %shard_map.65 = bf16[128,3584]{1,0:T(8,128)(2,1)} custom-call(s32[1]{0:T(128)} %bitcast.6.local_ref, bf16[128,3712]{1,0:T(8,128)(2,1)} %bitcast.22, bf16[1,3584,1024]{2,1,0:T(8,128)(2,1)} %refs_2_.5, bf16[1,3584,1024]{2,1,0:T(8,128)(2,1)} %refs_3_.7, bf16[1,1024,3584]{2,1,0:T(8,128)(2,1)} %refs_4_.5), custom_call_target="tpu_custom_call" | custom-call | flops 2818572288 | bytes 22020096 | tf_op jit(solution)/shard_map/pallas_call | solution.py:137
  46.2 3.7 %all-to-all-done.1 = bf16[16,8,3712]{2,1,0:T(8,128)(2,1)S(1)} async-done(((bf16[16,8,3712]{2,1,0:T(8,128)(2,1)}), bf16[16,8,3712]{2,1,0:T(8,128)(2,1)S(1)}, u32[]{:S(2)}, u32[]{:S(2)}) %all-to-all-start.1) | async-done | bytes 950304 | tf_op jit(solution)/shard_map/all_to_all | solution.py:203
  49.9 0.0 copy-start.4
  49.9 1.2 collective-permute-done.refs_0_
  51.1 0.0 collective-permute-done.1.refs_1_
  51.1 0.0 copy-start.8
  51.1 0.9 copy-done.8
  52.0 1.5 collective-permute-start.2
  53.5 1.7 %collective-permute-start.3 = (bf16[128,3712]{1,0:T(8,128)(2,1)S(1)}, bf16[128,3712]{1,0:T(8,128)(2,1)S(1)}, u32[]{:S(2)}, u32[]{:S(2)}) collective-permute-start(bf16[128,3712]{1,0:T(8,128)(2,1)S(1)} %bitcast.24), channel_id=1, source_target_pairs={{0,3},{1,0},{2,1},{3,2},{4,7},{5,4},{6,5},{7,6},{8,11},{9,8},{10,9... | collective-permute-start | bytes 2850824 | tf_op jit(solution)/shard_map/ppermute | solution.py:206
  55.2 0.0 copy-done.4
  55.2 17.3 %shard_map.66 = (bf16[128,3584]{1,0:T(8,128)(2,1)}, bf16[128,3584]{1,0:T(8,128)(2,1)}, bf16[128,3584]{1,0:T(8,128)(2,1)}) custom-call(s32[1]{0:T(128)} %bitcast.6.local_ref, bf16[128,3712]{1,0:T(8,128)(2,1)} %collective-permute-done.refs_0_, bf16[128,3712]{1,0:T(8,128)(2,1)} %copy-done.8, bf16[128,3712]{1,0:T(8,128)(2,1)} %bitcast.25, ...), custom_call_target="tpu_custom_call" | custom-call | flops 8455716864 | bytes 22020096 | tf_op jit(solution)/shard_map/pallas_call | solution.py:137
  72.6 1.7 collective-permute-done.2.refs_0_
  74.2 0.0 copy-start.7
  74.2 0.0 collective-permute-done.3.refs_1_
  74.2 0.0 copy-start.5
  74.2 0.8 collective-permute-start.6
  75.1 2.5 %collective-permute-start.7 = (bf16[128,3712]{1,0:T(8,128)(2,1)S(1)}, bf16[128,3712]{1,0:T(8,128)(2,1)}, u32[]{:S(2)}, u32[]{:S(2)}) collective-permute-start(bf16[128,3712]{1,0:T(8,128)(2,1)S(1)} %collective-permute-done.3.refs_1_), channel_id=1, source_target_pairs={{0,3},{1,0},{2,1},{3,2},{4,7},{5,4},{6,5},{7,6},{8,11},{9,8},{10,9... | collective-permute-start | bytes 2850824 | tf_op jit(solution)/shard_map/ppermute | solution.py:206
  77.5 0.0 copy-done.7
  77.5 0.0 copy-done.5
  77.5 14.0 %shard_map.67 = (bf16[128,3712]{1,0:T(8,128)(2,1)}, bf16[128,3584]{1,0:T(8,128)(2,1)}) custom-call(s32[1]{0:T(128)} %bitcast.6.local_ref, bf16[128,3712]{1,0:T(8,128)(2,1)} %copy-done.7, bf16[128,3712]{1,0:T(8,128)(2,1)} %copy-done.5, bf16[1,3584,1024]{2,1,0:T(8,128)(2,1)} %refs_2_.5, bf16[1,3584,1024]{2,1,0:T(8,128)(2,1)} %refs_3_.7, ...), custom_call_target="tpu_custom_call" | custom-call | flops 5637144576 | bytes 22020096 | tf_op jit(solution)/shard_map/pallas_call | solution.py:137
  91.5 0.0 collective-permute-start.5
  91.5 3.2 %collective-permute-start.4 = (bf16[128,3584]{1,0:T(8,128)(2,1)}, bf16[128,3584]{1,0:T(8,128)(2,1)}, u32[]{:S(2)}, u32[]{:S(2)}) collective-permute-start(bf16[128,3584]{1,0:T(8,128)(2,1)} %get-tuple-element.48), channel_id=1, source_target_pairs={{0,3},{1,0},{2,1},{3,2},{4,7},{5,4},{6,5},{7,6},{8,11},{9,8},{10,9... | collective-permute-start | bytes 2752520 | tf_op jit(solution)/shard_map/ppermute | solution.py:206
  94.7 4.0 %all-to-all-start.3 = ((bf16[16,8,3712]{2,1,0:T(8,128)(2,1)}), bf16[16,8,3712]{2,1,0:T(8,128)(2,1)S(1)}, u32[]{:S(2)}, u32[]{:S(2)}) async-start(bf16[16,8,3712]{2,1,0:T(8,128)(2,1)} %bitcast.28), calls=%async_computation.3 | async-start | bytes 1900544 | tf_op jit(solution)/shard_map/all_to_all | solution.py:203
  98.7 0.5 collective-permute-done.6.refs_0_
  99.2 0.0 copy-start.6
  99.2 0.0 collective-permute-done.7.refs_1_
  99.2 1.0 copy-done.6
  100.2 13.9 %shard_map.68 = (bf16[128,3584]{1,0:T(8,128)(2,1)}, bf16[128,3712]{1,0:T(8,128)(2,1)}) custom-call(s32[1]{0:T(128)} %bitcast.6.local_ref, bf16[128,3712]{1,0:T(8,128)(2,1)} %copy-done.6, bf16[128,3712]{1,0:T(8,128)(2,1)} %collective-permute-done.7.refs_1_, bf16[1,3584,1024]{2,1,0:T(8,128)(2,1)} %refs_2_.5, bf16[1,3584,1024]{2,1,0:T(8,128)(2,1)} %refs_3_.7, ...), custom_call_target="tpu_custom_call" | custom-call | flops 5637144576 | bytes 22020096 | tf_op jit(solution)/shard_map/pallas_call | solution.py:137
  114.1 0.0 copy-start.3
  114.1 0.0 all-to-all-done.3
  114.1 0.0 copy-start
  114.1 0.5 collective-permute-start.9
  114.6 2.8 %collective-permute-start.8 = (bf16[128,3584]{1,0:T(8,128)(2,1)}, bf16[128,3584]{1,0:T(8,128)(2,1)}, u32[]{:S(2)}, u32[]{:S(2)}) collective-permute-start(bf16[128,3584]{1,0:T(8,128)(2,1)} %get-tuple-element.59), channel_id=1, source_target_pairs={{0,3},{1,0},{2,1},{3,2},{4,7},{5,4},{6,5},{7,6},{8,11},{9,8},{10,9... | collective-permute-start | bytes 2752520 | tf_op jit(solution)/shard_map/ppermute | solution.py:206
  117.5 6.7 %all-to-all-start.5 = ((bf16[16,8,3712]{2,1,0:T(8,128)(2,1)}), bf16[16,8,3712]{2,1,0:T(8,128)(2,1)S(1)}, u32[]{:S(2)}, u32[]{:S(2)}) async-start(bf16[16,8,3712]{2,1,0:T(8,128)(2,1)} %bitcast.27), calls=%async_computation.5 | async-start | bytes 1900544 | tf_op jit(solution)/shard_map/all_to_all | solution.py:203
  124.1 0.0 collective-permute-done.5
  124.2 0.0 collective-permute-done.4
  124.2 0.0 copy-done.3
  124.2 2.7 %fusion = bf16[16,8,3584]{2,1,0:T(8,128)(2,1)} fusion(bf16[128,3584]{1,0:T(8,128)(2,1)} %collective-permute-done.5, bf16[128,3584]{1,0:T(8,128)(2,1)} %collective-permute-done.4, bf16[128,3584]{1,0:T(8,128)(2,1)S(1)} %copy-done.3), kind=kLoop, calls=%fused_computation.2 | loop fusion | flops 2752512 | bytes 3670016 | tf_op jit(solution)/shard_map/reshape | solution.py:202
  126.9 0.0 copy-done
  126.9 9.9 %all-to-all-done.5 = bf16[16,8,3712]{2,1,0:T(8,128)(2,1)S(1)} async-done(((bf16[16,8,3712]{2,1,0:T(8,128)(2,1)}), bf16[16,8,3712]{2,1,0:T(8,128)(2,1)S(1)}, u32[]{:S(2)}, u32[]{:S(2)}) %all-to-all-start.5) | async-done | bytes 950304 | tf_op jit(solution)/shard_map/all_to_all | solution.py:203
  136.8 0.0 copy-start.2
  136.8 3.6 %all-to-all-start.2 = ((bf16[16,8,3584]{2,1,0:T(8,128)(2,1)}), bf16[16,8,3584]{2,1,0:T(8,128)(2,1)S(1)}, u32[]{:S(2)}, u32[]{:S(2)}) async-start(bf16[16,8,3584]{2,1,0:T(8,128)(2,1)} %fusion), calls=%async_computation.2 | async-start | bytes 1835008 | tf_op jit(solution)/shard_map/all_to_all | solution.py:203
  140.5 0.0 copy-done.2
  140.5 3.1 %shard_map.69 = bf16[128,3584]{1,0:T(8,128)(2,1)} custom-call(bf16[128,3712]{1,0:T(8,128)(2,1)} %bitcast.19, bf16[128,3712]{1,0:T(8,128)(2,1)} %bitcast.23), custom_call_target="tpu_custom_call" | custom-call | flops 100000000 | bytes 5701632 | tf_op jit(solution)/shard_map/pallas_call | solution.py:166
  143.6 0.0 collective-permute-start.10
  143.6 0.0 collective-permute-done.9
  143.6 0.0 collective-permute-done.8
  143.6 3.0 %fusion.1 = bf16[16,8,3584]{2,1,0:T(8,128)(2,1)} fusion(bf16[128,3584]{1,0:T(8,128)(2,1)} %collective-permute-done.9, bf16[128,3584]{1,0:T(8,128)(2,1)} %collective-permute-done.8, bf16[128,3584]{1,0:T(8,128)(2,1)} %get-tuple-element.50), kind=kLoop, calls=%fused_computation.3 | loop fusion | flops 2752512 | bytes 3670016 | tf_op jit(solution)/shard_map/reshape | solution.py:202
  146.6 6.3 %all-to-all-done.2 = bf16[16,8,3584]{2,1,0:T(8,128)(2,1)S(1)} async-done(((bf16[16,8,3584]{2,1,0:T(8,128)(2,1)}), bf16[16,8,3584]{2,1,0:T(8,128)(2,1)S(1)}, u32[]{:S(2)}, u32[]{:S(2)}) %all-to-all-start.2) | async-done | bytes 917536 | tf_op jit(solution)/shard_map/all_to_all | solution.py:203
  152.9 15.9 %all_to_all.31 = bf16[16,8,3584]{2,1,0:T(8,128)(2,1)S(1)} all-to-all(bf16[16,8,3584]{2,1,0:T(8,128)(2,1)} %fusion.1), channel_id=1, replica_groups=mesh['dp'=2,'node'=16,'local'=4] {'node'}, dimensions={0} | all-to-all | bytes 1835008 | tf_op jit(solution)/shard_map/all_to_all | solution.py:203
  168.8 0.0 collective-permute-done.10.far
  168.8 2.4 %shard_map.70 = bf16[128,3584]{1,0:T(8,128)(2,1)} custom-call(bf16[256,128]{1,0:T(8,128)(2,1)} %get-tuple-element.34.pick, bf16[128,3584]{1,0:T(8,128)(2,1)S(1)} %bitcast.17, bf16[128,3584]{1,0:T(8,128)(2,1)S(1)} %bitcast.18, bf16[128,3584]{1,0:T(8,128)(2,1)S(1)} %collective-permute-done.10.far), custom_call_target="tpu_custom_call" | custom-call | flops 100000000 | bytes 8454144 | tf_op jit(solution)/shard_map/pallas_call | solution.py:166
Async XLA Ops:
  28.0 6.9 %copy-start.1 = (bf16[16,8,3712]{2,1,0:T(8,128)(2,1)}, bf16[16,8,3712]{2,1,0:T(8,128)(2,1)S(1)}, u32[]{:S(2)}) copy-start(bf16[16,8,3712]{2,1,0:T(8,128)(2,1)S(1)} %all_to_all.30) | copy-start | bytes 2850820
  28.0 23.0 %collective-permute-start = (bf16[128,3712]{1,0:T(8,128)(2,1)S(1)}, bf16[128,3712]{1,0:T(8,128)(2,1)}, u32[]{:S(2)}, u32[]{:S(2)}) collective-permute-start(bf16[128,3712]{1,0:T(8,128)(2,1)S(1)} %bitcast.20), channel_id=1, source_target_pairs={{0,1},{1,2},{2,3},{3,0},{4,5},{5,6},{6,7},{7,4},{8,9},{9,10},{10,1... | collective-permute-start | bytes 2850824 | tf_op jit(solution)/shard_map/ppermute | solution.py:206
  29.6 21.5 %collective-permute-start.1 = (bf16[128,3712]{1,0:T(8,128)(2,1)S(1)}, bf16[128,3712]{1,0:T(8,128)(2,1)S(1)}, u32[]{:S(2)}, u32[]{:S(2)}) collective-permute-start(bf16[128,3712]{1,0:T(8,128)(2,1)S(1)} %bitcast.21), channel_id=1, source_target_pairs={{0,3},{1,0},{2,1},{3,2},{4,7},{5,4},{6,5},{7,6},{8,11},{9,8},{10,9... | collective-permute-start | bytes 2850824 | tf_op jit(solution)/shard_map/ppermute | solution.py:206
  31.3 18.6 %all-to-all-start.1 = ((bf16[16,8,3712]{2,1,0:T(8,128)(2,1)}), bf16[16,8,3712]{2,1,0:T(8,128)(2,1)S(1)}, u32[]{:S(2)}, u32[]{:S(2)}) async-start(bf16[16,8,3712]{2,1,0:T(8,128)(2,1)} %bitcast.4), calls=%async_computation.1 | async-start | bytes 1900544 | tf_op jit(solution)/shard_map/all_to_all | solution.py:203
  49.9 5.4 %copy-start.4 = (bf16[16,8,3712]{2,1,0:T(8,128)(2,1)}, bf16[16,8,3712]{2,1,0:T(8,128)(2,1)S(1)}, u32[]{:S(2)}) copy-start(bf16[16,8,3712]{2,1,0:T(8,128)(2,1)S(1)} %all-to-all-done.1) | copy-start | bytes 2850820
  51.1 0.9 copy-start.8
  52.0 22.2 %collective-permute-start.2 = (bf16[128,3712]{1,0:T(8,128)(2,1)}, bf16[128,3712]{1,0:T(8,128)(2,1)S(1)}, u32[]{:S(2)}, u32[]{:S(2)}) collective-permute-start(bf16[128,3712]{1,0:T(8,128)(2,1)} %collective-permute-done.refs_0_), channel_id=1, source_target_pairs={{0,1},{1,2},{2,3},{3,0},{4,5},{5,6},{6,7},{7,4},{8,9},{9,10},{10,1... | collective-permute-start | bytes 2850824 | tf_op jit(solution)/shard_map/ppermute | solution.py:206
  53.5 20.7 %collective-permute-start.3 = (bf16[128,3712]{1,0:T(8,128)(2,1)S(1)}, bf16[128,3712]{1,0:T(8,128)(2,1)S(1)}, u32[]{:S(2)}, u32[]{:S(2)}) collective-permute-start(bf16[128,3712]{1,0:T(8,128)(2,1)S(1)} %bitcast.24), channel_id=1, source_target_pairs={{0,3},{1,0},{2,1},{3,2},{4,7},{5,4},{6,5},{7,6},{8,11},{9,8},{10,9... | collective-permute-start | bytes 2850824 | tf_op jit(solution)/shard_map/ppermute | solution.py:206
  74.2 3.3 %copy-start.7 = (bf16[128,3712]{1,0:T(8,128)(2,1)}, bf16[128,3712]{1,0:T(8,128)(2,1)S(1)}, u32[]{:S(2)}) copy-start(bf16[128,3712]{1,0:T(8,128)(2,1)S(1)} %collective-permute-done.2.refs_0_) | copy-start | bytes 2850820
  74.2 3.3 %copy-start.5 = (bf16[128,3712]{1,0:T(8,128)(2,1)}, bf16[128,3712]{1,0:T(8,128)(2,1)S(1)}, u32[]{:S(2)}) copy-start(bf16[128,3712]{1,0:T(8,128)(2,1)S(1)} %collective-permute-done.3.refs_1_) | copy-start | bytes 2850820
  74.2 25.0 %collective-permute-start.6 = (bf16[128,3712]{1,0:T(8,128)(2,1)}, bf16[128,3712]{1,0:T(8,128)(2,1)S(1)}, u32[]{:S(2)}, u32[]{:S(2)}) collective-permute-start(bf16[128,3712]{1,0:T(8,128)(2,1)} %bitcast.26), channel_id=1, source_target_pairs={{0,1},{1,2},{2,3},{3,0},{4,5},{5,6},{6,7},{7,4},{8,9},{9,10},{10,1... | collective-permute-start | bytes 2850824 | tf_op jit(solution)/shard_map/ppermute | solution.py:206
  75.1 24.2 %collective-permute-start.7 = (bf16[128,3712]{1,0:T(8,128)(2,1)S(1)}, bf16[128,3712]{1,0:T(8,128)(2,1)}, u32[]{:S(2)}, u32[]{:S(2)}) collective-permute-start(bf16[128,3712]{1,0:T(8,128)(2,1)S(1)} %collective-permute-done.3.refs_1_), channel_id=1, source_target_pairs={{0,3},{1,0},{2,1},{3,2},{4,7},{5,4},{6,5},{7,6},{8,11},{9,8},{10,9... | collective-permute-start | bytes 2850824 | tf_op jit(solution)/shard_map/ppermute | solution.py:206
  91.5 32.7 %collective-permute-start.5 = (bf16[128,3584]{1,0:T(8,128)(2,1)}, bf16[128,3584]{1,0:T(8,128)(2,1)}, u32[]{:S(2)}, u32[]{:S(2)}) collective-permute-start(bf16[128,3584]{1,0:T(8,128)(2,1)} %get-tuple-element.49), channel_id=1, source_target_pairs={{0,1},{1,2},{2,3},{3,0},{4,5},{5,6},{6,7},{7,4},{8,9},{9,10},{10,1... | collective-permute-start | bytes 2752520 | tf_op jit(solution)/shard_map/ppermute | solution.py:206
  91.5 32.7 %collective-permute-start.4 = (bf16[128,3584]{1,0:T(8,128)(2,1)}, bf16[128,3584]{1,0:T(8,128)(2,1)}, u32[]{:S(2)}, u32[]{:S(2)}) collective-permute-start(bf16[128,3584]{1,0:T(8,128)(2,1)} %get-tuple-element.48), channel_id=1, source_target_pairs={{0,3},{1,0},{2,1},{3,2},{4,7},{5,4},{6,5},{7,6},{8,11},{9,8},{10,9... | collective-permute-start | bytes 2752520 | tf_op jit(solution)/shard_map/ppermute | solution.py:206
  94.7 19.4 %all-to-all-start.3 = ((bf16[16,8,3712]{2,1,0:T(8,128)(2,1)}), bf16[16,8,3712]{2,1,0:T(8,128)(2,1)S(1)}, u32[]{:S(2)}, u32[]{:S(2)}) async-start(bf16[16,8,3712]{2,1,0:T(8,128)(2,1)} %bitcast.28), calls=%async_computation.3 | async-start | bytes 1900544 | tf_op jit(solution)/shard_map/all_to_all | solution.py:203
  99.2 1.0 copy-start.6
  114.1 10.0 %copy-start.3 = (bf16[128,3584]{1,0:T(8,128)(2,1)S(1)}, bf16[128,3584]{1,0:T(8,128)(2,1)}, u32[]{:S(2)}) copy-start(bf16[128,3584]{1,0:T(8,128)(2,1)} %shard_map.65) | copy-start | bytes 2752516
  114.1 12.8 %copy-start = (bf16[16,8,3712]{2,1,0:T(8,128)(2,1)}, bf16[16,8,3712]{2,1,0:T(8,128)(2,1)S(1)}, u32[]{:S(2)}) copy-start(bf16[16,8,3712]{2,1,0:T(8,128)(2,1)S(1)} %all-to-all-done.3) | copy-start | bytes 2850820
  114.1 29.5 %collective-permute-start.9 = (bf16[128,3584]{1,0:T(8,128)(2,1)}, bf16[128,3584]{1,0:T(8,128)(2,1)}, u32[]{:S(2)}, u32[]{:S(2)}) collective-permute-start(bf16[128,3584]{1,0:T(8,128)(2,1)} %get-tuple-element.60), channel_id=1, source_target_pairs={{0,1},{1,2},{2,3},{3,0},{4,5},{5,6},{6,7},{7,4},{8,9},{9,10},{10,1... | collective-permute-start | bytes 2752520 | tf_op jit(solution)/shard_map/ppermute | solution.py:206
  114.6 29.0 %collective-permute-start.8 = (bf16[128,3584]{1,0:T(8,128)(2,1)}, bf16[128,3584]{1,0:T(8,128)(2,1)}, u32[]{:S(2)}, u32[]{:S(2)}) collective-permute-start(bf16[128,3584]{1,0:T(8,128)(2,1)} %get-tuple-element.59), channel_id=1, source_target_pairs={{0,3},{1,0},{2,1},{3,2},{4,7},{5,4},{6,5},{7,6},{8,11},{9,8},{10,9... | collective-permute-start | bytes 2752520 | tf_op jit(solution)/shard_map/ppermute | solution.py:206
  117.5 19.4 %all-to-all-start.5 = ((bf16[16,8,3712]{2,1,0:T(8,128)(2,1)}), bf16[16,8,3712]{2,1,0:T(8,128)(2,1)S(1)}, u32[]{:S(2)}, u32[]{:S(2)}) async-start(bf16[16,8,3712]{2,1,0:T(8,128)(2,1)} %bitcast.27), calls=%async_computation.5 | async-start | bytes 1900544 | tf_op jit(solution)/shard_map/all_to_all | solution.py:203
  136.8 3.6 %copy-start.2 = (bf16[16,8,3712]{2,1,0:T(8,128)(2,1)}, bf16[16,8,3712]{2,1,0:T(8,128)(2,1)S(1)}, u32[]{:S(2)}) copy-start(bf16[16,8,3712]{2,1,0:T(8,128)(2,1)S(1)} %all-to-all-done.5) | copy-start | bytes 2850820
  136.8 16.1 %all-to-all-start.2 = ((bf16[16,8,3584]{2,1,0:T(8,128)(2,1)}), bf16[16,8,3584]{2,1,0:T(8,128)(2,1)S(1)}, u32[]{:S(2)}, u32[]{:S(2)}) async-start(bf16[16,8,3584]{2,1,0:T(8,128)(2,1)} %fusion), calls=%async_computation.2 | async-start | bytes 1835008 | tf_op jit(solution)/shard_map/all_to_all | solution.py:203
  143.6 25.2 %collective-permute-start.10 = (bf16[128,3584]{1,0:T(8,128)(2,1)}, bf16[128,3584]{1,0:T(8,128)(2,1)S(1)}, u32[]{:S(2)}, u32[]{:S(2)}) collective-permute-start(bf16[128,3584]{1,0:T(8,128)(2,1)} %shard_map.69), channel_id=1, source_target_pairs={{0,2},{1,3},{2,0},{3,1},{4,6},{5,7},{6,4},{7,5},{8,10},{9,11},{10,... | collective-permute-start | bytes 2752520 | tf_op jit(solution)/shard_map/ppermute | solution.py:206

commit v9 on v8

v9 whole, which is shorter than its diff:
```python
import functools

import jax
import jax.numpy as jnp
from jax import lax
from jax.experimental import pallas as pl
from jax.experimental.pallas import tpu as pltpu
from jax.sharding import PartitionSpec as P

LANES = 128
PIECE = 128
VMEM = 60 * 1024 * 1024
EXPERT_VMEM = 60 * 1024 * 1024


def slot_maps(ids, groups, per_group, parts):
    slots, tokens = groups * per_group, ids.shape[1]
    slot = lax.broadcasted_iota(jnp.int32, (slots, tokens), 0)
    part_rows, part = per_group // parts, slots // parts
    group = (slot % part) // part_rows
    rank = (slot // part) * part_rows + slot % part_rows
    named = jnp.zeros((slots, tokens), jnp.bool_)
    for k in range(ids.shape[0]):
        named = named | (ids[k : k + 1, :] // 4 == group)
    before = lax.broadcasted_iota(jnp.int32, (tokens, tokens), 0) < lax.broadcasted_iota(
        jnp.int32, (tokens, tokens), 1
    )
    earlier = jnp.dot(
        named.astype(jnp.bfloat16), before.astype(jnp.bfloat16), preferred_element_type=jnp.float32
    )
    return named & (earlier == rank.astype(jnp.float32)), group


def slot_meta(ids, gates, mine, group, locals_):
    lane = lax.broadcasted_iota(jnp.int32, (mine.shape[0], LANES), 1)
    meta = jnp.zeros((mine.shape[0], LANES), jnp.float32)
    for j in range(locals_):
        value = jnp.zeros(mine.shape, jnp.float32)
        for k in range(ids.shape[0]):
            value = value + jnp.where(
                mine & (ids[k : k + 1, :] == group * locals_ + j), gates[k : k + 1, :], 0.0
            )
        meta = jnp.where(lane == j, jnp.sum(value, axis=1, keepdims=True), meta)
    token = lax.broadcasted_iota(jnp.int32, mine.shape, 1).astype(jnp.float32)
    token = jnp.sum(jnp.where(mine, token, 0.0), axis=1, keepdims=True)
    return jnp.where(lane == locals_, token, meta).astype(jnp.bfloat16)


def prepare_kernel(locals_, groups, per_group, tok, scores_t, ids_t, out_a, out_b, plain, pick):
    ids = ids_t[...]
    names = ids.shape[0]
    mine, group = slot_maps(ids, groups, per_group, 2)
    onehot = mine.astype(jnp.bfloat16)
    pick[...] = onehot
    score = scores_t[...]
    total = score[0:1, :]
    for k in range(1, names):
        total = total + score[k : k + 1, :]
    gates = (2.5 * score / total).astype(jnp.bfloat16).astype(jnp.float32)
    width, half = tok.shape[1], mine.shape[0] // 2
    meta = slot_meta(ids, gates, mine, group, locals_)
    out_a[:, width : width + LANES] = meta[:half]
    out_b[:, width : width + LANES] = meta[half:]
    row = lax.broadcasted_iota(jnp.int32, (LANES, tok.shape[0]), 0)
    routes = jnp.zeros((LANES, tok.shape[0]), jnp.float32)
    for k in range(names):
        routes = jnp.where(row == k, ids[k : k + 1, :].astype(jnp.float32), routes)
        routes = jnp.where(row == names + k, gates[k : k + 1, :], routes)
    plain[:, width : width + LANES] = routes.T.astype(jnp.bfloat16)
    for start in range(0, width, 4 * LANES):
        restored = []
        for place in range(start, start + 4 * LANES, LANES):
            x = tok[:, place : place + LANES].astype(jnp.float32)
            largest = jnp.max(jnp.abs(x), axis=1, keepdims=True)
            scale = ((largest + 1e-06) / 448.0).astype(jnp.bfloat16).astype(jnp.float32)
            quantized = (x * (1.0 / scale)).astype(jnp.bfloat16).astype(jnp.float32)
            restored.append((quantized * scale).astype(jnp.bfloat16))
        cols = slice(start, start + 4 * LANES)
        restored = jnp.concatenate(restored, axis=1)
        plain[:, cols] = restored
        rows = jnp.dot(onehot, restored, preferred_element_type=jnp.float32).astype(jnp.bfloat16)
        out_a[:, cols] = rows[:half]
        out_b[:, cols] = rows[half:]


def prepare(tokens, gate_scores, expert_ids, groups, locals_):
    count, width = tokens.shape
    per_group = 2 * count // groups
    slots = groups * per_group
    return pl.pallas_call(
        functools.partial(prepare_kernel, locals_, groups, per_group),
        out_shape=[
            jax.ShapeDtypeStruct((slots // 2, width + LANES), jnp.bfloat16),
            jax.ShapeDtypeStruct((slots // 2, width + LANES), jnp.bfloat16),
            jax.ShapeDtypeStruct((count, width + LANES), jnp.bfloat16),
            jax.ShapeDtypeStruct((slots, count), jnp.bfloat16),
        ],
        compiler_params=pltpu.CompilerParams(vmem_limit_bytes=VMEM),
        cost_estimate=pl.CostEstimate(flops=10**9, bytes_accessed=4 * 10**6, transcendentals=0),
    )(tokens, gate_scores.T, expert_ids.T)


def regroup_kernel(locals_, groups, names, plain, out):
    width = plain.shape[1] - LANES
    routes = plain[:, width:].astype(jnp.float32).T
    ids, gates = routes[:names].astype(jnp.int32), routes[names : 2 * names]
    mine, group = slot_maps(ids, groups, out.shape[0] // groups, 1)
    out[:, width:] = slot_meta(ids, gates, mine, group, locals_)
    onehot = mine.astype(jnp.bfloat16)
    for start in range(0, width, 4 * LANES):
        cols = slice(start, start + 4 * LANES)
        rows = jnp.dot(onehot, plain[:, cols], preferred_element_type=jnp.float32)
        out[:, cols] = rows.astype(jnp.bfloat16)


def expert_kernel(blocks, local_ref, *refs):
    xs, (wg, wu, wd), outs = refs[:blocks], refs[blocks : blocks + 3], refs[blocks + 3 : -2]
    rows, acc = refs[-2:]
    step, steps = pl.program_id(0), pl.num_programs(0)
    width = rows.shape[1]
    starts = [sum(x.shape[0] for x in xs[:b]) for b in range(blocks)]

    @pl.when(step == 0)
    def _():
        for b in range(blocks):
            rows[starts[b] : starts[b] + xs[b].shape[0], :] = xs[b][:, :width]

    x = rows[...]
    gate = jnp.dot(x, wg[0], preferred_element_type=jnp.float32)
    up = jnp.dot(x, wu[0], preferred_element_type=jnp.float32)
    hidden = (gate / (1.0 + jnp.exp(-gate)) * up).astype(jnp.bfloat16)
    part = jnp.dot(hidden, wd[0], preferred_element_type=jnp.float32)

    @pl.when(step == 0)
    def _():
        acc[...] = part

    @pl.when((step > 0) & (step < steps - 1))
    def _():
        acc[...] += part

    @pl.when(step == steps - 1)
    def _():
        for b in range(blocks):
            meta = xs[b][:, width : width + LANES]
            lane = lax.broadcasted_iota(jnp.int32, meta.shape, 1)
            weight = jnp.where(lane == local_ref[0], meta.astype(jnp.float32), 0.0)
            weight = jnp.sum(weight, axis=1, keepdims=True)
            own = slice(starts[b], starts[b] + xs[b].shape[0])
            outs[b][:, :width] = ((acc[own, :] + part[own, :]) * weight).astype(jnp.bfloat16)
            if outs[b].shape[1] > width:
                outs[b][:, width:] = meta


def experts(xs, marked, local, w_gate, w_up, w_down, tile=256):
    blocks, wide = len(xs), xs[0].shape[1]
    high = sum(x.shape[0] for x in xs)
    width, hidden = w_gate.shape[1:]
    outs = [(x.shape[0], wide if b in marked else width) for b, x in enumerate(xs)]
    return pl.pallas_call(
        functools.partial(expert_kernel, blocks),
        grid=(hidden // tile,),
        in_specs=[pl.BlockSpec(memory_space=pltpu.SMEM)]
        + [pl.BlockSpec(x.shape, lambda i: (0, 0)) for x in xs]
        + [
            pl.BlockSpec((1, width, tile), lambda i: (0, 0, i)),
            pl.BlockSpec((1, width, tile), lambda i: (0, 0, i)),
            pl.BlockSpec((1, tile, width), lambda i: (0, i, 0)),
        ],
        out_specs=[pl.BlockSpec(out, lambda i: (0, 0)) for out in outs],
        out_shape=[jax.ShapeDtypeStruct(out, jnp.bfloat16) for out in outs],
        scratch_shapes=[
            pltpu.VMEM((high, width), jnp.bfloat16),
            pltpu.VMEM((high, width), jnp.float32),
        ],
        compiler_params=pltpu.CompilerParams(
            vmem_limit_bytes=EXPERT_VMEM, dimension_semantics=("arbitrary",)
        ),
        cost_estimate=pl.CostEstimate(
            flops=6 * high * width * hidden,
            bytes_accessed=6 * width * hidden,
            transcendentals=high * hidden,
        ),
    )(local, *xs, w_gate, w_up, w_down)


def whole(kernel, shapes, *arrays):
    moved = sum(x.size * x.dtype.itemsize for x in arrays)
    return pl.pallas_call(
        kernel,
        out_shape=shapes,
        compiler_params=pltpu.CompilerParams(vmem_limit_bytes=VMEM),
        cost_estimate=pl.CostEstimate(flops=10**8, bytes_accessed=3 * moved, transcendentals=0),
    )(*arrays)


def to_tokens(pick, rows):
    return lax.dot_general(pick, rows, (((0,), (0,)), ((), ())), preferred_element_type=jnp.float32)


def scatter_kernel(locals_, rows, out):
    count, width = out.shape
    meta = rows[:, width:].astype(jnp.float32)
    lane = lax.broadcasted_iota(jnp.int32, meta.shape, 1)
    token = jnp.sum(jnp.where(lane == locals_, meta, 0.0), axis=1, keepdims=True)
    lane = lax.broadcasted_iota(jnp.int32, (rows.shape[0], count), 1)
    pick = (lane.astype(jnp.float32) == token).astype(jnp.bfloat16)
    out[...] = to_tokens(pick, rows[:, :width]).astype(jnp.bfloat16)


def collect_kernel(pick, first, second, far, out):
    total = to_tokens(pick[:PIECE, :], first[...]) + to_tokens(pick[PIECE:, :], second[...])
    out[...] = (total + far[...].astype(jnp.float32)).astype(jnp.bfloat16)


def per_device(tokens, gate_scores, expert_ids, w_gate, w_up, w_down):
    groups, locals_ = lax.axis_size("node"), lax.axis_size("local")
    local = lax.axis_index("local").astype(jnp.int32).reshape(1)
    tie = lax.optimization_barrier

    def across(block):
        parts = block.reshape(groups, block.shape[0] // groups, block.shape[1])
        return lax.all_to_all(parts, "node", 0, 0, tiled=True).reshape(block.shape)

    def shift(block, by):
        return lax.ppermute(block, "local", [(i, (i + by) % locals_) for i in range(locals_)])

    def up(block):
        return shift(block, 1)

    def down(block):
        return shift(block, -1)

    def add(*blocks):
        total = blocks[0].astype(jnp.float32)
        for block in blocks[1:]:
            total = total + block.astype(jnp.float32)
        return total.astype(jnp.bfloat16)

    run = functools.partial(experts, local=local, w_gate=w_gate, w_up=w_up, w_down=w_down)

    send_a, send_b, plain, pick = prepare(tokens, gate_scores, expert_ids, groups, locals_)
    across_ring = locals_ // 2
    plain = shift(plain, across_ring)
    slots = jax.ShapeDtypeStruct((pick.shape[0], plain.shape[1]), jnp.bfloat16)
    send_far = whole(
        functools.partial(regroup_kernel, locals_, groups, expert_ids.shape[1]), slots, plain
    )
    own_a = across(send_a)
    below_a, above_a = up(own_a), down(own_a)
    send_b, _ = tie((send_b, own_a))
    own_b = across(send_b)
    [own_pa] = run([own_a], ())
    send_far, own_b, own_pa, below_a, above_a = tie((send_far, own_b, own_pa, below_a, above_a))
    far = across(send_far)
    below_b, above_b = up(own_b), down(own_b)
    below_pa, above_pa, own_pb = run([below_a, above_a, own_b], ())
    far, own_pb = tie((far, own_pb))
    [far_p] = run([far], (0,))
    below_b, above_b, far_p = tie((below_b, above_b, far_p))
    below_pb, above_pb = run([below_b, above_b], ())

    far_t = jax.ShapeDtypeStruct(tokens.shape, jnp.bfloat16)
    far = shift(whole(functools.partial(scatter_kernel, locals_), far_t, across(far_p)), across_ring)

    final_a = across(add(own_pa, down(below_pa), up(above_pa)))
    final_b = across(add(own_pb, down(below_pb), up(above_pb)))
    near = [pltpu.with_memory_space_constraint(x, pltpu.VMEM) for x in (final_a, final_b, far)]
    return whole(collect_kernel, jax.ShapeDtypeStruct(tokens.shape, jnp.bfloat16), pick, *near)


def solution(mesh):
    in_specs = (
        P(("dp", "node", "local"), None),
        P(("dp", "node", "local"), None),
        P(("dp", "node", "local"), None),
        P(("node", "local"), None, None),
        P(("node", "local"), None, None),
        P(("node", "local"), None, None),
    )
    out_specs = P(("dp", "node", "local"), None)
    return jax.shard_map(
        per_device, mesh=mesh, in_specs=in_specs, out_specs=out_specs, check_vma=False
    )
```

time: 172 us -> 181 us (1.052)
  blocking collectives: 39.9 us -> 18.3 us
  waiting for transfers between devices: 23.3 us -> 37.3 us
  starting transfers between devices: 34.2 us -> 46.2 us
  Pallas kernels: 66.1 us -> 69.9 us
    all_to_all x2 -> x1, blocking collectives: 39.9 us -> 18.3 us  [across(): return lax.all_to_all(parts, 'node', 0, 0, tiled=True).reshape(block.shape)]
    all_to_all x4 -> x5, waiting for transfers between devices: 19.9 us -> 31.3 us  [across(): return lax.all_to_all(parts, 'node', 0, 0, tiled=True).reshape(block.shape)]
    all_to_all x4 -> x5, starting transfers between devices: 17.9 us -> 25.8 us  [across(): return lax.all_to_all(parts, 'node', 0, 0, tiled=True).reshape(block.shape)]
    ppermute x11 -> x10, starting transfers between devices: 16.3 us -> 20.4 us  [shift(): lax.ppermute(block, 'local', [(i, (i + by) % locals_) for i in range(loca...]
    pallas_call x2 -> x3, Pallas kernels: 5.57 us -> 8.88 us  [whole(): pl.pallas_call(kernel, out_shape=shapes, compiler_params=pltpu.CompilerPa...]
    ppermute x11 -> x10, waiting for transfers between devices: 3.39 us -> 6.04 us  [shift(): lax.ppermute(block, 'local', [(i, (i + by) % locals_) for i in range(loca...]
where the time goes in v9:
time: 181 us; the launch traced here: 180 us
  Pallas kernels  69.9 us (39%)
  starting transfers between devices  46.2 us (26%)
  waiting for transfers between devices  37.3 us (21%)
  blocking collectives  18.3 us (10%)
  other arithmetic  5.69 us (3%)
  local copies, waits for them, and re-layouts  2.22 us (1%)
    pallas_call x4, Pallas kernels, experts(): pl.pallas_call(functools.partial(expert_kernel, blocks), grid=(hidden //...  56.8 us
    all_to_all x5, waiting for transfers between devices, across(): return lax.all_to_all(parts, 'node', 0, 0, tiled=True).reshape(block.shape)  31.3 us
    all_to_all x5, starting transfers between devices, across(): return lax.all_to_all(parts, 'node', 0, 0, tiled=True).reshape(block.shape)  25.8 us
    ppermute x10, starting transfers between devices, shift(): lax.ppermute(block, 'local', [(i, (i + by) % locals_) for i in range(loca...  20.4 us
    all_to_all x1, blocking collectives, across(): return lax.all_to_all(parts, 'node', 0, 0, tiled=True).reshape(block.shape)  18.3 us
    pallas_call x3, Pallas kernels, whole(): pl.pallas_call(kernel, out_shape=shapes, compiler_params=pltpu.CompilerPa...  8.88 us
    ppermute x10, waiting for transfers between devices, shift(): lax.ppermute(block, 'local', [(i, (i + by) % locals_) for i in range(loca...  6.04 us
    reshape x2, other arithmetic, across(): parts = block.reshape(groups, block.shape[0] // groups, block.shape[1])  5.69 us
  transfers between devices with their start and end apart: 15, of which 6 were waited for; matrix products, arithmetic and copies ran while one was open for 3% of the time, Pallas kernels for 35%

profile of v9, /device:TPU:0, one launch (start us, length us, event | category | flops | bytes accessed | tf_op | source)
XLA Modules:
  0.0 179.7 jit_solution(2099066906309774748)
XLA Ops:
  0.0 4.3 %shard_map.64 = (bf16[128,3712]{1,0:T(8,128)(2,1)}, bf16[128,3712]{1,0:T(8,128)(2,1)}, bf16[128,3712]{1,0:T(8,128)(2,1)}, bf16[256,128]{1,0:T(8,128)(2,1)}) custom-call(bf16[128,3584]{1,0:T(8,128)(2,1)} %tok.1, f32[4,128]{1,0:T(4,128)} %bitcast.31, s32[4,128]{1,0:T(4,128)} %bitcast.32), custom_call_target="tpu_custom_call" | custom-call | flops 1000000000 | bytes 4000000 | tf_op jit(solution)/shard_map/pallas_call | solution.py:90
  4.3 8.0 %all-to-all-start = ((bf16[16,8,3712]{2,1,0:T(8,128)(2,1)}), bf16[16,8,3712]{2,1,0:T(8,128)(2,1)S(1)}, u32[]{:S(2)}, u32[]{:S(2)}) async-start(bf16[16,8,3712]{2,1,0:T(8,128)(2,1)} %bitcast.30), calls=%async_computation | async-start | bytes 1900544 | tf_op jit(solution)/shard_map/all_to_all | solution.py:223
  12.2 3.3 %collective-permute-start = (bf16[128,3712]{1,0:T(8,128)(2,1)}, bf16[128,3712]{1,0:T(8,128)(2,1)S(1)}, u32[]{:S(2)}, u32[]{:S(2)}) collective-permute-start(bf16[128,3712]{1,0:T(8,128)(2,1)} %get-tuple-element.26), channel_id=1, source_target_pairs={{0,2},{1,3},{2,0},{3,1},{4,6},{5,7},{6,4},{7,5},{8,10},{9,11},{10,... | collective-permute-start | bytes 2850824 | tf_op jit(solution)/shard_map/ppermute | solution.py:226
  15.5 13.2 %all-to-all-done = bf16[16,8,3712]{2,1,0:T(8,128)(2,1)S(1)} async-done(((bf16[16,8,3712]{2,1,0:T(8,128)(2,1)}), bf16[16,8,3712]{2,1,0:T(8,128)(2,1)S(1)}, u32[]{:S(2)}, u32[]{:S(2)}) %all-to-all-start) | async-done | bytes 950304 | tf_op jit(solution)/shard_map/all_to_all | solution.py:223
  28.7 0.0 copy-start.2
  28.7 1.6 collective-permute-start.1
  30.3 1.7 collective-permute-start.2
  31.9 3.6 %all-to-all-start.1 = ((bf16[16,8,3712]{2,1,0:T(8,128)(2,1)}), bf16[16,8,3712]{2,1,0:T(8,128)(2,1)S(1)}, u32[]{:S(2)}, u32[]{:S(2)}) async-start(bf16[16,8,3712]{2,1,0:T(8,128)(2,1)} %bitcast.29), calls=%async_computation.1 | async-start | bytes 1900544 | tf_op jit(solution)/shard_map/all_to_all | solution.py:223
  35.6 0.0 copy-done.2
  35.6 11.3 %shard_map.66 = bf16[128,3584]{1,0:T(8,128)(2,1)} custom-call(s32[1]{0:T(128)} %bitcast.6.local_ref, bf16[128,3712]{1,0:T(8,128)(2,1)} %bitcast.25, bf16[1,3584,1024]{2,1,0:T(8,128)(2,1)} %refs_2_.5, bf16[1,3584,1024]{2,1,0:T(8,128)(2,1)} %refs_3_.7, bf16[1,1024,3584]{2,1,0:T(8,128)(2,1)} %refs_4_.3), custom_call_target="tpu_custom_call" | custom-call | flops 2818572288 | bytes 22020096 | tf_op jit(solution)/shard_map/pallas_call | solution.py:160
  46.9 0.0 collective-permute-done.plain
  46.9 0.0 copy-start.4
  46.9 1.0 copy-done.4
  47.9 3.5 %shard_map.65 = bf16[256,3712]{1,0:T(8,128)(2,1)} custom-call(bf16[128,3712]{1,0:T(8,128)(2,1)} %copy-done.4), custom_call_target="tpu_custom_call" | custom-call | flops 100000000 | bytes 2850816 | tf_op jit(solution)/shard_map/pallas_call | solution.py:189
  51.4 0.0 all-to-all-done.1
  51.4 0.0 copy-start.5
  51.4 5.6 %collective-permute-done.1.refs_0_ = bf16[128,3712]{1,0:T(8,128)(2,1)} collective-permute-done((bf16[128,3712]{1,0:T(8,128)(2,1)S(1)}, bf16[128,3712]{1,0:T(8,128)(2,1)}, u32[]{:S(2)}, u32[]{:S(2)}) %collective-permute-start.1) | collective-permute-done | bytes 950304 | tf_op jit(solution)/shard_map/ppermute | solution.py:226
  57.0 0.4 collective-permute-done.2.refs_1_
  57.4 6.9 %all-to-all-start.3 = ((bf16[16,16,3712]{2,1,0:T(8,128)(2,1)}), bf16[16,16,3712]{2,1,0:T(8,128)(2,1)S(1)}, u32[]{:S(2)}, u32[]{:S(2)}) async-start(bf16[16,16,3712]{2,1,0:T(8,128)(2,1)} %bitcast.20), calls=%async_computation.3 | async-start | bytes 3801088 | tf_op jit(solution)/shard_map/all_to_all | solution.py:223
  64.3 1.4 collective-permute-start.5
  65.7 0.0 copy-done.5
  65.7 1.9 %collective-permute-start.6 = (bf16[128,3712]{1,0:T(8,128)(2,1)S(1)}, bf16[128,3712]{1,0:T(8,128)(2,1)}, u32[]{:S(2)}, u32[]{:S(2)}) collective-permute-start(bf16[128,3712]{1,0:T(8,128)(2,1)S(1)} %bitcast.27), channel_id=1, source_target_pairs={{0,3},{1,0},{2,1},{3,2},{4,7},{5,4},{6,5},{7,6},{8,11},{9,8},{10,9... | collective-permute-start | bytes 2850824 | tf_op jit(solution)/shard_map/ppermute | solution.py:226
  67.6 17.4 %shard_map.67 = (bf16[128,3584]{1,0:T(8,128)(2,1)}, bf16[128,3584]{1,0:T(8,128)(2,1)}, bf16[128,3584]{1,0:T(8,128)(2,1)}) custom-call(s32[1]{0:T(128)} %bitcast.6.local_ref, bf16[128,3712]{1,0:T(8,128)(2,1)} %collective-permute-done.1.refs_0_, bf16[128,3712]{1,0:T(8,128)(2,1)} %collective-permute-done.2.refs_1_, bf16[128,3712]{1,0:T(8,128)(2,1)} %bitcast.28, ...), custom_call_target="tpu_custom_call" | custom-call | flops 8455716864 | bytes 22020096 | tf_op jit(solution)/shard_map/pallas_call | solution.py:160
  84.9 0.1 collective-permute-start.4
  85.1 3.1 %collective-permute-start.3 = (bf16[128,3584]{1,0:T(8,128)(2,1)}, bf16[128,3584]{1,0:T(8,128)(2,1)}, u32[]{:S(2)}, u32[]{:S(2)}) collective-permute-start(bf16[128,3584]{1,0:T(8,128)(2,1)} %get-tuple-element.34), channel_id=1, source_target_pairs={{0,3},{1,0},{2,1},{3,2},{4,7},{5,4},{6,5},{7,6},{8,11},{9,8},{10,9... | collective-permute-start | bytes 2752520 | tf_op jit(solution)/shard_map/ppermute | solution.py:226
  88.2 4.4 %all-to-all-done.3 = bf16[16,16,3712]{2,1,0:T(8,128)(2,1)S(1)} async-done(((bf16[16,16,3712]{2,1,0:T(8,128)(2,1)}), bf16[16,16,3712]{2,1,0:T(8,128)(2,1)S(1)}, u32[]{:S(2)}, u32[]{:S(2)}) %all-to-all-start.3) | async-done | bytes 1900576 | tf_op jit(solution)/shard_map/all_to_all | solution.py:223
  92.6 0.0 copy-start.1
  92.6 1.2 copy-done.1
  93.8 14.0 %shard_map.68 = bf16[256,3712]{1,0:T(8,128)(2,1)} custom-call(s32[1]{0:T(128)} %bitcast.6.local_ref, bf16[256,3712]{1,0:T(8,128)(2,1)} %bitcast.22, bf16[1,3584,1024]{2,1,0:T(8,128)(2,1)} %refs_2_.5, bf16[1,3584,1024]{2,1,0:T(8,128)(2,1)} %refs_3_.7, bf16[1,1024,3584]{2,1,0:T(8,128)(2,1)} %refs_4_.3), custom_call_target="tpu_custom_call" | custom-call | flops 5637144576 | bytes 22020096 | tf_op jit(solution)/shard_map/pallas_call | solution.py:160
  107.9 0.0 collective-permute-done.5.refs_0_
  107.9 0.0 collective-permute-done.6.refs_1_
  107.9 3.7 %all-to-all-start.5 = ((bf16[16,16,3712]{2,1,0:T(8,128)(2,1)}), bf16[16,16,3712]{2,1,0:T(8,128)(2,1)S(1)}, u32[]{:S(2)}, u32[]{:S(2)}) async-start(bf16[16,16,3712]{2,1,0:T(8,128)(2,1)} %bitcast.21), calls=%async_computation.5 | async-start | bytes 3801088 | tf_op jit(solution)/shard_map/all_to_all | solution.py:223
  111.6 0.0 copy-start.3
  111.6 14.0 %shard_map.69 = (bf16[128,3584]{1,0:T(8,128)(2,1)}, bf16[128,3584]{1,0:T(8,128)(2,1)}) custom-call(s32[1]{0:T(128)} %bitcast.6.local_ref, bf16[128,3712]{1,0:T(8,128)(2,1)} %collective-permute-done.5.refs_0_, bf16[128,3712]{1,0:T(8,128)(2,1)} %collective-permute-done.6.refs_1_, bf16[1,3584,1024]{2,1,0:T(8,128)(2,1)} %refs_2_.5, ...), custom_call_target="tpu_custom_call" | custom-call | flops 5637144576 | bytes 22020096 | tf_op jit(solution)/shard_map/pallas_call | solution.py:160
  125.6 1.9 %collective-permute-start.8 = (bf16[128,3584]{1,0:T(8,128)(2,1)}, bf16[128,3584]{1,0:T(8,128)(2,1)}, u32[]{:S(2)}, u32[]{:S(2)}) collective-permute-start(bf16[128,3584]{1,0:T(8,128)(2,1)} %get-tuple-element.43), channel_id=1, source_target_pairs={{0,1},{1,2},{2,3},{3,0},{4,5},{5,6},{6,7},{7,4},{8,9},{9,10},{10,1... | collective-permute-start | bytes 2752520 | tf_op jit(solution)/shard_map/ppermute | solution.py:226
  127.6 1.8 collective-permute-start.7
  129.3 0.0 collective-permute-done.4
  129.3 0.0 collective-permute-done.3
  129.3 0.0 copy-done.3
  129.4 2.7 %fusion = bf16[16,8,3584]{2,1,0:T(8,128)(2,1)} fusion(bf16[128,3584]{1,0:T(8,128)(2,1)} %collective-permute-done.4, bf16[128,3584]{1,0:T(8,128)(2,1)} %collective-permute-done.3, bf16[128,3584]{1,0:T(8,128)(2,1)S(1)} %copy-done.3), kind=kLoop, calls=%fused_computation.2 | loop fusion | flops 2752512 | bytes 3670016 | tf_op jit(solution)/shard_map/reshape | solution.py:222
  132.1 7.6 %all-to-all-done.5 = bf16[16,16,3712]{2,1,0:T(8,128)(2,1)S(1)} async-done(((bf16[16,16,3712]{2,1,0:T(8,128)(2,1)}), bf16[16,16,3712]{2,1,0:T(8,128)(2,1)S(1)}, u32[]{:S(2)}, u32[]{:S(2)}) %all-to-all-start.5) | async-done | bytes 1900576 | tf_op jit(solution)/shard_map/all_to_all | solution.py:223
  139.7 0.0 copy-start
  139.7 3.6 %all-to-all-start.2 = ((bf16[16,8,3584]{2,1,0:T(8,128)(2,1)}), bf16[16,8,3584]{2,1,0:T(8,128)(2,1)S(1)}, u32[]{:S(2)}, u32[]{:S(2)}) async-start(bf16[16,8,3584]{2,1,0:T(8,128)(2,1)} %fusion), calls=%async_computation.2 | async-start | bytes 1835008 | tf_op jit(solution)/shard_map/all_to_all | solution.py:223
  143.3 0.0 copy-done
  143.3 3.0 %shard_map.70 = bf16[128,3584]{1,0:T(8,128)(2,1)} custom-call(bf16[256,3712]{1,0:T(8,128)(2,1)} %bitcast.19), custom_call_target="tpu_custom_call" | custom-call | flops 100000000 | bytes 5701632 | tf_op jit(solution)/shard_map/pallas_call | solution.py:189
  146.3 3.6 %collective-permute-start.9 = (bf16[128,3584]{1,0:T(8,128)(2,1)}, bf16[128,3584]{1,0:T(8,128)(2,1)S(1)}, u32[]{:S(2)}, u32[]{:S(2)}) collective-permute-start(bf16[128,3584]{1,0:T(8,128)(2,1)} %shard_map.70), channel_id=1, source_target_pairs={{0,2},{1,3},{2,0},{3,1},{4,6},{5,7},{6,4},{7,5},{8,10},{9,11},{10,... | collective-permute-start | bytes 2752520 | tf_op jit(solution)/shard_map/ppermute | solution.py:226
  149.9 0.0 collective-permute-done.8
  149.9 0.0 collective-permute-done.7
  149.9 3.0 %fusion.1 = bf16[16,8,3584]{2,1,0:T(8,128)(2,1)} fusion(bf16[128,3584]{1,0:T(8,128)(2,1)} %collective-permute-done.8, bf16[128,3584]{1,0:T(8,128)(2,1)} %collective-permute-done.7, bf16[128,3584]{1,0:T(8,128)(2,1)} %get-tuple-element.38), kind=kLoop, calls=%fused_computation.3 | loop fusion | flops 2752512 | bytes 3670016 | tf_op jit(solution)/shard_map/reshape | solution.py:222
  152.9 6.0 %all-to-all-done.2 = bf16[16,8,3584]{2,1,0:T(8,128)(2,1)S(1)} async-done(((bf16[16,8,3584]{2,1,0:T(8,128)(2,1)}), bf16[16,8,3584]{2,1,0:T(8,128)(2,1)S(1)}, u32[]{:S(2)}, u32[]{:S(2)}) %all-to-all-start.2) | async-done | bytes 917536 | tf_op jit(solution)/shard_map/all_to_all | solution.py:223
  159.0 18.3 %all_to_all.30 = bf16[16,8,3584]{2,1,0:T(8,128)(2,1)S(1)} all-to-all(bf16[16,8,3584]{2,1,0:T(8,128)(2,1)} %fusion.1), channel_id=1, replica_groups=mesh['dp'=2,'node'=16,'local'=4] {'node'}, dimensions={0} | all-to-all | bytes 1835008 | tf_op jit(solution)/shard_map/all_to_all | solution.py:223
  177.3 0.0 collective-permute-done.9.far
  177.3 2.4 %shard_map.71 = bf16[128,3584]{1,0:T(8,128)(2,1)} custom-call(bf16[256,128]{1,0:T(8,128)(2,1)} %get-tuple-element.25.pick, bf16[128,3584]{1,0:T(8,128)(2,1)S(1)} %bitcast.17, bf16[128,3584]{1,0:T(8,128)(2,1)S(1)} %bitcast.18, bf16[128,3584]{1,0:T(8,128)(2,1)S(1)} %collective-permute-done.9.far), custom_call_target="tpu_custom_call" | custom-call | flops 100000000 | bytes 8454144 | tf_op jit(solution)/shard_map/pallas_call | solution.py:189
Async XLA Ops:
  4.3 24.4 %all-to-all-start = ((bf16[16,8,3712]{2,1,0:T(8,128)(2,1)}), bf16[16,8,3712]{2,1,0:T(8,128)(2,1)S(1)}, u32[]{:S(2)}, u32[]{:S(2)}) async-start(bf16[16,8,3712]{2,1,0:T(8,128)(2,1)} %bitcast.30), calls=%async_computation | async-start | bytes 1900544 | tf_op jit(solution)/shard_map/all_to_all | solution.py:223
  12.2 34.7 %collective-permute-start = (bf16[128,3712]{1,0:T(8,128)(2,1)}, bf16[128,3712]{1,0:T(8,128)(2,1)S(1)}, u32[]{:S(2)}, u32[]{:S(2)}) collective-permute-start(bf16[128,3712]{1,0:T(8,128)(2,1)} %get-tuple-element.26), channel_id=1, source_target_pairs={{0,2},{1,3},{2,0},{3,1},{4,6},{5,7},{6,4},{7,5},{8,10},{9,11},{10,... | collective-permute-start | bytes 2850824 | tf_op jit(solution)/shard_map/ppermute | solution.py:226
  28.7 6.9 %copy-start.2 = (bf16[16,8,3712]{2,1,0:T(8,128)(2,1)}, bf16[16,8,3712]{2,1,0:T(8,128)(2,1)S(1)}, u32[]{:S(2)}) copy-start(bf16[16,8,3712]{2,1,0:T(8,128)(2,1)S(1)} %all-to-all-done) | copy-start | bytes 2850820
  28.7 28.3 %collective-permute-start.1 = (bf16[128,3712]{1,0:T(8,128)(2,1)S(1)}, bf16[128,3712]{1,0:T(8,128)(2,1)}, u32[]{:S(2)}, u32[]{:S(2)}) collective-permute-start(bf16[128,3712]{1,0:T(8,128)(2,1)S(1)} %bitcast.23), channel_id=1, source_target_pairs={{0,1},{1,2},{2,3},{3,0},{4,5},{5,6},{6,7},{7,4},{8,9},{9,10},{10,1... | collective-permute-start | bytes 2850824 | tf_op jit(solution)/shard_map/ppermute | solution.py:226
  30.3 27.1 %collective-permute-start.2 = (bf16[128,3712]{1,0:T(8,128)(2,1)S(1)}, bf16[128,3712]{1,0:T(8,128)(2,1)}, u32[]{:S(2)}, u32[]{:S(2)}) collective-permute-start(bf16[128,3712]{1,0:T(8,128)(2,1)S(1)} %bitcast.24), channel_id=1, source_target_pairs={{0,3},{1,0},{2,1},{3,2},{4,7},{5,4},{6,5},{7,6},{8,11},{9,8},{10,9... | collective-permute-start | bytes 2850824 | tf_op jit(solution)/shard_map/ppermute | solution.py:226
  31.9 19.4 %all-to-all-start.1 = ((bf16[16,8,3712]{2,1,0:T(8,128)(2,1)}), bf16[16,8,3712]{2,1,0:T(8,128)(2,1)S(1)}, u32[]{:S(2)}, u32[]{:S(2)}) async-start(bf16[16,8,3712]{2,1,0:T(8,128)(2,1)} %bitcast.29), calls=%async_computation.1 | async-start | bytes 1900544 | tf_op jit(solution)/shard_map/all_to_all | solution.py:223
  46.9 1.0 copy-start.4
  51.4 14.3 %copy-start.5 = (bf16[16,8,3712]{2,1,0:T(8,128)(2,1)}, bf16[16,8,3712]{2,1,0:T(8,128)(2,1)S(1)}, u32[]{:S(2)}) copy-start(bf16[16,8,3712]{2,1,0:T(8,128)(2,1)S(1)} %all-to-all-done.1) | copy-start | bytes 2850820
  57.4 35.2 %all-to-all-start.3 = ((bf16[16,16,3712]{2,1,0:T(8,128)(2,1)}), bf16[16,16,3712]{2,1,0:T(8,128)(2,1)S(1)}, u32[]{:S(2)}, u32[]{:S(2)}) async-start(bf16[16,16,3712]{2,1,0:T(8,128)(2,1)} %bitcast.20), calls=%async_computation.3 | async-start | bytes 3801088 | tf_op jit(solution)/shard_map/all_to_all | solution.py:223
  64.3 43.6 %collective-permute-start.5 = (bf16[128,3712]{1,0:T(8,128)(2,1)S(1)}, bf16[128,3712]{1,0:T(8,128)(2,1)}, u32[]{:S(2)}, u32[]{:S(2)}) collective-permute-start(bf16[128,3712]{1,0:T(8,128)(2,1)S(1)} %bitcast.26), channel_id=1, source_target_pairs={{0,1},{1,2},{2,3},{3,0},{4,5},{5,6},{6,7},{7,4},{8,9},{9,10},{10,1... | collective-permute-start | bytes 2850824 | tf_op jit(solution)/shard_map/ppermute | solution.py:226
  65.7 42.2 %collective-permute-start.6 = (bf16[128,3712]{1,0:T(8,128)(2,1)S(1)}, bf16[128,3712]{1,0:T(8,128)(2,1)}, u32[]{:S(2)}, u32[]{:S(2)}) collective-permute-start(bf16[128,3712]{1,0:T(8,128)(2,1)S(1)} %bitcast.27), channel_id=1, source_target_pairs={{0,3},{1,0},{2,1},{3,2},{4,7},{5,4},{6,5},{7,6},{8,11},{9,8},{10,9... | collective-permute-start | bytes 2850824 | tf_op jit(solution)/shard_map/ppermute | solution.py:226
  84.9 44.4 %collective-permute-start.4 = (bf16[128,3584]{1,0:T(8,128)(2,1)}, bf16[128,3584]{1,0:T(8,128)(2,1)}, u32[]{:S(2)}, u32[]{:S(2)}) collective-permute-start(bf16[128,3584]{1,0:T(8,128)(2,1)} %get-tuple-element.35), channel_id=1, source_target_pairs={{0,1},{1,2},{2,3},{3,0},{4,5},{5,6},{6,7},{7,4},{8,9},{9,10},{10,1... | collective-permute-start | bytes 2752520 | tf_op jit(solution)/shard_map/ppermute | solution.py:226
  85.1 44.3 %collective-permute-start.3 = (bf16[128,3584]{1,0:T(8,128)(2,1)}, bf16[128,3584]{1,0:T(8,128)(2,1)}, u32[]{:S(2)}, u32[]{:S(2)}) collective-permute-start(bf16[128,3584]{1,0:T(8,128)(2,1)} %get-tuple-element.34), channel_id=1, source_target_pairs={{0,3},{1,0},{2,1},{3,2},{4,7},{5,4},{6,5},{7,6},{8,11},{9,8},{10,9... | collective-permute-start | bytes 2752520 | tf_op jit(solution)/shard_map/ppermute | solution.py:226
  92.6 1.2 copy-start.1
  107.9 31.8 %all-to-all-start.5 = ((bf16[16,16,3712]{2,1,0:T(8,128)(2,1)}), bf16[16,16,3712]{2,1,0:T(8,128)(2,1)S(1)}, u32[]{:S(2)}, u32[]{:S(2)}) async-start(bf16[16,16,3712]{2,1,0:T(8,128)(2,1)} %bitcast.21), calls=%async_computation.5 | async-start | bytes 3801088 | tf_op jit(solution)/shard_map/all_to_all | solution.py:223
  111.6 17.7 %copy-start.3 = (bf16[128,3584]{1,0:T(8,128)(2,1)S(1)}, bf16[128,3584]{1,0:T(8,128)(2,1)}, u32[]{:S(2)}) copy-start(bf16[128,3584]{1,0:T(8,128)(2,1)} %shard_map.66) | copy-start | bytes 2752516
  125.6 24.3 %collective-permute-start.8 = (bf16[128,3584]{1,0:T(8,128)(2,1)}, bf16[128,3584]{1,0:T(8,128)(2,1)}, u32[]{:S(2)}, u32[]{:S(2)}) collective-permute-start(bf16[128,3584]{1,0:T(8,128)(2,1)} %get-tuple-element.43), channel_id=1, source_target_pairs={{0,1},{1,2},{2,3},{3,0},{4,5},{5,6},{6,7},{7,4},{8,9},{9,10},{10,1... | collective-permute-start | bytes 2752520 | tf_op jit(solution)/shard_map/ppermute | solution.py:226
  127.6 22.4 %collective-permute-start.7 = (bf16[128,3584]{1,0:T(8,128)(2,1)}, bf16[128,3584]{1,0:T(8,128)(2,1)}, u32[]{:S(2)}, u32[]{:S(2)}) collective-permute-start(bf16[128,3584]{1,0:T(8,128)(2,1)} %get-tuple-element.42), channel_id=1, source_target_pairs={{0,3},{1,0},{2,1},{3,2},{4,7},{5,4},{6,5},{7,6},{8,11},{9,8},{10,9... | collective-permute-start | bytes 2752520 | tf_op jit(solution)/shard_map/ppermute | solution.py:226
  139.7 3.6 %copy-start = (bf16[16,16,3712]{2,1,0:T(8,128)(2,1)}, bf16[16,16,3712]{2,1,0:T(8,128)(2,1)S(1)}, u32[]{:S(2)}) copy-start(bf16[16,16,3712]{2,1,0:T(8,128)(2,1)S(1)} %all-to-all-done.5) | copy-start | bytes 5701636
  139.7 19.3 %all-to-all-start.2 = ((bf16[16,8,3584]{2,1,0:T(8,128)(2,1)}), bf16[16,8,3584]{2,1,0:T(8,128)(2,1)S(1)}, u32[]{:S(2)}, u32[]{:S(2)}) async-start(bf16[16,8,3584]{2,1,0:T(8,128)(2,1)} %fusion), calls=%async_computation.2 | async-start | bytes 1835008 | tf_op jit(solution)/shard_map/all_to_all | solution.py:223
  146.3 31.0 %collective-permute-start.9 = (bf16[128,3584]{1,0:T(8,128)(2,1)}, bf16[128,3584]{1,0:T(8,128)(2,1)S(1)}, u32[]{:S(2)}, u32[]{:S(2)}) collective-permute-start(bf16[128,3584]{1,0:T(8,128)(2,1)} %shard_map.70), channel_id=1, source_target_pairs={{0,2},{1,3},{2,0},{3,1},{4,6},{5,7},{6,4},{7,5},{8,10},{9,11},{10,... | collective-permute-start | bytes 2752520 | tf_op jit(solution)/shard_map/ppermute | solution.py:226

commit v10 on v9

--- a/solution.py
+++ b/solution.py
@@ -46,21 +46,19 @@
     return jnp.where(lane == locals_, token, meta).astype(jnp.bfloat16)
 
 
-def prepare_kernel(locals_, groups, per_group, tok, scores_t, ids_t, out_a, out_b, plain, pick):
+def prepare_kernel(locals_, groups, per_group, tok, scores_t, ids_t, out, plain, pick):
     ids = ids_t[...]
     names = ids.shape[0]
-    mine, group = slot_maps(ids, groups, per_group, 2)
+    pick[...] = slot_maps(ids, groups, per_group, 2)[0].astype(jnp.bfloat16)
+    mine, group = slot_maps(ids, groups, per_group, 1)
     onehot = mine.astype(jnp.bfloat16)
-    pick[...] = onehot
     score = scores_t[...]
     total = score[0:1, :]
     for k in range(1, names):
         total = total + score[k : k + 1, :]
     gates = (2.5 * score / total).astype(jnp.bfloat16).astype(jnp.float32)
-    width, half = tok.shape[1], mine.shape[0] // 2
-    meta = slot_meta(ids, gates, mine, group, locals_)
-    out_a[:, width : width + LANES] = meta[:half]
-    out_b[:, width : width + LANES] = meta[half:]
+    width = tok.shape[1]
+    out[:, width : width + LANES] = slot_meta(ids, gates, mine, group, locals_)
     row = lax.broadcasted_iota(jnp.int32, (LANES, tok.shape[0]), 0)
     routes = jnp.zeros((LANES, tok.shape[0]), jnp.float32)
     for k in range(names):
@@ -78,9 +76,8 @@
         cols = slice(start, start + 4 * LANES)
         restored = jnp.concatenate(restored, axis=1)
         plain[:, cols] = restored
-        rows = jnp.dot(onehot, restored, preferred_element_type=jnp.float32).astype(jnp.bfloat16)
-        out_a[:, cols] = rows[:half]
-        out_b[:, cols] = rows[half:]
+        rows = jnp.dot(onehot, restored, preferred_element_type=jnp.float32)
+        out[:, cols] = rows.astype(jnp.bfloat16)
 
 
 def prepare(tokens, gate_scores, expert_ids, groups, locals_):
@@ -90,8 +87,7 @@
     return pl.pallas_call(
         functools.partial(prepare_kernel, locals_, groups, per_group),
         out_shape=[
-            jax.ShapeDtypeStruct((slots // 2, width + LANES), jnp.bfloat16),
-            jax.ShapeDtypeStruct((slots // 2, width + LANES), jnp.bfloat16),
+            jax.ShapeDtypeStruct((slots, width + LANES), jnp.bfloat16),
             jax.ShapeDtypeStruct((count, width + LANES), jnp.bfloat16),
             jax.ShapeDtypeStruct((slots, count), jnp.bfloat16),
         ],
@@ -239,23 +235,23 @@
 
     run = functools.partial(experts, local=local, w_gate=w_gate, w_up=w_up, w_down=w_down)
 
-    send_a, send_b, plain, pick = prepare(tokens, gate_scores, expert_ids, groups, locals_)
+    send, plain, pick = prepare(tokens, gate_scores, expert_ids, groups, locals_)
     across_ring = locals_ // 2
     plain = shift(plain, across_ring)
-    slots = jax.ShapeDtypeStruct((pick.shape[0], plain.shape[1]), jnp.bfloat16)
+    slots = jax.ShapeDtypeStruct(send.shape, jnp.bfloat16)
     send_far = whole(
         functools.partial(regroup_kernel, locals_, groups, expert_ids.shape[1]), slots, plain
     )
-    own_a = across(send_a)
+    own = across(send).reshape(groups, 2, PIECE // groups, send.shape[1])
+    own_a, own_b = (own[:, half].reshape(PIECE, send.shape[1]) for half in range(2))
     below_a, above_a = up(own_a), down(own_a)
-    send_b, _ = tie((send_b, own_a))
-    own_b = across(send_b)
-    [own_pa] = run([own_a], ())
-    send_far, own_b, own_pa, below_a, above_a = tie((send_far, own_b, own_pa, below_a, above_a))
+    send_far, own_b = tie((send_far, own_b))
     far = across(send_far)
+    own_pa, own_pb = run([own_a, own_b], ())
+    below_a, above_a, own_b, own_pa = tie((below_a, above_a, own_b, own_pa))
     below_b, above_b = up(own_b), down(own_b)
-    below_pa, above_pa, own_pb = run([below_a, above_a, own_b], ())
-    far, own_pb = tie((far, own_pb))
+    below_pa, above_pa = run([below_a, above_a], ())
+    far, below_pa = tie((far, below_pa))
     [far_p] = run([far], (0,))
     below_b, above_b, far_p = tie((below_b, above_b, far_p))
     below_pb, above_pb = run([below_b, above_b], ())

time: 181 us -> 192 us (1.061)
  waiting for transfers between devices: 37.3 us -> 51.6 us
  starting transfers between devices: 46.2 us -> 42.8 us
    ppermute x10, waiting for transfers between devices: 6.04 us -> 47 us  [shift(): lax.ppermute(block, 'local', [(i, (i + by) % locals_) for i in range(loca...]
    all_to_all x5 -> x4, waiting for transfers between devices: 31.3 us -> 4.6 us  [across(): return lax.all_to_all(parts, 'node', 0, 0, tiled=True).reshape(block.shape)]
    ppermute x10, starting transfers between devices: 20.4 us -> 17.6 us  [shift(): lax.ppermute(block, 'local', [(i, (i + by) % locals_) for i in range(loca...]
    all_to_all x5 -> x4, starting transfers between devices: 25.8 us -> 25.2 us  [across(): return lax.all_to_all(parts, 'node', 0, 0, tiled=True).reshape(block.shape)]
  transfers between devices with their start and end apart: 15 -> 14, of which waited for: 6 -> 5; matrix products, arithmetic and copies ran while one was open for 3% -> 3% of each run, Pallas kernels for 35% -> 33%
where the time goes in v10:
time: 192 us; the launch traced here: 191 us
  Pallas kernels  69.3 us (36%)
  waiting for transfers between devices  51.6 us (27%)
  starting transfers between devices  42.8 us (22%)
  blocking collectives  19.2 us (10%)
  other arithmetic  5.71 us (3%)
  local copies, waits for them, and re-layouts  2.36 us (1%)
    pallas_call x4, Pallas kernels, experts(): pl.pallas_call(functools.partial(expert_kernel, blocks), grid=(hidden //...  56 us
    ppermute x10, waiting for transfers between devices, shift(): lax.ppermute(block, 'local', [(i, (i + by) % locals_) for i in range(loca...  47 us
    all_to_all x4, starting transfers between devices, across(): return lax.all_to_all(parts, 'node', 0, 0, tiled=True).reshape(block.shape)  25.2 us
    all_to_all x1, blocking collectives, across(): return lax.all_to_all(parts, 'node', 0, 0, tiled=True).reshape(block.shape)  19.2 us
    ppermute x10, starting transfers between devices, shift(): lax.ppermute(block, 'local', [(i, (i + by) % locals_) for i in range(loca...  17.6 us
    pallas_call x3, Pallas kernels, whole(): pl.pallas_call(kernel, out_shape=shapes, compiler_params=pltpu.CompilerPa...  8.85 us
    reshape x2, other arithmetic, across(): parts = block.reshape(groups, block.shape[0] // groups, block.shape[1])  5.71 us
    all_to_all x4, waiting for transfers between devices, across(): return lax.all_to_all(parts, 'node', 0, 0, tiled=True).reshape(block.shape)  4.6 us
  transfers between devices with their start and end apart: 14, of which 5 were waited for; matrix products, arithmetic and copies ran while one was open for 3% of the time, Pallas kernels for 33%

profile of v10, /device:TPU:0, one launch (start us, length us, event | category | flops | bytes accessed | tf_op | source)
XLA Modules:
  0.0 191.1 jit_solution(3884409549473670901)
XLA Ops:
  0.0 4.4 %shard_map.64 = (bf16[256,3712]{1,0:T(8,128)(2,1)}, bf16[128,3712]{1,0:T(8,128)(2,1)}, bf16[256,128]{1,0:T(8,128)(2,1)}) custom-call(bf16[128,3584]{1,0:T(8,128)(2,1)} %tok.1, f32[4,128]{1,0:T(4,128)} %bitcast.26, s32[4,128]{1,0:T(4,128)} %bitcast.27), custom_call_target="tpu_custom_call" | custom-call | flops 1000000000 | bytes 4000000 | tf_op jit(solution)/shard_map/pallas_call | solution.py:87
  4.4 8.0 %all-to-all-start = ((bf16[16,16,3712]{2,1,0:T(8,128)(2,1)}), bf16[16,16,3712]{2,1,0:T(8,128)(2,1)S(1)}, u32[]{:S(2)}, u32[]{:S(2)}) async-start(bf16[16,16,3712]{2,1,0:T(8,128)(2,1)} %bitcast.25), calls=%async_computation | async-start | bytes 3801088 | tf_op jit(solution)/shard_map/all_to_all | solution.py:219
  12.4 3.3 %collective-permute-start.2 = (bf16[128,3712]{1,0:T(8,128)(2,1)}, bf16[128,3712]{1,0:T(8,128)(2,1)S(1)}, u32[]{:S(2)}, u32[]{:S(2)}) collective-permute-start(bf16[128,3712]{1,0:T(8,128)(2,1)} %get-tuple-element.27), channel_id=1, source_target_pairs={{0,2},{1,3},{2,0},{3,1},{4,6},{5,7},{6,4},{7,5},{8,10},{9,11},{10,... | collective-permute-start | bytes 2850824 | tf_op jit(solution)/shard_map/ppermute | solution.py:222
  15.6 21.0 %collective-permute-done.2.plain = bf16[128,3712]{1,0:T(8,128)(2,1)S(1)} collective-permute-done((bf16[128,3712]{1,0:T(8,128)(2,1)}, bf16[128,3712]{1,0:T(8,128)(2,1)S(1)}, u32[]{:S(2)}, u32[]{:S(2)}) %collective-permute-start.2) | collective-permute-done | bytes 950304 | tf_op jit(solution)/shard_map/ppermute | solution.py:222
  36.7 0.0 copy-start.3
  36.7 0.9 copy-done.3
  37.6 3.5 %shard_map.65 = bf16[256,3712]{1,0:T(8,128)(2,1)} custom-call(bf16[128,3712]{1,0:T(8,128)(2,1)} %copy-done.3), custom_call_target="tpu_custom_call" | custom-call | flops 100000000 | bytes 2850816 | tf_op jit(solution)/shard_map/pallas_call | solution.py:185
  41.1 0.2 all-to-all-done
  41.3 1.4 slice_bitcast_fusion
  42.7 6.7 %all-to-all-start.1 = ((bf16[16,16,3712]{2,1,0:T(8,128)(2,1)}), bf16[16,16,3712]{2,1,0:T(8,128)(2,1)S(1)}, u32[]{:S(2)}, u32[]{:S(2)}) async-start(bf16[16,16,3712]{2,1,0:T(8,128)(2,1)} %bitcast.7), calls=%async_computation.1 | async-start | bytes 3801088 | tf_op jit(solution)/shard_map/all_to_all | solution.py:219
  49.4 1.6 collective-permute-start
  51.0 1.7 collective-permute-start.1
  52.7 0.0 copy-start.2
  52.7 14.0 %shard_map.66 = (bf16[128,3584]{1,0:T(8,128)(2,1)}, bf16[128,3584]{1,0:T(8,128)(2,1)}) custom-call(s32[1]{0:T(128)} %bitcast.6.local_ref, bf16[128,3712]{1,0:T(8,128)(2,1)} %get-tuple-element.46.refs_0_, bf16[128,3712]{1,0:T(8,128)(2,1)} %get-tuple-element.38.refs_1_, bf16[1,3584,1024]{2,1,0:T(8,128)(2,1)} %refs_2_.7, bf16[1,3584,1024]{2,1,0:T(8,128)(2,1)} %refs_3_.7, ...), custom_call_target="tpu_custom_call" | custom-call | flops 5637144576 | bytes 22020096 | tf_op jit(solution)/shard_map/pallas_call | solution.py:156
  66.7 5.4 %collective-permute-done.refs_0_ = bf16[128,3712]{1,0:T(8,128)(2,1)} collective-permute-done((bf16[128,3712]{1,0:T(8,128)(2,1)}, bf16[128,3712]{1,0:T(8,128)(2,1)}, u32[]{:S(2)}, u32[]{:S(2)}) %collective-permute-start) | collective-permute-done | bytes 950304 | tf_op jit(solution)/shard_map/ppermute | solution.py:222
  72.0 0.0 collective-permute-done.1.refs_1_
  72.1 0.0 copy-done.2
  72.1 1.6 collective-permute-start.5
  73.6 1.7 collective-permute-start.6
  75.3 14.0 %shard_map.67 = (bf16[128,3584]{1,0:T(8,128)(2,1)}, bf16[128,3584]{1,0:T(8,128)(2,1)}) custom-call(s32[1]{0:T(128)} %bitcast.6.local_ref, bf16[128,3712]{1,0:T(8,128)(2,1)} %collective-permute-done.refs_0_, bf16[128,3712]{1,0:T(8,128)(2,1)} %collective-permute-done.1.refs_1_, bf16[1,3584,1024]{2,1,0:T(8,128)(2,1)} %refs_2_.7, ...), custom_call_target="tpu_custom_call" | custom-call | flops 5637144576 | bytes 22020096 | tf_op jit(solution)/shard_map/pallas_call | solution.py:156
  89.3 0.4 collective-permute-start.4
  89.7 0.0 all-to-all-done.1
  89.7 0.0 copy-start.1
  89.7 2.9 %collective-permute-start.3 = (bf16[128,3584]{1,0:T(8,128)(2,1)}, bf16[128,3584]{1,0:T(8,128)(2,1)}, u32[]{:S(2)}, u32[]{:S(2)}) collective-permute-start(bf16[128,3584]{1,0:T(8,128)(2,1)} %get-tuple-element.35), channel_id=1, source_target_pairs={{0,3},{1,0},{2,1},{3,2},{4,7},{5,4},{6,5},{7,6},{8,11},{9,8},{10,9... | collective-permute-start | bytes 2752520 | tf_op jit(solution)/shard_map/ppermute | solution.py:222
  92.6 0.0 copy-done.1
  92.6 14.0 %shard_map.68 = bf16[256,3712]{1,0:T(8,128)(2,1)} custom-call(s32[1]{0:T(128)} %bitcast.6.local_ref, bf16[256,3712]{1,0:T(8,128)(2,1)} %bitcast.23, bf16[1,3584,1024]{2,1,0:T(8,128)(2,1)} %refs_2_.7, bf16[1,3584,1024]{2,1,0:T(8,128)(2,1)} %refs_3_.7, bf16[1,1024,3584]{2,1,0:T(8,128)(2,1)} %refs_4_.5), custom_call_target="tpu_custom_call" | custom-call | flops 5637144576 | bytes 22020096 | tf_op jit(solution)/shard_map/pallas_call | solution.py:156
  106.6 0.0 collective-permute-done.5.refs_0_
  106.6 0.0 collective-permute-done.6.refs_1_
  106.6 6.9 %all-to-all-start.4 = ((bf16[16,16,3712]{2,1,0:T(8,128)(2,1)}), bf16[16,16,3712]{2,1,0:T(8,128)(2,1)S(1)}, u32[]{:S(2)}, u32[]{:S(2)}) async-start(bf16[16,16,3712]{2,1,0:T(8,128)(2,1)} %bitcast.24), calls=%async_computation.4 | async-start | bytes 3801088 | tf_op jit(solution)/shard_map/all_to_all | solution.py:219
  113.5 0.0 copy-start.4
  113.5 14.0 %shard_map.69 = (bf16[128,3584]{1,0:T(8,128)(2,1)}, bf16[128,3584]{1,0:T(8,128)(2,1)}) custom-call(s32[1]{0:T(128)} %bitcast.6.local_ref, bf16[128,3712]{1,0:T(8,128)(2,1)} %collective-permute-done.5.refs_0_, bf16[128,3712]{1,0:T(8,128)(2,1)} %collective-permute-done.6.refs_1_, bf16[1,3584,1024]{2,1,0:T(8,128)(2,1)} %refs_2_.7, ...), custom_call_target="tpu_custom_call" | custom-call | flops 5637144576 | bytes 22020096 | tf_op jit(solution)/shard_map/pallas_call | solution.py:156
  127.5 0.0 collective-permute-start.8
  127.5 3.2 %collective-permute-start.7 = (bf16[128,3584]{1,0:T(8,128)(2,1)}, bf16[128,3584]{1,0:T(8,128)(2,1)}, u32[]{:S(2)}, u32[]{:S(2)}) collective-permute-start(bf16[128,3584]{1,0:T(8,128)(2,1)} %get-tuple-element.42), channel_id=1, source_target_pairs={{0,3},{1,0},{2,1},{3,2},{4,7},{5,4},{6,5},{7,6},{8,11},{9,8},{10,9... | collective-permute-start | bytes 2752520 | tf_op jit(solution)/shard_map/ppermute | solution.py:222
  130.7 0.0 collective-permute-done.4
  130.7 0.0 collective-permute-done.3
  130.7 0.0 copy-done.4
  130.8 2.7 %fusion = bf16[16,8,3584]{2,1,0:T(8,128)(2,1)} fusion(bf16[128,3584]{1,0:T(8,128)(2,1)} %collective-permute-done.4, bf16[128,3584]{1,0:T(8,128)(2,1)} %collective-permute-done.3, bf16[128,3584]{1,0:T(8,128)(2,1)S(1)} %copy-done.4), kind=kLoop, calls=%fused_computation.4 | loop fusion | flops 2752512 | bytes 3670016 | tf_op jit(solution)/shard_map/reshape | solution.py:218
  133.5 4.4 %all-to-all-done.4 = bf16[16,16,3712]{2,1,0:T(8,128)(2,1)S(1)} async-done(((bf16[16,16,3712]{2,1,0:T(8,128)(2,1)}), bf16[16,16,3712]{2,1,0:T(8,128)(2,1)S(1)}, u32[]{:S(2)}, u32[]{:S(2)}) %all-to-all-start.4) | async-done | bytes 1900576 | tf_op jit(solution)/shard_map/all_to_all | solution.py:219
  137.9 0.0 copy-start
  137.9 3.6 %all-to-all-start.2 = ((bf16[16,8,3584]{2,1,0:T(8,128)(2,1)}), bf16[16,8,3584]{2,1,0:T(8,128)(2,1)S(1)}, u32[]{:S(2)}, u32[]{:S(2)}) async-start(bf16[16,8,3584]{2,1,0:T(8,128)(2,1)} %fusion), calls=%async_computation.2 | async-start | bytes 1835008 | tf_op jit(solution)/shard_map/all_to_all | solution.py:219
  141.5 0.0 copy-done
  141.5 3.0 %shard_map.70 = bf16[128,3584]{1,0:T(8,128)(2,1)} custom-call(bf16[256,3712]{1,0:T(8,128)(2,1)} %bitcast.21), custom_call_target="tpu_custom_call" | custom-call | flops 100000000 | bytes 5701632 | tf_op jit(solution)/shard_map/pallas_call | solution.py:185
  144.5 1.4 collective-permute-start.9
  145.9 20.6 %collective-permute-done.8 = bf16[128,3584]{1,0:T(8,128)(2,1)} collective-permute-done((bf16[128,3584]{1,0:T(8,128)(2,1)}, bf16[128,3584]{1,0:T(8,128)(2,1)}, u32[]{:S(2)}, u32[]{:S(2)}) %collective-permute-start.8) | collective-permute-done | bytes 917536 | tf_op jit(solution)/shard_map/ppermute | solution.py:222
  166.4 0.0 collective-permute-done.7
  166.4 3.0 %fusion.1 = bf16[16,8,3584]{2,1,0:T(8,128)(2,1)} fusion(bf16[128,3584]{1,0:T(8,128)(2,1)} %collective-permute-done.8, bf16[128,3584]{1,0:T(8,128)(2,1)} %collective-permute-done.7, bf16[128,3584]{1,0:T(8,128)(2,1)} %get-tuple-element.37), kind=kLoop, calls=%fused_computation.5 | loop fusion | flops 2752512 | bytes 3670016 | tf_op jit(solution)/shard_map/reshape | solution.py:218
  169.4 0.0 all-to-all-done.2
  169.4 19.2 %all_to_all.25 = bf16[16,8,3584]{2,1,0:T(8,128)(2,1)S(1)} all-to-all(bf16[16,8,3584]{2,1,0:T(8,128)(2,1)} %fusion.1), channel_id=1, replica_groups=mesh['dp'=2,'node'=16,'local'=4] {'node'}, dimensions={0} | all-to-all | bytes 1835008 | tf_op jit(solution)/shard_map/all_to_all | solution.py:219
  188.7 0.0 collective-permute-done.9.far
  188.7 2.4 %shard_map.71 = bf16[128,3584]{1,0:T(8,128)(2,1)} custom-call(bf16[256,128]{1,0:T(8,128)(2,1)} %get-tuple-element.25.pick, bf16[128,3584]{1,0:T(8,128)(2,1)S(1)} %bitcast.19, bf16[128,3584]{1,0:T(8,128)(2,1)S(1)} %bitcast.20, bf16[128,3584]{1,0:T(8,128)(2,1)S(1)} %collective-permute-done.9.far), custom_call_target="tpu_custom_call" | custom-call | flops 100000000 | bytes 8454144 | tf_op jit(solution)/shard_map/pallas_call | solution.py:185
Async XLA Ops:
  4.4 36.9 %all-to-all-start = ((bf16[16,16,3712]{2,1,0:T(8,128)(2,1)}), bf16[16,16,3712]{2,1,0:T(8,128)(2,1)S(1)}, u32[]{:S(2)}, u32[]{:S(2)}) async-start(bf16[16,16,3712]{2,1,0:T(8,128)(2,1)} %bitcast.25), calls=%async_computation | async-start | bytes 3801088 | tf_op jit(solution)/shard_map/all_to_all | solution.py:219
  12.4 24.3 %collective-permute-start.2 = (bf16[128,3712]{1,0:T(8,128)(2,1)}, bf16[128,3712]{1,0:T(8,128)(2,1)S(1)}, u32[]{:S(2)}, u32[]{:S(2)}) collective-permute-start(bf16[128,3712]{1,0:T(8,128)(2,1)} %get-tuple-element.27), channel_id=1, source_target_pairs={{0,2},{1,3},{2,0},{3,1},{4,6},{5,7},{6,4},{7,5},{8,10},{9,11},{10,... | collective-permute-start | bytes 2850824 | tf_op jit(solution)/shard_map/ppermute | solution.py:222
  36.7 0.9 copy-start.3
  42.7 47.0 %all-to-all-start.1 = ((bf16[16,16,3712]{2,1,0:T(8,128)(2,1)}), bf16[16,16,3712]{2,1,0:T(8,128)(2,1)S(1)}, u32[]{:S(2)}, u32[]{:S(2)}) async-start(bf16[16,16,3712]{2,1,0:T(8,128)(2,1)} %bitcast.7), calls=%async_computation.1 | async-start | bytes 3801088 | tf_op jit(solution)/shard_map/all_to_all | solution.py:219
  49.4 22.7 %collective-permute-start = (bf16[128,3712]{1,0:T(8,128)(2,1)}, bf16[128,3712]{1,0:T(8,128)(2,1)}, u32[]{:S(2)}, u32[]{:S(2)}) collective-permute-start(bf16[128,3712]{1,0:T(8,128)(2,1)} %get-tuple-element.46.refs_0_), channel_id=1, source_target_pairs={{0,1},{1,2},{2,3},{3,0},{4,5},{5,6},{6,7},{7,4},{8,9},{9,10},{10,1... | collective-permute-start | bytes 2850824 | tf_op jit(solution)/shard_map/ppermute | solution.py:222
  51.0 21.1 %collective-permute-start.1 = (bf16[128,3712]{1,0:T(8,128)(2,1)}, bf16[128,3712]{1,0:T(8,128)(2,1)}, u32[]{:S(2)}, u32[]{:S(2)}) collective-permute-start(bf16[128,3712]{1,0:T(8,128)(2,1)} %get-tuple-element.46.refs_0_), channel_id=1, source_target_pairs={{0,3},{1,0},{2,1},{3,2},{4,7},{5,4},{6,5},{7,6},{8,11},{9,8},{10,9... | collective-permute-start | bytes 2850824 | tf_op jit(solution)/shard_map/ppermute | solution.py:222
  52.7 19.4 %copy-start.2 = (bf16[128,3712]{1,0:T(8,128)(2,1)S(1)}, bf16[128,3712]{1,0:T(8,128)(2,1)}, u32[]{:S(2)}) copy-start(bf16[128,3712]{1,0:T(8,128)(2,1)} %get-tuple-element.38.refs_1_) | copy-start | bytes 2850820
  72.1 34.5 %collective-permute-start.5 = (bf16[128,3712]{1,0:T(8,128)(2,1)S(1)}, bf16[128,3712]{1,0:T(8,128)(2,1)}, u32[]{:S(2)}, u32[]{:S(2)}) collective-permute-start(bf16[128,3712]{1,0:T(8,128)(2,1)S(1)} %copy-done.2), channel_id=1, source_target_pairs={{0,1},{1,2},{2,3},{3,0},{4,5},{5,6},{6,7},{7,4},{8,9},{9,10},{10,1... | collective-permute-start | bytes 2850824 | tf_op jit(solution)/shard_map/ppermute | solution.py:222
  73.6 33.0 %collective-permute-start.6 = (bf16[128,3712]{1,0:T(8,128)(2,1)S(1)}, bf16[128,3712]{1,0:T(8,128)(2,1)}, u32[]{:S(2)}, u32[]{:S(2)}) collective-permute-start(bf16[128,3712]{1,0:T(8,128)(2,1)S(1)} %copy-done.2), channel_id=1, source_target_pairs={{0,3},{1,0},{2,1},{3,2},{4,7},{5,4},{6,5},{7,6},{8,11},{9,8},{10,9... | collective-permute-start | bytes 2850824 | tf_op jit(solution)/shard_map/ppermute | solution.py:222
  89.3 41.4 %collective-permute-start.4 = (bf16[128,3584]{1,0:T(8,128)(2,1)}, bf16[128,3584]{1,0:T(8,128)(2,1)}, u32[]{:S(2)}, u32[]{:S(2)}) collective-permute-start(bf16[128,3584]{1,0:T(8,128)(2,1)} %get-tuple-element.36), channel_id=1, source_target_pairs={{0,1},{1,2},{2,3},{3,0},{4,5},{5,6},{6,7},{7,4},{8,9},{9,10},{10,1... | collective-permute-start | bytes 2752520 | tf_op jit(solution)/shard_map/ppermute | solution.py:222
  89.7 2.9 %copy-start.1 = (bf16[16,16,3712]{2,1,0:T(8,128)(2,1)}, bf16[16,16,3712]{2,1,0:T(8,128)(2,1)S(1)}, u32[]{:S(2)}) copy-start(bf16[16,16,3712]{2,1,0:T(8,128)(2,1)S(1)} %all-to-all-done.1) | copy-start | bytes 5701636
  89.7 41.1 %collective-permute-start.3 = (bf16[128,3584]{1,0:T(8,128)(2,1)}, bf16[128,3584]{1,0:T(8,128)(2,1)}, u32[]{:S(2)}, u32[]{:S(2)}) collective-permute-start(bf16[128,3584]{1,0:T(8,128)(2,1)} %get-tuple-element.35), channel_id=1, source_target_pairs={{0,3},{1,0},{2,1},{3,2},{4,7},{5,4},{6,5},{7,6},{8,11},{9,8},{10,9... | collective-permute-start | bytes 2752520 | tf_op jit(solution)/shard_map/ppermute | solution.py:222
  106.6 31.3 %all-to-all-start.4 = ((bf16[16,16,3712]{2,1,0:T(8,128)(2,1)}), bf16[16,16,3712]{2,1,0:T(8,128)(2,1)S(1)}, u32[]{:S(2)}, u32[]{:S(2)}) async-start(bf16[16,16,3712]{2,1,0:T(8,128)(2,1)} %bitcast.24), calls=%async_computation.4 | async-start | bytes 3801088 | tf_op jit(solution)/shard_map/all_to_all | solution.py:219
  113.5 17.3 %copy-start.4 = (bf16[128,3584]{1,0:T(8,128)(2,1)S(1)}, bf16[128,3584]{1,0:T(8,128)(2,1)}, u32[]{:S(2)}) copy-start(bf16[128,3584]{1,0:T(8,128)(2,1)} %get-tuple-element.30) | copy-start | bytes 2752516
  127.5 38.9 %collective-permute-start.8 = (bf16[128,3584]{1,0:T(8,128)(2,1)}, bf16[128,3584]{1,0:T(8,128)(2,1)}, u32[]{:S(2)}, u32[]{:S(2)}) collective-permute-start(bf16[128,3584]{1,0:T(8,128)(2,1)} %get-tuple-element.43), channel_id=1, source_target_pairs={{0,1},{1,2},{2,3},{3,0},{4,5},{5,6},{6,7},{7,4},{8,9},{9,10},{10,1... | collective-permute-start | bytes 2752520 | tf_op jit(solution)/shard_map/ppermute | solution.py:222
  127.5 38.9 %collective-permute-start.7 = (bf16[128,3584]{1,0:T(8,128)(2,1)}, bf16[128,3584]{1,0:T(8,128)(2,1)}, u32[]{:S(2)}, u32[]{:S(2)}) collective-permute-start(bf16[128,3584]{1,0:T(8,128)(2,1)} %get-tuple-element.42), channel_id=1, source_target_pairs={{0,3},{1,0},{2,1},{3,2},{4,7},{5,4},{6,5},{7,6},{8,11},{9,8},{10,9... | collective-permute-start | bytes 2752520 | tf_op jit(solution)/shard_map/ppermute | solution.py:222
  137.9 3.6 %copy-start = (bf16[16,16,3712]{2,1,0:T(8,128)(2,1)}, bf16[16,16,3712]{2,1,0:T(8,128)(2,1)S(1)}, u32[]{:S(2)}) copy-start(bf16[16,16,3712]{2,1,0:T(8,128)(2,1)S(1)} %all-to-all-done.4) | copy-start | bytes 5701636
  137.9 31.6 %all-to-all-start.2 = ((bf16[16,8,3584]{2,1,0:T(8,128)(2,1)}), bf16[16,8,3584]{2,1,0:T(8,128)(2,1)S(1)}, u32[]{:S(2)}, u32[]{:S(2)}) async-start(bf16[16,8,3584]{2,1,0:T(8,128)(2,1)} %fusion), calls=%async_computation.2 | async-start | bytes 1835008 | tf_op jit(solution)/shard_map/all_to_all | solution.py:219
  144.5 44.2 %collective-permute-start.9 = (bf16[128,3584]{1,0:T(8,128)(2,1)}, bf16[128,3584]{1,0:T(8,128)(2,1)S(1)}, u32[]{:S(2)}, u32[]{:S(2)}) collective-permute-start(bf16[128,3584]{1,0:T(8,128)(2,1)} %shard_map.70), channel_id=1, source_target_pairs={{0,2},{1,3},{2,0},{3,1},{4,6},{5,7},{6,4},{7,5},{8,10},{9,11},{10,... | collective-permute-start | bytes 2752520 | tf_op jit(solution)/shard_map/ppermute | solution.py:222

commit v11 on v8

--- a/solution.py
+++ b/solution.py
@@ -10,6 +10,7 @@
 LANES = 128
 PIECE = 128
 VMEM = 60 * 1024 * 1024
+EXPERT_VMEM = 48 * 1024 * 1024
 
 
 def slot_maps(ids_t, groups, per_group):
@@ -151,7 +152,7 @@
             pltpu.VMEM((blocks * piece, width), jnp.float32),
         ],
         compiler_params=pltpu.CompilerParams(
-            vmem_limit_bytes=VMEM, dimension_semantics=("arbitrary",)
+            vmem_limit_bytes=EXPERT_VMEM, dimension_semantics=("arbitrary",)
         ),
         cost_estimate=pl.CostEstimate(
             flops=6 * blocks * piece * width * hidden,
@@ -227,16 +228,22 @@
     [own_pa] = run([own_a], ())
     below_a, above_a, next_b, own_pa = tie((below_a, above_a, own_b, own_pa))
     far_a, above_b = up(below_a), down(next_b)
-    below_pa, above_pa, own_pb = run([below_a, above_a, next_b], ())
+    kept = pltpu.with_memory_space_constraint(next_b, pltpu.VMEM)
+    below_pa, above_pa, own_pb = run([below_a, above_a, kept], ())
     far_a, above_b, last_b, below_pa = tie((far_a, above_b, next_b, below_pa))
     below_b, far_b = up(last_b), down(above_b)
     far_pa, above_pb = run([far_a, above_b], (0,))
     below_pa, above_pa, far_pa = tie((below_pa, above_pa, far_pa))
     below_b, far_b, above_pb = tie((below_b, far_b, above_pb))
-    below_pb, far_pb = run([below_b, far_b], (1,))
+    kept = [pltpu.with_memory_space_constraint(x, pltpu.VMEM) for x in (below_b, far_b)]
+    below_pb, far_pb = run(kept, (1,))
 
     home_a = across(far_pa)
-    above_pb, below_pb, far_pb, home_a = tie((above_pb, below_pb, far_pb, home_a))
+    from_above, from_below = down(below_pa), up(above_pa)
+    far_pb, home_a = tie((far_pb, home_a))
+    above_pb, below_pb, from_above, from_below, home_a = tie(
+        (above_pb, below_pb, from_above, from_below, home_a)
+    )
     home_b = across(far_pb)
     far = whole(
         functools.partial(scatter_kernel, locals_),
@@ -244,7 +251,7 @@
     )
     far = shift(far, locals_ // 2)
 
-    final_a = across(add(own_pa, down(below_pa), up(above_pa)))
+    final_a = across(add(own_pa, from_above, from_below))
     final_b = across(add(own_pb, down(below_pb), up(above_pb)))
     near = [pltpu.with_memory_space_constraint(x, pltpu.VMEM) for x in (final_a, final_b, far)]
     return whole(collect_kernel, jax.ShapeDtypeStruct(tokens.shape, jnp.bfloat16), pick, *near)

time: 172 us -> 184 us (1.070)
  waiting for transfers between devices: 23.3 us -> 38.9 us
  blocking collectives: 39.9 us -> 43.3 us
  Pallas kernels: 66.1 us -> 63 us
  starting transfers between devices: 34.2 us -> 31.7 us
    ppermute x11, waiting for transfers between devices: 3.39 us -> 26.5 us  [shift(): lax.ppermute(block, 'local', [(i, (i + by) % locals_) for i in range(loca...]
    all_to_all x4, waiting for transfers between devices: 19.9 us -> 12.4 us  [across(): return lax.all_to_all(parts, 'node', 0, 0, tiled=True).reshape(block.shape)]
    all_to_all x2, blocking collectives: 39.9 us -> 43.3 us  [across(): return lax.all_to_all(parts, 'node', 0, 0, tiled=True).reshape(block.shape)]
    pallas_call x4, Pallas kernels: 56.5 us -> 53.4 us  [experts(): pl.pallas_call(functools.partial(expert_kernel, blocks), grid=(hidden //...]
  transfers between devices with their start and end apart: 15 -> 15, of which waited for: 6 -> 7; matrix products, arithmetic and copies ran while one was open for 3% -> 3% of each run, Pallas kernels for 35% -> 31%
where the time goes in v11:
time: 184 us; the launch traced here: 183 us
  Pallas kernels  63 us (34%)
  blocking collectives  43.3 us (24%)
  waiting for transfers between devices  38.9 us (21%)
  starting transfers between devices  31.7 us (17%)
  other arithmetic  5.44 us (3%)
    pallas_call x4, Pallas kernels, experts(): pl.pallas_call(functools.partial(expert_kernel, blocks), grid=(hidden //...  53.4 us
    all_to_all x2, blocking collectives, across(): return lax.all_to_all(parts, 'node', 0, 0, tiled=True).reshape(block.shape)  43.3 us
    ppermute x11, waiting for transfers between devices, shift(): lax.ppermute(block, 'local', [(i, (i + by) % locals_) for i in range(loca...  26.5 us
    all_to_all x4, starting transfers between devices, across(): return lax.all_to_all(parts, 'node', 0, 0, tiled=True).reshape(block.shape)  16.3 us
    ppermute x11, starting transfers between devices, shift(): lax.ppermute(block, 'local', [(i, (i + by) % locals_) for i in range(loca...  15.4 us
    all_to_all x4, waiting for transfers between devices, across(): return lax.all_to_all(parts, 'node', 0, 0, tiled=True).reshape(block.shape)  12.4 us
    pallas_call x2, Pallas kernels, whole(): pl.pallas_call(kernel, out_shape=shapes, compiler_params=pltpu.CompilerPa...  5.67 us
    reshape x2, other arithmetic, across(): parts = block.reshape(groups, block.shape[0] // groups, block.shape[1])  5.44 us
  transfers between devices with their start and end apart: 15, of which 7 were waited for; matrix products, arithmetic and copies ran while one was open for 3% of the time, Pallas kernels for 31%

profile of v11, /device:TPU:0, one launch (start us, length us, event | category | flops | bytes accessed | tf_op | source)
XLA Modules:
  0.0 183.3 jit_solution(7448332896788233801)
XLA Ops:
  0.0 3.9 %shard_map.64 = (bf16[128,3712]{1,0:T(8,128)(2,1)}, bf16[128,3712]{1,0:T(8,128)(2,1)}, bf16[256,128]{1,0:T(8,128)(2,1)}) custom-call(bf16[128,3584]{1,0:T(8,128)(2,1)} %tok.1, f32[4,128]{1,0:T(4,128)} %bitcast.28, s32[4,128]{1,0:T(4,128)} %bitcast.29), custom_call_target="tpu_custom_call" | custom-call | flops 1000000000 | bytes 3000000 | tf_op jit(solution)/shard_map/pallas_call | solution.py:82
  3.9 24.1 %all_to_all.30 = bf16[16,8,3712]{2,1,0:T(8,128)(2,1)S(1)} all-to-all(bf16[16,8,3712]{2,1,0:T(8,128)(2,1)} %bitcast.27), channel_id=1, replica_groups=mesh['dp'=2,'node'=16,'local'=4] {'node'}, dimensions={0} | all-to-all | bytes 1900544 | tf_op jit(solution)/shard_map/all_to_all | solution.py:204
  28.0 1.6 collective-permute-start
  29.6 1.7 collective-permute-start.1
  31.2 3.6 %all-to-all-start.1 = ((bf16[16,8,3712]{2,1,0:T(8,128)(2,1)}), bf16[16,8,3712]{2,1,0:T(8,128)(2,1)S(1)}, u32[]{:S(2)}, u32[]{:S(2)}) async-start(bf16[16,8,3712]{2,1,0:T(8,128)(2,1)} %bitcast.26), calls=%async_computation.1 | async-start | bytes 1900544 | tf_op jit(solution)/shard_map/all_to_all | solution.py:204
  34.9 9.6 %shard_map.65 = bf16[128,3584]{1,0:T(8,128)(2,1)S(1)} custom-call(s32[1]{0:T(128)} %bitcast.6.local_ref, bf16[128,3712]{1,0:T(8,128)(2,1)S(1)} %bitcast.19, bf16[1,3584,1024]{2,1,0:T(8,128)(2,1)} %refs_2_.5, bf16[1,3584,1024]{2,1,0:T(8,128)(2,1)} %refs_3_.7, bf16[1,1024,3584]{2,1,0:T(8,128)(2,1)} %refs_4_.5), custom_call_target="tpu_custom_call" | custom-call | flops 2818572288 | bytes 22020096 | tf_op jit(solution)/shard_map/pallas_call | solution.py:138
  44.5 5.3 %all-to-all-done.1 = bf16[16,8,3712]{2,1,0:T(8,128)(2,1)S(1)} async-done(((bf16[16,8,3712]{2,1,0:T(8,128)(2,1)}), bf16[16,8,3712]{2,1,0:T(8,128)(2,1)S(1)}, u32[]{:S(2)}, u32[]{:S(2)}) %all-to-all-start.1) | async-done | bytes 950304 | tf_op jit(solution)/shard_map/all_to_all | solution.py:204
  49.9 1.2 collective-permute-done.refs_0_
  51.0 0.0 collective-permute-done.1.refs_1_
  51.1 2.9 %collective-permute-start.3 = (bf16[128,3712]{1,0:T(8,128)(2,1)S(1)}, bf16[128,3712]{1,0:T(8,128)(2,1)S(1)}, u32[]{:S(2)}, u32[]{:S(2)}) collective-permute-start(bf16[128,3712]{1,0:T(8,128)(2,1)S(1)} %bitcast.22), channel_id=1, source_target_pairs={{0,3},{1,0},{2,1},{3,2},{4,7},{5,4},{6,5},{7,6},{8,11},{9,8},{10,9... | collective-permute-start | bytes 2850824 | tf_op jit(solution)/shard_map/ppermute | solution.py:207
  54.0 0.0 collective-permute-start.2
  54.0 16.7 %shard_map.66 = (bf16[128,3584]{1,0:T(8,128)(2,1)}, bf16[128,3584]{1,0:T(8,128)(2,1)}, bf16[128,3584]{1,0:T(8,128)(2,1)S(1)}) custom-call(s32[1]{0:T(128)} %bitcast.6.local_ref, bf16[128,3712]{1,0:T(8,128)(2,1)} %collective-permute-done.refs_0_, bf16[128,3712]{1,0:T(8,128)(2,1)} %collective-permute-done.1.refs_1_, bf16[128,3712]{1,0:T(8,128)(2,1)S(1)} %bitcast.23, ...), custom_call_target="tpu_custom_call" | custom-call | flops 8455716864 | bytes 22020096 | tf_op jit(solution)/shard_map/pallas_call | solution.py:138
  70.7 0.0 copy-start
  70.7 1.3 collective-permute-done.3.refs_1_
  72.0 3.6 %collective-permute-done.2.refs_0_ = bf16[128,3712]{1,0:T(8,128)(2,1)S(1)} collective-permute-done((bf16[128,3712]{1,0:T(8,128)(2,1)}, bf16[128,3712]{1,0:T(8,128)(2,1)S(1)}, u32[]{:S(2)}, u32[]{:S(2)}) %collective-permute-start.2) | collective-permute-done | bytes 950304 | tf_op jit(solution)/shard_map/ppermute | solution.py:207
  75.6 0.0 collective-permute-start.4
  75.6 3.2 %collective-permute-start.5 = (bf16[128,3712]{1,0:T(8,128)(2,1)S(1)}, bf16[128,3712]{1,0:T(8,128)(2,1)}, u32[]{:S(2)}, u32[]{:S(2)}) collective-permute-start(bf16[128,3712]{1,0:T(8,128)(2,1)S(1)} %collective-permute-done.3.refs_1_), channel_id=1, source_target_pairs={{0,3},{1,0},{2,1},{3,2},{4,7},{5,4},{6,5},{7,6},{8,11},{9,8},{10,9... | collective-permute-start | bytes 2850824 | tf_op jit(solution)/shard_map/ppermute | solution.py:207
  78.9 13.0 %shard_map.67 = (bf16[128,3712]{1,0:T(8,128)(2,1)}, bf16[128,3584]{1,0:T(8,128)(2,1)}) custom-call(s32[1]{0:T(128)} %bitcast.6.local_ref, bf16[128,3712]{1,0:T(8,128)(2,1)S(1)} %collective-permute-done.2.refs_0_, bf16[128,3712]{1,0:T(8,128)(2,1)S(1)} %collective-permute-done.3.refs_1_, bf16[1,3584,1024]{2,1,0:T(8,128)(2,1)} %refs_2_.5, ...), custom_call_target="tpu_custom_call" | custom-call | flops 5637144576 | bytes 22020096 | tf_op jit(solution)/shard_map/pallas_call | solution.py:138
  91.8 0.0 copy-done
  91.8 0.0 collective-permute-start.6
  91.9 2.0 %collective-permute-start.7 = (bf16[128,3584]{1,0:T(8,128)(2,1)}, bf16[128,3584]{1,0:T(8,128)(2,1)}, u32[]{:S(2)}, u32[]{:S(2)}) collective-permute-start(bf16[128,3584]{1,0:T(8,128)(2,1)} %get-tuple-element.58), channel_id=1, source_target_pairs={{0,1},{1,2},{2,3},{3,0},{4,5},{5,6},{6,7},{7,4},{8,9},{9,10},{10,1... | collective-permute-start | bytes 2752520 | tf_op jit(solution)/shard_map/ppermute | solution.py:207
  93.9 4.3 %all-to-all-start.2 = ((bf16[16,8,3712]{2,1,0:T(8,128)(2,1)}), bf16[16,8,3712]{2,1,0:T(8,128)(2,1)}, u32[]{:S(2)}, u32[]{:S(2)}) async-start(bf16[16,8,3712]{2,1,0:T(8,128)(2,1)} %bitcast.7), calls=%async_computation.2 | async-start | bytes 1900544 | tf_op jit(solution)/shard_map/all_to_all | solution.py:204
  98.2 2.5 %collective-permute-done.4.refs_0_ = bf16[128,3712]{1,0:T(8,128)(2,1)} collective-permute-done((bf16[128,3712]{1,0:T(8,128)(2,1)S(1)}, bf16[128,3712]{1,0:T(8,128)(2,1)}, u32[]{:S(2)}, u32[]{:S(2)}) %collective-permute-start.4) | collective-permute-done | bytes 950304 | tf_op jit(solution)/shard_map/ppermute | solution.py:207
  100.6 0.0 collective-permute-done.5.refs_1_
  100.6 14.1 %shard_map.68 = (bf16[128,3584]{1,0:T(8,128)(2,1)}, bf16[128,3712]{1,0:T(8,128)(2,1)}) custom-call(s32[1]{0:T(128)} %bitcast.6.local_ref, bf16[128,3712]{1,0:T(8,128)(2,1)} %collective-permute-done.4.refs_0_, bf16[128,3712]{1,0:T(8,128)(2,1)} %collective-permute-done.5.refs_1_, bf16[1,3584,1024]{2,1,0:T(8,128)(2,1)} %refs_2_.5, ...), custom_call_target="tpu_custom_call" | custom-call | flops 5637144576 | bytes 22020096 | tf_op jit(solution)/shard_map/pallas_call | solution.py:138
  114.7 0.0 all-to-all-done.2
  114.7 4.7 %all-to-all-start.5 = ((bf16[16,8,3712]{2,1,0:T(8,128)(2,1)}), bf16[16,8,3712]{2,1,0:T(8,128)(2,1)S(1)}, u32[]{:S(2)}, u32[]{:S(2)}) async-start(bf16[16,8,3712]{2,1,0:T(8,128)(2,1)} %bitcast.13), calls=%async_computation.5 | async-start | bytes 1900544 | tf_op jit(solution)/shard_map/all_to_all | solution.py:204
  119.4 0.0 collective-permute-done.6
  119.4 0.0 collective-permute-done.7
  119.4 2.9 %collective-permute-start.8 = (bf16[128,3584]{1,0:T(8,128)(2,1)}, bf16[128,3584]{1,0:T(8,128)(2,1)}, u32[]{:S(2)}, u32[]{:S(2)}) collective-permute-start(bf16[128,3584]{1,0:T(8,128)(2,1)} %get-tuple-element.65), channel_id=1, source_target_pairs={{0,3},{1,0},{2,1},{3,2},{4,7},{5,4},{6,5},{7,6},{8,11},{9,8},{10,9... | collective-permute-start | bytes 2752520 | tf_op jit(solution)/shard_map/ppermute | solution.py:207
  122.3 0.0 collective-permute-start.9
  122.3 2.7 %fusion = bf16[16,8,3584]{2,1,0:T(8,128)(2,1)} fusion(bf16[128,3584]{1,0:T(8,128)(2,1)} %collective-permute-done.7, bf16[128,3584]{1,0:T(8,128)(2,1)} %collective-permute-done.6, bf16[128,3584]{1,0:T(8,128)(2,1)S(1)} %shard_map.65), kind=kLoop, calls=%fused_computation.2 | loop fusion | flops 2752512 | bytes 3670016 | tf_op jit(solution)/shard_map/reshape | solution.py:203
  125.1 7.1 %all-to-all-done.5 = bf16[16,8,3712]{2,1,0:T(8,128)(2,1)S(1)} async-done(((bf16[16,8,3712]{2,1,0:T(8,128)(2,1)}), bf16[16,8,3712]{2,1,0:T(8,128)(2,1)S(1)}, u32[]{:S(2)}, u32[]{:S(2)}) %all-to-all-start.5) | async-done | bytes 950304 | tf_op jit(solution)/shard_map/all_to_all | solution.py:204
  132.1 0.0 copy-start.2
  132.1 0.9 copy-done.2
  133.1 3.6 %all-to-all-start.3 = ((bf16[16,8,3584]{2,1,0:T(8,128)(2,1)}), bf16[16,8,3584]{2,1,0:T(8,128)(2,1)S(1)}, u32[]{:S(2)}, u32[]{:S(2)}) async-start(bf16[16,8,3584]{2,1,0:T(8,128)(2,1)} %fusion), calls=%async_computation.3 | async-start | bytes 1835008 | tf_op jit(solution)/shard_map/all_to_all | solution.py:204
  136.7 0.0 copy-start.1
  136.7 3.2 %shard_map.69 = bf16[128,3584]{1,0:T(8,128)(2,1)} custom-call(bf16[128,3712]{1,0:T(8,128)(2,1)} %bitcast.8.first, bf16[128,3712]{1,0:T(8,128)(2,1)} %bitcast.25), custom_call_target="tpu_custom_call" | custom-call | flops 100000000 | bytes 5701632 | tf_op jit(solution)/shard_map/pallas_call | solution.py:167
  140.0 1.1 collective-permute-start.10
  141.0 0.0 collective-permute-done.8
  141.0 17.9 %collective-permute-done.9 = bf16[128,3584]{1,0:T(8,128)(2,1)} collective-permute-done((bf16[128,3584]{1,0:T(8,128)(2,1)}, bf16[128,3584]{1,0:T(8,128)(2,1)}, u32[]{:S(2)}, u32[]{:S(2)}) %collective-permute-start.9) | collective-permute-done | bytes 917536 | tf_op jit(solution)/shard_map/ppermute | solution.py:207
  158.9 0.0 copy-done.1
  158.9 2.7 %fusion.1 = bf16[16,8,3584]{2,1,0:T(8,128)(2,1)} fusion(bf16[128,3584]{1,0:T(8,128)(2,1)} %collective-permute-done.9, bf16[128,3584]{1,0:T(8,128)(2,1)} %collective-permute-done.8, bf16[128,3584]{1,0:T(8,128)(2,1)S(1)} %copy-done.1), kind=kLoop, calls=%fused_computation.3 | loop fusion | flops 2752512 | bytes 3670016 | tf_op jit(solution)/shard_map/reshape | solution.py:203
  161.7 0.0 all-to-all-done.3
  161.7 19.2 %all_to_all.31 = bf16[16,8,3584]{2,1,0:T(8,128)(2,1)S(1)} all-to-all(bf16[16,8,3584]{2,1,0:T(8,128)(2,1)} %fusion.1), channel_id=1, replica_groups=mesh['dp'=2,'node'=16,'local'=4] {'node'}, dimensions={0} | all-to-all | bytes 1835008 | tf_op jit(solution)/shard_map/all_to_all | solution.py:204
  180.9 0.0 collective-permute-done.10.far
  180.9 2.4 %shard_map.70 = bf16[128,3584]{1,0:T(8,128)(2,1)} custom-call(bf16[256,128]{1,0:T(8,128)(2,1)} %get-tuple-element.37.pick, bf16[128,3584]{1,0:T(8,128)(2,1)S(1)} %bitcast.20, bf16[128,3584]{1,0:T(8,128)(2,1)S(1)} %bitcast.21, bf16[128,3584]{1,0:T(8,128)(2,1)S(1)} %collective-permute-done.10.far), custom_call_target="tpu_custom_call" | custom-call | flops 100000000 | bytes 8454144 | tf_op jit(solution)/shard_map/pallas_call | solution.py:167
Async XLA Ops:
  28.0 23.0 %collective-permute-start = (bf16[128,3712]{1,0:T(8,128)(2,1)S(1)}, bf16[128,3712]{1,0:T(8,128)(2,1)}, u32[]{:S(2)}, u32[]{:S(2)}) collective-permute-start(bf16[128,3712]{1,0:T(8,128)(2,1)S(1)} %bitcast.17), channel_id=1, source_target_pairs={{0,1},{1,2},{2,3},{3,0},{4,5},{5,6},{6,7},{7,4},{8,9},{9,10},{10,1... | collective-permute-start | bytes 2850824 | tf_op jit(solution)/shard_map/ppermute | solution.py:207
  29.6 21.5 %collective-permute-start.1 = (bf16[128,3712]{1,0:T(8,128)(2,1)S(1)}, bf16[128,3712]{1,0:T(8,128)(2,1)}, u32[]{:S(2)}, u32[]{:S(2)}) collective-permute-start(bf16[128,3712]{1,0:T(8,128)(2,1)S(1)} %bitcast.18), channel_id=1, source_target_pairs={{0,3},{1,0},{2,1},{3,2},{4,7},{5,4},{6,5},{7,6},{8,11},{9,8},{10,9... | collective-permute-start | bytes 2850824 | tf_op jit(solution)/shard_map/ppermute | solution.py:207
  31.2 18.6 %all-to-all-start.1 = ((bf16[16,8,3712]{2,1,0:T(8,128)(2,1)}), bf16[16,8,3712]{2,1,0:T(8,128)(2,1)S(1)}, u32[]{:S(2)}, u32[]{:S(2)}) async-start(bf16[16,8,3712]{2,1,0:T(8,128)(2,1)} %bitcast.26), calls=%async_computation.1 | async-start | bytes 1900544 | tf_op jit(solution)/shard_map/all_to_all | solution.py:204
  51.1 21.0 %collective-permute-start.3 = (bf16[128,3712]{1,0:T(8,128)(2,1)S(1)}, bf16[128,3712]{1,0:T(8,128)(2,1)S(1)}, u32[]{:S(2)}, u32[]{:S(2)}) collective-permute-start(bf16[128,3712]{1,0:T(8,128)(2,1)S(1)} %bitcast.22), channel_id=1, source_target_pairs={{0,3},{1,0},{2,1},{3,2},{4,7},{5,4},{6,5},{7,6},{8,11},{9,8},{10,9... | collective-permute-start | bytes 2850824 | tf_op jit(solution)/shard_map/ppermute | solution.py:207
  54.0 21.7 %collective-permute-start.2 = (bf16[128,3712]{1,0:T(8,128)(2,1)}, bf16[128,3712]{1,0:T(8,128)(2,1)S(1)}, u32[]{:S(2)}, u32[]{:S(2)}) collective-permute-start(bf16[128,3712]{1,0:T(8,128)(2,1)} %collective-permute-done.refs_0_), channel_id=1, source_target_pairs={{0,1},{1,2},{2,3},{3,0},{4,5},{5,6},{6,7},{7,4},{8,9},{9,10},{10,1... | collective-permute-start | bytes 2850824 | tf_op jit(solution)/shard_map/ppermute | solution.py:207
  70.7 21.1 %copy-start = (bf16[128,3584]{1,0:T(8,128)(2,1)}, bf16[128,3584]{1,0:T(8,128)(2,1)S(1)}, u32[]{:S(2)}) copy-start(bf16[128,3584]{1,0:T(8,128)(2,1)S(1)} %get-tuple-element.64) | copy-start | bytes 2752516
  75.6 25.0 %collective-permute-start.4 = (bf16[128,3712]{1,0:T(8,128)(2,1)S(1)}, bf16[128,3712]{1,0:T(8,128)(2,1)}, u32[]{:S(2)}, u32[]{:S(2)}) collective-permute-start(bf16[128,3712]{1,0:T(8,128)(2,1)S(1)} %bitcast.24), channel_id=1, source_target_pairs={{0,1},{1,2},{2,3},{3,0},{4,5},{5,6},{6,7},{7,4},{8,9},{9,10},{10,1... | collective-permute-start | bytes 2850824 | tf_op jit(solution)/shard_map/ppermute | solution.py:207
  75.6 25.0 %collective-permute-start.5 = (bf16[128,3712]{1,0:T(8,128)(2,1)S(1)}, bf16[128,3712]{1,0:T(8,128)(2,1)}, u32[]{:S(2)}, u32[]{:S(2)}) collective-permute-start(bf16[128,3712]{1,0:T(8,128)(2,1)S(1)} %collective-permute-done.3.refs_1_), channel_id=1, source_target_pairs={{0,3},{1,0},{2,1},{3,2},{4,7},{5,4},{6,5},{7,6},{8,11},{9,8},{10,9... | collective-permute-start | bytes 2850824 | tf_op jit(solution)/shard_map/ppermute | solution.py:207
  91.8 27.6 %collective-permute-start.6 = (bf16[128,3584]{1,0:T(8,128)(2,1)}, bf16[128,3584]{1,0:T(8,128)(2,1)}, u32[]{:S(2)}, u32[]{:S(2)}) collective-permute-start(bf16[128,3584]{1,0:T(8,128)(2,1)} %get-tuple-element.57), channel_id=1, source_target_pairs={{0,3},{1,0},{2,1},{3,2},{4,7},{5,4},{6,5},{7,6},{8,11},{9,8},{10,9... | collective-permute-start | bytes 2752520 | tf_op jit(solution)/shard_map/ppermute | solution.py:207
  91.9 27.6 %collective-permute-start.7 = (bf16[128,3584]{1,0:T(8,128)(2,1)}, bf16[128,3584]{1,0:T(8,128)(2,1)}, u32[]{:S(2)}, u32[]{:S(2)}) collective-permute-start(bf16[128,3584]{1,0:T(8,128)(2,1)} %get-tuple-element.58), channel_id=1, source_target_pairs={{0,1},{1,2},{2,3},{3,0},{4,5},{5,6},{6,7},{7,4},{8,9},{9,10},{10,1... | collective-permute-start | bytes 2752520 | tf_op jit(solution)/shard_map/ppermute | solution.py:207
  93.9 20.9 %all-to-all-start.2 = ((bf16[16,8,3712]{2,1,0:T(8,128)(2,1)}), bf16[16,8,3712]{2,1,0:T(8,128)(2,1)}, u32[]{:S(2)}, u32[]{:S(2)}) async-start(bf16[16,8,3712]{2,1,0:T(8,128)(2,1)} %bitcast.7), calls=%async_computation.2 | async-start | bytes 1900544 | tf_op jit(solution)/shard_map/all_to_all | solution.py:204
  114.7 17.4 %all-to-all-start.5 = ((bf16[16,8,3712]{2,1,0:T(8,128)(2,1)}), bf16[16,8,3712]{2,1,0:T(8,128)(2,1)S(1)}, u32[]{:S(2)}, u32[]{:S(2)}) async-start(bf16[16,8,3712]{2,1,0:T(8,128)(2,1)} %bitcast.13), calls=%async_computation.5 | async-start | bytes 1900544 | tf_op jit(solution)/shard_map/all_to_all | solution.py:204
  119.4 21.6 %collective-permute-start.8 = (bf16[128,3584]{1,0:T(8,128)(2,1)}, bf16[128,3584]{1,0:T(8,128)(2,1)}, u32[]{:S(2)}, u32[]{:S(2)}) collective-permute-start(bf16[128,3584]{1,0:T(8,128)(2,1)} %get-tuple-element.65), channel_id=1, source_target_pairs={{0,3},{1,0},{2,1},{3,2},{4,7},{5,4},{6,5},{7,6},{8,11},{9,8},{10,9... | collective-permute-start | bytes 2752520 | tf_op jit(solution)/shard_map/ppermute | solution.py:207
  122.3 36.6 %collective-permute-start.9 = (bf16[128,3584]{1,0:T(8,128)(2,1)}, bf16[128,3584]{1,0:T(8,128)(2,1)}, u32[]{:S(2)}, u32[]{:S(2)}) collective-permute-start(bf16[128,3584]{1,0:T(8,128)(2,1)} %get-tuple-element.66), channel_id=1, source_target_pairs={{0,1},{1,2},{2,3},{3,0},{4,5},{5,6},{6,7},{7,4},{8,9},{9,10},{10,1... | collective-permute-start | bytes 2752520 | tf_op jit(solution)/shard_map/ppermute | solution.py:207
  132.1 0.9 copy-start.2
  133.1 28.6 %all-to-all-start.3 = ((bf16[16,8,3584]{2,1,0:T(8,128)(2,1)}), bf16[16,8,3584]{2,1,0:T(8,128)(2,1)S(1)}, u32[]{:S(2)}, u32[]{:S(2)}) async-start(bf16[16,8,3584]{2,1,0:T(8,128)(2,1)} %fusion), calls=%async_computation.3 | async-start | bytes 1835008 | tf_op jit(solution)/shard_map/all_to_all | solution.py:204
  136.7 22.2 %copy-start.1 = (bf16[128,3584]{1,0:T(8,128)(2,1)S(1)}, bf16[128,3584]{1,0:T(8,128)(2,1)}, u32[]{:S(2)}) copy-start(bf16[128,3584]{1,0:T(8,128)(2,1)} %copy-done) | copy-start | bytes 2752516
  140.0 40.9 %collective-permute-start.10 = (bf16[128,3584]{1,0:T(8,128)(2,1)}, bf16[128,3584]{1,0:T(8,128)(2,1)S(1)}, u32[]{:S(2)}, u32[]{:S(2)}) collective-permute-start(bf16[128,3584]{1,0:T(8,128)(2,1)} %shard_map.69), channel_id=1, source_target_pairs={{0,2},{1,3},{2,0},{3,1},{4,6},{5,7},{6,4},{7,5},{8,10},{9,11},{10,... | collective-permute-start | bytes 2752520 | tf_op jit(solution)/shard_map/ppermute | solution.py:207

commit v12 on v11

--- a/solution.py
+++ b/solution.py
@@ -249,10 +249,12 @@
         functools.partial(scatter_kernel, locals_),
         jax.ShapeDtypeStruct(tokens.shape, jnp.bfloat16), home_a, home_b,
     )
+    last_above, last_below = down(below_pb), up(above_pb)
+    far, last_above, last_below = tie((far, last_above, last_below))
     far = shift(far, locals_ // 2)
 
     final_a = across(add(own_pa, from_above, from_below))
-    final_b = across(add(own_pb, down(below_pb), up(above_pb)))
+    final_b = across(add(own_pb, last_above, last_below))
     near = [pltpu.with_memory_space_constraint(x, pltpu.VMEM) for x in (final_a, final_b, far)]
     return whole(collect_kernel, jax.ShapeDtypeStruct(tokens.shape, jnp.bfloat16), pick, *near)
 

time: 184 us -> 175 us (0.951)
  waiting for transfers between devices: 38.9 us -> 30.1 us
    ppermute x11, waiting for transfers between devices: 26.5 us -> 17.7 us  [shift(): lax.ppermute(block, 'local', [(i, (i + by) % locals_) for i in range(loca...]
  transfers between devices with their start and end apart: 15 -> 15, of which waited for: 7 -> 7; matrix products, arithmetic and copies ran while one was open for 3% -> 3% of each run, Pallas kernels for 31% -> 33%
where the time goes in v12:
time: 175 us; the launch traced here: 173 us
  Pallas kernels  63 us (36%)
  blocking collectives  43.3 us (25%)
  starting transfers between devices  30.6 us (17%)
  waiting for transfers between devices  30.1 us (17%)
  other arithmetic  5.44 us (3%)
    pallas_call x4, Pallas kernels, experts(): pl.pallas_call(functools.partial(expert_kernel, blocks), grid=(hidden //...  53.4 us
    all_to_all x2, blocking collectives, across(): return lax.all_to_all(parts, 'node', 0, 0, tiled=True).reshape(block.shape)  43.3 us
    ppermute x11, waiting for transfers between devices, shift(): lax.ppermute(block, 'local', [(i, (i + by) % locals_) for i in range(loca...  17.7 us
    all_to_all x4, starting transfers between devices, across(): return lax.all_to_all(parts, 'node', 0, 0, tiled=True).reshape(block.shape)  16.3 us
    ppermute x11, starting transfers between devices, shift(): lax.ppermute(block, 'local', [(i, (i + by) % locals_) for i in range(loca...  14.3 us
    all_to_all x4, waiting for transfers between devices, across(): return lax.all_to_all(parts, 'node', 0, 0, tiled=True).reshape(block.shape)  12.4 us
    pallas_call x2, Pallas kernels, whole(): pl.pallas_call(kernel, out_shape=shapes, compiler_params=pltpu.CompilerPa...  5.67 us
    reshape x2, other arithmetic, across(): parts = block.reshape(groups, block.shape[0] // groups, block.shape[1])  5.44 us
  transfers between devices with their start and end apart: 15, of which 7 were waited for; matrix products, arithmetic and copies ran while one was open for 3% of the time, Pallas kernels for 33%

profile of v12, /device:TPU:0, one launch (start us, length us, event | category | flops | bytes accessed | tf_op | source)
XLA Modules:
  0.0 173.5 jit_solution(16425067483113496937)
XLA Ops:
  0.0 3.9 %shard_map.64 = (bf16[128,3712]{1,0:T(8,128)(2,1)}, bf16[128,3712]{1,0:T(8,128)(2,1)}, bf16[256,128]{1,0:T(8,128)(2,1)}) custom-call(bf16[128,3584]{1,0:T(8,128)(2,1)} %tok.1, f32[4,128]{1,0:T(4,128)} %bitcast.28, s32[4,128]{1,0:T(4,128)} %bitcast.29), custom_call_target="tpu_custom_call" | custom-call | flops 1000000000 | bytes 3000000 | tf_op jit(solution)/shard_map/pallas_call | solution.py:82
  3.9 24.1 %all_to_all.30 = bf16[16,8,3712]{2,1,0:T(8,128)(2,1)S(1)} all-to-all(bf16[16,8,3712]{2,1,0:T(8,128)(2,1)} %bitcast.27), channel_id=1, replica_groups=mesh['dp'=2,'node'=16,'local'=4] {'node'}, dimensions={0} | all-to-all | bytes 1900544 | tf_op jit(solution)/shard_map/all_to_all | solution.py:204
  28.0 1.6 collective-permute-start
  29.6 1.7 collective-permute-start.1
  31.2 3.6 %all-to-all-start.1 = ((bf16[16,8,3712]{2,1,0:T(8,128)(2,1)}), bf16[16,8,3712]{2,1,0:T(8,128)(2,1)S(1)}, u32[]{:S(2)}, u32[]{:S(2)}) async-start(bf16[16,8,3712]{2,1,0:T(8,128)(2,1)} %bitcast.26), calls=%async_computation.1 | async-start | bytes 1900544 | tf_op jit(solution)/shard_map/all_to_all | solution.py:204
  34.9 9.6 %shard_map.65 = bf16[128,3584]{1,0:T(8,128)(2,1)S(1)} custom-call(s32[1]{0:T(128)} %bitcast.6.local_ref, bf16[128,3712]{1,0:T(8,128)(2,1)S(1)} %bitcast.19, bf16[1,3584,1024]{2,1,0:T(8,128)(2,1)} %refs_2_.5, bf16[1,3584,1024]{2,1,0:T(8,128)(2,1)} %refs_3_.7, bf16[1,1024,3584]{2,1,0:T(8,128)(2,1)} %refs_4_.5), custom_call_target="tpu_custom_call" | custom-call | flops 2818572288 | bytes 22020096 | tf_op jit(solution)/shard_map/pallas_call | solution.py:138
  44.5 5.3 %all-to-all-done.1 = bf16[16,8,3712]{2,1,0:T(8,128)(2,1)S(1)} async-done(((bf16[16,8,3712]{2,1,0:T(8,128)(2,1)}), bf16[16,8,3712]{2,1,0:T(8,128)(2,1)S(1)}, u32[]{:S(2)}, u32[]{:S(2)}) %all-to-all-start.1) | async-done | bytes 950304 | tf_op jit(solution)/shard_map/all_to_all | solution.py:204
  49.9 1.2 collective-permute-done.refs_0_
  51.0 0.0 collective-permute-done.1.refs_1_
  51.1 2.9 %collective-permute-start.3 = (bf16[128,3712]{1,0:T(8,128)(2,1)S(1)}, bf16[128,3712]{1,0:T(8,128)(2,1)S(1)}, u32[]{:S(2)}, u32[]{:S(2)}) collective-permute-start(bf16[128,3712]{1,0:T(8,128)(2,1)S(1)} %bitcast.22), channel_id=1, source_target_pairs={{0,3},{1,0},{2,1},{3,2},{4,7},{5,4},{6,5},{7,6},{8,11},{9,8},{10,9... | collective-permute-start | bytes 2850824 | tf_op jit(solution)/shard_map/ppermute | solution.py:207
  54.0 0.0 collective-permute-start.2
  54.0 16.7 %shard_map.66 = (bf16[128,3584]{1,0:T(8,128)(2,1)}, bf16[128,3584]{1,0:T(8,128)(2,1)}, bf16[128,3584]{1,0:T(8,128)(2,1)S(1)}) custom-call(s32[1]{0:T(128)} %bitcast.6.local_ref, bf16[128,3712]{1,0:T(8,128)(2,1)} %collective-permute-done.refs_0_, bf16[128,3712]{1,0:T(8,128)(2,1)} %collective-permute-done.1.refs_1_, bf16[128,3712]{1,0:T(8,128)(2,1)S(1)} %bitcast.23, ...), custom_call_target="tpu_custom_call" | custom-call | flops 8455716864 | bytes 22020096 | tf_op jit(solution)/shard_map/pallas_call | solution.py:138
  70.7 0.0 copy-start
  70.7 1.3 collective-permute-done.3.refs_1_
  72.0 3.6 %collective-permute-done.2.refs_0_ = bf16[128,3712]{1,0:T(8,128)(2,1)S(1)} collective-permute-done((bf16[128,3712]{1,0:T(8,128)(2,1)}, bf16[128,3712]{1,0:T(8,128)(2,1)S(1)}, u32[]{:S(2)}, u32[]{:S(2)}) %collective-permute-start.2) | collective-permute-done | bytes 950304 | tf_op jit(solution)/shard_map/ppermute | solution.py:207
  75.6 0.0 collective-permute-start.4
  75.6 3.2 %collective-permute-start.5 = (bf16[128,3712]{1,0:T(8,128)(2,1)S(1)}, bf16[128,3712]{1,0:T(8,128)(2,1)}, u32[]{:S(2)}, u32[]{:S(2)}) collective-permute-start(bf16[128,3712]{1,0:T(8,128)(2,1)S(1)} %collective-permute-done.3.refs_1_), channel_id=1, source_target_pairs={{0,3},{1,0},{2,1},{3,2},{4,7},{5,4},{6,5},{7,6},{8,11},{9,8},{10,9... | collective-permute-start | bytes 2850824 | tf_op jit(solution)/shard_map/ppermute | solution.py:207
  78.9 13.0 %shard_map.67 = (bf16[128,3712]{1,0:T(8,128)(2,1)}, bf16[128,3584]{1,0:T(8,128)(2,1)}) custom-call(s32[1]{0:T(128)} %bitcast.6.local_ref, bf16[128,3712]{1,0:T(8,128)(2,1)S(1)} %collective-permute-done.2.refs_0_, bf16[128,3712]{1,0:T(8,128)(2,1)S(1)} %collective-permute-done.3.refs_1_, bf16[1,3584,1024]{2,1,0:T(8,128)(2,1)} %refs_2_.5, ...), custom_call_target="tpu_custom_call" | custom-call | flops 5637144576 | bytes 22020096 | tf_op jit(solution)/shard_map/pallas_call | solution.py:138
  91.8 0.0 copy-done
  91.8 0.0 collective-permute-start.6
  91.9 2.0 %collective-permute-start.7 = (bf16[128,3584]{1,0:T(8,128)(2,1)}, bf16[128,3584]{1,0:T(8,128)(2,1)}, u32[]{:S(2)}, u32[]{:S(2)}) collective-permute-start(bf16[128,3584]{1,0:T(8,128)(2,1)} %get-tuple-element.61), channel_id=1, source_target_pairs={{0,1},{1,2},{2,3},{3,0},{4,5},{5,6},{6,7},{7,4},{8,9},{9,10},{10,1... | collective-permute-start | bytes 2752520 | tf_op jit(solution)/shard_map/ppermute | solution.py:207
  93.9 4.3 %all-to-all-start.2 = ((bf16[16,8,3712]{2,1,0:T(8,128)(2,1)}), bf16[16,8,3712]{2,1,0:T(8,128)(2,1)}, u32[]{:S(2)}, u32[]{:S(2)}) async-start(bf16[16,8,3712]{2,1,0:T(8,128)(2,1)} %bitcast.7), calls=%async_computation.2 | async-start | bytes 1900544 | tf_op jit(solution)/shard_map/all_to_all | solution.py:204
  98.2 2.5 %collective-permute-done.4.refs_0_ = bf16[128,3712]{1,0:T(8,128)(2,1)} collective-permute-done((bf16[128,3712]{1,0:T(8,128)(2,1)S(1)}, bf16[128,3712]{1,0:T(8,128)(2,1)}, u32[]{:S(2)}, u32[]{:S(2)}) %collective-permute-start.4) | collective-permute-done | bytes 950304 | tf_op jit(solution)/shard_map/ppermute | solution.py:207
  100.6 0.0 collective-permute-done.5.refs_1_
  100.6 14.1 %shard_map.68 = (bf16[128,3584]{1,0:T(8,128)(2,1)}, bf16[128,3712]{1,0:T(8,128)(2,1)}) custom-call(s32[1]{0:T(128)} %bitcast.6.local_ref, bf16[128,3712]{1,0:T(8,128)(2,1)} %collective-permute-done.4.refs_0_, bf16[128,3712]{1,0:T(8,128)(2,1)} %collective-permute-done.5.refs_1_, bf16[1,3584,1024]{2,1,0:T(8,128)(2,1)} %refs_2_.5, ...), custom_call_target="tpu_custom_call" | custom-call | flops 5637144576 | bytes 22020096 | tf_op jit(solution)/shard_map/pallas_call | solution.py:138
  114.7 0.0 all-to-all-done.2
  114.7 4.7 %all-to-all-start.4 = ((bf16[16,8,3712]{2,1,0:T(8,128)(2,1)}), bf16[16,8,3712]{2,1,0:T(8,128)(2,1)S(1)}, u32[]{:S(2)}, u32[]{:S(2)}) async-start(bf16[16,8,3712]{2,1,0:T(8,128)(2,1)} %bitcast.11), calls=%async_computation.4 | async-start | bytes 1900544 | tf_op jit(solution)/shard_map/all_to_all | solution.py:204
  119.4 0.0 collective-permute-done.6
  119.4 0.0 collective-permute-done.7
  119.4 2.9 %collective-permute-start.8 = (bf16[128,3584]{1,0:T(8,128)(2,1)}, bf16[128,3584]{1,0:T(8,128)(2,1)}, u32[]{:S(2)}, u32[]{:S(2)}) collective-permute-start(bf16[128,3584]{1,0:T(8,128)(2,1)} %get-tuple-element.70), channel_id=1, source_target_pairs={{0,3},{1,0},{2,1},{3,2},{4,7},{5,4},{6,5},{7,6},{8,11},{9,8},{10,9... | collective-permute-start | bytes 2752520 | tf_op jit(solution)/shard_map/ppermute | solution.py:207
  122.3 0.0 collective-permute-start.9
  122.3 2.7 %fusion = bf16[16,8,3584]{2,1,0:T(8,128)(2,1)} fusion(bf16[128,3584]{1,0:T(8,128)(2,1)} %collective-permute-done.7, bf16[128,3584]{1,0:T(8,128)(2,1)} %collective-permute-done.6, bf16[128,3584]{1,0:T(8,128)(2,1)S(1)} %shard_map.65), kind=kLoop, calls=%fused_computation.2 | loop fusion | flops 2752512 | bytes 3670016 | tf_op jit(solution)/shard_map/reshape | solution.py:203
  125.1 7.1 %all-to-all-done.4 = bf16[16,8,3712]{2,1,0:T(8,128)(2,1)S(1)} async-done(((bf16[16,8,3712]{2,1,0:T(8,128)(2,1)}), bf16[16,8,3712]{2,1,0:T(8,128)(2,1)S(1)}, u32[]{:S(2)}, u32[]{:S(2)}) %all-to-all-start.4) | async-done | bytes 950304 | tf_op jit(solution)/shard_map/all_to_all | solution.py:204
  132.1 0.0 copy-start.2
  132.1 0.9 copy-done.2
  133.1 3.6 %all-to-all-start.3 = ((bf16[16,8,3584]{2,1,0:T(8,128)(2,1)}), bf16[16,8,3584]{2,1,0:T(8,128)(2,1)S(1)}, u32[]{:S(2)}, u32[]{:S(2)}) async-start(bf16[16,8,3584]{2,1,0:T(8,128)(2,1)} %fusion), calls=%async_computation.3 | async-start | bytes 1835008 | tf_op jit(solution)/shard_map/all_to_all | solution.py:204
  136.7 0.0 copy-start.1
  136.7 3.2 %shard_map.69 = bf16[128,3584]{1,0:T(8,128)(2,1)} custom-call(bf16[128,3712]{1,0:T(8,128)(2,1)} %bitcast.8.first, bf16[128,3712]{1,0:T(8,128)(2,1)} %bitcast.25), custom_call_target="tpu_custom_call" | custom-call | flops 100000000 | bytes 5701632 | tf_op jit(solution)/shard_map/pallas_call | solution.py:167
  140.0 0.0 collective-permute-done.8
  140.0 9.1 %collective-permute-done.9 = bf16[128,3584]{1,0:T(8,128)(2,1)} collective-permute-done((bf16[128,3584]{1,0:T(8,128)(2,1)}, bf16[128,3584]{1,0:T(8,128)(2,1)}, u32[]{:S(2)}, u32[]{:S(2)}) %collective-permute-start.9) | collective-permute-done | bytes 917536 | tf_op jit(solution)/shard_map/ppermute | solution.py:207
  149.1 0.0 collective-permute-start.10
  149.1 0.0 copy-done.1
  149.1 2.7 %fusion.1 = bf16[16,8,3584]{2,1,0:T(8,128)(2,1)} fusion(bf16[128,3584]{1,0:T(8,128)(2,1)} %collective-permute-done.9, bf16[128,3584]{1,0:T(8,128)(2,1)} %collective-permute-done.8, bf16[128,3584]{1,0:T(8,128)(2,1)S(1)} %copy-done.1), kind=kLoop, calls=%fused_computation.3 | loop fusion | flops 2752512 | bytes 3670016 | tf_op jit(solution)/shard_map/reshape | solution.py:203
  151.8 0.0 all-to-all-done.3
  151.8 19.2 %all_to_all.31 = bf16[16,8,3584]{2,1,0:T(8,128)(2,1)S(1)} all-to-all(bf16[16,8,3584]{2,1,0:T(8,128)(2,1)} %fusion.1), channel_id=1, replica_groups=mesh['dp'=2,'node'=16,'local'=4] {'node'}, dimensions={0} | all-to-all | bytes 1835008 | tf_op jit(solution)/shard_map/all_to_all | solution.py:204
  171.1 0.0 collective-permute-done.10.far
  171.1 2.4 %shard_map.70 = bf16[128,3584]{1,0:T(8,128)(2,1)} custom-call(bf16[256,128]{1,0:T(8,128)(2,1)} %get-tuple-element.40.pick, bf16[128,3584]{1,0:T(8,128)(2,1)S(1)} %bitcast.20, bf16[128,3584]{1,0:T(8,128)(2,1)S(1)} %bitcast.21, bf16[128,3584]{1,0:T(8,128)(2,1)S(1)} %collective-permute-done.10.far), custom_call_target="tpu_custom_call" | custom-call | flops 100000000 | bytes 8454144 | tf_op jit(solution)/shard_map/pallas_call | solution.py:167
Async XLA Ops:
  28.0 23.0 %collective-permute-start = (bf16[128,3712]{1,0:T(8,128)(2,1)S(1)}, bf16[128,3712]{1,0:T(8,128)(2,1)}, u32[]{:S(2)}, u32[]{:S(2)}) collective-permute-start(bf16[128,3712]{1,0:T(8,128)(2,1)S(1)} %bitcast.17), channel_id=1, source_target_pairs={{0,1},{1,2},{2,3},{3,0},{4,5},{5,6},{6,7},{7,4},{8,9},{9,10},{10,1... | collective-permute-start | bytes 2850824 | tf_op jit(solution)/shard_map/ppermute | solution.py:207
  29.6 21.5 %collective-permute-start.1 = (bf16[128,3712]{1,0:T(8,128)(2,1)S(1)}, bf16[128,3712]{1,0:T(8,128)(2,1)}, u32[]{:S(2)}, u32[]{:S(2)}) collective-permute-start(bf16[128,3712]{1,0:T(8,128)(2,1)S(1)} %bitcast.18), channel_id=1, source_target_pairs={{0,3},{1,0},{2,1},{3,2},{4,7},{5,4},{6,5},{7,6},{8,11},{9,8},{10,9... | collective-permute-start | bytes 2850824 | tf_op jit(solution)/shard_map/ppermute | solution.py:207
  31.2 18.6 %all-to-all-start.1 = ((bf16[16,8,3712]{2,1,0:T(8,128)(2,1)}), bf16[16,8,3712]{2,1,0:T(8,128)(2,1)S(1)}, u32[]{:S(2)}, u32[]{:S(2)}) async-start(bf16[16,8,3712]{2,1,0:T(8,128)(2,1)} %bitcast.26), calls=%async_computation.1 | async-start | bytes 1900544 | tf_op jit(solution)/shard_map/all_to_all | solution.py:204
  51.1 21.0 %collective-permute-start.3 = (bf16[128,3712]{1,0:T(8,128)(2,1)S(1)}, bf16[128,3712]{1,0:T(8,128)(2,1)S(1)}, u32[]{:S(2)}, u32[]{:S(2)}) collective-permute-start(bf16[128,3712]{1,0:T(8,128)(2,1)S(1)} %bitcast.22), channel_id=1, source_target_pairs={{0,3},{1,0},{2,1},{3,2},{4,7},{5,4},{6,5},{7,6},{8,11},{9,8},{10,9... | collective-permute-start | bytes 2850824 | tf_op jit(solution)/shard_map/ppermute | solution.py:207
  54.0 21.7 %collective-permute-start.2 = (bf16[128,3712]{1,0:T(8,128)(2,1)}, bf16[128,3712]{1,0:T(8,128)(2,1)S(1)}, u32[]{:S(2)}, u32[]{:S(2)}) collective-permute-start(bf16[128,3712]{1,0:T(8,128)(2,1)} %collective-permute-done.refs_0_), channel_id=1, source_target_pairs={{0,1},{1,2},{2,3},{3,0},{4,5},{5,6},{6,7},{7,4},{8,9},{9,10},{10,1... | collective-permute-start | bytes 2850824 | tf_op jit(solution)/shard_map/ppermute | solution.py:207
  70.7 21.1 %copy-start = (bf16[128,3584]{1,0:T(8,128)(2,1)}, bf16[128,3584]{1,0:T(8,128)(2,1)S(1)}, u32[]{:S(2)}) copy-start(bf16[128,3584]{1,0:T(8,128)(2,1)S(1)} %get-tuple-element.67) | copy-start | bytes 2752516
  75.6 25.0 %collective-permute-start.4 = (bf16[128,3712]{1,0:T(8,128)(2,1)S(1)}, bf16[128,3712]{1,0:T(8,128)(2,1)}, u32[]{:S(2)}, u32[]{:S(2)}) collective-permute-start(bf16[128,3712]{1,0:T(8,128)(2,1)S(1)} %bitcast.24), channel_id=1, source_target_pairs={{0,1},{1,2},{2,3},{3,0},{4,5},{5,6},{6,7},{7,4},{8,9},{9,10},{10,1... | collective-permute-start | bytes 2850824 | tf_op jit(solution)/shard_map/ppermute | solution.py:207
  75.6 25.0 %collective-permute-start.5 = (bf16[128,3712]{1,0:T(8,128)(2,1)S(1)}, bf16[128,3712]{1,0:T(8,128)(2,1)}, u32[]{:S(2)}, u32[]{:S(2)}) collective-permute-start(bf16[128,3712]{1,0:T(8,128)(2,1)S(1)} %collective-permute-done.3.refs_1_), channel_id=1, source_target_pairs={{0,3},{1,0},{2,1},{3,2},{4,7},{5,4},{6,5},{7,6},{8,11},{9,8},{10,9... | collective-permute-start | bytes 2850824 | tf_op jit(solution)/shard_map/ppermute | solution.py:207
  91.8 27.6 %collective-permute-start.6 = (bf16[128,3584]{1,0:T(8,128)(2,1)}, bf16[128,3584]{1,0:T(8,128)(2,1)}, u32[]{:S(2)}, u32[]{:S(2)}) collective-permute-start(bf16[128,3584]{1,0:T(8,128)(2,1)} %get-tuple-element.60), channel_id=1, source_target_pairs={{0,3},{1,0},{2,1},{3,2},{4,7},{5,4},{6,5},{7,6},{8,11},{9,8},{10,9... | collective-permute-start | bytes 2752520 | tf_op jit(solution)/shard_map/ppermute | solution.py:207
  91.9 27.6 %collective-permute-start.7 = (bf16[128,3584]{1,0:T(8,128)(2,1)}, bf16[128,3584]{1,0:T(8,128)(2,1)}, u32[]{:S(2)}, u32[]{:S(2)}) collective-permute-start(bf16[128,3584]{1,0:T(8,128)(2,1)} %get-tuple-element.61), channel_id=1, source_target_pairs={{0,1},{1,2},{2,3},{3,0},{4,5},{5,6},{6,7},{7,4},{8,9},{9,10},{10,1... | collective-permute-start | bytes 2752520 | tf_op jit(solution)/shard_map/ppermute | solution.py:207
  93.9 20.9 %all-to-all-start.2 = ((bf16[16,8,3712]{2,1,0:T(8,128)(2,1)}), bf16[16,8,3712]{2,1,0:T(8,128)(2,1)}, u32[]{:S(2)}, u32[]{:S(2)}) async-start(bf16[16,8,3712]{2,1,0:T(8,128)(2,1)} %bitcast.7), calls=%async_computation.2 | async-start | bytes 1900544 | tf_op jit(solution)/shard_map/all_to_all | solution.py:204
  114.7 17.4 %all-to-all-start.4 = ((bf16[16,8,3712]{2,1,0:T(8,128)(2,1)}), bf16[16,8,3712]{2,1,0:T(8,128)(2,1)S(1)}, u32[]{:S(2)}, u32[]{:S(2)}) async-start(bf16[16,8,3712]{2,1,0:T(8,128)(2,1)} %bitcast.11), calls=%async_computation.4 | async-start | bytes 1900544 | tf_op jit(solution)/shard_map/all_to_all | solution.py:204
  119.4 20.5 %collective-permute-start.8 = (bf16[128,3584]{1,0:T(8,128)(2,1)}, bf16[128,3584]{1,0:T(8,128)(2,1)}, u32[]{:S(2)}, u32[]{:S(2)}) collective-permute-start(bf16[128,3584]{1,0:T(8,128)(2,1)} %get-tuple-element.70), channel_id=1, source_target_pairs={{0,3},{1,0},{2,1},{3,2},{4,7},{5,4},{6,5},{7,6},{8,11},{9,8},{10,9... | collective-permute-start | bytes 2752520 | tf_op jit(solution)/shard_map/ppermute | solution.py:207
  122.3 26.8 %collective-permute-start.9 = (bf16[128,3584]{1,0:T(8,128)(2,1)}, bf16[128,3584]{1,0:T(8,128)(2,1)}, u32[]{:S(2)}, u32[]{:S(2)}) collective-permute-start(bf16[128,3584]{1,0:T(8,128)(2,1)} %get-tuple-element.71), channel_id=1, source_target_pairs={{0,1},{1,2},{2,3},{3,0},{4,5},{5,6},{6,7},{7,4},{8,9},{9,10},{10,1... | collective-permute-start | bytes 2752520 | tf_op jit(solution)/shard_map/ppermute | solution.py:207
  132.1 0.9 copy-start.2
  133.1 18.8 %all-to-all-start.3 = ((bf16[16,8,3584]{2,1,0:T(8,128)(2,1)}), bf16[16,8,3584]{2,1,0:T(8,128)(2,1)S(1)}, u32[]{:S(2)}, u32[]{:S(2)}) async-start(bf16[16,8,3584]{2,1,0:T(8,128)(2,1)} %fusion), calls=%async_computation.3 | async-start | bytes 1835008 | tf_op jit(solution)/shard_map/all_to_all | solution.py:204
  136.7 12.4 %copy-start.1 = (bf16[128,3584]{1,0:T(8,128)(2,1)S(1)}, bf16[128,3584]{1,0:T(8,128)(2,1)}, u32[]{:S(2)}) copy-start(bf16[128,3584]{1,0:T(8,128)(2,1)} %copy-done) | copy-start | bytes 2752516
  149.1 22.0 %collective-permute-start.10 = (bf16[128,3584]{1,0:T(8,128)(2,1)}, bf16[128,3584]{1,0:T(8,128)(2,1)S(1)}, u32[]{:S(2)}, u32[]{:S(2)}) collective-permute-start(bf16[128,3584]{1,0:T(8,128)(2,1)} %shard_map.69), channel_id=1, source_target_pairs={{0,2},{1,3},{2,0},{3,1},{4,6},{5,7},{6,4},{7,5},{8,10},{9,11},{10,... | collective-permute-start | bytes 2752520 | tf_op jit(solution)/shard_map/ppermute | solution.py:207

commit v13 on v12

--- a/solution.py
+++ b/solution.py
@@ -230,8 +230,9 @@
     far_a, above_b = up(below_a), down(next_b)
     kept = pltpu.with_memory_space_constraint(next_b, pltpu.VMEM)
     below_pa, above_pa, own_pb = run([below_a, above_a, kept], ())
-    far_a, above_b, last_b, below_pa = tie((far_a, above_b, next_b, below_pa))
-    below_b, far_b = up(last_b), down(above_b)
+    below_b = up(next_b)
+    far_a, above_b, below_pa = tie((far_a, above_b, below_pa))
+    far_b = down(above_b)
     far_pa, above_pb = run([far_a, above_b], (0,))
     below_pa, above_pa, far_pa = tie((below_pa, above_pa, far_pa))
     below_b, far_b, above_pb = tie((below_b, far_b, above_pb))
@@ -250,11 +251,11 @@
         jax.ShapeDtypeStruct(tokens.shape, jnp.bfloat16), home_a, home_b,
     )
     last_above, last_below = down(below_pb), up(above_pb)
-    far, last_above, last_below = tie((far, last_above, last_below))
+    total_b, far = tie((add(own_pb, last_above, last_below), far))
     far = shift(far, locals_ // 2)
 
     final_a = across(add(own_pa, from_above, from_below))
-    final_b = across(add(own_pb, last_above, last_below))
+    final_b = across(total_b)
     near = [pltpu.with_memory_space_constraint(x, pltpu.VMEM) for x in (final_a, final_b, far)]
     return whole(collect_kernel, jax.ShapeDtypeStruct(tokens.shape, jnp.bfloat16), pick, *near)
 

time: 175 us -> 171 us (0.977)
  blocking collectives: 43.3 us -> 39.9 us
    all_to_all x4, waiting for transfers between devices: 12.4 us -> 19.3 us  [across(): return lax.all_to_all(parts, 'node', 0, 0, tiled=True).reshape(block.shape)]
    ppermute x11, waiting for transfers between devices: 17.7 us -> 11.4 us  [shift(): lax.ppermute(block, 'local', [(i, (i + by) % locals_) for i in range(loca...]
    all_to_all x2, blocking collectives: 43.3 us -> 39.9 us  [across(): return lax.all_to_all(parts, 'node', 0, 0, tiled=True).reshape(block.shape)]
    reshape x2 -> x1, other arithmetic: 5.44 us -> 2.71 us  [across(): parts = block.reshape(groups, block.shape[0] // groups, block.shape[1])]
    convert_element_type x0 -> x1, other arithmetic: none -> 2.46 us  [add(): return total.astype(jnp.bfloat16)]
  transfers between devices with their start and end apart: 15 -> 15, of which waited for: 7 -> 8; matrix products, arithmetic and copies ran while one was open for 3% -> 3% of each run, Pallas kernels for 33% -> 34%
where the time goes in v13:
time: 171 us; the launch traced here: 170 us
  Pallas kernels  63.3 us (37%)
  blocking collectives  39.9 us (23%)
  waiting for transfers between devices  30.7 us (18%)
  starting transfers between devices  29.7 us (17%)
  other arithmetic  5.16 us (3%)
    pallas_call x4, Pallas kernels, experts(): pl.pallas_call(functools.partial(expert_kernel, blocks), grid=(hidden //...  53.7 us
    all_to_all x2, blocking collectives, across(): return lax.all_to_all(parts, 'node', 0, 0, tiled=True).reshape(block.shape)  39.9 us
    all_to_all x4, waiting for transfers between devices, across(): return lax.all_to_all(parts, 'node', 0, 0, tiled=True).reshape(block.shape)  19.3 us
    all_to_all x4, starting transfers between devices, across(): return lax.all_to_all(parts, 'node', 0, 0, tiled=True).reshape(block.shape)  16.6 us
    ppermute x11, starting transfers between devices, shift(): lax.ppermute(block, 'local', [(i, (i + by) % locals_) for i in range(loca...  13.1 us
    ppermute x11, waiting for transfers between devices, shift(): lax.ppermute(block, 'local', [(i, (i + by) % locals_) for i in range(loca...  11.4 us
    pallas_call x2, Pallas kernels, whole(): pl.pallas_call(kernel, out_shape=shapes, compiler_params=pltpu.CompilerPa...  5.66 us
    pallas_call x1, Pallas kernels, prepare(): pl.pallas_call(functools.partial(prepare_kernel, locals_, groups, per_gro...  3.95 us
  transfers between devices with their start and end apart: 15, of which 8 were waited for; matrix products, arithmetic and copies ran while one was open for 3% of the time, Pallas kernels for 34%

profile of v13, /device:TPU:0, one launch (start us, length us, event | category | flops | bytes accessed | tf_op | source)
XLA Modules:
  0.0 169.8 jit_solution(1519837689160415467)
XLA Ops:
  0.0 3.9 %shard_map.64 = (bf16[128,3712]{1,0:T(8,128)(2,1)}, bf16[128,3712]{1,0:T(8,128)(2,1)}, bf16[256,128]{1,0:T(8,128)(2,1)}) custom-call(bf16[128,3584]{1,0:T(8,128)(2,1)} %tok.1, f32[4,128]{1,0:T(4,128)} %bitcast.28, s32[4,128]{1,0:T(4,128)} %bitcast.29), custom_call_target="tpu_custom_call" | custom-call | flops 1000000000 | bytes 3000000 | tf_op jit(solution)/shard_map/pallas_call | solution.py:82
  3.9 24.1 %all_to_all.30 = bf16[16,8,3712]{2,1,0:T(8,128)(2,1)S(1)} all-to-all(bf16[16,8,3712]{2,1,0:T(8,128)(2,1)} %bitcast.27), channel_id=1, replica_groups=mesh['dp'=2,'node'=16,'local'=4] {'node'}, dimensions={0} | all-to-all | bytes 1900544 | tf_op jit(solution)/shard_map/all_to_all | solution.py:204
  28.0 1.6 collective-permute-start
  29.6 1.7 collective-permute-start.1
  31.2 3.6 %all-to-all-start.1 = ((bf16[16,8,3712]{2,1,0:T(8,128)(2,1)}), bf16[16,8,3712]{2,1,0:T(8,128)(2,1)S(1)}, u32[]{:S(2)}, u32[]{:S(2)}) async-start(bf16[16,8,3712]{2,1,0:T(8,128)(2,1)} %bitcast.26), calls=%async_computation.1 | async-start | bytes 1900544 | tf_op jit(solution)/shard_map/all_to_all | solution.py:204
  34.9 9.6 %shard_map.65 = bf16[128,3584]{1,0:T(8,128)(2,1)S(1)} custom-call(s32[1]{0:T(128)} %bitcast.6.local_ref, bf16[128,3712]{1,0:T(8,128)(2,1)S(1)} %bitcast.18, bf16[1,3584,1024]{2,1,0:T(8,128)(2,1)} %refs_2_.5, bf16[1,3584,1024]{2,1,0:T(8,128)(2,1)} %refs_3_.7, bf16[1,1024,3584]{2,1,0:T(8,128)(2,1)} %refs_4_.5), custom_call_target="tpu_custom_call" | custom-call | flops 2818572288 | bytes 22020096 | tf_op jit(solution)/shard_map/pallas_call | solution.py:138
  44.5 5.3 %all-to-all-done.1 = bf16[16,8,3712]{2,1,0:T(8,128)(2,1)S(1)} async-done(((bf16[16,8,3712]{2,1,0:T(8,128)(2,1)}), bf16[16,8,3712]{2,1,0:T(8,128)(2,1)S(1)}, u32[]{:S(2)}, u32[]{:S(2)}) %all-to-all-start.1) | async-done | bytes 950304 | tf_op jit(solution)/shard_map/all_to_all | solution.py:204
  49.9 1.2 collective-permute-done.refs_0_
  51.0 0.0 collective-permute-done.1.refs_1_
  51.1 2.9 %collective-permute-start.4 = (bf16[128,3712]{1,0:T(8,128)(2,1)S(1)}, bf16[128,3712]{1,0:T(8,128)(2,1)}, u32[]{:S(2)}, u32[]{:S(2)}) collective-permute-start(bf16[128,3712]{1,0:T(8,128)(2,1)S(1)} %bitcast.21), channel_id=1, source_target_pairs={{0,3},{1,0},{2,1},{3,2},{4,7},{5,4},{6,5},{7,6},{8,11},{9,8},{10,9... | collective-permute-start | bytes 2850824 | tf_op jit(solution)/shard_map/ppermute | solution.py:207
  54.0 0.0 collective-permute-start.3
  54.0 0.7 collective-permute-start.2
  54.7 16.7 %shard_map.66 = (bf16[128,3584]{1,0:T(8,128)(2,1)}, bf16[128,3584]{1,0:T(8,128)(2,1)}, bf16[128,3584]{1,0:T(8,128)(2,1)S(1)}) custom-call(s32[1]{0:T(128)} %bitcast.6.local_ref, bf16[128,3712]{1,0:T(8,128)(2,1)} %collective-permute-done.refs_0_, bf16[128,3712]{1,0:T(8,128)(2,1)} %collective-permute-done.1.refs_1_, bf16[128,3712]{1,0:T(8,128)(2,1)S(1)} %bitcast.23, ...), custom_call_target="tpu_custom_call" | custom-call | flops 8455716864 | bytes 22020096 | tf_op jit(solution)/shard_map/pallas_call | solution.py:138
  71.4 0.0 copy-start
  71.4 0.6 collective-permute-done.4.refs_1_
  72.0 7.4 %collective-permute-done.3.refs_0_ = bf16[128,3712]{1,0:T(8,128)(2,1)S(1)} collective-permute-done((bf16[128,3712]{1,0:T(8,128)(2,1)}, bf16[128,3712]{1,0:T(8,128)(2,1)S(1)}, u32[]{:S(2)}, u32[]{:S(2)}) %collective-permute-start.3) | collective-permute-done | bytes 950304 | tf_op jit(solution)/shard_map/ppermute | solution.py:207
  79.4 0.0 collective-permute-start.5
  79.4 13.7 %shard_map.67 = (bf16[128,3712]{1,0:T(8,128)(2,1)}, bf16[128,3584]{1,0:T(8,128)(2,1)}) custom-call(s32[1]{0:T(128)} %bitcast.6.local_ref, bf16[128,3712]{1,0:T(8,128)(2,1)S(1)} %collective-permute-done.3.refs_0_, bf16[128,3712]{1,0:T(8,128)(2,1)} %collective-permute-done.4.refs_1_, bf16[1,3584,1024]{2,1,0:T(8,128)(2,1)} %refs_2_.5, ...), custom_call_target="tpu_custom_call" | custom-call | flops 5637144576 | bytes 22020096 | tf_op jit(solution)/shard_map/pallas_call | solution.py:138
  93.1 0.0 copy-done
  93.1 0.1 collective-permute-start.6
  93.2 2.0 %collective-permute-start.7 = (bf16[128,3584]{1,0:T(8,128)(2,1)}, bf16[128,3584]{1,0:T(8,128)(2,1)}, u32[]{:S(2)}, u32[]{:S(2)}) collective-permute-start(bf16[128,3584]{1,0:T(8,128)(2,1)} %get-tuple-element.58), channel_id=1, source_target_pairs={{0,1},{1,2},{2,3},{3,0},{4,5},{5,6},{6,7},{7,4},{8,9},{9,10},{10,1... | collective-permute-start | bytes 2752520 | tf_op jit(solution)/shard_map/ppermute | solution.py:207
  95.2 4.3 %all-to-all-start.2 = ((bf16[16,8,3712]{2,1,0:T(8,128)(2,1)}), bf16[16,8,3712]{2,1,0:T(8,128)(2,1)}, u32[]{:S(2)}, u32[]{:S(2)}) async-start(bf16[16,8,3712]{2,1,0:T(8,128)(2,1)} %bitcast.7), calls=%async_computation.2 | async-start | bytes 1900544 | tf_op jit(solution)/shard_map/all_to_all | solution.py:204
  99.5 0.2 collective-permute-done.2.refs_0_
  99.8 1.9 %collective-permute-done.5.refs_1_ = bf16[128,3712]{1,0:T(8,128)(2,1)} collective-permute-done((bf16[128,3712]{1,0:T(8,128)(2,1)}, bf16[128,3712]{1,0:T(8,128)(2,1)}, u32[]{:S(2)}, u32[]{:S(2)}) %collective-permute-start.5) | collective-permute-done | bytes 950304 | tf_op jit(solution)/shard_map/ppermute | solution.py:207
  101.7 13.7 %shard_map.68 = (bf16[128,3584]{1,0:T(8,128)(2,1)}, bf16[128,3712]{1,0:T(8,128)(2,1)}) custom-call(s32[1]{0:T(128)} %bitcast.6.local_ref, bf16[128,3712]{1,0:T(8,128)(2,1)S(1)} %collective-permute-done.2.refs_0_, bf16[128,3712]{1,0:T(8,128)(2,1)} %collective-permute-done.5.refs_1_, bf16[1,3584,1024]{2,1,0:T(8,128)(2,1)} %refs_2_.5, ...), custom_call_target="tpu_custom_call" | custom-call | flops 5637144576 | bytes 22020096 | tf_op jit(solution)/shard_map/pallas_call | solution.py:138
  115.4 0.0 all-to-all-done.2
  115.4 5.0 %all-to-all-start.4 = ((bf16[16,8,3712]{2,1,0:T(8,128)(2,1)}), bf16[16,8,3712]{2,1,0:T(8,128)(2,1)S(1)}, u32[]{:S(2)}, u32[]{:S(2)}) async-start(bf16[16,8,3712]{2,1,0:T(8,128)(2,1)} %bitcast.11), calls=%async_computation.4 | async-start | bytes 1900544 | tf_op jit(solution)/shard_map/all_to_all | solution.py:204
  120.4 0.0 collective-permute-done.6
  120.4 0.0 collective-permute-done.7
  120.4 1.3 collective-permute-start.8
  121.7 0.8 collective-permute-start.9
  122.5 2.7 %fusion = bf16[16,8,3584]{2,1,0:T(8,128)(2,1)} fusion(bf16[128,3584]{1,0:T(8,128)(2,1)} %collective-permute-done.7, bf16[128,3584]{1,0:T(8,128)(2,1)} %collective-permute-done.6, bf16[128,3584]{1,0:T(8,128)(2,1)S(1)} %shard_map.65), kind=kLoop, calls=%fused_computation.2 | loop fusion | flops 2752512 | bytes 3670016 | tf_op jit(solution)/shard_map/reshape | solution.py:203
  125.2 8.0 %all-to-all-done.4 = bf16[16,8,3712]{2,1,0:T(8,128)(2,1)S(1)} async-done(((bf16[16,8,3712]{2,1,0:T(8,128)(2,1)}), bf16[16,8,3712]{2,1,0:T(8,128)(2,1)S(1)}, u32[]{:S(2)}, u32[]{:S(2)}) %all-to-all-start.4) | async-done | bytes 950304 | tf_op jit(solution)/shard_map/all_to_all | solution.py:204
  133.2 0.0 copy-start.2
  133.2 0.9 copy-done.2
  134.1 3.6 %all-to-all-start.3 = ((bf16[16,8,3584]{2,1,0:T(8,128)(2,1)}), bf16[16,8,3584]{2,1,0:T(8,128)(2,1)S(1)}, u32[]{:S(2)}, u32[]{:S(2)}) async-start(bf16[16,8,3584]{2,1,0:T(8,128)(2,1)} %fusion), calls=%async_computation.3 | async-start | bytes 1835008 | tf_op jit(solution)/shard_map/all_to_all | solution.py:204
  137.8 0.0 copy-start.1
  137.8 3.2 %shard_map.69 = bf16[128,3584]{1,0:T(8,128)(2,1)} custom-call(bf16[128,3712]{1,0:T(8,128)(2,1)} %bitcast.8.first, bf16[128,3712]{1,0:T(8,128)(2,1)} %bitcast.24), custom_call_target="tpu_custom_call" | custom-call | flops 100000000 | bytes 5701632 | tf_op jit(solution)/shard_map/pallas_call | solution.py:167
  141.0 0.0 collective-permute-done.8
  141.0 0.0 collective-permute-done.9
  141.0 0.0 copy-done.1
  141.0 2.5 %add_convert_fusion = bf16[128,3584]{1,0:T(8,128)(2,1)} fusion(bf16[128,3584]{1,0:T(8,128)(2,1)} %collective-permute-done.9, bf16[128,3584]{1,0:T(8,128)(2,1)S(1)} %collective-permute-done.8, bf16[128,3584]{1,0:T(8,128)(2,1)S(1)} %copy-done.1), kind=kLoop, calls=%fused_computation | loop fusion | flops 2752512 | bytes 3670016 | tf_op jit(solution)/shard_map/convert_element_type | solution.py:219
  143.5 2.0 %collective-permute-start.10 = (bf16[128,3584]{1,0:T(8,128)(2,1)}, bf16[128,3584]{1,0:T(8,128)(2,1)S(1)}, u32[]{:S(2)}, u32[]{:S(2)}) collective-permute-start(bf16[128,3584]{1,0:T(8,128)(2,1)} %shard_map.69), channel_id=1, source_target_pairs={{0,2},{1,3},{2,0},{3,1},{4,6},{5,7},{6,4},{7,5},{8,10},{9,11},{10,... | collective-permute-start | bytes 2752520 | tf_op jit(solution)/shard_map/ppermute | solution.py:207
  145.5 6.0 %all-to-all-done.3 = bf16[16,8,3584]{2,1,0:T(8,128)(2,1)S(1)} async-done(((bf16[16,8,3584]{2,1,0:T(8,128)(2,1)}), bf16[16,8,3584]{2,1,0:T(8,128)(2,1)S(1)}, u32[]{:S(2)}, u32[]{:S(2)}) %all-to-all-start.3) | async-done | bytes 917536 | tf_op jit(solution)/shard_map/all_to_all | solution.py:204
  151.5 15.9 %all_to_all.31 = bf16[16,8,3584]{2,1,0:T(8,128)(2,1)S(1)} all-to-all(bf16[16,8,3584]{2,1,0:T(8,128)(2,1)} %bitcast.25), channel_id=1, replica_groups=mesh['dp'=2,'node'=16,'local'=4] {'node'}, dimensions={0} | all-to-all | bytes 1835008 | tf_op jit(solution)/shard_map/all_to_all | solution.py:204
  167.4 0.0 collective-permute-done.10.far
  167.4 2.4 %shard_map.70 = bf16[128,3584]{1,0:T(8,128)(2,1)} custom-call(bf16[256,128]{1,0:T(8,128)(2,1)} %get-tuple-element.38.pick, bf16[128,3584]{1,0:T(8,128)(2,1)S(1)} %bitcast.19, bf16[128,3584]{1,0:T(8,128)(2,1)S(1)} %bitcast.20, bf16[128,3584]{1,0:T(8,128)(2,1)S(1)} %collective-permute-done.10.far), custom_call_target="tpu_custom_call" | custom-call | flops 100000000 | bytes 8454144 | tf_op jit(solution)/shard_map/pallas_call | solution.py:167
Async XLA Ops:
  28.0 23.0 %collective-permute-start = (bf16[128,3712]{1,0:T(8,128)(2,1)S(1)}, bf16[128,3712]{1,0:T(8,128)(2,1)}, u32[]{:S(2)}, u32[]{:S(2)}) collective-permute-start(bf16[128,3712]{1,0:T(8,128)(2,1)S(1)} %bitcast.16), channel_id=1, source_target_pairs={{0,1},{1,2},{2,3},{3,0},{4,5},{5,6},{6,7},{7,4},{8,9},{9,10},{10,1... | collective-permute-start | bytes 2850824 | tf_op jit(solution)/shard_map/ppermute | solution.py:207
  29.6 21.5 %collective-permute-start.1 = (bf16[128,3712]{1,0:T(8,128)(2,1)S(1)}, bf16[128,3712]{1,0:T(8,128)(2,1)}, u32[]{:S(2)}, u32[]{:S(2)}) collective-permute-start(bf16[128,3712]{1,0:T(8,128)(2,1)S(1)} %bitcast.17), channel_id=1, source_target_pairs={{0,3},{1,0},{2,1},{3,2},{4,7},{5,4},{6,5},{7,6},{8,11},{9,8},{10,9... | collective-permute-start | bytes 2850824 | tf_op jit(solution)/shard_map/ppermute | solution.py:207
  31.2 18.6 %all-to-all-start.1 = ((bf16[16,8,3712]{2,1,0:T(8,128)(2,1)}), bf16[16,8,3712]{2,1,0:T(8,128)(2,1)S(1)}, u32[]{:S(2)}, u32[]{:S(2)}) async-start(bf16[16,8,3712]{2,1,0:T(8,128)(2,1)} %bitcast.26), calls=%async_computation.1 | async-start | bytes 1900544 | tf_op jit(solution)/shard_map/all_to_all | solution.py:204
  51.1 21.0 %collective-permute-start.4 = (bf16[128,3712]{1,0:T(8,128)(2,1)S(1)}, bf16[128,3712]{1,0:T(8,128)(2,1)}, u32[]{:S(2)}, u32[]{:S(2)}) collective-permute-start(bf16[128,3712]{1,0:T(8,128)(2,1)S(1)} %bitcast.21), channel_id=1, source_target_pairs={{0,3},{1,0},{2,1},{3,2},{4,7},{5,4},{6,5},{7,6},{8,11},{9,8},{10,9... | collective-permute-start | bytes 2850824 | tf_op jit(solution)/shard_map/ppermute | solution.py:207
  54.0 25.4 %collective-permute-start.3 = (bf16[128,3712]{1,0:T(8,128)(2,1)}, bf16[128,3712]{1,0:T(8,128)(2,1)S(1)}, u32[]{:S(2)}, u32[]{:S(2)}) collective-permute-start(bf16[128,3712]{1,0:T(8,128)(2,1)} %collective-permute-done.refs_0_), channel_id=1, source_target_pairs={{0,1},{1,2},{2,3},{3,0},{4,5},{5,6},{6,7},{7,4},{8,9},{9,10},{10,1... | collective-permute-start | bytes 2850824 | tf_op jit(solution)/shard_map/ppermute | solution.py:207
  54.0 45.8 %collective-permute-start.2 = (bf16[128,3712]{1,0:T(8,128)(2,1)S(1)}, bf16[128,3712]{1,0:T(8,128)(2,1)S(1)}, u32[]{:S(2)}, u32[]{:S(2)}) collective-permute-start(bf16[128,3712]{1,0:T(8,128)(2,1)S(1)} %bitcast.22), channel_id=1, source_target_pairs={{0,1},{1,2},{2,3},{3,0},{4,5},{5,6},{6,7},{7,4},{8,9},{9,10},{10,1... | collective-permute-start | bytes 2850824 | tf_op jit(solution)/shard_map/ppermute | solution.py:207
  71.4 21.7 %copy-start = (bf16[128,3584]{1,0:T(8,128)(2,1)}, bf16[128,3584]{1,0:T(8,128)(2,1)S(1)}, u32[]{:S(2)}) copy-start(bf16[128,3584]{1,0:T(8,128)(2,1)S(1)} %get-tuple-element.64) | copy-start | bytes 2752516
  79.4 22.3 %collective-permute-start.5 = (bf16[128,3712]{1,0:T(8,128)(2,1)}, bf16[128,3712]{1,0:T(8,128)(2,1)}, u32[]{:S(2)}, u32[]{:S(2)}) collective-permute-start(bf16[128,3712]{1,0:T(8,128)(2,1)} %collective-permute-done.4.refs_1_), channel_id=1, source_target_pairs={{0,3},{1,0},{2,1},{3,2},{4,7},{5,4},{6,5},{7,6},{8,11},{9,8},{10,9... | collective-permute-start | bytes 2850824 | tf_op jit(solution)/shard_map/ppermute | solution.py:207
  93.1 27.3 %collective-permute-start.6 = (bf16[128,3584]{1,0:T(8,128)(2,1)}, bf16[128,3584]{1,0:T(8,128)(2,1)}, u32[]{:S(2)}, u32[]{:S(2)}) collective-permute-start(bf16[128,3584]{1,0:T(8,128)(2,1)} %get-tuple-element.57), channel_id=1, source_target_pairs={{0,3},{1,0},{2,1},{3,2},{4,7},{5,4},{6,5},{7,6},{8,11},{9,8},{10,9... | collective-permute-start | bytes 2752520 | tf_op jit(solution)/shard_map/ppermute | solution.py:207
  93.2 27.2 %collective-permute-start.7 = (bf16[128,3584]{1,0:T(8,128)(2,1)}, bf16[128,3584]{1,0:T(8,128)(2,1)}, u32[]{:S(2)}, u32[]{:S(2)}) collective-permute-start(bf16[128,3584]{1,0:T(8,128)(2,1)} %get-tuple-element.58), channel_id=1, source_target_pairs={{0,1},{1,2},{2,3},{3,0},{4,5},{5,6},{6,7},{7,4},{8,9},{9,10},{10,1... | collective-permute-start | bytes 2752520 | tf_op jit(solution)/shard_map/ppermute | solution.py:207
  95.2 20.2 %all-to-all-start.2 = ((bf16[16,8,3712]{2,1,0:T(8,128)(2,1)}), bf16[16,8,3712]{2,1,0:T(8,128)(2,1)}, u32[]{:S(2)}, u32[]{:S(2)}) async-start(bf16[16,8,3712]{2,1,0:T(8,128)(2,1)} %bitcast.7), calls=%async_computation.2 | async-start | bytes 1900544 | tf_op jit(solution)/shard_map/all_to_all | solution.py:204
  115.4 17.8 %all-to-all-start.4 = ((bf16[16,8,3712]{2,1,0:T(8,128)(2,1)}), bf16[16,8,3712]{2,1,0:T(8,128)(2,1)S(1)}, u32[]{:S(2)}, u32[]{:S(2)}) async-start(bf16[16,8,3712]{2,1,0:T(8,128)(2,1)} %bitcast.11), calls=%async_computation.4 | async-start | bytes 1900544 | tf_op jit(solution)/shard_map/all_to_all | solution.py:204
  120.4 20.6 %collective-permute-start.8 = (bf16[128,3584]{1,0:T(8,128)(2,1)}, bf16[128,3584]{1,0:T(8,128)(2,1)S(1)}, u32[]{:S(2)}, u32[]{:S(2)}) collective-permute-start(bf16[128,3584]{1,0:T(8,128)(2,1)} %get-tuple-element.65), channel_id=1, source_target_pairs={{0,3},{1,0},{2,1},{3,2},{4,7},{5,4},{6,5},{7,6},{8,11},{9,8},{10,9... | collective-permute-start | bytes 2752520 | tf_op jit(solution)/shard_map/ppermute | solution.py:207
  121.7 19.3 %collective-permute-start.9 = (bf16[128,3584]{1,0:T(8,128)(2,1)}, bf16[128,3584]{1,0:T(8,128)(2,1)}, u32[]{:S(2)}, u32[]{:S(2)}) collective-permute-start(bf16[128,3584]{1,0:T(8,128)(2,1)} %get-tuple-element.66), channel_id=1, source_target_pairs={{0,1},{1,2},{2,3},{3,0},{4,5},{5,6},{6,7},{7,4},{8,9},{9,10},{10,1... | collective-permute-start | bytes 2752520 | tf_op jit(solution)/shard_map/ppermute | solution.py:207
  133.2 0.9 copy-start.2
  134.1 17.4 %all-to-all-start.3 = ((bf16[16,8,3584]{2,1,0:T(8,128)(2,1)}), bf16[16,8,3584]{2,1,0:T(8,128)(2,1)S(1)}, u32[]{:S(2)}, u32[]{:S(2)}) async-start(bf16[16,8,3584]{2,1,0:T(8,128)(2,1)} %fusion), calls=%async_computation.3 | async-start | bytes 1835008 | tf_op jit(solution)/shard_map/all_to_all | solution.py:204
  137.8 3.3 %copy-start.1 = (bf16[128,3584]{1,0:T(8,128)(2,1)S(1)}, bf16[128,3584]{1,0:T(8,128)(2,1)}, u32[]{:S(2)}) copy-start(bf16[128,3584]{1,0:T(8,128)(2,1)} %copy-done) | copy-start | bytes 2752516
  143.5 23.9 %collective-permute-start.10 = (bf16[128,3584]{1,0:T(8,128)(2,1)}, bf16[128,3584]{1,0:T(8,128)(2,1)S(1)}, u32[]{:S(2)}, u32[]{:S(2)}) collective-permute-start(bf16[128,3584]{1,0:T(8,128)(2,1)} %shard_map.69), channel_id=1, source_target_pairs={{0,2},{1,3},{2,0},{3,1},{4,6},{5,7},{6,4},{7,5},{8,10},{9,11},{10,... | collective-permute-start | bytes 2752520 | tf_op jit(solution)/shard_map/ppermute | solution.py:207

commit v14 on v12

--- a/solution.py
+++ b/solution.py
@@ -235,8 +235,10 @@
     far_pa, above_pb = run([far_a, above_b], (0,))
     below_pa, above_pa, far_pa = tie((below_pa, above_pa, far_pa))
     below_b, far_b, above_pb = tie((below_b, far_b, above_pb))
-    kept = [pltpu.with_memory_space_constraint(x, pltpu.VMEM) for x in (below_b, far_b)]
-    below_pb, far_pb = run(kept, (1,))
+    keep = functools.partial(pltpu.with_memory_space_constraint, memory_space=pltpu.VMEM)
+    [far_pb] = run([keep(far_b)], (0,))
+    below_b, far_pb = tie((below_b, far_pb))
+    [below_pb] = run([keep(below_b)], ())
 
     home_a = across(far_pa)
     from_above, from_below = down(below_pa), up(above_pa)
@@ -250,11 +252,11 @@
         jax.ShapeDtypeStruct(tokens.shape, jnp.bfloat16), home_a, home_b,
     )
     last_above, last_below = down(below_pb), up(above_pb)
-    far, last_above, last_below = tie((far, last_above, last_below))
+    total_b, far = tie((add(own_pb, last_above, last_below), far))
     far = shift(far, locals_ // 2)
 
     final_a = across(add(own_pa, from_above, from_below))
-    final_b = across(add(own_pb, last_above, last_below))
+    final_b = across(total_b)
     near = [pltpu.with_memory_space_constraint(x, pltpu.VMEM) for x in (final_a, final_b, far)]
     return whole(collect_kernel, jax.ShapeDtypeStruct(tokens.shape, jnp.bfloat16), pick, *near)
 

time: 175 us -> 173 us (0.989)
  waiting for transfers between devices: 30.1 us -> 17.6 us
  Pallas kernels: 63 us -> 70.3 us
  starting transfers between devices: 30.6 us -> 35.9 us
  blocking collectives: 43.3 us -> 41.1 us
    ppermute x11, waiting for transfers between devices: 17.7 us -> 10.1 us  [shift(): lax.ppermute(block, 'local', [(i, (i + by) % locals_) for i in range(loca...]
    pallas_call x4 -> x5, Pallas kernels: 53.4 us -> 60.7 us  [experts(): pl.pallas_call(functools.partial(expert_kernel, blocks), grid=(hidden //...]
    all_to_all x4, starting transfers between devices: 16.3 us -> 22.3 us  [across(): return lax.all_to_all(parts, 'node', 0, 0, tiled=True).reshape(block.shape)]
    all_to_all x4, waiting for transfers between devices: 12.4 us -> 7.52 us  [across(): return lax.all_to_all(parts, 'node', 0, 0, tiled=True).reshape(block.shape)]
    reshape x2 -> x1, other arithmetic: 5.44 us -> 2.71 us  [across(): parts = block.reshape(groups, block.shape[0] // groups, block.shape[1])]
    convert_element_type x0 -> x1, other arithmetic: none -> 2.45 us  [add(): return total.astype(jnp.bfloat16)]
    all_to_all x2, blocking collectives: 43.3 us -> 41.1 us  [across(): return lax.all_to_all(parts, 'node', 0, 0, tiled=True).reshape(block.shape)]
  transfers between devices with their start and end apart: 15 -> 15, of which waited for: 7 -> 7; matrix products, arithmetic and copies ran while one was open for 3% -> 3% of each run, Pallas kernels for 33% -> 37%
where the time goes in v14:
time: 173 us; the launch traced here: 172 us
  Pallas kernels  70.3 us (41%)
  blocking collectives  41.1 us (24%)
  starting transfers between devices  35.9 us (21%)
  waiting for transfers between devices  17.6 us (10%)
  other arithmetic  5.16 us (3%)
  local copies, waits for them, and re-layouts  1.85 us (1%)
    pallas_call x5, Pallas kernels, experts(): pl.pallas_call(functools.partial(expert_kernel, blocks), grid=(hidden //...  60.7 us
    all_to_all x2, blocking collectives, across(): return lax.all_to_all(parts, 'node', 0, 0, tiled=True).reshape(block.shape)  41.1 us
    all_to_all x4, starting transfers between devices, across(): return lax.all_to_all(parts, 'node', 0, 0, tiled=True).reshape(block.shape)  22.3 us
    ppermute x11, starting transfers between devices, shift(): lax.ppermute(block, 'local', [(i, (i + by) % locals_) for i in range(loca...  13.6 us
    ppermute x11, waiting for transfers between devices, shift(): lax.ppermute(block, 'local', [(i, (i + by) % locals_) for i in range(loca...  10.1 us
    all_to_all x4, waiting for transfers between devices, across(): return lax.all_to_all(parts, 'node', 0, 0, tiled=True).reshape(block.shape)  7.52 us
    pallas_call x2, Pallas kernels, whole(): pl.pallas_call(kernel, out_shape=shapes, compiler_params=pltpu.CompilerPa...  5.66 us
    pallas_call x1, Pallas kernels, prepare(): pl.pallas_call(functools.partial(prepare_kernel, locals_, groups, per_gro...  3.95 us
  transfers between devices with their start and end apart: 15, of which 7 were waited for; matrix products, arithmetic and copies ran while one was open for 3% of the time, Pallas kernels for 37%

profile of v14, /device:TPU:0, one launch (start us, length us, event | category | flops | bytes accessed | tf_op | source)
XLA Modules:
  0.0 172.0 jit_solution(10601340055874906133)
XLA Ops:
  0.0 3.9 %shard_map.64 = (bf16[128,3712]{1,0:T(8,128)(2,1)}, bf16[128,3712]{1,0:T(8,128)(2,1)}, bf16[256,128]{1,0:T(8,128)(2,1)}) custom-call(bf16[128,3584]{1,0:T(8,128)(2,1)} %tok.1, f32[4,128]{1,0:T(4,128)} %bitcast.27, s32[4,128]{1,0:T(4,128)} %bitcast.28), custom_call_target="tpu_custom_call" | custom-call | flops 1000000000 | bytes 3000000 | tf_op jit(solution)/shard_map/pallas_call | solution.py:82
  3.9 24.1 %all_to_all.30 = bf16[16,8,3712]{2,1,0:T(8,128)(2,1)S(1)} all-to-all(bf16[16,8,3712]{2,1,0:T(8,128)(2,1)} %bitcast.26), channel_id=1, replica_groups=mesh['dp'=2,'node'=16,'local'=4] {'node'}, dimensions={0} | all-to-all | bytes 1900544 | tf_op jit(solution)/shard_map/all_to_all | solution.py:204
  28.0 1.6 collective-permute-start
  29.6 1.7 collective-permute-start.1
  31.2 3.6 %all-to-all-start.1 = ((bf16[16,8,3712]{2,1,0:T(8,128)(2,1)}), bf16[16,8,3712]{2,1,0:T(8,128)(2,1)S(1)}, u32[]{:S(2)}, u32[]{:S(2)}) async-start(bf16[16,8,3712]{2,1,0:T(8,128)(2,1)} %bitcast.25), calls=%async_computation.1 | async-start | bytes 1900544 | tf_op jit(solution)/shard_map/all_to_all | solution.py:204
  34.9 9.6 %shard_map.65 = bf16[128,3584]{1,0:T(8,128)(2,1)S(1)} custom-call(s32[1]{0:T(128)} %bitcast.6.local_ref, bf16[128,3712]{1,0:T(8,128)(2,1)S(1)} %bitcast.18, bf16[1,3584,1024]{2,1,0:T(8,128)(2,1)} %refs_1_.5, bf16[1,3584,1024]{2,1,0:T(8,128)(2,1)} %refs_2_.7, bf16[1,1024,3584]{2,1,0:T(8,128)(2,1)} %refs_3_.9), custom_call_target="tpu_custom_call" | custom-call | flops 2818572288 | bytes 22020096 | tf_op jit(solution)/shard_map/pallas_call | solution.py:138
  44.5 5.3 %all-to-all-done.1 = bf16[16,8,3712]{2,1,0:T(8,128)(2,1)S(1)} async-done(((bf16[16,8,3712]{2,1,0:T(8,128)(2,1)}), bf16[16,8,3712]{2,1,0:T(8,128)(2,1)S(1)}, u32[]{:S(2)}, u32[]{:S(2)}) %all-to-all-start.1) | async-done | bytes 950304 | tf_op jit(solution)/shard_map/all_to_all | solution.py:204
  49.9 1.2 collective-permute-done.refs_0_
  51.0 0.0 collective-permute-done.1.refs_1_
  51.1 2.9 %collective-permute-start.3 = (bf16[128,3712]{1,0:T(8,128)(2,1)S(1)}, bf16[128,3712]{1,0:T(8,128)(2,1)}, u32[]{:S(2)}, u32[]{:S(2)}) collective-permute-start(bf16[128,3712]{1,0:T(8,128)(2,1)S(1)} %bitcast.21), channel_id=1, source_target_pairs={{0,3},{1,0},{2,1},{3,2},{4,7},{5,4},{6,5},{7,6},{8,11},{9,8},{10,9... | collective-permute-start | bytes 2850824 | tf_op jit(solution)/shard_map/ppermute | solution.py:207
  54.0 0.0 collective-permute-start.2
  54.0 15.5 %shard_map.66 = (bf16[128,3584]{1,0:T(8,128)(2,1)S(1)}, bf16[128,3584]{1,0:T(8,128)(2,1)S(1)}, bf16[128,3584]{1,0:T(8,128)(2,1)S(1)}) custom-call(s32[1]{0:T(128)} %bitcast.6.local_ref, bf16[128,3712]{1,0:T(8,128)(2,1)} %collective-permute-done.refs_0_, bf16[128,3712]{1,0:T(8,128)(2,1)} %collective-permute-done.1.refs_1_, bf16[128,3712]{1,0:T(8,128)(2,1)S(1)} %bitcast.22, ...), custom_call_target="tpu_custom_call" | custom-call | flops 8455716864 | bytes 22020096 | tf_op jit(solution)/shard_map/pallas_call | solution.py:138
  69.5 0.0 copy-start.2
  69.5 0.9 copy-done.2
  70.4 0.0 copy-start.3
  70.4 0.9 copy-done.3
  71.3 0.0 copy-start
  71.3 0.7 collective-permute-done.3.refs_1_
  72.0 3.6 %collective-permute-done.2.refs_0_ = bf16[128,3712]{1,0:T(8,128)(2,1)S(1)} collective-permute-done((bf16[128,3712]{1,0:T(8,128)(2,1)}, bf16[128,3712]{1,0:T(8,128)(2,1)S(1)}, u32[]{:S(2)}, u32[]{:S(2)}) %collective-permute-start.2) | collective-permute-done | bytes 950304 | tf_op jit(solution)/shard_map/ppermute | solution.py:207
  75.6 0.0 collective-permute-start.4
  75.6 3.2 %collective-permute-start.5 = (bf16[128,3712]{1,0:T(8,128)(2,1)}, bf16[128,3712]{1,0:T(8,128)(2,1)}, u32[]{:S(2)}, u32[]{:S(2)}) collective-permute-start(bf16[128,3712]{1,0:T(8,128)(2,1)} %collective-permute-done.3.refs_1_), channel_id=1, source_target_pairs={{0,3},{1,0},{2,1},{3,2},{4,7},{5,4},{6,5},{7,6},{8,11},{9,8},{10,9... | collective-permute-start | bytes 2850824 | tf_op jit(solution)/shard_map/ppermute | solution.py:207
  78.9 13.7 %shard_map.67 = (bf16[128,3712]{1,0:T(8,128)(2,1)}, bf16[128,3584]{1,0:T(8,128)(2,1)}) custom-call(s32[1]{0:T(128)} %bitcast.6.local_ref, bf16[128,3712]{1,0:T(8,128)(2,1)S(1)} %collective-permute-done.2.refs_0_, bf16[128,3712]{1,0:T(8,128)(2,1)} %collective-permute-done.3.refs_1_, bf16[1,3584,1024]{2,1,0:T(8,128)(2,1)} %refs_1_.5, ...), custom_call_target="tpu_custom_call" | custom-call | flops 5637144576 | bytes 22020096 | tf_op jit(solution)/shard_map/pallas_call | solution.py:138
  92.6 0.0 copy-done
  92.6 4.5 %all-to-all-start.2 = ((bf16[16,8,3712]{2,1,0:T(8,128)(2,1)}), bf16[16,8,3712]{2,1,0:T(8,128)(2,1)}, u32[]{:S(2)}, u32[]{:S(2)}) async-start(bf16[16,8,3712]{2,1,0:T(8,128)(2,1)} %bitcast.7), calls=%async_computation.2 | async-start | bytes 1900544 | tf_op jit(solution)/shard_map/all_to_all | solution.py:204
  97.1 0.1 collective-permute-start.6
  97.2 2.0 %collective-permute-start.7 = (bf16[128,3584]{1,0:T(8,128)(2,1)}, bf16[128,3584]{1,0:T(8,128)(2,1)}, u32[]{:S(2)}, u32[]{:S(2)}) collective-permute-start(bf16[128,3584]{1,0:T(8,128)(2,1)} %copy-done.2), channel_id=1, source_target_pairs={{0,1},{1,2},{2,3},{3,0},{4,5},{5,6},{6,7},{7,4},{8,9},{9,10},{10,1... | collective-permute-start | bytes 2752520 | tf_op jit(solution)/shard_map/ppermute | solution.py:207
  99.2 0.0 collective-permute-done.4.refs_0_
  99.2 0.0 collective-permute-done.5.refs_0_
  99.2 11.3 %shard_map.68 = bf16[128,3712]{1,0:T(8,128)(2,1)} custom-call(s32[1]{0:T(128)} %bitcast.6.local_ref, bf16[128,3712]{1,0:T(8,128)(2,1)} %collective-permute-done.5.refs_0_, bf16[1,3584,1024]{2,1,0:T(8,128)(2,1)} %refs_1_.5, bf16[1,3584,1024]{2,1,0:T(8,128)(2,1)} %refs_2_.7, bf16[1,1024,3584]{2,1,0:T(8,128)(2,1)} %refs_3_.9), custom_call_target="tpu_custom_call" | custom-call | flops 2818572288 | bytes 22020096 | tf_op jit(solution)/shard_map/pallas_call | solution.py:138
  110.5 0.0 all-to-all-done.2
  110.5 7.0 %all-to-all-start.4 = ((bf16[16,8,3712]{2,1,0:T(8,128)(2,1)}), bf16[16,8,3712]{2,1,0:T(8,128)(2,1)}, u32[]{:S(2)}, u32[]{:S(2)}) async-start(bf16[16,8,3712]{2,1,0:T(8,128)(2,1)} %bitcast.11), calls=%async_computation.4 | async-start | bytes 1900544 | tf_op jit(solution)/shard_map/all_to_all | solution.py:204
  117.5 10.6 %shard_map.69 = bf16[128,3584]{1,0:T(8,128)(2,1)} custom-call(s32[1]{0:T(128)} %bitcast.6.local_ref, bf16[128,3712]{1,0:T(8,128)(2,1)S(1)} %collective-permute-done.4.refs_0_, bf16[1,3584,1024]{2,1,0:T(8,128)(2,1)} %refs_1_.5, bf16[1,3584,1024]{2,1,0:T(8,128)(2,1)} %refs_2_.7, bf16[1,1024,3584]{2,1,0:T(8,128)(2,1)} %refs_3_.9), custom_call_target="tpu_custom_call" | custom-call | flops 2818572288 | bytes 22020096 | tf_op jit(solution)/shard_map/pallas_call | solution.py:138
  128.1 0.0 collective-permute-done.6
  128.1 0.0 collective-permute-done.7
  128.1 1.4 collective-permute-start.8
  129.4 0.7 collective-permute-start.9
  130.2 2.7 %fusion = bf16[16,8,3584]{2,1,0:T(8,128)(2,1)} fusion(bf16[128,3584]{1,0:T(8,128)(2,1)} %collective-permute-done.7, bf16[128,3584]{1,0:T(8,128)(2,1)} %collective-permute-done.6, bf16[128,3584]{1,0:T(8,128)(2,1)S(1)} %shard_map.65), kind=kLoop, calls=%fused_computation.2 | loop fusion | flops 2752512 | bytes 3670016 | tf_op jit(solution)/shard_map/reshape | solution.py:203
  132.9 0.0 all-to-all-done.4
  132.9 7.2 %all-to-all-start.3 = ((bf16[16,8,3584]{2,1,0:T(8,128)(2,1)}), bf16[16,8,3584]{2,1,0:T(8,128)(2,1)S(1)}, u32[]{:S(2)}, u32[]{:S(2)}) async-start(bf16[16,8,3584]{2,1,0:T(8,128)(2,1)} %fusion), calls=%async_computation.3 | async-start | bytes 1835008 | tf_op jit(solution)/shard_map/all_to_all | solution.py:204
  140.1 0.0 copy-start.1
  140.1 3.2 %shard_map.70 = bf16[128,3584]{1,0:T(8,128)(2,1)} custom-call(bf16[128,3712]{1,0:T(8,128)(2,1)} %bitcast.8.first, bf16[128,3712]{1,0:T(8,128)(2,1)} %bitcast.12.second), custom_call_target="tpu_custom_call" | custom-call | flops 100000000 | bytes 5701632 | tf_op jit(solution)/shard_map/pallas_call | solution.py:167
  143.3 2.0 %collective-permute-done.8 = bf16[128,3584]{1,0:T(8,128)(2,1)S(1)} collective-permute-done((bf16[128,3584]{1,0:T(8,128)(2,1)}, bf16[128,3584]{1,0:T(8,128)(2,1)S(1)}, u32[]{:S(2)}, u32[]{:S(2)}) %collective-permute-start.8) | collective-permute-done | bytes 917536 | tf_op jit(solution)/shard_map/ppermute | solution.py:207
  145.3 2.6 %collective-permute-done.9 = bf16[128,3584]{1,0:T(8,128)(2,1)} collective-permute-done((bf16[128,3584]{1,0:T(8,128)(2,1)}, bf16[128,3584]{1,0:T(8,128)(2,1)}, u32[]{:S(2)}, u32[]{:S(2)}) %collective-permute-start.9) | collective-permute-done | bytes 917536 | tf_op jit(solution)/shard_map/ppermute | solution.py:207
  147.9 0.0 copy-done.1
  147.9 2.5 %add_convert_fusion = bf16[128,3584]{1,0:T(8,128)(2,1)} fusion(bf16[128,3584]{1,0:T(8,128)(2,1)} %collective-permute-done.9, bf16[128,3584]{1,0:T(8,128)(2,1)S(1)} %collective-permute-done.8, bf16[128,3584]{1,0:T(8,128)(2,1)S(1)} %copy-done.1), kind=kLoop, calls=%fused_computation | loop fusion | flops 2752512 | bytes 3670016 | tf_op jit(solution)/shard_map/convert_element_type | solution.py:219
  150.3 0.0 collective-permute-start.10
  150.3 2.2 %all-to-all-done.3 = bf16[16,8,3584]{2,1,0:T(8,128)(2,1)S(1)} async-done(((bf16[16,8,3584]{2,1,0:T(8,128)(2,1)}), bf16[16,8,3584]{2,1,0:T(8,128)(2,1)S(1)}, u32[]{:S(2)}, u32[]{:S(2)}) %all-to-all-start.3) | async-done | bytes 917536 | tf_op jit(solution)/shard_map/all_to_all | solution.py:204
  152.5 17.0 %all_to_all.31 = bf16[16,8,3584]{2,1,0:T(8,128)(2,1)S(1)} all-to-all(bf16[16,8,3584]{2,1,0:T(8,128)(2,1)} %bitcast.24), channel_id=1, replica_groups=mesh['dp'=2,'node'=16,'local'=4] {'node'}, dimensions={0} | all-to-all | bytes 1835008 | tf_op jit(solution)/shard_map/all_to_all | solution.py:204
  169.5 0.0 collective-permute-done.10.far
  169.5 2.4 %shard_map.71 = bf16[128,3584]{1,0:T(8,128)(2,1)} custom-call(bf16[256,128]{1,0:T(8,128)(2,1)} %get-tuple-element.39.pick, bf16[128,3584]{1,0:T(8,128)(2,1)S(1)} %bitcast.19, bf16[128,3584]{1,0:T(8,128)(2,1)S(1)} %bitcast.20, bf16[128,3584]{1,0:T(8,128)(2,1)S(1)} %collective-permute-done.10.far), custom_call_target="tpu_custom_call" | custom-call | flops 100000000 | bytes 8454144 | tf_op jit(solution)/shard_map/pallas_call | solution.py:167
Async XLA Ops:
  28.0 23.0 %collective-permute-start = (bf16[128,3712]{1,0:T(8,128)(2,1)S(1)}, bf16[128,3712]{1,0:T(8,128)(2,1)}, u32[]{:S(2)}, u32[]{:S(2)}) collective-permute-start(bf16[128,3712]{1,0:T(8,128)(2,1)S(1)} %bitcast.16), channel_id=1, source_target_pairs={{0,1},{1,2},{2,3},{3,0},{4,5},{5,6},{6,7},{7,4},{8,9},{9,10},{10,1... | collective-permute-start | bytes 2850824 | tf_op jit(solution)/shard_map/ppermute | solution.py:207
  29.6 21.5 %collective-permute-start.1 = (bf16[128,3712]{1,0:T(8,128)(2,1)S(1)}, bf16[128,3712]{1,0:T(8,128)(2,1)}, u32[]{:S(2)}, u32[]{:S(2)}) collective-permute-start(bf16[128,3712]{1,0:T(8,128)(2,1)S(1)} %bitcast.17), channel_id=1, source_target_pairs={{0,3},{1,0},{2,1},{3,2},{4,7},{5,4},{6,5},{7,6},{8,11},{9,8},{10,9... | collective-permute-start | bytes 2850824 | tf_op jit(solution)/shard_map/ppermute | solution.py:207
  31.2 18.6 %all-to-all-start.1 = ((bf16[16,8,3712]{2,1,0:T(8,128)(2,1)}), bf16[16,8,3712]{2,1,0:T(8,128)(2,1)S(1)}, u32[]{:S(2)}, u32[]{:S(2)}) async-start(bf16[16,8,3712]{2,1,0:T(8,128)(2,1)} %bitcast.25), calls=%async_computation.1 | async-start | bytes 1900544 | tf_op jit(solution)/shard_map/all_to_all | solution.py:204
  51.1 21.0 %collective-permute-start.3 = (bf16[128,3712]{1,0:T(8,128)(2,1)S(1)}, bf16[128,3712]{1,0:T(8,128)(2,1)}, u32[]{:S(2)}, u32[]{:S(2)}) collective-permute-start(bf16[128,3712]{1,0:T(8,128)(2,1)S(1)} %bitcast.21), channel_id=1, source_target_pairs={{0,3},{1,0},{2,1},{3,2},{4,7},{5,4},{6,5},{7,6},{8,11},{9,8},{10,9... | collective-permute-start | bytes 2850824 | tf_op jit(solution)/shard_map/ppermute | solution.py:207
  54.0 21.7 %collective-permute-start.2 = (bf16[128,3712]{1,0:T(8,128)(2,1)}, bf16[128,3712]{1,0:T(8,128)(2,1)S(1)}, u32[]{:S(2)}, u32[]{:S(2)}) collective-permute-start(bf16[128,3712]{1,0:T(8,128)(2,1)} %collective-permute-done.refs_0_), channel_id=1, source_target_pairs={{0,1},{1,2},{2,3},{3,0},{4,5},{5,6},{6,7},{7,4},{8,9},{9,10},{10,1... | collective-permute-start | bytes 2850824 | tf_op jit(solution)/shard_map/ppermute | solution.py:207
  69.5 0.9 copy-start.2
  70.4 0.9 copy-start.3
  71.3 21.3 %copy-start = (bf16[128,3584]{1,0:T(8,128)(2,1)}, bf16[128,3584]{1,0:T(8,128)(2,1)S(1)}, u32[]{:S(2)}) copy-start(bf16[128,3584]{1,0:T(8,128)(2,1)S(1)} %get-tuple-element.66) | copy-start | bytes 2752516
  75.6 23.6 %collective-permute-start.4 = (bf16[128,3712]{1,0:T(8,128)(2,1)S(1)}, bf16[128,3712]{1,0:T(8,128)(2,1)S(1)}, u32[]{:S(2)}, u32[]{:S(2)}) collective-permute-start(bf16[128,3712]{1,0:T(8,128)(2,1)S(1)} %bitcast.23), channel_id=1, source_target_pairs={{0,1},{1,2},{2,3},{3,0},{4,5},{5,6},{6,7},{7,4},{8,9},{9,10},{10,1... | collective-permute-start | bytes 2850824 | tf_op jit(solution)/shard_map/ppermute | solution.py:207
  75.6 23.6 %collective-permute-start.5 = (bf16[128,3712]{1,0:T(8,128)(2,1)}, bf16[128,3712]{1,0:T(8,128)(2,1)}, u32[]{:S(2)}, u32[]{:S(2)}) collective-permute-start(bf16[128,3712]{1,0:T(8,128)(2,1)} %collective-permute-done.3.refs_1_), channel_id=1, source_target_pairs={{0,3},{1,0},{2,1},{3,2},{4,7},{5,4},{6,5},{7,6},{8,11},{9,8},{10,9... | collective-permute-start | bytes 2850824 | tf_op jit(solution)/shard_map/ppermute | solution.py:207
  92.6 17.9 %all-to-all-start.2 = ((bf16[16,8,3712]{2,1,0:T(8,128)(2,1)}), bf16[16,8,3712]{2,1,0:T(8,128)(2,1)}, u32[]{:S(2)}, u32[]{:S(2)}) async-start(bf16[16,8,3712]{2,1,0:T(8,128)(2,1)} %bitcast.7), calls=%async_computation.2 | async-start | bytes 1900544 | tf_op jit(solution)/shard_map/all_to_all | solution.py:204
  97.1 31.0 %collective-permute-start.6 = (bf16[128,3584]{1,0:T(8,128)(2,1)}, bf16[128,3584]{1,0:T(8,128)(2,1)}, u32[]{:S(2)}, u32[]{:S(2)}) collective-permute-start(bf16[128,3584]{1,0:T(8,128)(2,1)} %copy-done.3), channel_id=1, source_target_pairs={{0,3},{1,0},{2,1},{3,2},{4,7},{5,4},{6,5},{7,6},{8,11},{9,8},{10,9... | collective-permute-start | bytes 2752520 | tf_op jit(solution)/shard_map/ppermute | solution.py:207
  97.2 30.9 %collective-permute-start.7 = (bf16[128,3584]{1,0:T(8,128)(2,1)}, bf16[128,3584]{1,0:T(8,128)(2,1)}, u32[]{:S(2)}, u32[]{:S(2)}) collective-permute-start(bf16[128,3584]{1,0:T(8,128)(2,1)} %copy-done.2), channel_id=1, source_target_pairs={{0,1},{1,2},{2,3},{3,0},{4,5},{5,6},{6,7},{7,4},{8,9},{9,10},{10,1... | collective-permute-start | bytes 2752520 | tf_op jit(solution)/shard_map/ppermute | solution.py:207
  110.5 22.3 %all-to-all-start.4 = ((bf16[16,8,3712]{2,1,0:T(8,128)(2,1)}), bf16[16,8,3712]{2,1,0:T(8,128)(2,1)}, u32[]{:S(2)}, u32[]{:S(2)}) async-start(bf16[16,8,3712]{2,1,0:T(8,128)(2,1)} %bitcast.11), calls=%async_computation.4 | async-start | bytes 1900544 | tf_op jit(solution)/shard_map/all_to_all | solution.py:204
  128.1 17.2 %collective-permute-start.8 = (bf16[128,3584]{1,0:T(8,128)(2,1)}, bf16[128,3584]{1,0:T(8,128)(2,1)S(1)}, u32[]{:S(2)}, u32[]{:S(2)}) collective-permute-start(bf16[128,3584]{1,0:T(8,128)(2,1)} %shard_map.69), channel_id=1, source_target_pairs={{0,3},{1,0},{2,1},{3,2},{4,7},{5,4},{6,5},{7,6},{8,11},{9,8},{10,9... | collective-permute-start | bytes 2752520 | tf_op jit(solution)/shard_map/ppermute | solution.py:207
  129.4 18.4 %collective-permute-start.9 = (bf16[128,3584]{1,0:T(8,128)(2,1)}, bf16[128,3584]{1,0:T(8,128)(2,1)}, u32[]{:S(2)}, u32[]{:S(2)}) collective-permute-start(bf16[128,3584]{1,0:T(8,128)(2,1)} %get-tuple-element.68), channel_id=1, source_target_pairs={{0,1},{1,2},{2,3},{3,0},{4,5},{5,6},{6,7},{7,4},{8,9},{9,10},{10,1... | collective-permute-start | bytes 2752520 | tf_op jit(solution)/shard_map/ppermute | solution.py:207
  132.9 19.6 %all-to-all-start.3 = ((bf16[16,8,3584]{2,1,0:T(8,128)(2,1)}), bf16[16,8,3584]{2,1,0:T(8,128)(2,1)S(1)}, u32[]{:S(2)}, u32[]{:S(2)}) async-start(bf16[16,8,3584]{2,1,0:T(8,128)(2,1)} %fusion), calls=%async_computation.3 | async-start | bytes 1835008 | tf_op jit(solution)/shard_map/all_to_all | solution.py:204
  140.1 7.8 %copy-start.1 = (bf16[128,3584]{1,0:T(8,128)(2,1)S(1)}, bf16[128,3584]{1,0:T(8,128)(2,1)}, u32[]{:S(2)}) copy-start(bf16[128,3584]{1,0:T(8,128)(2,1)} %copy-done) | copy-start | bytes 2752516
  150.3 19.2 %collective-permute-start.10 = (bf16[128,3584]{1,0:T(8,128)(2,1)}, bf16[128,3584]{1,0:T(8,128)(2,1)S(1)}, u32[]{:S(2)}, u32[]{:S(2)}) collective-permute-start(bf16[128,3584]{1,0:T(8,128)(2,1)} %shard_map.70), channel_id=1, source_target_pairs={{0,2},{1,3},{2,0},{3,1},{4,6},{5,7},{6,4},{7,5},{8,10},{9,11},{10,... | collective-permute-start | bytes 2752520 | tf_op jit(solution)/shard_map/ppermute | solution.py:207

commit v15 on v12

--- a/solution.py
+++ b/solution.py
@@ -247,14 +247,15 @@
     home_b = across(far_pb)
     far = whole(
         functools.partial(scatter_kernel, locals_),
-        jax.ShapeDtypeStruct(tokens.shape, jnp.bfloat16), home_a, home_b,
+        jax.ShapeDtypeStruct(tokens.shape, jnp.bfloat16), home_a,
+        pltpu.with_memory_space_constraint(home_b, pltpu.VMEM),
     )
     last_above, last_below = down(below_pb), up(above_pb)
-    far, last_above, last_below = tie((far, last_above, last_below))
+    total_b, far = tie((add(own_pb, last_above, last_below), far))
     far = shift(far, locals_ // 2)
 
     final_a = across(add(own_pa, from_above, from_below))
-    final_b = across(add(own_pb, last_above, last_below))
+    final_b = across(total_b)
     near = [pltpu.with_memory_space_constraint(x, pltpu.VMEM) for x in (final_a, final_b, far)]
     return whole(collect_kernel, jax.ShapeDtypeStruct(tokens.shape, jnp.bfloat16), pick, *near)
 

time: 175 us -> 167 us (0.954)
  blocking collectives: 43.3 us -> 39.9 us
  waiting for transfers between devices: 30.1 us -> 27.2 us
    ppermute x11, waiting for transfers between devices: 17.7 us -> 9.15 us  [shift(): lax.ppermute(block, 'local', [(i, (i + by) % locals_) for i in range(loca...]
    all_to_all x4, waiting for transfers between devices: 12.4 us -> 18.1 us  [across(): return lax.all_to_all(parts, 'node', 0, 0, tiled=True).reshape(block.shape)]
    all_to_all x2, blocking collectives: 43.3 us -> 39.9 us  [across(): return lax.all_to_all(parts, 'node', 0, 0, tiled=True).reshape(block.shape)]
    reshape x2 -> x1, other arithmetic: 5.44 us -> 2.71 us  [across(): parts = block.reshape(groups, block.shape[0] // groups, block.shape[1])]
    convert_element_type x0 -> x1, other arithmetic: none -> 2.72 us  [add(): return total.astype(jnp.bfloat16)]
  transfers between devices with their start and end apart: 15 -> 15, of which waited for: 7 -> 8; matrix products, arithmetic and copies ran while one was open for 3% -> 3% of each run, Pallas kernels for 33% -> 34%
where the time goes in v15:
time: 167 us
  Pallas kernels  62.7 us (38%)
  blocking collectives  39.9 us (24%)
  starting transfers between devices  31.2 us (19%)
  waiting for transfers between devices  27.2 us (16%)
  other arithmetic  5.43 us (3%)
    pallas_call x4, Pallas kernels, experts(): pl.pallas_call(functools.partial(expert_kernel, blocks), grid=(hidden //...  53.3 us
    all_to_all x2, blocking collectives, across(): return lax.all_to_all(parts, 'node', 0, 0, tiled=True).reshape(block.shape)  39.9 us
    all_to_all x4, waiting for transfers between devices, across(): return lax.all_to_all(parts, 'node', 0, 0, tiled=True).reshape(block.shape)  18.1 us
    all_to_all x4, starting transfers between devices, across(): return lax.all_to_all(parts, 'node', 0, 0, tiled=True).reshape(block.shape)  16.3 us
    ppermute x11, starting transfers between devices, shift(): lax.ppermute(block, 'local', [(i, (i + by) % locals_) for i in range(loca...  14.9 us
    ppermute x11, waiting for transfers between devices, shift(): lax.ppermute(block, 'local', [(i, (i + by) % locals_) for i in range(loca...  9.15 us
    pallas_call x2, Pallas kernels, whole(): pl.pallas_call(kernel, out_shape=shapes, compiler_params=pltpu.CompilerPa...  5.4 us
    pallas_call x1, Pallas kernels, prepare(): pl.pallas_call(functools.partial(prepare_kernel, locals_, groups, per_gro...  3.99 us
  transfers between devices with their start and end apart: 15, of which 8 were waited for; matrix products, arithmetic and copies ran while one was open for 3% of the time, Pallas kernels for 34%

profile of v15, /device:TPU:0, one launch (start us, length us, event | category | flops | bytes accessed | tf_op | source)
XLA Modules:
  0.0 166.5 jit_solution(11711374455096333646)
XLA Ops:
  0.0 4.0 %shard_map.64 = (bf16[128,3712]{1,0:T(8,128)(2,1)}, bf16[128,3712]{1,0:T(8,128)(2,1)}, bf16[256,128]{1,0:T(8,128)(2,1)}) custom-call(bf16[128,3584]{1,0:T(8,128)(2,1)} %tok.1, f32[4,128]{1,0:T(4,128)} %bitcast.28, s32[4,128]{1,0:T(4,128)} %bitcast.29), custom_call_target="tpu_custom_call" | custom-call | flops 1000000000 | bytes 3000000 | tf_op jit(solution)/shard_map/pallas_call | solution.py:82
  4.0 24.1 %all_to_all.30 = bf16[16,8,3712]{2,1,0:T(8,128)(2,1)S(1)} all-to-all(bf16[16,8,3712]{2,1,0:T(8,128)(2,1)} %bitcast.27), channel_id=1, replica_groups=mesh['dp'=2,'node'=16,'local'=4] {'node'}, dimensions={0} | all-to-all | bytes 1900544 | tf_op jit(solution)/shard_map/all_to_all | solution.py:204
  28.0 1.6 collective-permute-start
  29.6 1.7 collective-permute-start.1
  31.3 3.6 %all-to-all-start.1 = ((bf16[16,8,3712]{2,1,0:T(8,128)(2,1)}), bf16[16,8,3712]{2,1,0:T(8,128)(2,1)S(1)}, u32[]{:S(2)}, u32[]{:S(2)}) async-start(bf16[16,8,3712]{2,1,0:T(8,128)(2,1)} %bitcast.26), calls=%async_computation.1 | async-start | bytes 1900544 | tf_op jit(solution)/shard_map/all_to_all | solution.py:204
  34.9 9.6 %shard_map.65 = bf16[128,3584]{1,0:T(8,128)(2,1)S(1)} custom-call(s32[1]{0:T(128)} %bitcast.6.local_ref, bf16[128,3712]{1,0:T(8,128)(2,1)S(1)} %bitcast.19, bf16[1,3584,1024]{2,1,0:T(8,128)(2,1)} %refs_2_.5, bf16[1,3584,1024]{2,1,0:T(8,128)(2,1)} %refs_3_.7, bf16[1,1024,3584]{2,1,0:T(8,128)(2,1)} %refs_4_.5), custom_call_target="tpu_custom_call" | custom-call | flops 2818572288 | bytes 22020096 | tf_op jit(solution)/shard_map/pallas_call | solution.py:138
  44.6 5.3 %all-to-all-done.1 = bf16[16,8,3712]{2,1,0:T(8,128)(2,1)S(1)} async-done(((bf16[16,8,3712]{2,1,0:T(8,128)(2,1)}), bf16[16,8,3712]{2,1,0:T(8,128)(2,1)S(1)}, u32[]{:S(2)}, u32[]{:S(2)}) %all-to-all-start.1) | async-done | bytes 950304 | tf_op jit(solution)/shard_map/all_to_all | solution.py:204
  49.9 1.2 collective-permute-done.refs_0_
  51.1 0.0 collective-permute-done.1.refs_1_
  51.1 2.9 %collective-permute-start.3 = (bf16[128,3712]{1,0:T(8,128)(2,1)S(1)}, bf16[128,3712]{1,0:T(8,128)(2,1)S(1)}, u32[]{:S(2)}, u32[]{:S(2)}) collective-permute-start(bf16[128,3712]{1,0:T(8,128)(2,1)S(1)} %bitcast.22), channel_id=1, source_target_pairs={{0,3},{1,0},{2,1},{3,2},{4,7},{5,4},{6,5},{7,6},{8,11},{9,8},{10,9... | collective-permute-start | bytes 2850824 | tf_op jit(solution)/shard_map/ppermute | solution.py:207
  54.0 0.0 collective-permute-start.2
  54.0 16.7 %shard_map.66 = (bf16[128,3584]{1,0:T(8,128)(2,1)}, bf16[128,3584]{1,0:T(8,128)(2,1)}, bf16[128,3584]{1,0:T(8,128)(2,1)S(1)}) custom-call(s32[1]{0:T(128)} %bitcast.6.local_ref, bf16[128,3712]{1,0:T(8,128)(2,1)} %collective-permute-done.refs_0_, bf16[128,3712]{1,0:T(8,128)(2,1)} %collective-permute-done.1.refs_1_, bf16[128,3712]{1,0:T(8,128)(2,1)S(1)} %bitcast.23, ...), custom_call_target="tpu_custom_call" | custom-call | flops 8455716864 | bytes 22020096 | tf_op jit(solution)/shard_map/pallas_call | solution.py:138
  70.7 0.0 copy-start
  70.7 1.4 collective-permute-done.3.refs_1_
  72.1 3.6 %collective-permute-done.2.refs_0_ = bf16[128,3712]{1,0:T(8,128)(2,1)S(1)} collective-permute-done((bf16[128,3712]{1,0:T(8,128)(2,1)}, bf16[128,3712]{1,0:T(8,128)(2,1)S(1)}, u32[]{:S(2)}, u32[]{:S(2)}) %collective-permute-start.2) | collective-permute-done | bytes 950304 | tf_op jit(solution)/shard_map/ppermute | solution.py:207
  75.7 0.0 collective-permute-start.4
  75.7 3.2 %collective-permute-start.5 = (bf16[128,3712]{1,0:T(8,128)(2,1)S(1)}, bf16[128,3712]{1,0:T(8,128)(2,1)}, u32[]{:S(2)}, u32[]{:S(2)}) collective-permute-start(bf16[128,3712]{1,0:T(8,128)(2,1)S(1)} %collective-permute-done.3.refs_1_), channel_id=1, source_target_pairs={{0,3},{1,0},{2,1},{3,2},{4,7},{5,4},{6,5},{7,6},{8,11},{9,8},{10,9... | collective-permute-start | bytes 2850824 | tf_op jit(solution)/shard_map/ppermute | solution.py:207
  78.9 13.0 %shard_map.67 = (bf16[128,3712]{1,0:T(8,128)(2,1)}, bf16[128,3584]{1,0:T(8,128)(2,1)}) custom-call(s32[1]{0:T(128)} %bitcast.6.local_ref, bf16[128,3712]{1,0:T(8,128)(2,1)S(1)} %collective-permute-done.2.refs_0_, bf16[128,3712]{1,0:T(8,128)(2,1)S(1)} %collective-permute-done.3.refs_1_, bf16[1,3584,1024]{2,1,0:T(8,128)(2,1)} %refs_2_.5, ...), custom_call_target="tpu_custom_call" | custom-call | flops 5637144576 | bytes 22020096 | tf_op jit(solution)/shard_map/pallas_call | solution.py:138
  91.9 0.0 copy-done
  91.9 0.0 collective-permute-start.6
  91.9 2.0 %collective-permute-start.7 = (bf16[128,3584]{1,0:T(8,128)(2,1)}, bf16[128,3584]{1,0:T(8,128)(2,1)}, u32[]{:S(2)}, u32[]{:S(2)}) collective-permute-start(bf16[128,3584]{1,0:T(8,128)(2,1)} %get-tuple-element.60), channel_id=1, source_target_pairs={{0,1},{1,2},{2,3},{3,0},{4,5},{5,6},{6,7},{7,4},{8,9},{9,10},{10,1... | collective-permute-start | bytes 2752520 | tf_op jit(solution)/shard_map/ppermute | solution.py:207
  93.9 4.3 %all-to-all-start.2 = ((bf16[16,8,3712]{2,1,0:T(8,128)(2,1)}), bf16[16,8,3712]{2,1,0:T(8,128)(2,1)}, u32[]{:S(2)}, u32[]{:S(2)}) async-start(bf16[16,8,3712]{2,1,0:T(8,128)(2,1)} %bitcast.7), calls=%async_computation.2 | async-start | bytes 1900544 | tf_op jit(solution)/shard_map/all_to_all | solution.py:204
  98.2 2.5 %collective-permute-done.4.refs_0_ = bf16[128,3712]{1,0:T(8,128)(2,1)} collective-permute-done((bf16[128,3712]{1,0:T(8,128)(2,1)S(1)}, bf16[128,3712]{1,0:T(8,128)(2,1)}, u32[]{:S(2)}, u32[]{:S(2)}) %collective-permute-start.4) | collective-permute-done | bytes 950304 | tf_op jit(solution)/shard_map/ppermute | solution.py:207
  100.7 0.0 collective-permute-done.5.refs_1_
  100.7 14.1 %shard_map.68 = (bf16[128,3584]{1,0:T(8,128)(2,1)}, bf16[128,3712]{1,0:T(8,128)(2,1)}) custom-call(s32[1]{0:T(128)} %bitcast.6.local_ref, bf16[128,3712]{1,0:T(8,128)(2,1)} %collective-permute-done.4.refs_0_, bf16[128,3712]{1,0:T(8,128)(2,1)} %collective-permute-done.5.refs_1_, bf16[1,3584,1024]{2,1,0:T(8,128)(2,1)} %refs_2_.5, ...), custom_call_target="tpu_custom_call" | custom-call | flops 5637144576 | bytes 22020096 | tf_op jit(solution)/shard_map/pallas_call | solution.py:138
  114.8 0.0 all-to-all-done.2
  114.8 4.7 %all-to-all-start.4 = ((bf16[16,8,3712]{2,1,0:T(8,128)(2,1)}), bf16[16,8,3712]{2,1,0:T(8,128)(2,1)S(1)}, u32[]{:S(2)}, u32[]{:S(2)}) async-start(bf16[16,8,3712]{2,1,0:T(8,128)(2,1)} %bitcast.11), calls=%async_computation.4 | async-start | bytes 1900544 | tf_op jit(solution)/shard_map/all_to_all | solution.py:204
  119.5 0.0 collective-permute-done.6
  119.5 0.0 collective-permute-done.7
  119.5 2.9 %collective-permute-start.8 = (bf16[128,3584]{1,0:T(8,128)(2,1)}, bf16[128,3584]{1,0:T(8,128)(2,1)}, u32[]{:S(2)}, u32[]{:S(2)}) collective-permute-start(bf16[128,3584]{1,0:T(8,128)(2,1)} %get-tuple-element.67), channel_id=1, source_target_pairs={{0,3},{1,0},{2,1},{3,2},{4,7},{5,4},{6,5},{7,6},{8,11},{9,8},{10,9... | collective-permute-start | bytes 2752520 | tf_op jit(solution)/shard_map/ppermute | solution.py:207
  122.4 0.0 collective-permute-start.9
  122.4 2.7 %fusion = bf16[16,8,3584]{2,1,0:T(8,128)(2,1)} fusion(bf16[128,3584]{1,0:T(8,128)(2,1)} %collective-permute-done.7, bf16[128,3584]{1,0:T(8,128)(2,1)} %collective-permute-done.6, bf16[128,3584]{1,0:T(8,128)(2,1)S(1)} %shard_map.65), kind=kLoop, calls=%fused_computation.2 | loop fusion | flops 2752512 | bytes 3670016 | tf_op jit(solution)/shard_map/reshape | solution.py:203
  125.1 7.1 %all-to-all-done.4 = bf16[16,8,3712]{2,1,0:T(8,128)(2,1)S(1)} async-done(((bf16[16,8,3712]{2,1,0:T(8,128)(2,1)}), bf16[16,8,3712]{2,1,0:T(8,128)(2,1)S(1)}, u32[]{:S(2)}, u32[]{:S(2)}) %all-to-all-start.4) | async-done | bytes 950304 | tf_op jit(solution)/shard_map/all_to_all | solution.py:204
  132.2 3.6 %all-to-all-start.3 = ((bf16[16,8,3584]{2,1,0:T(8,128)(2,1)}), bf16[16,8,3584]{2,1,0:T(8,128)(2,1)S(1)}, u32[]{:S(2)}, u32[]{:S(2)}) async-start(bf16[16,8,3584]{2,1,0:T(8,128)(2,1)} %fusion), calls=%async_computation.3 | async-start | bytes 1835008 | tf_op jit(solution)/shard_map/all_to_all | solution.py:204
  135.8 0.0 copy-start.1
  135.8 3.0 %shard_map.69 = bf16[128,3584]{1,0:T(8,128)(2,1)} custom-call(bf16[128,3712]{1,0:T(8,128)(2,1)} %bitcast.8.first, bf16[128,3712]{1,0:T(8,128)(2,1)S(1)} %bitcast.16), custom_call_target="tpu_custom_call" | custom-call | flops 100000000 | bytes 5701632 | tf_op jit(solution)/shard_map/pallas_call | solution.py:167
  138.8 0.0 collective-permute-done.8
  138.8 0.5 collective-permute-done.9
  139.3 0.0 copy-done.1
  139.3 2.7 %add_convert_fusion = bf16[128,3584]{1,0:T(8,128)(2,1)} fusion(bf16[128,3584]{1,0:T(8,128)(2,1)} %collective-permute-done.9, bf16[128,3584]{1,0:T(8,128)(2,1)} %collective-permute-done.8, bf16[128,3584]{1,0:T(8,128)(2,1)S(1)} %copy-done.1), kind=kLoop, calls=%fused_computation | loop fusion | flops 2752512 | bytes 3670016 | tf_op jit(solution)/shard_map/convert_element_type | solution.py:219
  142.0 0.6 collective-permute-start.10
  142.6 5.7 %all-to-all-done.3 = bf16[16,8,3584]{2,1,0:T(8,128)(2,1)S(1)} async-done(((bf16[16,8,3584]{2,1,0:T(8,128)(2,1)}), bf16[16,8,3584]{2,1,0:T(8,128)(2,1)S(1)}, u32[]{:S(2)}, u32[]{:S(2)}) %all-to-all-start.3) | async-done | bytes 917536 | tf_op jit(solution)/shard_map/all_to_all | solution.py:204
  148.2 15.9 %all_to_all.31 = bf16[16,8,3584]{2,1,0:T(8,128)(2,1)S(1)} all-to-all(bf16[16,8,3584]{2,1,0:T(8,128)(2,1)} %bitcast.25), channel_id=1, replica_groups=mesh['dp'=2,'node'=16,'local'=4] {'node'}, dimensions={0} | all-to-all | bytes 1835008 | tf_op jit(solution)/shard_map/all_to_all | solution.py:204
  164.1 0.0 collective-permute-done.10.far
  164.1 2.4 %shard_map.70 = bf16[128,3584]{1,0:T(8,128)(2,1)} custom-call(bf16[256,128]{1,0:T(8,128)(2,1)} %get-tuple-element.39.pick, bf16[128,3584]{1,0:T(8,128)(2,1)S(1)} %bitcast.20, bf16[128,3584]{1,0:T(8,128)(2,1)S(1)} %bitcast.21, bf16[128,3584]{1,0:T(8,128)(2,1)S(1)} %collective-permute-done.10.far), custom_call_target="tpu_custom_call" | custom-call | flops 100000000 | bytes 8454144 | tf_op jit(solution)/shard_map/pallas_call | solution.py:167
Async XLA Ops:
  28.0 23.0 %collective-permute-start = (bf16[128,3712]{1,0:T(8,128)(2,1)S(1)}, bf16[128,3712]{1,0:T(8,128)(2,1)}, u32[]{:S(2)}, u32[]{:S(2)}) collective-permute-start(bf16[128,3712]{1,0:T(8,128)(2,1)S(1)} %bitcast.17), channel_id=1, source_target_pairs={{0,1},{1,2},{2,3},{3,0},{4,5},{5,6},{6,7},{7,4},{8,9},{9,10},{10,1... | collective-permute-start | bytes 2850824 | tf_op jit(solution)/shard_map/ppermute | solution.py:207
  29.6 21.5 %collective-permute-start.1 = (bf16[128,3712]{1,0:T(8,128)(2,1)S(1)}, bf16[128,3712]{1,0:T(8,128)(2,1)}, u32[]{:S(2)}, u32[]{:S(2)}) collective-permute-start(bf16[128,3712]{1,0:T(8,128)(2,1)S(1)} %bitcast.18), channel_id=1, source_target_pairs={{0,3},{1,0},{2,1},{3,2},{4,7},{5,4},{6,5},{7,6},{8,11},{9,8},{10,9... | collective-permute-start | bytes 2850824 | tf_op jit(solution)/shard_map/ppermute | solution.py:207
  31.3 18.6 %all-to-all-start.1 = ((bf16[16,8,3712]{2,1,0:T(8,128)(2,1)}), bf16[16,8,3712]{2,1,0:T(8,128)(2,1)S(1)}, u32[]{:S(2)}, u32[]{:S(2)}) async-start(bf16[16,8,3712]{2,1,0:T(8,128)(2,1)} %bitcast.26), calls=%async_computation.1 | async-start | bytes 1900544 | tf_op jit(solution)/shard_map/all_to_all | solution.py:204
  51.1 21.0 %collective-permute-start.3 = (bf16[128,3712]{1,0:T(8,128)(2,1)S(1)}, bf16[128,3712]{1,0:T(8,128)(2,1)S(1)}, u32[]{:S(2)}, u32[]{:S(2)}) collective-permute-start(bf16[128,3712]{1,0:T(8,128)(2,1)S(1)} %bitcast.22), channel_id=1, source_target_pairs={{0,3},{1,0},{2,1},{3,2},{4,7},{5,4},{6,5},{7,6},{8,11},{9,8},{10,9... | collective-permute-start | bytes 2850824 | tf_op jit(solution)/shard_map/ppermute | solution.py:207
  54.0 21.7 %collective-permute-start.2 = (bf16[128,3712]{1,0:T(8,128)(2,1)}, bf16[128,3712]{1,0:T(8,128)(2,1)S(1)}, u32[]{:S(2)}, u32[]{:S(2)}) collective-permute-start(bf16[128,3712]{1,0:T(8,128)(2,1)} %collective-permute-done.refs_0_), channel_id=1, source_target_pairs={{0,1},{1,2},{2,3},{3,0},{4,5},{5,6},{6,7},{7,4},{8,9},{9,10},{10,1... | collective-permute-start | bytes 2850824 | tf_op jit(solution)/shard_map/ppermute | solution.py:207
  70.7 21.2 %copy-start = (bf16[128,3584]{1,0:T(8,128)(2,1)}, bf16[128,3584]{1,0:T(8,128)(2,1)S(1)}, u32[]{:S(2)}) copy-start(bf16[128,3584]{1,0:T(8,128)(2,1)S(1)} %get-tuple-element.66) | copy-start | bytes 2752516
  75.7 25.0 %collective-permute-start.4 = (bf16[128,3712]{1,0:T(8,128)(2,1)S(1)}, bf16[128,3712]{1,0:T(8,128)(2,1)}, u32[]{:S(2)}, u32[]{:S(2)}) collective-permute-start(bf16[128,3712]{1,0:T(8,128)(2,1)S(1)} %bitcast.24), channel_id=1, source_target_pairs={{0,1},{1,2},{2,3},{3,0},{4,5},{5,6},{6,7},{7,4},{8,9},{9,10},{10,1... | collective-permute-start | bytes 2850824 | tf_op jit(solution)/shard_map/ppermute | solution.py:207
  75.7 25.0 %collective-permute-start.5 = (bf16[128,3712]{1,0:T(8,128)(2,1)S(1)}, bf16[128,3712]{1,0:T(8,128)(2,1)}, u32[]{:S(2)}, u32[]{:S(2)}) collective-permute-start(bf16[128,3712]{1,0:T(8,128)(2,1)S(1)} %collective-permute-done.3.refs_1_), channel_id=1, source_target_pairs={{0,3},{1,0},{2,1},{3,2},{4,7},{5,4},{6,5},{7,6},{8,11},{9,8},{10,9... | collective-permute-start | bytes 2850824 | tf_op jit(solution)/shard_map/ppermute | solution.py:207
  91.9 27.6 %collective-permute-start.6 = (bf16[128,3584]{1,0:T(8,128)(2,1)}, bf16[128,3584]{1,0:T(8,128)(2,1)}, u32[]{:S(2)}, u32[]{:S(2)}) collective-permute-start(bf16[128,3584]{1,0:T(8,128)(2,1)} %get-tuple-element.59), channel_id=1, source_target_pairs={{0,3},{1,0},{2,1},{3,2},{4,7},{5,4},{6,5},{7,6},{8,11},{9,8},{10,9... | collective-permute-start | bytes 2752520 | tf_op jit(solution)/shard_map/ppermute | solution.py:207
  91.9 27.6 %collective-permute-start.7 = (bf16[128,3584]{1,0:T(8,128)(2,1)}, bf16[128,3584]{1,0:T(8,128)(2,1)}, u32[]{:S(2)}, u32[]{:S(2)}) collective-permute-start(bf16[128,3584]{1,0:T(8,128)(2,1)} %get-tuple-element.60), channel_id=1, source_target_pairs={{0,1},{1,2},{2,3},{3,0},{4,5},{5,6},{6,7},{7,4},{8,9},{9,10},{10,1... | collective-permute-start | bytes 2752520 | tf_op jit(solution)/shard_map/ppermute | solution.py:207
  93.9 20.9 %all-to-all-start.2 = ((bf16[16,8,3712]{2,1,0:T(8,128)(2,1)}), bf16[16,8,3712]{2,1,0:T(8,128)(2,1)}, u32[]{:S(2)}, u32[]{:S(2)}) async-start(bf16[16,8,3712]{2,1,0:T(8,128)(2,1)} %bitcast.7), calls=%async_computation.2 | async-start | bytes 1900544 | tf_op jit(solution)/shard_map/all_to_all | solution.py:204
  114.8 17.4 %all-to-all-start.4 = ((bf16[16,8,3712]{2,1,0:T(8,128)(2,1)}), bf16[16,8,3712]{2,1,0:T(8,128)(2,1)S(1)}, u32[]{:S(2)}, u32[]{:S(2)}) async-start(bf16[16,8,3712]{2,1,0:T(8,128)(2,1)} %bitcast.11), calls=%async_computation.4 | async-start | bytes 1900544 | tf_op jit(solution)/shard_map/all_to_all | solution.py:204
  119.5 19.3 %collective-permute-start.8 = (bf16[128,3584]{1,0:T(8,128)(2,1)}, bf16[128,3584]{1,0:T(8,128)(2,1)}, u32[]{:S(2)}, u32[]{:S(2)}) collective-permute-start(bf16[128,3584]{1,0:T(8,128)(2,1)} %get-tuple-element.67), channel_id=1, source_target_pairs={{0,3},{1,0},{2,1},{3,2},{4,7},{5,4},{6,5},{7,6},{8,11},{9,8},{10,9... | collective-permute-start | bytes 2752520 | tf_op jit(solution)/shard_map/ppermute | solution.py:207
  122.4 16.9 %collective-permute-start.9 = (bf16[128,3584]{1,0:T(8,128)(2,1)}, bf16[128,3584]{1,0:T(8,128)(2,1)}, u32[]{:S(2)}, u32[]{:S(2)}) collective-permute-start(bf16[128,3584]{1,0:T(8,128)(2,1)} %get-tuple-element.68), channel_id=1, source_target_pairs={{0,1},{1,2},{2,3},{3,0},{4,5},{5,6},{6,7},{7,4},{8,9},{9,10},{10,1... | collective-permute-start | bytes 2752520 | tf_op jit(solution)/shard_map/ppermute | solution.py:207
  132.2 16.1 %all-to-all-start.3 = ((bf16[16,8,3584]{2,1,0:T(8,128)(2,1)}), bf16[16,8,3584]{2,1,0:T(8,128)(2,1)S(1)}, u32[]{:S(2)}, u32[]{:S(2)}) async-start(bf16[16,8,3584]{2,1,0:T(8,128)(2,1)} %fusion), calls=%async_computation.3 | async-start | bytes 1835008 | tf_op jit(solution)/shard_map/all_to_all | solution.py:204
  135.8 3.5 %copy-start.1 = (bf16[128,3584]{1,0:T(8,128)(2,1)S(1)}, bf16[128,3584]{1,0:T(8,128)(2,1)}, u32[]{:S(2)}) copy-start(bf16[128,3584]{1,0:T(8,128)(2,1)} %copy-done) | copy-start | bytes 2752516
  142.0 22.1 %collective-permute-start.10 = (bf16[128,3584]{1,0:T(8,128)(2,1)}, bf16[128,3584]{1,0:T(8,128)(2,1)S(1)}, u32[]{:S(2)}, u32[]{:S(2)}) collective-permute-start(bf16[128,3584]{1,0:T(8,128)(2,1)} %shard_map.69), channel_id=1, source_target_pairs={{0,2},{1,3},{2,0},{3,1},{4,6},{5,7},{6,4},{7,5},{8,10},{9,11},{10,... | collective-permute-start | bytes 2752520 | tf_op jit(solution)/shard_map/ppermute | solution.py:207

commit v16 on v15

--- a/solution.py
+++ b/solution.py
@@ -10,6 +10,7 @@
 LANES = 128
 PIECE = 128
 VMEM = 60 * 1024 * 1024
+PREPARE_VMEM = 34 * 1024 * 1024
 EXPERT_VMEM = 48 * 1024 * 1024
 
 
@@ -86,7 +87,7 @@
             jax.ShapeDtypeStruct((slots // 2, width + LANES), jnp.bfloat16),
             jax.ShapeDtypeStruct((slots, count), jnp.bfloat16),
         ],
-        compiler_params=pltpu.CompilerParams(vmem_limit_bytes=VMEM),
+        compiler_params=pltpu.CompilerParams(vmem_limit_bytes=PREPARE_VMEM),
         cost_estimate=pl.CostEstimate(flops=10**9, bytes_accessed=3 * 10**6, transcendentals=0),
     )(tokens, gate_scores.T, expert_ids.T)
 

time: 167 us -> 168 us (level)
  local copies, waits for them, and re-layouts: 0.01 us -> 2.55 us
    unnamed x4 -> x12, local copies, waits for them, and re-layouts: 0.01 us -> 2.55 us
where the time goes in v16:
time: 168 us; the launch traced here: 167 us
  Pallas kernels  61.1 us (36%)
  blocking collectives  39.7 us (24%)
  starting transfers between devices  31.1 us (19%)
  waiting for transfers between devices  27.2 us (16%)
  other arithmetic  5.45 us (3%)
  local copies, waits for them, and re-layouts  2.55 us (2%)
    pallas_call x4, Pallas kernels, experts(): pl.pallas_call(functools.partial(expert_kernel, blocks), grid=(hidden //...  53.3 us
    all_to_all x2, blocking collectives, across(): return lax.all_to_all(parts, 'node', 0, 0, tiled=True).reshape(block.shape)  39.7 us
    all_to_all x4, waiting for transfers between devices, across(): return lax.all_to_all(parts, 'node', 0, 0, tiled=True).reshape(block.shape)  17.9 us
    all_to_all x4, starting transfers between devices, across(): return lax.all_to_all(parts, 'node', 0, 0, tiled=True).reshape(block.shape)  16.1 us
    ppermute x11, starting transfers between devices, shift(): lax.ppermute(block, 'local', [(i, (i + by) % locals_) for i in range(loca...  15 us
    ppermute x11, waiting for transfers between devices, shift(): lax.ppermute(block, 'local', [(i, (i + by) % locals_) for i in range(loca...  9.27 us
    pallas_call x2, Pallas kernels, whole(): pl.pallas_call(kernel, out_shape=shapes, compiler_params=pltpu.CompilerPa...  5.37 us
  transfers between devices with their start and end apart: 15, of which 8 were waited for; matrix products, arithmetic and copies ran while one was open for 3% of the time, Pallas kernels for 34%

profile of v16, /device:TPU:0, one launch (start us, length us, event | category | flops | bytes accessed | tf_op | source)
XLA Modules:
  0.0 167.3 jit_solution(16404202715742529350)
XLA Ops:
  0.0 0.0 copy-start.3
  0.0 1.2 copy-done.3
  1.2 0.0 copy-start.4
  1.2 0.7 copy-done.4
  1.9 0.0 copy-start.5
  1.9 0.7 copy-done.5
  2.5 2.4 %shard_map.64 = (bf16[128,3712]{1,0:T(8,128)(2,1)S(1)}, bf16[128,3712]{1,0:T(8,128)(2,1)}, bf16[256,128]{1,0:T(8,128)(2,1)S(1)}) custom-call(bf16[128,3584]{1,0:T(8,128)(2,1)S(1)} %copy-done.3, f32[4,128]{1,0:T(4,128)S(1)} %bitcast.26, s32[4,128]{1,0:T(4,128)S(1)} %bitcast.27), custom_call_target="tpu_custom_call" | custom-call | flops 1000000000 | bytes 3000000 | tf_op jit(solution)/shard_map/pallas_call | solution.py:83
  5.0 0.0 copy-start.2
  5.0 23.8 %all_to_all.30 = bf16[16,8,3712]{2,1,0:T(8,128)(2,1)S(1)} all-to-all(bf16[16,8,3712]{2,1,0:T(8,128)(2,1)S(1)} %bitcast.25), channel_id=1, replica_groups=mesh['dp'=2,'node'=16,'local'=4] {'node'}, dimensions={0} | all-to-all | bytes 1900544 | tf_op jit(solution)/shard_map/all_to_all | solution.py:205
  28.8 0.0 copy-done.2
  28.8 1.6 collective-permute-start
  30.4 1.7 collective-permute-start.1
  32.1 3.6 %all-to-all-start.1 = ((bf16[16,8,3712]{2,1,0:T(8,128)(2,1)}), bf16[16,8,3712]{2,1,0:T(8,128)(2,1)S(1)}, u32[]{:S(2)}, u32[]{:S(2)}) async-start(bf16[16,8,3712]{2,1,0:T(8,128)(2,1)} %bitcast.4), calls=%async_computation.1 | async-start | bytes 1900544 | tf_op jit(solution)/shard_map/all_to_all | solution.py:205
  35.7 9.6 %shard_map.65 = bf16[128,3584]{1,0:T(8,128)(2,1)S(1)} custom-call(s32[1]{0:T(128)} %bitcast.6.local_ref, bf16[128,3712]{1,0:T(8,128)(2,1)S(1)} %bitcast.19, bf16[1,3584,1024]{2,1,0:T(8,128)(2,1)} %refs_2_.5, bf16[1,3584,1024]{2,1,0:T(8,128)(2,1)} %refs_3_.7, bf16[1,1024,3584]{2,1,0:T(8,128)(2,1)} %refs_4_.5), custom_call_target="tpu_custom_call" | custom-call | flops 2818572288 | bytes 22020096 | tf_op jit(solution)/shard_map/pallas_call | solution.py:139
  45.4 5.3 %all-to-all-done.1 = bf16[16,8,3712]{2,1,0:T(8,128)(2,1)S(1)} async-done(((bf16[16,8,3712]{2,1,0:T(8,128)(2,1)}), bf16[16,8,3712]{2,1,0:T(8,128)(2,1)S(1)}, u32[]{:S(2)}, u32[]{:S(2)}) %all-to-all-start.1) | async-done | bytes 950304 | tf_op jit(solution)/shard_map/all_to_all | solution.py:205
  50.7 1.2 collective-permute-done.refs_0_
  51.9 0.0 collective-permute-done.1.refs_1_
  51.9 2.9 %collective-permute-start.3 = (bf16[128,3712]{1,0:T(8,128)(2,1)S(1)}, bf16[128,3712]{1,0:T(8,128)(2,1)S(1)}, u32[]{:S(2)}, u32[]{:S(2)}) collective-permute-start(bf16[128,3712]{1,0:T(8,128)(2,1)S(1)} %bitcast.22), channel_id=1, source_target_pairs={{0,3},{1,0},{2,1},{3,2},{4,7},{5,4},{6,5},{7,6},{8,11},{9,8},{10,9... | collective-permute-start | bytes 2850824 | tf_op jit(solution)/shard_map/ppermute | solution.py:208
  54.8 0.0 collective-permute-start.2
  54.8 16.7 %shard_map.66 = (bf16[128,3584]{1,0:T(8,128)(2,1)}, bf16[128,3584]{1,0:T(8,128)(2,1)}, bf16[128,3584]{1,0:T(8,128)(2,1)S(1)}) custom-call(s32[1]{0:T(128)} %bitcast.6.local_ref, bf16[128,3712]{1,0:T(8,128)(2,1)} %collective-permute-done.refs_0_, bf16[128,3712]{1,0:T(8,128)(2,1)} %collective-permute-done.1.refs_1_, bf16[128,3712]{1,0:T(8,128)(2,1)S(1)} %bitcast.23, ...), custom_call_target="tpu_custom_call" | custom-call | flops 8455716864 | bytes 22020096 | tf_op jit(solution)/shard_map/pallas_call | solution.py:139
  71.5 0.0 copy-start
  71.5 1.3 collective-permute-done.3.refs_1_
  72.9 3.6 %collective-permute-done.2.refs_0_ = bf16[128,3712]{1,0:T(8,128)(2,1)S(1)} collective-permute-done((bf16[128,3712]{1,0:T(8,128)(2,1)}, bf16[128,3712]{1,0:T(8,128)(2,1)S(1)}, u32[]{:S(2)}, u32[]{:S(2)}) %collective-permute-start.2) | collective-permute-done | bytes 950304 | tf_op jit(solution)/shard_map/ppermute | solution.py:208
  76.5 0.0 collective-permute-start.4
  76.5 3.2 %collective-permute-start.5 = (bf16[128,3712]{1,0:T(8,128)(2,1)S(1)}, bf16[128,3712]{1,0:T(8,128)(2,1)}, u32[]{:S(2)}, u32[]{:S(2)}) collective-permute-start(bf16[128,3712]{1,0:T(8,128)(2,1)S(1)} %collective-permute-done.3.refs_1_), channel_id=1, source_target_pairs={{0,3},{1,0},{2,1},{3,2},{4,7},{5,4},{6,5},{7,6},{8,11},{9,8},{10,9... | collective-permute-start | bytes 2850824 | tf_op jit(solution)/shard_map/ppermute | solution.py:208
  79.7 12.9 %shard_map.67 = (bf16[128,3712]{1,0:T(8,128)(2,1)}, bf16[128,3584]{1,0:T(8,128)(2,1)}) custom-call(s32[1]{0:T(128)} %bitcast.6.local_ref, bf16[128,3712]{1,0:T(8,128)(2,1)S(1)} %collective-permute-done.2.refs_0_, bf16[128,3712]{1,0:T(8,128)(2,1)S(1)} %collective-permute-done.3.refs_1_, bf16[1,3584,1024]{2,1,0:T(8,128)(2,1)} %refs_2_.5, ...), custom_call_target="tpu_custom_call" | custom-call | flops 5637144576 | bytes 22020096 | tf_op jit(solution)/shard_map/pallas_call | solution.py:139
  92.6 0.0 copy-done
  92.6 0.0 collective-permute-start.6
  92.6 2.0 %collective-permute-start.7 = (bf16[128,3584]{1,0:T(8,128)(2,1)}, bf16[128,3584]{1,0:T(8,128)(2,1)}, u32[]{:S(2)}, u32[]{:S(2)}) collective-permute-start(bf16[128,3584]{1,0:T(8,128)(2,1)} %get-tuple-element.60), channel_id=1, source_target_pairs={{0,1},{1,2},{2,3},{3,0},{4,5},{5,6},{6,7},{7,4},{8,9},{9,10},{10,1... | collective-permute-start | bytes 2752520 | tf_op jit(solution)/shard_map/ppermute | solution.py:208
  94.7 4.3 %all-to-all-start.2 = ((bf16[16,8,3712]{2,1,0:T(8,128)(2,1)}), bf16[16,8,3712]{2,1,0:T(8,128)(2,1)}, u32[]{:S(2)}, u32[]{:S(2)}) async-start(bf16[16,8,3712]{2,1,0:T(8,128)(2,1)} %bitcast.7), calls=%async_computation.2 | async-start | bytes 1900544 | tf_op jit(solution)/shard_map/all_to_all | solution.py:205
  99.0 2.6 %collective-permute-done.4.refs_0_ = bf16[128,3712]{1,0:T(8,128)(2,1)} collective-permute-done((bf16[128,3712]{1,0:T(8,128)(2,1)S(1)}, bf16[128,3712]{1,0:T(8,128)(2,1)}, u32[]{:S(2)}, u32[]{:S(2)}) %collective-permute-start.4) | collective-permute-done | bytes 950304 | tf_op jit(solution)/shard_map/ppermute | solution.py:208
  101.5 0.0 collective-permute-done.5.refs_1_
  101.5 14.1 %shard_map.68 = (bf16[128,3584]{1,0:T(8,128)(2,1)}, bf16[128,3712]{1,0:T(8,128)(2,1)}) custom-call(s32[1]{0:T(128)} %bitcast.6.local_ref, bf16[128,3712]{1,0:T(8,128)(2,1)} %collective-permute-done.4.refs_0_, bf16[128,3712]{1,0:T(8,128)(2,1)} %collective-permute-done.5.refs_1_, bf16[1,3584,1024]{2,1,0:T(8,128)(2,1)} %refs_2_.5, ...), custom_call_target="tpu_custom_call" | custom-call | flops 5637144576 | bytes 22020096 | tf_op jit(solution)/shard_map/pallas_call | solution.py:139
  115.6 0.0 all-to-all-done.2
  115.6 4.6 %all-to-all-start.4 = ((bf16[16,8,3712]{2,1,0:T(8,128)(2,1)}), bf16[16,8,3712]{2,1,0:T(8,128)(2,1)S(1)}, u32[]{:S(2)}, u32[]{:S(2)}) async-start(bf16[16,8,3712]{2,1,0:T(8,128)(2,1)} %bitcast.11), calls=%async_computation.4 | async-start | bytes 1900544 | tf_op jit(solution)/shard_map/all_to_all | solution.py:205
  120.2 0.0 collective-permute-done.6
  120.2 0.0 collective-permute-done.7
  120.2 3.0 %collective-permute-start.8 = (bf16[128,3584]{1,0:T(8,128)(2,1)}, bf16[128,3584]{1,0:T(8,128)(2,1)}, u32[]{:S(2)}, u32[]{:S(2)}) collective-permute-start(bf16[128,3584]{1,0:T(8,128)(2,1)} %get-tuple-element.67), channel_id=1, source_target_pairs={{0,3},{1,0},{2,1},{3,2},{4,7},{5,4},{6,5},{7,6},{8,11},{9,8},{10,9... | collective-permute-start | bytes 2752520 | tf_op jit(solution)/shard_map/ppermute | solution.py:208
  123.2 0.0 collective-permute-start.9
  123.2 2.7 %fusion = bf16[16,8,3584]{2,1,0:T(8,128)(2,1)} fusion(bf16[128,3584]{1,0:T(8,128)(2,1)} %collective-permute-done.7, bf16[128,3584]{1,0:T(8,128)(2,1)} %collective-permute-done.6, bf16[128,3584]{1,0:T(8,128)(2,1)S(1)} %shard_map.65), kind=kLoop, calls=%fused_computation.2 | loop fusion | flops 2752512 | bytes 3670016 | tf_op jit(solution)/shard_map/reshape | solution.py:204
  125.9 7.0 %all-to-all-done.4 = bf16[16,8,3712]{2,1,0:T(8,128)(2,1)S(1)} async-done(((bf16[16,8,3712]{2,1,0:T(8,128)(2,1)}), bf16[16,8,3712]{2,1,0:T(8,128)(2,1)S(1)}, u32[]{:S(2)}, u32[]{:S(2)}) %all-to-all-start.4) | async-done | bytes 950304 | tf_op jit(solution)/shard_map/all_to_all | solution.py:205
  132.9 3.6 %all-to-all-start.3 = ((bf16[16,8,3584]{2,1,0:T(8,128)(2,1)}), bf16[16,8,3584]{2,1,0:T(8,128)(2,1)S(1)}, u32[]{:S(2)}, u32[]{:S(2)}) async-start(bf16[16,8,3584]{2,1,0:T(8,128)(2,1)} %fusion), calls=%async_computation.3 | async-start | bytes 1835008 | tf_op jit(solution)/shard_map/all_to_all | solution.py:205
  136.5 0.0 copy-start.1
  136.5 2.9 %shard_map.69 = bf16[128,3584]{1,0:T(8,128)(2,1)} custom-call(bf16[128,3712]{1,0:T(8,128)(2,1)} %bitcast.8.first, bf16[128,3712]{1,0:T(8,128)(2,1)S(1)} %bitcast.16), custom_call_target="tpu_custom_call" | custom-call | flops 100000000 | bytes 5701632 | tf_op jit(solution)/shard_map/pallas_call | solution.py:168
  139.5 0.0 collective-permute-done.8
  139.5 0.5 collective-permute-done.9
  140.0 0.0 copy-done.1
  140.0 2.7 %add_convert_fusion = bf16[128,3584]{1,0:T(8,128)(2,1)} fusion(bf16[128,3584]{1,0:T(8,128)(2,1)} %collective-permute-done.9, bf16[128,3584]{1,0:T(8,128)(2,1)} %collective-permute-done.8, bf16[128,3584]{1,0:T(8,128)(2,1)S(1)} %copy-done.1), kind=kLoop, calls=%fused_computation | loop fusion | flops 2752512 | bytes 3670016 | tf_op jit(solution)/shard_map/convert_element_type | solution.py:220
  142.8 0.6 collective-permute-start.10
  143.3 5.6 %all-to-all-done.3 = bf16[16,8,3584]{2,1,0:T(8,128)(2,1)S(1)} async-done(((bf16[16,8,3584]{2,1,0:T(8,128)(2,1)}), bf16[16,8,3584]{2,1,0:T(8,128)(2,1)S(1)}, u32[]{:S(2)}, u32[]{:S(2)}) %all-to-all-start.3) | async-done | bytes 917536 | tf_op jit(solution)/shard_map/all_to_all | solution.py:205
  148.9 15.9 %all_to_all.31 = bf16[16,8,3584]{2,1,0:T(8,128)(2,1)S(1)} all-to-all(bf16[16,8,3584]{2,1,0:T(8,128)(2,1)} %bitcast.28), channel_id=1, replica_groups=mesh['dp'=2,'node'=16,'local'=4] {'node'}, dimensions={0} | all-to-all | bytes 1835008 | tf_op jit(solution)/shard_map/all_to_all | solution.py:205
  164.8 0.0 collective-permute-done.10.far
  164.8 2.4 %shard_map.70 = bf16[128,3584]{1,0:T(8,128)(2,1)} custom-call(bf16[256,128]{1,0:T(8,128)(2,1)} %copy-done.2, bf16[128,3584]{1,0:T(8,128)(2,1)S(1)} %bitcast.20, bf16[128,3584]{1,0:T(8,128)(2,1)S(1)} %bitcast.21, bf16[128,3584]{1,0:T(8,128)(2,1)S(1)} %collective-permute-done.10.far), custom_call_target="tpu_custom_call" | custom-call | flops 100000000 | bytes 8454144 | tf_op jit(solution)/shard_map/pallas_call | solution.py:168
Async XLA Ops:
  0.0 1.2 copy-start.3
  1.2 0.7 copy-start.4
  1.9 0.7 copy-start.5
  5.0 23.8 %copy-start.2 = (bf16[256,128]{1,0:T(8,128)(2,1)}, bf16[256,128]{1,0:T(8,128)(2,1)S(1)}, u32[]{:S(2)}) copy-start(bf16[256,128]{1,0:T(8,128)(2,1)S(1)} %get-tuple-element.39.pick) | copy-start | bytes 196612
  28.8 23.0 %collective-permute-start = (bf16[128,3712]{1,0:T(8,128)(2,1)S(1)}, bf16[128,3712]{1,0:T(8,128)(2,1)}, u32[]{:S(2)}, u32[]{:S(2)}) collective-permute-start(bf16[128,3712]{1,0:T(8,128)(2,1)S(1)} %bitcast.17), channel_id=1, source_target_pairs={{0,1},{1,2},{2,3},{3,0},{4,5},{5,6},{6,7},{7,4},{8,9},{9,10},{10,1... | collective-permute-start | bytes 2850824 | tf_op jit(solution)/shard_map/ppermute | solution.py:208
  30.4 21.5 %collective-permute-start.1 = (bf16[128,3712]{1,0:T(8,128)(2,1)S(1)}, bf16[128,3712]{1,0:T(8,128)(2,1)}, u32[]{:S(2)}, u32[]{:S(2)}) collective-permute-start(bf16[128,3712]{1,0:T(8,128)(2,1)S(1)} %bitcast.18), channel_id=1, source_target_pairs={{0,3},{1,0},{2,1},{3,2},{4,7},{5,4},{6,5},{7,6},{8,11},{9,8},{10,9... | collective-permute-start | bytes 2850824 | tf_op jit(solution)/shard_map/ppermute | solution.py:208
  32.1 18.6 %all-to-all-start.1 = ((bf16[16,8,3712]{2,1,0:T(8,128)(2,1)}), bf16[16,8,3712]{2,1,0:T(8,128)(2,1)S(1)}, u32[]{:S(2)}, u32[]{:S(2)}) async-start(bf16[16,8,3712]{2,1,0:T(8,128)(2,1)} %bitcast.4), calls=%async_computation.1 | async-start | bytes 1900544 | tf_op jit(solution)/shard_map/all_to_all | solution.py:205
  51.9 21.0 %collective-permute-start.3 = (bf16[128,3712]{1,0:T(8,128)(2,1)S(1)}, bf16[128,3712]{1,0:T(8,128)(2,1)S(1)}, u32[]{:S(2)}, u32[]{:S(2)}) collective-permute-start(bf16[128,3712]{1,0:T(8,128)(2,1)S(1)} %bitcast.22), channel_id=1, source_target_pairs={{0,3},{1,0},{2,1},{3,2},{4,7},{5,4},{6,5},{7,6},{8,11},{9,8},{10,9... | collective-permute-start | bytes 2850824 | tf_op jit(solution)/shard_map/ppermute | solution.py:208
  54.8 21.7 %collective-permute-start.2 = (bf16[128,3712]{1,0:T(8,128)(2,1)}, bf16[128,3712]{1,0:T(8,128)(2,1)S(1)}, u32[]{:S(2)}, u32[]{:S(2)}) collective-permute-start(bf16[128,3712]{1,0:T(8,128)(2,1)} %collective-permute-done.refs_0_), channel_id=1, source_target_pairs={{0,1},{1,2},{2,3},{3,0},{4,5},{5,6},{6,7},{7,4},{8,9},{9,10},{10,1... | collective-permute-start | bytes 2850824 | tf_op jit(solution)/shard_map/ppermute | solution.py:208
  71.5 21.1 %copy-start = (bf16[128,3584]{1,0:T(8,128)(2,1)}, bf16[128,3584]{1,0:T(8,128)(2,1)S(1)}, u32[]{:S(2)}) copy-start(bf16[128,3584]{1,0:T(8,128)(2,1)S(1)} %get-tuple-element.66) | copy-start | bytes 2752516
  76.5 25.0 %collective-permute-start.4 = (bf16[128,3712]{1,0:T(8,128)(2,1)S(1)}, bf16[128,3712]{1,0:T(8,128)(2,1)}, u32[]{:S(2)}, u32[]{:S(2)}) collective-permute-start(bf16[128,3712]{1,0:T(8,128)(2,1)S(1)} %bitcast.24), channel_id=1, source_target_pairs={{0,1},{1,2},{2,3},{3,0},{4,5},{5,6},{6,7},{7,4},{8,9},{9,10},{10,1... | collective-permute-start | bytes 2850824 | tf_op jit(solution)/shard_map/ppermute | solution.py:208
  76.5 25.0 %collective-permute-start.5 = (bf16[128,3712]{1,0:T(8,128)(2,1)S(1)}, bf16[128,3712]{1,0:T(8,128)(2,1)}, u32[]{:S(2)}, u32[]{:S(2)}) collective-permute-start(bf16[128,3712]{1,0:T(8,128)(2,1)S(1)} %collective-permute-done.3.refs_1_), channel_id=1, source_target_pairs={{0,3},{1,0},{2,1},{3,2},{4,7},{5,4},{6,5},{7,6},{8,11},{9,8},{10,9... | collective-permute-start | bytes 2850824 | tf_op jit(solution)/shard_map/ppermute | solution.py:208
  92.6 27.6 %collective-permute-start.6 = (bf16[128,3584]{1,0:T(8,128)(2,1)}, bf16[128,3584]{1,0:T(8,128)(2,1)}, u32[]{:S(2)}, u32[]{:S(2)}) collective-permute-start(bf16[128,3584]{1,0:T(8,128)(2,1)} %get-tuple-element.59), channel_id=1, source_target_pairs={{0,3},{1,0},{2,1},{3,2},{4,7},{5,4},{6,5},{7,6},{8,11},{9,8},{10,9... | collective-permute-start | bytes 2752520 | tf_op jit(solution)/shard_map/ppermute | solution.py:208
  92.6 27.6 %collective-permute-start.7 = (bf16[128,3584]{1,0:T(8,128)(2,1)}, bf16[128,3584]{1,0:T(8,128)(2,1)}, u32[]{:S(2)}, u32[]{:S(2)}) collective-permute-start(bf16[128,3584]{1,0:T(8,128)(2,1)} %get-tuple-element.60), channel_id=1, source_target_pairs={{0,1},{1,2},{2,3},{3,0},{4,5},{5,6},{6,7},{7,4},{8,9},{9,10},{10,1... | collective-permute-start | bytes 2752520 | tf_op jit(solution)/shard_map/ppermute | solution.py:208
  94.7 21.0 %all-to-all-start.2 = ((bf16[16,8,3712]{2,1,0:T(8,128)(2,1)}), bf16[16,8,3712]{2,1,0:T(8,128)(2,1)}, u32[]{:S(2)}, u32[]{:S(2)}) async-start(bf16[16,8,3712]{2,1,0:T(8,128)(2,1)} %bitcast.7), calls=%async_computation.2 | async-start | bytes 1900544 | tf_op jit(solution)/shard_map/all_to_all | solution.py:205
  115.6 17.3 %all-to-all-start.4 = ((bf16[16,8,3712]{2,1,0:T(8,128)(2,1)}), bf16[16,8,3712]{2,1,0:T(8,128)(2,1)S(1)}, u32[]{:S(2)}, u32[]{:S(2)}) async-start(bf16[16,8,3712]{2,1,0:T(8,128)(2,1)} %bitcast.11), calls=%async_computation.4 | async-start | bytes 1900544 | tf_op jit(solution)/shard_map/all_to_all | solution.py:205
  120.2 19.3 %collective-permute-start.8 = (bf16[128,3584]{1,0:T(8,128)(2,1)}, bf16[128,3584]{1,0:T(8,128)(2,1)}, u32[]{:S(2)}, u32[]{:S(2)}) collective-permute-start(bf16[128,3584]{1,0:T(8,128)(2,1)} %get-tuple-element.67), channel_id=1, source_target_pairs={{0,3},{1,0},{2,1},{3,2},{4,7},{5,4},{6,5},{7,6},{8,11},{9,8},{10,9... | collective-permute-start | bytes 2752520 | tf_op jit(solution)/shard_map/ppermute | solution.py:208
  123.2 16.9 %collective-permute-start.9 = (bf16[128,3584]{1,0:T(8,128)(2,1)}, bf16[128,3584]{1,0:T(8,128)(2,1)}, u32[]{:S(2)}, u32[]{:S(2)}) collective-permute-start(bf16[128,3584]{1,0:T(8,128)(2,1)} %get-tuple-element.68), channel_id=1, source_target_pairs={{0,1},{1,2},{2,3},{3,0},{4,5},{5,6},{6,7},{7,4},{8,9},{9,10},{10,1... | collective-permute-start | bytes 2752520 | tf_op jit(solution)/shard_map/ppermute | solution.py:208
  132.9 16.1 %all-to-all-start.3 = ((bf16[16,8,3584]{2,1,0:T(8,128)(2,1)}), bf16[16,8,3584]{2,1,0:T(8,128)(2,1)S(1)}, u32[]{:S(2)}, u32[]{:S(2)}) async-start(bf16[16,8,3584]{2,1,0:T(8,128)(2,1)} %fusion), calls=%async_computation.3 | async-start | bytes 1835008 | tf_op jit(solution)/shard_map/all_to_all | solution.py:205
  136.5 3.5 %copy-start.1 = (bf16[128,3584]{1,0:T(8,128)(2,1)S(1)}, bf16[128,3584]{1,0:T(8,128)(2,1)}, u32[]{:S(2)}) copy-start(bf16[128,3584]{1,0:T(8,128)(2,1)} %copy-done) | copy-start | bytes 2752516
  142.8 22.1 %collective-permute-start.10 = (bf16[128,3584]{1,0:T(8,128)(2,1)}, bf16[128,3584]{1,0:T(8,128)(2,1)S(1)}, u32[]{:S(2)}, u32[]{:S(2)}) collective-permute-start(bf16[128,3584]{1,0:T(8,128)(2,1)} %shard_map.69), channel_id=1, source_target_pairs={{0,2},{1,3},{2,0},{3,1},{4,6},{5,7},{6,4},{7,5},{8,10},{9,11},{10,... | collective-permute-start | bytes 2752520 | tf_op jit(solution)/shard_map/ppermute | solution.py:208
